TPU v7x, 32 devices: a whole 2x2x4 slice. The times are simulated.
32 devices in a mesh: wa: 4 (over y, x), ha: 4 (over z), row: 2 (over core).
Axes of the slice: x: 2, y: 2, z: 4, core: 2. Of those that a mesh axis runs over, the one named last changes fastest.
Arguments:
- tokens: bfloat16 [160, 5120], P(('row', 'ha'), 'wa'), may hold values from -6 to 6
- cotangent: bfloat16 [160, 5120], P(('row', 'ha'), 'wa'), may hold values from -6 to 6
- gate_weight: bfloat16 [5120, 13824], P('wa', 'ha'), may hold values from -0.078125 to 0.078125
- up_weight: bfloat16 [5120, 13824], P('wa', 'ha'), may hold values from -0.078125 to 0.078125
- down_weight: bfloat16 [13824, 5120], P('ha', 'wa'), may hold values from -0.0546875 to 0.0546875
Outputs:
- grad_tokens: bfloat16 [160, 5120], P(('row', 'ha'), 'wa')
- grad_gate: bfloat16 [5120, 13824], P('wa', 'ha')
- grad_up: bfloat16 [5120, 13824], P('wa', 'ha')
- grad_down: bfloat16 [13824, 5120], P('ha', 'wa')
All inputs are finite; a program needn't handle non-finite values.
Results may differ from a plain program's by a relative error of at most 0.0059.
Values may be sent and summed in bfloat16 or wider, within the bound.
No kernel may reach another device: no remote copies, remote signals or barrier semaphores. Data moves between devices by JAX's collectives and lax.ppermute only.
A program may use at most 128 MiB of HBM per device.

v0:
```python
import jax
import jax.numpy as jnp
from jax import lax
from jax.sharding import PartitionSpec as P


def pointwise(summed, hidden_width):
    gate_sum = summed[:, :hidden_width]
    up_sum = summed[:, hidden_width : 2 * hidden_width]
    dh_sum = summed[:, 2 * hidden_width :]
    sig = jax.nn.sigmoid(gate_sum)
    active = gate_sum * sig
    hidden = (active * up_sum).astype(jnp.bfloat16)
    d_up = (dh_sum * active).astype(jnp.bfloat16)
    d_gate = (dh_sum * up_sum * sig * (1.0 + gate_sum * (1.0 - sig))).astype(jnp.bfloat16)
    return (hidden, d_gate, d_up)


def body(tokens, cotangent, gate_weight, up_weight, down_weight):
    hidden_width = gate_weight.shape[1]
    rows_in, grads_in = (
        lax.all_gather(tokens, "ha", axis=0, tiled=True),
        lax.all_gather(cotangent, "ha", axis=0, tiled=True),
    )
    contract_last = (((1,), (1,)), ((), ()))
    contract_first = (((0,), (0,)), ((), ()))
    gate_part = jnp.dot(rows_in, gate_weight, preferred_element_type=jnp.float32)
    up_part = jnp.dot(rows_in, up_weight, preferred_element_type=jnp.float32)
    dh_part = lax.dot_general(
        grads_in, down_weight, contract_last, preferred_element_type=jnp.float32
    )
    summed = lax.psum(jnp.concatenate([gate_part, up_part, dh_part], axis=1), "wa")
    hidden, d_gate, d_up = pointwise(summed, hidden_width)
    first_term = lax.dot_general(
        d_gate, gate_weight, contract_last, preferred_element_type=jnp.float32
    )
    second_term = lax.dot_general(
        d_up, up_weight, contract_last, preferred_element_type=jnp.float32
    )
    grad_tokens = lax.psum_scatter(
        first_term + second_term, "ha", scatter_dimension=0, tiled=True
    ).astype(jnp.bfloat16)
    part_gate = lax.dot_general(rows_in, d_gate, contract_first, preferred_element_type=jnp.float32)
    part_up = lax.dot_general(rows_in, d_up, contract_first, preferred_element_type=jnp.float32)
    part_down = lax.dot_general(
        hidden, grads_in, contract_first, preferred_element_type=jnp.float32
    )
    total_gate, total_up, total_down = (
        lax.psum(part_gate.astype(jnp.bfloat16), "row").astype(jnp.float32),
        lax.psum(part_up.astype(jnp.bfloat16), "row").astype(jnp.float32),
        lax.psum(part_down.astype(jnp.bfloat16), "row").astype(jnp.float32),
    )
    return (
        grad_tokens,
        total_gate.astype(jnp.bfloat16),
        total_up.astype(jnp.bfloat16),
        total_down.astype(jnp.bfloat16),
    )


def solution(mesh):
    return jax.shard_map(
        body,
        mesh=mesh,
        in_specs=(
            P(("row", "ha"), "wa"),
            P(("row", "ha"), "wa"),
            P("wa", "ha"),
            P("wa", "ha"),
            P("ha", "wa"),
        ),
        out_specs=(P(("row", "ha"), "wa"), P("wa", "ha"), P("wa", "ha"), P("ha", "wa")),
        check_vma=False,
    )
```

profile of v0, /device:TPU:0, one launch (start us, length us, event | category | flops | bytes accessed | tf_op | source)
XLA Modules:
  0.0 287.1 jit_solution(11726342023124939239)
XLA Ops:
  7.2 0.0 all-reduce.6.cloned.1.call-start
  7.2 15.8 %all-gather = bf16[4,20,1280]{2,1,0:T(8,128)(2,1)S(1)} all-gather(bf16[1,20,1280]{2,1,0:T(8,128)(2,1)} %bitcast.28), channel_id=1, replica_groups=mesh['wa'=4,'ha'=4,'row'=2] {'ha'}, dimensions={0}, use_global_device_ids=true | all-gather | bytes 256000 | tf_op jit(solution)/shard_map/all_gather | solution.py:22
  23.0 14.7 %all-gather.1 = bf16[4,20,1280]{2,1,0:T(8,128)(2,1)S(1)} all-gather(bf16[1,20,1280]{2,1,0:T(8,128)(2,1)} %bitcast.29), channel_id=1, replica_groups=mesh['wa'=4,'ha'=4,'row'=2] {'ha'}, dimensions={0}, use_global_device_ids=true | all-gather | bytes 256000 | tf_op jit(solution)/shard_map/all_gather | solution.py:23
  37.8 0.0 slice-start
  37.8 0.0 slice-start.1
  37.8 0.0 slice-start.2
  37.8 0.0 slice-start.3
  37.8 0.0 slice-start.4
  37.9 5.3 %fusion.7 = f32[80,3456]{1,0:T(8,128)S(1)} fusion(bf16[80,1280]{1,0:T(8,128)(2,1)S(1)} %reshape.9, bf16[1280,3456]{1,0:T(8,128)(2,1)} %param.8), kind=kOutput, calls=%fused_computation.15 | convolution fusion | flops 707788800 | bytes 10158080 | tf_op jit(solution)/shard_map/dot_general | solution.py:28
  43.2 0.0 slice-done
  43.2 0.0 slice-done.1
  43.2 0.7 slice-done.2
  43.9 0.0 slice-start.5
  43.9 1.6 fusion.6
  45.6 0.0 slice-done.3
  45.6 0.7 slice-done.4
  46.3 0.2 slice-done.5
  46.5 2.8 fusion.8
  49.3 1.9 pad_maximum_fusion
  51.2 0.0 all-reduce.6.cloned.1.call-update
  51.2 0.2 all-reduce.8.cloned.1.call-start
  51.5 91.0 %all-reduce.6.cloned.1.call-done = f32[80,10368]{1,0:T(8,128)} async-done(((f32[80,10368]{1,0:T(8,128)}), f32[80,10368]{1,0:T(8,128)}) %all-reduce.6.cloned.1.call-update) | async-done | bytes 3317776 | tf_op jit(solution)/shard_map/psum | solution.py:32
  142.4 2.4 multiply_convert_fusion.1
  144.9 6.1 %fusion.2 = bf16[1280,3456]{0,1:T(8,128)(2,1)} fusion(bf16[80,3456]{1,0:T(8,128)(2,1)S(1)} %get-tuple-element.19, bf16[80,1280]{1,0:T(8,128)(2,1)S(1)} %reshape.9), kind=kOutput, calls=%fused_computation.4 | convolution fusion | flops 712212480 | bytes 9605120 | tf_op jit(solution)/shard_map/dot_general | solution.py:44
  150.9 0.0 copy-start
  150.9 6.1 %fusion.1 = bf16[1280,3456]{0,1:T(8,128)(2,1)} fusion(bf16[80,3456]{1,0:T(8,128)(2,1)S(1)} %get-tuple-element.20, bf16[80,1280]{1,0:T(8,128)(2,1)S(1)} %reshape.9), kind=kOutput, calls=%fused_computation.3 | convolution fusion | flops 712212480 | bytes 9605120 | tf_op jit(solution)/shard_map/dot_general | solution.py:43
  157.0 0.0 copy-done
  157.0 6.1 %convolution_convert_fusion = bf16[3456,1280]{1,0:T(8,128)(2,1)} fusion(bf16[80,1280]{1,0:T(8,128)(2,1)S(1)} %reshape.11, f32[80,10368]{1,0:T(8,128)S(1)} %copy-done), kind=kOutput, calls=%fused_computation | convolution fusion | flops 713871360 | bytes 11264000 | tf_op jit(solution)/shard_map/dot_general | solution.py:45
  163.1 0.0 all-reduce.8.cloned.1.call-update
  163.1 6.0 %fusion.9 = f32[80,1280]{1,0:T(8,128)S(1)} fusion(bf16[80,3456]{1,0:T(8,128)(2,1)S(1)} %get-tuple-element.20, bf16[1280,3456]{1,0:T(8,128)(2,1)} %param.7), kind=kOutput, calls=%fused_computation.17 | convolution fusion | flops 707788800 | bytes 9809920 | tf_op jit(solution)/shard_map/dot_general | solution.py:34
  169.1 0.0 copy-start.1
  169.1 7.4 %convolution_add_fusion = f32[80,1280]{1,0:T(8,128)S(1)} fusion(f32[80,1280]{1,0:T(8,128)S(1)} %fusion.9, bf16[80,3456]{1,0:T(8,128)(2,1)S(1)} %get-tuple-element.19, bf16[1280,3456]{1,0:T(8,128)(2,1)} %param.8), kind=kOutput, calls=%fused_computation.6 | convolution fusion | flops 707891200 | bytes 10219520 | tf_op jit(solution)/shard_map/dot_general | solution.py:37
  176.5 18.5 %fusion = f32[24,1280]{1,0:T(8,128)S(1)} fusion(f32[80,1280]{1,0:T(8,128)S(1)} %convolution_add_fusion), kind=kCustom, calls=%all-reduce-scatter | all-reduce-scatter fusion | flops 122881 | bytes 532992
  195.1 1.8 collective-permute-start
  196.9 0.0 copy-done.1
  196.9 0.6 dynamic-slice.4
  198.2 0.4 collective-permute-done
  198.6 0.1 concatenate.4
  198.7 0.6 dynamic-slice_convert_fusion
  199.4 47.9 %all-reduce.8.cloned.1.call-done = (bf16[1280,3456]{0,1:T(8,128)(2,1)}, bf16[1280,3456]{0,1:T(8,128)(2,1)}, bf16[3456,1280]{1,0:T(8,128)(2,1)}) async-done(((bf16[1280,3456]{0,1:T(8,128)(2,1)}, bf16[1280,3456]{0,1:T(8,128)(2,1)}, bf16[3456,1280]{1,0:T(8,128)(2,1)}), (bf16[1280,3456]{0,1:T(8,128)(2,1)}, bf16[1280,3456]{0,1:T(8,128)(2,1)}, bf16[3456,1280]{1,0:T(8,128)(2,1)})) %all-reduce.8.cloned.1.call-update) | async-done | bytes 26542096 | tf_op jit(solution)/shard_map/psum | solution.py:49
  247.3 12.7 %copy.13 = bf16[1280,3456]{1,0:T(8,128)(2,1)} copy(bf16[1280,3456]{0,1:T(8,128)(2,1)} %get-tuple-element.16) | data formatting | bytes 17694720
  260.0 12.7 %copy.14 = bf16[1280,3456]{1,0:T(8,128)(2,1)} copy(bf16[1280,3456]{0,1:T(8,128)(2,1)} %get-tuple-element.17) | data formatting | bytes 17694720
  272.6 7.6 %copy.19 = bf16[3456,1280]{1,0:T(8,128)(2,1)} copy(bf16[3456,1280]{1,0:T(8,128)(2,1)} %get-tuple-element.24) | data formatting | bytes 17694720
  (5 shorter events, 0.1 us)
Async XLA Ops:
  7.2 135.3 %all-reduce.6.cloned.1.call-start = ((), (), s32[]{:S(2)}) async-start(), calls=%async_computation | async-start | bytes 6635520 | tf_op jit(solution)/shard_map/psum | solution.py:32
  37.8 5.4 %slice-start = ((s8[8847360]{0:T(1024)(128)(4,1)}), s8[458752]{0:T(1024)(128)(4,1)S(1)}, s32[]{:S(2)}) async-start(s8[8847360]{0:T(1024)(128)(4,1)} %bitcast.24), calls=%async_computation.2 | async-start | bytes 917504
  37.8 5.4 %slice-start.1 = ((s8[8847360]{0:T(1024)(128)(4,1)}), s8[4194304]{0:T(1024)(128)(4,1)S(1)}, s32[]{:S(2)}) async-start(s8[8847360]{0:T(1024)(128)(4,1)} %bitcast.24), calls=%async_computation.3 | async-start | bytes 8388608
  37.8 6.1 %slice-start.2 = ((s8[8847360]{0:T(1024)(128)(4,1)}), s8[4194304]{0:T(1024)(128)(4,1)S(1)}, s32[]{:S(2)}) async-start(s8[8847360]{0:T(1024)(128)(4,1)} %bitcast.24), calls=%async_computation.4 | async-start | bytes 8388608
  37.8 7.7 %slice-start.3 = ((s8[8847360]{0:T(1024)(128)(4,1)}), s8[4194304]{0:T(1024)(128)(4,1)S(1)}, s32[]{:S(2)}) async-start(s8[8847360]{0:T(1024)(128)(4,1)} %bitcast.26), calls=%async_computation.5 | async-start | bytes 8388608
  37.8 8.4 %slice-start.4 = ((s8[8847360]{0:T(1024)(128)(4,1)}), s8[4194304]{0:T(1024)(128)(4,1)S(1)}, s32[]{:S(2)}) async-start(s8[8847360]{0:T(1024)(128)(4,1)} %bitcast.26), calls=%async_computation.6 | async-start | bytes 8388608
  43.9 2.6 slice-start.5
  51.2 196.1 %all-reduce.8.cloned.1.call-start = ((), (), s32[]{:S(2)}) async-start(), calls=%async_computation.1 | async-start | bytes 53084160 | tf_op jit(solution)/shard_map/psum | solution.py:49
  150.9 6.1 %copy-start = (f32[80,10368]{1,0:T(8,128)S(1)}, f32[80,10368]{1,0:T(8,128)}, u32[]{:S(2)}) copy-start(f32[80,10368]{1,0:T(8,128)} %all-reduce.6.cloned.1.call-done) | copy-start | bytes 9953284
  169.1 27.8 %copy-start.1 = (u32[32]{0:T(128)S(1)}, u32[32]{0:T(128)}, u32[]{:S(2)}) copy-start(u32[32]{0:T(128)} %constant.6) | copy-start | bytes 388
  195.1 3.5 %collective-permute-start = (bf16[12,1280]{1,0:T(8,128)(2,1)S(1)}, bf16[12,1280]{1,0:T(8,128)(2,1)S(1)}, u32[]{:S(2)}, u32[]{:S(2)}) collective-permute-start(bf16[12,1280]{1,0:T(8,128)(2,1)S(1)} %slice.15), channel_id=1, source_target_pairs={{0,2},{2,4},{4,6},{1,3},{3,5},{5,7},{8,10},{10,12},{12,14},{9,11},... | collective-permute-start | bytes 92168
Sparse Core Ops, SparseCore 0:
  51.4 91.0 all-reduce.5
  163.2 84.0 all-reduce.7
where the time goes:
time: 288 us; the launch traced here: 287 us
  waiting for transfers between devices  139 us (48%)
  blocking collectives  49 us (17%)
  matrix products  41.3 us (14%)
  local copies, waits for them, and re-layouts  36.1 us (13%)
  between operations  14.9 us (5%)
  other arithmetic  4.37 us (2%)
    psum x1, waiting for transfers between devices, body(): lax.psum(jnp.concatenate([gate_part, up_part, dh_part], axis=1), 'wa')  91 us
    psum x1, waiting for transfers between devices, body(): lax.psum(part_gate.astype(jnp.bfloat16), 'row').astype(jnp.float32)  47.9 us
    unnamed x24, local copies, waits for them, and re-layouts  35.5 us
    unnamed x1, blocking collectives  18.5 us
    all_gather x1, blocking collectives, body(): lax.all_gather(tokens, 'ha', axis=0, tiled=True)  15.8 us
    all_gather x1, blocking collectives, body(): lax.all_gather(cotangent, 'ha', axis=0, tiled=True)  14.7 us
    dot_general x1, matrix products, body(): lax.dot_general(d_up, up_weight, contract_last, preferred_element_type=jn...  7.36 us
    dot_general x1, matrix products, body(): lax.dot_general(hidden, grads_in, contract_first, preferred_element_type=...  6.09 us
  transfers between devices with their start and end apart: 3, of which 3 were waited for; matrix products, arithmetic and copies ran while one was open for 12% of the time, Pallas kernels for 0%

commit v1 on v0

v1 whole, which is shorter than its diff:
```python
import functools

import jax
import jax.numpy as jnp
from jax import lax
from jax.experimental import pallas as pl
from jax.experimental.pallas import tpu as pltpu
from jax.sharding import PartitionSpec as P

BF16 = jnp.bfloat16
F32 = jnp.float32
NT = (((1,), (1,)), ((), ()))
TN = (((0,), (0,)), ((), ()))
LANES = 128
CHUNKS = 3
VMEM_LIMIT = 48 * 1024 * 1024


def pointwise(gate_sum, up_sum, dh_sum):
    sig = jax.nn.sigmoid(gate_sum)
    active = gate_sum * sig
    hidden = (active * up_sum).astype(BF16)
    d_up = (dh_sum * active).astype(BF16)
    d_gate = (dh_sum * up_sum * sig * (1.0 + gate_sum * (1.0 - sig))).astype(BF16)
    return (hidden, d_gate, d_up)


def call(kernel, grid, in_specs, out_specs, out_shape, flops, moved, scratch=(), aliases=None):
    return pl.pallas_call(
        kernel,
        grid=grid,
        in_specs=in_specs,
        out_specs=out_specs,
        out_shape=out_shape,
        scratch_shapes=list(scratch),
        input_output_aliases=aliases or {},
        cost_estimate=pl.CostEstimate(flops=flops, bytes_accessed=moved, transcendentals=0),
        compiler_params=pltpu.CompilerParams(vmem_limit_bytes=VMEM_LIMIT),
    )


def whole(shape):
    return pl.BlockSpec(shape, lambda i: (0,) * len(shape))


SCALAR = pl.BlockSpec(memory_space=pltpu.SMEM)


def order_kernel(parts, rows, wa_ref, *refs):
    pieces = [ref[...].astype(F32) for ref in refs[:parts]]
    x_ref, y_ref = refs[parts:]
    wa = wa_ref[0]
    xs, ys = [], []
    for slot in range(parts):
        at = wa ^ slot
        piece = pieces[0]
        for other in range(1, parts):
            piece = jnp.where(at == other, pieces[other], piece)
        xs.append(piece[:rows])
        ys.append(piece[rows:])
    x_ref[...] = jnp.concatenate(xs, axis=0).astype(BF16)
    y_ref[...] = jnp.concatenate(ys, axis=0).astype(BF16)


def order_rows(wa, pieces):
    parts = len(pieces)
    rows, width = pieces[0].shape[0] // 2, pieces[0].shape[1]
    shape = (parts * rows, width)
    return call(
        functools.partial(order_kernel, parts, rows),
        (1,),
        [SCALAR] + [whole((2 * rows, width))] * parts,
        [whole(shape)] * 2,
        [jax.ShapeDtypeStruct(shape, BF16)] * 2,
        0,
        8 * shape[0] * width,
    )(wa, *pieces)


def forward_kernel(parts, rows, x_ref, y_ref, gate_ref, up_ref, down_ref, own_ref, *send_refs):
    gate = jnp.dot(x_ref[...], gate_ref[...], preferred_element_type=F32)
    up = jnp.dot(x_ref[...], up_ref[...], preferred_element_type=F32)
    dh = lax.dot_general(y_ref[...], down_ref[...], NT, preferred_element_type=F32)
    for slot in range(parts):
        cut = slice(slot * rows, (slot + 1) * rows)
        block = jnp.concatenate([gate[cut], up[cut], dh[cut]], axis=0)
        if slot == 0:
            own_ref[...] = block
        else:
            send_refs[slot - 1][...] = block.astype(BF16)


def forward(parts, first, count, tile, x, y, gate_weight, up_weight, down_weight):
    group, width = x.shape
    rows = group // parts
    columns = count * tile
    return call(
        functools.partial(forward_kernel, parts, rows),
        (count,),
        [
            whole((group, width)),
            whole((group, width)),
            pl.BlockSpec((width, tile), lambda i: (0, first + i)),
            pl.BlockSpec((width, tile), lambda i: (0, first + i)),
            pl.BlockSpec((tile, width), lambda i: (first + i, 0)),
        ],
        [pl.BlockSpec((3 * rows, tile), lambda i: (0, i))] * parts,
        [jax.ShapeDtypeStruct((3 * rows, columns), F32)]
        + [jax.ShapeDtypeStruct((3 * rows, columns), BF16)] * (parts - 1),
        6 * group * width * columns,
        6 * width * columns,
    )(x, y, gate_weight, up_weight, down_weight)


def middle_kernel(rows, own_ref, *refs):
    total = own_ref[...]
    for ref in refs[:-1]:
        total = total + ref[...].astype(F32)
    hidden, d_gate, d_up = pointwise(total[:rows], total[rows : 2 * rows], total[2 * rows :])
    refs[-1][...] = jnp.concatenate(
        [d_gate.astype(F32), d_up.astype(F32), hidden.astype(F32)], axis=0
    ).astype(BF16)


def middle(own, received):
    shape = own.shape
    return call(
        functools.partial(middle_kernel, shape[0] // 3),
        (1,),
        [whole(shape)] * (1 + len(received)),
        whole(shape),
        jax.ShapeDtypeStruct(shape, BF16),
        20 * shape[0] * shape[1],
        12 * shape[0] * shape[1],
    )(own, *received)


def stack_kernel(rows, *refs):
    blocks = [ref[...].astype(F32) for ref in refs[:-1]]
    cuts = [
        block[at * rows : (at + 1) * rows] for at in range(3) for block in blocks
    ]
    refs[-1][...] = jnp.concatenate(cuts, axis=0).astype(BF16)


def stack(blocks):
    parts = len(blocks)
    rows, columns = blocks[0].shape[0] // 3, blocks[0].shape[1]
    shape = (3 * parts * rows, columns)
    return call(
        functools.partial(stack_kernel, rows),
        (1,),
        [whole(blocks[0].shape)] * parts,
        whole(shape),
        jax.ShapeDtypeStruct(shape, BF16),
        0,
        4 * shape[0] * columns,
    )(*blocks)


def input_grad_kernel(group, start_ref, d_gate_ref, d_up_ref, gate_ref, up_ref, out_ref):
    @pl.when(pl.program_id(0) == 0)
    def _():
        out_ref[...] = start_ref[...]

    out_ref[...] += lax.dot_general(
        d_gate_ref[...], gate_ref[...], NT, preferred_element_type=F32
    ) + lax.dot_general(d_up_ref[...], up_ref[...], NT, preferred_element_type=F32)


def input_grad(first, count, tile, start, stacked, gate_weight, up_weight):
    group = stacked.shape[0] // 3
    width = gate_weight.shape[0]
    return call(
        functools.partial(input_grad_kernel, group),
        (count,),
        [
            whole((group, width)),
            pl.BlockSpec((group, tile), lambda i: (0, i)),
            pl.BlockSpec((group, tile), lambda i: (1, i)),
            pl.BlockSpec((width, tile), lambda i: (0, first + i)),
            pl.BlockSpec((width, tile), lambda i: (0, first + i)),
        ],
        whole((group, width)),
        jax.ShapeDtypeStruct((group, width), F32),
        4 * group * width * count * tile,
        4 * width * count * tile,
    )(start, stacked, stacked, gate_weight, up_weight)


def weight_grad_kernel(group, has_start, row_ref, xt_ref, y_ref, mine_ref, other_ref, *refs):
    gate_ref, up_ref, down_ref, both = refs[3 * has_start :]
    first = row_ref[0] == 0
    for at in range(3):
        cut = slice(at * group, (at + 1) * group)
        both[at, :group] = jnp.where(first, mine_ref[cut], other_ref[cut])
        both[at, group:] = jnp.where(first, other_ref[cut], mine_ref[cut])
    gate_ref[...] = jnp.dot(xt_ref[...], both[0], preferred_element_type=F32).astype(BF16)
    up_ref[...] = jnp.dot(xt_ref[...], both[1], preferred_element_type=F32).astype(BF16)
    down_ref[...] = lax.dot_general(
        both[2], y_ref[...], TN, preferred_element_type=F32
    ).astype(BF16)


def weight_grad(first, count, tile, hidden_width, row, xt, y, mine, other, start):
    width = xt.shape[0]
    group = mine.shape[0] // 3
    has_start = start is not None
    start = start or ()
    return call(
        functools.partial(weight_grad_kernel, group, has_start),
        (count,),
        [
            SCALAR,
            whole((width, 2 * group)),
            whole((2 * group, width)),
            pl.BlockSpec((3 * group, tile), lambda i: (0, i)),
            pl.BlockSpec((3 * group, tile), lambda i: (0, i)),
        ]
        + [pl.BlockSpec(memory_space=pl.ANY)] * len(start),
        [
            pl.BlockSpec((width, tile), lambda i: (0, first + i)),
            pl.BlockSpec((width, tile), lambda i: (0, first + i)),
            pl.BlockSpec((tile, width), lambda i: (first + i, 0)),
        ],
        [
            jax.ShapeDtypeStruct((width, hidden_width), BF16),
            jax.ShapeDtypeStruct((width, hidden_width), BF16),
            jax.ShapeDtypeStruct((hidden_width, width), BF16),
        ],
        12 * group * width * count * tile,
        6 * width * count * tile,
        scratch=[pltpu.VMEM((3, 2 * group, tile), BF16)],
        aliases={5 + i: i for i in range(len(start))},
    )(row, xt, y, mine, other, *start)


def last_kernel(parts, rows, wa_ref, grad_ref, own_ref, *send_refs):
    grad = grad_ref[...]
    cuts = [grad[slot * rows : (slot + 1) * rows] for slot in range(parts)]
    wa = wa_ref[0]
    for step in range(parts):
        at = wa ^ step
        piece = cuts[0]
        for slot in range(1, parts):
            piece = jnp.where(at == slot, cuts[slot], piece)
        if step == 0:
            own_ref[...] = piece
        else:
            send_refs[step - 1][...] = piece.astype(BF16)


def last_pieces(parts, wa, grad):
    rows, width = grad.shape[0] // parts, grad.shape[1]
    return call(
        functools.partial(last_kernel, parts, rows),
        (1,),
        [SCALAR, whole(grad.shape)],
        [whole((rows, width))] * parts,
        [jax.ShapeDtypeStruct((rows, width), F32)]
        + [jax.ShapeDtypeStruct((rows, width), BF16)] * (parts - 1),
        0,
        8 * grad.shape[0] * width,
    )(wa, grad)


def swap(value, axis, size, step):
    return lax.ppermute(value, axis, [(at, at ^ step) for at in range(size)])


def fast_body(n_wa, n_ha, n_row, tokens, cotangent, gate_weight, up_weight, down_weight):
    rows, width = tokens.shape
    hidden_width = gate_weight.shape[1]
    columns = hidden_width // CHUNKS
    tile = max(t for t in range(LANES, 513, LANES) if columns % t == 0)
    count = columns // tile
    group = n_ha * rows
    wa = lax.axis_index("wa").astype(jnp.int32).reshape(1)
    row = lax.axis_index("row").astype(jnp.int32).reshape(1)

    both = jnp.concatenate([tokens, cotangent], axis=0)
    pieces = [both] + [swap(both, "ha", n_ha, step) for step in range(1, n_ha)]
    x, y = order_rows(wa, pieces)

    blocks = []
    for chunk in range(CHUNKS):
        own, *sends = forward(
            n_wa, chunk * count, count, tile, x, y, gate_weight, up_weight, down_weight
        )
        blocks.append((own, [swap(s, "wa", n_wa, k + 1) for k, s in enumerate(sends)]))

    xy = jnp.concatenate([x, y], axis=0)
    xy_other = swap(xy, "row", n_row, 1)
    first = row[0] == 0
    x_low, x_high = jnp.where(first, xy[:group], xy_other[:group]), jnp.where(first, xy_other[:group], xy[:group])
    y_low, y_high = jnp.where(first, xy[group:], xy_other[group:]), jnp.where(first, xy_other[group:], xy[group:])
    xt = jnp.concatenate([x_low, x_high], axis=0).T
    y_all = jnp.concatenate([y_low, y_high], axis=0)

    gathered = []
    for own, received in blocks:
        mine = middle(own, received)
        gathered.append([mine] + [swap(mine, "wa", n_wa, step) for step in range(1, n_wa)])

    grad = jnp.zeros((group, width), F32)
    stacks = []
    for chunk in range(CHUNKS):
        mine = stack(gathered[chunk])
        stacks.append((mine, swap(mine, "row", n_row, 1)))
        grad = input_grad(chunk * count, count, tile, grad, mine, gate_weight, up_weight)
    own, *sends = last_pieces(n_ha, wa, grad)
    for step, sent in enumerate(sends):
        own = own + swap(sent, "ha", n_ha, step + 1).astype(F32)

    grads = None
    for chunk, (mine, other) in enumerate(stacks):
        grads = weight_grad(
            chunk * count, count, tile, hidden_width, row, xt, y_all, mine, other, grads
        )
    return (own.astype(BF16), *grads)


def plain_body(tokens, cotangent, gate_weight, up_weight, down_weight):
    hidden_width = gate_weight.shape[1]
    x = lax.all_gather(tokens, "ha", axis=0, tiled=True)
    y = lax.all_gather(cotangent, "ha", axis=0, tiled=True)
    gate_part = jnp.dot(x, gate_weight, preferred_element_type=F32)
    up_part = jnp.dot(x, up_weight, preferred_element_type=F32)
    dh_part = lax.dot_general(y, down_weight, NT, preferred_element_type=F32)
    summed = lax.psum(jnp.concatenate([gate_part, up_part, dh_part], axis=1), "wa")
    hidden, d_gate, d_up = pointwise(
        summed[:, :hidden_width],
        summed[:, hidden_width : 2 * hidden_width],
        summed[:, 2 * hidden_width :],
    )
    partial = lax.dot_general(
        d_gate, gate_weight, NT, preferred_element_type=F32
    ) + lax.dot_general(d_up, up_weight, NT, preferred_element_type=F32)
    grad_tokens = lax.psum_scatter(partial, "ha", scatter_dimension=0, tiled=True)
    grads = (
        lax.dot_general(x, d_gate, TN, preferred_element_type=F32),
        lax.dot_general(x, d_up, TN, preferred_element_type=F32),
        lax.dot_general(hidden, y, TN, preferred_element_type=F32),
    )
    return (
        grad_tokens.astype(BF16),
        *(lax.psum(g.astype(BF16), "row").astype(BF16) for g in grads),
    )


def solution(mesh):
    n_wa, n_ha, n_row = (mesh.shape[name] for name in ("wa", "ha", "row"))

    def body(tokens, cotangent, gate_weight, up_weight, down_weight):
        width, hidden_width = gate_weight.shape
        fits = (
            n_wa == n_ha == 4
            and n_row == 2
            and width % LANES == 0
            and hidden_width % (LANES * CHUNKS) == 0
            and (tokens.shape[0] * n_ha) % 16 == 0
        )
        if fits:
            return fast_body(
                n_wa, n_ha, n_row, tokens, cotangent, gate_weight, up_weight, down_weight
            )
        return plain_body(tokens, cotangent, gate_weight, up_weight, down_weight)

    return jax.shard_map(
        body,
        mesh=mesh,
        in_specs=(
            P(("row", "ha"), "wa"),
            P(("row", "ha"), "wa"),
            P("wa", "ha"),
            P("wa", "ha"),
            P("ha", "wa"),
        ),
        out_specs=(P(("row", "ha"), "wa"), P("wa", "ha"), P("wa", "ha"), P("ha", "wa")),
        check_vma=False,
    )
```

time: 288 us -> 106 us (0.37)
  waiting for transfers between devices: 139 us -> 17.7 us
  blocking collectives: 49 us -> 0 us
  Pallas kernels: 0 us -> 46.5 us
  matrix products: 41.3 us -> 0 us
  local copies, waits for them, and re-layouts: 36.1 us -> 1.26 us
  starting transfers between devices: 2.11 us -> 35.4 us
  between operations: 14.9 us -> 0.83 us
    psum x2 -> x0, waiting for transfers between devices: 139 us -> none  [the longest x1 91 us: body(): lax.psum(jnp.concatenate([gate_part, up_part, dh_part], axis=1), 'wa')]
    pallas_call x0 -> x17, Pallas kernels: none -> 46.5 us  [the longest x3 16.1 us: weight_grad(): call(functools.partial(weight_grad_kernel, group, has_start), (count,), [...]
    dot_general x8 -> x0, matrix products: 41.3 us -> none  [the longest x1 7.36 us: body(): lax.dot_general(d_up, up_weight, contract_last, preferred_element_type=jn...]
    unnamed x24 -> x0, local copies, waits for them, and re-layouts: 35.5 us -> none
    ppermute x0 -> x28, starting transfers between devices: none -> 35.4 us  [swap(): return lax.ppermute(value, axis, [(at, at ^ step) for at in range(size)])]
    all_gather x2 -> x0, blocking collectives: 30.5 us -> none  [the longest x1 15.8 us: body(): lax.all_gather(tokens, 'ha', axis=0, tiled=True)]
    unnamed x1 -> x0, blocking collectives: 18.5 us -> none
    ppermute x0 -> x28, waiting for transfers between devices: none -> 17.7 us  [swap(): return lax.ppermute(value, axis, [(at, at ^ step) for at in range(size)])]
  transfers between devices with their start and end apart: 3 -> 28, of which waited for: 3 -> 9; matrix products, arithmetic and copies ran while one was open for 12% -> 4% of each run, Pallas kernels for 0% -> 29%
where the time goes in v1:
time: 106 us
  Pallas kernels  46.5 us (44%)
  starting transfers between devices  35.4 us (33%)
  waiting for transfers between devices  17.7 us (17%)
  other arithmetic  4.22 us (4%)
  local copies, waits for them, and re-layouts  1.26 us (1%)
    ppermute x28, starting transfers between devices, swap(): return lax.ppermute(value, axis, [(at, at ^ step) for at in range(size)])  35.4 us
    ppermute x28, waiting for transfers between devices, swap(): return lax.ppermute(value, axis, [(at, at ^ step) for at in range(size)])  17.7 us
    pallas_call x3, Pallas kernels, weight_grad(): call(functools.partial(weight_grad_kernel, group, has_start), (count,), [...  16.1 us
    pallas_call x3, Pallas kernels, forward(): call(functools.partial(forward_kernel, parts, rows), (count,), [whole((gr...  15.7 us
    pallas_call x3, Pallas kernels, input_grad(): call(functools.partial(input_grad_kernel, group), (count,), [whole((group...  13.8 us
  transfers between devices with their start and end apart: 28, of which 9 were waited for; matrix products, arithmetic and copies ran while one was open for 4% of the time, Pallas kernels for 29%

profile of v1, /device:TPU:0, one launch (start us, length us, event | category | flops | bytes accessed | tf_op | source)
XLA Modules:
  0.0 105.9 jit_solution(11980352169505733011)
XLA Ops:
  0.6 0.9 pad_maximum_fusion.2.refs_0_
  1.5 3.1 %collective-permute-start = (bf16[40,1280]{1,0:T(8,128)(2,1)S(1)}, bf16[40,1280]{1,0:T(8,128)(2,1)S(1)}, u32[]{:S(2)}, u32[]{:S(2)}) collective-permute-start(bf16[40,1280]{1,0:T(8,128)(2,1)S(1)} %pad_maximum_fusion.2.refs_0_), channel_id=1, source_target_pairs={{0,2},{2,0},{4,6},{6,4},{1,3},{3,1},{5,7},{7,5},{8,10},{10,8},{12,... | collective-permute-start | bytes 307208 | tf_op jit(solution)/shard_map/ppermute | solution.py:268
  4.6 2.6 %collective-permute-start.1 = (bf16[40,1280]{1,0:T(8,128)(2,1)S(1)}, bf16[40,1280]{1,0:T(8,128)(2,1)S(1)}, u32[]{:S(2)}, u32[]{:S(2)}) collective-permute-start(bf16[40,1280]{1,0:T(8,128)(2,1)S(1)} %pad_maximum_fusion.2.refs_0_), channel_id=1, source_target_pairs={{0,4},{2,6},{4,0},{6,2},{1,5},{3,7},{5,1},{7,3},{8,12},{10,14},{12... | collective-permute-start | bytes 307208 | tf_op jit(solution)/shard_map/ppermute | solution.py:268
  7.2 0.3 collective-permute-done.refs_1_
  7.5 7.8 %collective-permute-done.1.refs_2_ = bf16[40,1280]{1,0:T(8,128)(2,1)S(1)} collective-permute-done((bf16[40,1280]{1,0:T(8,128)(2,1)S(1)}, bf16[40,1280]{1,0:T(8,128)(2,1)S(1)}, u32[]{:S(2)}, u32[]{:S(2)}) %collective-permute-start.1) | collective-permute-done | bytes 102432 | tf_op jit(solution)/shard_map/ppermute | solution.py:268
  15.3 0.2 shard_map.84
  15.5 5.2 %shard_map.85 = (f32[60,1152]{1,0:T(8,128)S(1)}, bf16[60,1152]{1,0:T(8,128)(2,1)S(1)}, bf16[60,1152]{1,0:T(8,128)(2,1)S(1)}, bf16[60,1152]{1,0:T(8,128)(2,1)S(1)}) custom-call(bf16[80,1280]{1,0:T(8,128)(2,1)S(1)} %get-tuple-element.31.x_ref, bf16[80,1280]{1,0:T(8,128)(2,1)S(1)} %get-tuple-element.32.y_ref, bf16[1280,3456]{1,0:T(8,128)(2,1)} %gate_ref.11, ...), custom_call_target="tpu_custom_call" | custom-call | flops 707788800 | bytes 8847360 | tf_op jit(solution)/shard_map/pallas_call | solution.py:97
  20.7 1.6 %collective-permute-start.3 = (bf16[60,1152]{1,0:T(8,128)(2,1)S(1)}, bf16[60,1152]{1,0:T(8,128)(2,1)S(1)}, u32[]{:S(2)}, u32[]{:S(2)}) collective-permute-start(bf16[60,1152]{1,0:T(8,128)(2,1)S(1)} %get-tuple-element.34), channel_id=1, source_target_pairs={{0,8},{8,0},{16,24},{24,16},{1,9},{9,1},{17,25},{25,17},{2,10},{10... | collective-permute-start | bytes 414728 | tf_op jit(solution)/shard_map/ppermute | solution.py:268
  22.3 1.5 %collective-permute-start.4 = (bf16[60,1152]{1,0:T(8,128)(2,1)S(1)}, bf16[60,1152]{1,0:T(8,128)(2,1)S(1)}, u32[]{:S(2)}, u32[]{:S(2)}) collective-permute-start(bf16[60,1152]{1,0:T(8,128)(2,1)S(1)} %get-tuple-element.35), channel_id=1, source_target_pairs={{0,16},{8,24},{16,0},{24,8},{1,17},{9,25},{17,1},{25,9},{2,18},{10... | collective-permute-start | bytes 414728 | tf_op jit(solution)/shard_map/ppermute | solution.py:268
  23.8 0.5 collective-permute-start.5
  24.3 5.2 %shard_map.89 = (f32[60,1152]{1,0:T(8,128)S(1)}, bf16[60,1152]{1,0:T(8,128)(2,1)S(1)}, bf16[60,1152]{1,0:T(8,128)(2,1)S(1)}, bf16[60,1152]{1,0:T(8,128)(2,1)S(1)}) custom-call(bf16[80,1280]{1,0:T(8,128)(2,1)S(1)} %get-tuple-element.31.x_ref, bf16[80,1280]{1,0:T(8,128)(2,1)S(1)} %get-tuple-element.32.y_ref, bf16[1280,3456]{1,0:T(8,128)(2,1)} %gate_ref.11, ...), custom_call_target="tpu_custom_call" | custom-call | flops 707788800 | bytes 8847360 | tf_op jit(solution)/shard_map/pallas_call | solution.py:97
  29.5 1.6 %collective-permute-start.10 = (bf16[60,1152]{1,0:T(8,128)(2,1)S(1)}, bf16[60,1152]{1,0:T(8,128)(2,1)S(1)}, u32[]{:S(2)}, u32[]{:S(2)}) collective-permute-start(bf16[60,1152]{1,0:T(8,128)(2,1)S(1)} %get-tuple-element.39), channel_id=1, source_target_pairs={{0,16},{8,24},{16,0},{24,8},{1,17},{9,25},{17,1},{25,9},{2,18},{10... | collective-permute-start | bytes 414728 | tf_op jit(solution)/shard_map/ppermute | solution.py:268
  31.1 1.4 %collective-permute-start.11 = (bf16[60,1152]{1,0:T(8,128)(2,1)S(1)}, bf16[60,1152]{1,0:T(8,128)(2,1)S(1)}, u32[]{:S(2)}, u32[]{:S(2)}) collective-permute-start(bf16[60,1152]{1,0:T(8,128)(2,1)S(1)} %get-tuple-element.40), channel_id=1, source_target_pairs={{0,24},{8,16},{16,8},{24,0},{1,25},{9,17},{17,9},{25,1},{2,26},{10... | collective-permute-start | bytes 414728 | tf_op jit(solution)/shard_map/ppermute | solution.py:268
  32.5 0.0 collective-permute-done.3.refs_0_
  32.6 0.5 collective-permute-start.9
  33.1 5.2 %shard_map.93 = (f32[60,1152]{1,0:T(8,128)S(1)}, bf16[60,1152]{1,0:T(8,128)(2,1)S(1)}, bf16[60,1152]{1,0:T(8,128)(2,1)S(1)}, bf16[60,1152]{1,0:T(8,128)(2,1)S(1)}) custom-call(bf16[80,1280]{1,0:T(8,128)(2,1)S(1)} %get-tuple-element.31.x_ref, bf16[80,1280]{1,0:T(8,128)(2,1)S(1)} %get-tuple-element.32.y_ref, bf16[1280,3456]{1,0:T(8,128)(2,1)} %gate_ref.11, ...), custom_call_target="tpu_custom_call" | custom-call | flops 707788800 | bytes 8847360 | tf_op jit(solution)/shard_map/pallas_call | solution.py:97
  38.3 1.6 %collective-permute-start.15 = (bf16[60,1152]{1,0:T(8,128)(2,1)S(1)}, bf16[60,1152]{1,0:T(8,128)(2,1)S(1)}, u32[]{:S(2)}, u32[]{:S(2)}) collective-permute-start(bf16[60,1152]{1,0:T(8,128)(2,1)S(1)} %get-tuple-element.42), channel_id=1, source_target_pairs={{0,8},{8,0},{16,24},{24,16},{1,9},{9,1},{17,25},{25,17},{2,10},{10... | collective-permute-start | bytes 414728 | tf_op jit(solution)/shard_map/ppermute | solution.py:268
  39.9 0.0 collective-permute-done.5.refs_2_
  39.9 1.5 %collective-permute-start.16 = (bf16[60,1152]{1,0:T(8,128)(2,1)S(1)}, bf16[60,1152]{1,0:T(8,128)(2,1)S(1)}, u32[]{:S(2)}, u32[]{:S(2)}) collective-permute-start(bf16[60,1152]{1,0:T(8,128)(2,1)S(1)} %get-tuple-element.43), channel_id=1, source_target_pairs={{0,16},{8,24},{16,0},{24,8},{1,17},{9,25},{17,1},{25,9},{2,18},{10... | collective-permute-start | bytes 414728 | tf_op jit(solution)/shard_map/ppermute | solution.py:268
  41.4 0.1 shard_map.86.refs_0_
  41.5 0.5 collective-permute-start.17
  42.1 0.0 collective-permute-done.11.refs_2_
  42.1 1.5 %collective-permute-start.6 = (bf16[60,1152]{1,0:T(8,128)(2,1)S(1)}, bf16[60,1152]{1,0:T(8,128)(2,1)S(1)}, u32[]{:S(2)}, u32[]{:S(2)}) collective-permute-start(bf16[60,1152]{1,0:T(8,128)(2,1)S(1)} %shard_map.86.refs_0_), channel_id=1, source_target_pairs={{0,8},{8,0},{16,24},{24,16},{1,9},{9,1},{17,25},{25,17},{2,10},{10... | collective-permute-start | bytes 414728 | tf_op jit(solution)/shard_map/ppermute | solution.py:268
  43.6 1.5 %collective-permute-start.7 = (bf16[60,1152]{1,0:T(8,128)(2,1)S(1)}, bf16[60,1152]{1,0:T(8,128)(2,1)S(1)}, u32[]{:S(2)}, u32[]{:S(2)}) collective-permute-start(bf16[60,1152]{1,0:T(8,128)(2,1)S(1)} %shard_map.86.refs_0_), channel_id=1, source_target_pairs={{0,16},{8,24},{16,0},{24,8},{1,17},{9,25},{17,1},{25,9},{2,18},{10... | collective-permute-start | bytes 414728 | tf_op jit(solution)/shard_map/ppermute | solution.py:268
  45.1 0.1 shard_map.90.refs_0_
  45.3 2.4 %collective-permute-start.8 = (bf16[60,1152]{1,0:T(8,128)(2,1)S(1)}, bf16[60,1152]{1,0:T(8,128)(2,1)S(1)}, u32[]{:S(2)}, u32[]{:S(2)}) collective-permute-start(bf16[60,1152]{1,0:T(8,128)(2,1)S(1)} %shard_map.86.refs_0_), channel_id=1, source_target_pairs={{0,24},{8,16},{16,8},{24,0},{1,25},{9,17},{17,9},{25,1},{2,26},{10... | collective-permute-start | bytes 414728 | tf_op jit(solution)/shard_map/ppermute | solution.py:268
  47.6 1.5 %collective-permute-done.16.refs_1_ = bf16[60,1152]{1,0:T(8,128)(2,1)S(1)} collective-permute-done((bf16[60,1152]{1,0:T(8,128)(2,1)S(1)}, bf16[60,1152]{1,0:T(8,128)(2,1)S(1)}, u32[]{:S(2)}, u32[]{:S(2)}) %collective-permute-start.16) | collective-permute-done | bytes 138272 | tf_op jit(solution)/shard_map/ppermute | solution.py:268
  49.1 0.8 collective-permute-start.12
  49.9 0.8 collective-permute-start.13
  50.7 0.8 collective-permute-done.6.refs_1_
  51.5 2.4 %collective-permute-start.14 = (bf16[60,1152]{1,0:T(8,128)(2,1)S(1)}, bf16[60,1152]{1,0:T(8,128)(2,1)S(1)}, u32[]{:S(2)}, u32[]{:S(2)}) collective-permute-start(bf16[60,1152]{1,0:T(8,128)(2,1)S(1)} %shard_map.90.refs_0_), channel_id=1, source_target_pairs={{0,24},{8,16},{16,8},{24,0},{1,25},{9,17},{17,9},{25,1},{2,26},{10... | collective-permute-start | bytes 414728 | tf_op jit(solution)/shard_map/ppermute | solution.py:268
  54.0 0.1 shard_map.94.refs_0_
  54.1 1.3 %collective-permute-done.7.refs_2_ = bf16[60,1152]{1,0:T(8,128)(2,1)S(1)} collective-permute-done((bf16[60,1152]{1,0:T(8,128)(2,1)S(1)}, bf16[60,1152]{1,0:T(8,128)(2,1)S(1)}, u32[]{:S(2)}, u32[]{:S(2)}) %collective-permute-start.7) | collective-permute-done | bytes 138272 | tf_op jit(solution)/shard_map/ppermute | solution.py:268
  55.4 0.8 collective-permute-start.18
  56.2 0.0 collective-permute-done.8.refs_3_
  56.2 0.9 collective-permute-start.19
  57.1 0.8 collective-permute-done.12.refs_1_
  57.9 2.4 %collective-permute-start.20 = (bf16[60,1152]{1,0:T(8,128)(2,1)S(1)}, bf16[60,1152]{1,0:T(8,128)(2,1)S(1)}, u32[]{:S(2)}, u32[]{:S(2)}) collective-permute-start(bf16[60,1152]{1,0:T(8,128)(2,1)S(1)} %shard_map.94.refs_0_), channel_id=1, source_target_pairs={{0,24},{8,16},{16,8},{24,0},{1,25},{9,17},{17,9},{25,1},{2,26},{10... | collective-permute-start | bytes 414728 | tf_op jit(solution)/shard_map/ppermute | solution.py:268
  60.3 0.1 shard_map.87.d_gate_ref.d_up_ref.mine_ref
  60.4 0.0 collective-permute-done.13.refs_2_
  60.5 1.0 collective-permute-done.14.refs_3_
  61.5 0.1 shard_map.91.d_gate_ref.d_up_ref.mine_ref
  61.6 4.6 %shard_map.88.start_ref = f32[80,1280]{1,0:T(8,128)S(1)} custom-call(f32[80,1280]{1,0:T(8,128)S(1)} %broadcast_in_dim.3.start_ref, bf16[240,1152]{1,0:T(8,128)(2,1)S(1)} %shard_map.87.d_gate_ref.d_up_ref.mine_ref, bf16[240,1152]{1,0:T(8,128)(2,1)S(1)} %shard_map.87.d_gate_ref.d_up_ref.mine_ref, bf16[1280,3456]{1,0:T(8,128)(2,1)} %gate_ref.11, ...), custom_call_target="tpu_custom_call" | custom-call | flops 471859200 | bytes 5898240 | tf_op jit(solution)/shard_map/pallas_call | solution.py:174
  66.2 4.6 %shard_map.92.start_ref = f32[80,1280]{1,0:T(8,128)S(1)} custom-call(f32[80,1280]{1,0:T(8,128)S(1)} %shard_map.88.start_ref, bf16[240,1152]{1,0:T(8,128)(2,1)S(1)} %shard_map.91.d_gate_ref.d_up_ref.mine_ref, bf16[240,1152]{1,0:T(8,128)(2,1)S(1)} %shard_map.91.d_gate_ref.d_up_ref.mine_ref, bf16[1280,3456]{1,0:T(8,128)(2,1)} %gate_ref.11, ...), custom_call_target="tpu_custom_call" | custom-call | flops 471859200 | bytes 5898240 | tf_op jit(solution)/shard_map/pallas_call | solution.py:174
  70.8 0.0 collective-permute-done.18.refs_1_
  70.8 0.1 shard_map.95.d_gate_ref.d_up_ref.mine_ref
  70.9 4.6 %shard_map.96.grad_ref = f32[80,1280]{1,0:T(8,128)S(1)} custom-call(f32[80,1280]{1,0:T(8,128)S(1)} %shard_map.92.start_ref, bf16[240,1152]{1,0:T(8,128)(2,1)S(1)} %shard_map.95.d_gate_ref.d_up_ref.mine_ref, bf16[240,1152]{1,0:T(8,128)(2,1)S(1)} %shard_map.95.d_gate_ref.d_up_ref.mine_ref, bf16[1280,3456]{1,0:T(8,128)(2,1)} %gate_ref.11, ...), custom_call_target="tpu_custom_call" | custom-call | flops 471859200 | bytes 5898240 | tf_op jit(solution)/shard_map/pallas_call | solution.py:174
  75.5 0.2 shard_map.97
  75.7 2.3 %collective-permute-start.21 = (bf16[20,1280]{1,0:T(8,128)(2,1)S(1)}, bf16[20,1280]{1,0:T(8,128)(2,1)S(1)}, u32[]{:S(2)}, u32[]{:S(2)}) collective-permute-start(bf16[20,1280]{1,0:T(8,128)(2,1)S(1)} %get-tuple-element.46), channel_id=1, source_target_pairs={{0,2},{2,0},{4,6},{6,4},{1,3},{3,1},{5,7},{7,5},{8,10},{10,8},{12,... | collective-permute-start | bytes 153608 | tf_op jit(solution)/shard_map/ppermute | solution.py:268
  78.0 1.1 %collective-permute-start.22 = (bf16[20,1280]{1,0:T(8,128)(2,1)S(1)}, bf16[20,1280]{1,0:T(8,128)(2,1)S(1)}, u32[]{:S(2)}, u32[]{:S(2)}) collective-permute-start(bf16[20,1280]{1,0:T(8,128)(2,1)S(1)} %get-tuple-element.47), channel_id=1, source_target_pairs={{0,4},{2,6},{4,0},{6,2},{1,5},{3,7},{5,1},{7,3},{8,12},{10,14},{12... | collective-permute-start | bytes 153608 | tf_op jit(solution)/shard_map/ppermute | solution.py:268
  79.1 1.4 %collective-permute-start.23 = (bf16[20,1280]{1,0:T(8,128)(2,1)S(1)}, bf16[20,1280]{1,0:T(8,128)(2,1)S(1)}, u32[]{:S(2)}, u32[]{:S(2)}) collective-permute-start(bf16[20,1280]{1,0:T(8,128)(2,1)S(1)} %get-tuple-element.48), channel_id=1, source_target_pairs={{0,6},{2,4},{4,2},{6,0},{1,7},{3,5},{5,3},{7,1},{8,14},{10,12},{12... | collective-permute-start | bytes 153608 | tf_op jit(solution)/shard_map/ppermute | solution.py:268
  80.5 0.1 collective-permute-start.24
  80.6 0.5 collective-permute-start.27
  81.1 0.1 collective-permute-start.26
  81.2 2.6 %collective-permute-done.22 = bf16[20,1280]{1,0:T(8,128)(2,1)S(1)} collective-permute-done((bf16[20,1280]{1,0:T(8,128)(2,1)S(1)}, bf16[20,1280]{1,0:T(8,128)(2,1)S(1)}, u32[]{:S(2)}, u32[]{:S(2)}) %collective-permute-start.22) | collective-permute-done | bytes 51232 | tf_op jit(solution)/shard_map/ppermute | solution.py:268
  83.8 1.4 %collective-permute-done.23 = bf16[20,1280]{1,0:T(8,128)(2,1)S(1)} collective-permute-done((bf16[20,1280]{1,0:T(8,128)(2,1)S(1)}, bf16[20,1280]{1,0:T(8,128)(2,1)S(1)}, u32[]{:S(2)}, u32[]{:S(2)}) %collective-permute-start.23) | collective-permute-done | bytes 51232 | tf_op jit(solution)/shard_map/ppermute | solution.py:268
  85.2 0.7 add_convert_fusion
  85.9 0.8 broadcast_select_fusion.1
  86.7 0.8 maximum_bitcast_fusion
  87.5 1.2 %copy.17.xt_ref = bf16[1280,160]{1,0:T(8,128)(2,1)S(1)} copy(bf16[1280,160]{0,1:T(8,128)(2,1)} %maximum_bitcast_fusion) | data formatting | bytes 819200 | tf_op jit(solution)/shard_map/transpose | solution.py:297
  88.7 1.1 pad_maximum_fusion.1.y_ref
  89.8 5.9 %shard_map.98 = (bf16[1280,3456]{1,0:T(8,128)(2,1)}, bf16[1280,3456]{1,0:T(8,128)(2,1)}, bf16[3456,1280]{1,0:T(8,128)(2,1)}) custom-call(s32[1]{0:T(128)} %bitcast.1.row_ref, bf16[1280,160]{1,0:T(8,128)(2,1)S(1)} %copy.17.xt_ref, bf16[160,1280]{1,0:T(8,128)(2,1)S(1)} %pad_maximum_fusion.1.y_ref, ...), custom_call_target="tpu_custom_call" | custom-call | flops 1415577600 | bytes 8847360 | tf_op jit(solution)/shard_map/pallas_call | solution.py:210
  95.7 5.1 %shard_map.99 = (bf16[1280,3456]{1,0:T(8,128)(2,1)}, bf16[1280,3456]{1,0:T(8,128)(2,1)}, bf16[3456,1280]{1,0:T(8,128)(2,1)}) custom-call(s32[1]{0:T(128)} %bitcast.1.row_ref, bf16[1280,160]{1,0:T(8,128)(2,1)S(1)} %copy.17.xt_ref, bf16[160,1280]{1,0:T(8,128)(2,1)S(1)} %pad_maximum_fusion.1.y_ref, ...), custom_call_target="tpu_custom_call", output_to_operand_aliasing={{0}: (5, {}), {1}: (6, {}), {2}: (7, {})} | custom-call | flops 1415577600 | bytes 8847360 | tf_op jit(solution)/shard_map/pallas_call | solution.py:210
  100.8 5.1 %shard_map.100 = (bf16[1280,3456]{1,0:T(8,128)(2,1)}, bf16[1280,3456]{1,0:T(8,128)(2,1)}, bf16[3456,1280]{1,0:T(8,128)(2,1)}) custom-call(s32[1]{0:T(128)} %bitcast.1.row_ref, bf16[1280,160]{1,0:T(8,128)(2,1)S(1)} %copy.17.xt_ref, bf16[160,1280]{1,0:T(8,128)(2,1)S(1)} %pad_maximum_fusion.1.y_ref, ...), custom_call_target="tpu_custom_call", output_to_operand_aliasing={{0}: (5, {}), {1}: (6, {}), {2}: (7, {})} | custom-call | flops 1415577600 | bytes 8847360 | tf_op jit(solution)/shard_map/pallas_call | solution.py:210
  (17 shorter events, 0.1 us)
Async XLA Ops:
  1.5 6.0 %collective-permute-start = (bf16[40,1280]{1,0:T(8,128)(2,1)S(1)}, bf16[40,1280]{1,0:T(8,128)(2,1)S(1)}, u32[]{:S(2)}, u32[]{:S(2)}) collective-permute-start(bf16[40,1280]{1,0:T(8,128)(2,1)S(1)} %pad_maximum_fusion.2.refs_0_), channel_id=1, source_target_pairs={{0,2},{2,0},{4,6},{6,4},{1,3},{3,1},{5,7},{7,5},{8,10},{10,8},{12,... | collective-permute-start | bytes 307208 | tf_op jit(solution)/shard_map/ppermute | solution.py:268
  4.6 10.7 %collective-permute-start.1 = (bf16[40,1280]{1,0:T(8,128)(2,1)S(1)}, bf16[40,1280]{1,0:T(8,128)(2,1)S(1)}, u32[]{:S(2)}, u32[]{:S(2)}) collective-permute-start(bf16[40,1280]{1,0:T(8,128)(2,1)S(1)} %pad_maximum_fusion.2.refs_0_), channel_id=1, source_target_pairs={{0,4},{2,6},{4,0},{6,2},{1,5},{3,7},{5,1},{7,3},{8,12},{10,14},{12... | collective-permute-start | bytes 307208 | tf_op jit(solution)/shard_map/ppermute | solution.py:268
  7.2 8.1 %collective-permute-start.2 = (bf16[40,1280]{1,0:T(8,128)(2,1)S(1)}, bf16[40,1280]{1,0:T(8,128)(2,1)S(1)}, u32[]{:S(2)}, u32[]{:S(2)}) collective-permute-start(bf16[40,1280]{1,0:T(8,128)(2,1)S(1)} %pad_maximum_fusion.2.refs_0_), channel_id=1, source_target_pairs={{0,6},{2,4},{4,2},{6,0},{1,7},{3,5},{5,3},{7,1},{8,14},{10,12},{12... | collective-permute-start | bytes 307208 | tf_op jit(solution)/shard_map/ppermute | solution.py:268
  20.7 11.8 %collective-permute-start.3 = (bf16[60,1152]{1,0:T(8,128)(2,1)S(1)}, bf16[60,1152]{1,0:T(8,128)(2,1)S(1)}, u32[]{:S(2)}, u32[]{:S(2)}) collective-permute-start(bf16[60,1152]{1,0:T(8,128)(2,1)S(1)} %get-tuple-element.34), channel_id=1, source_target_pairs={{0,8},{8,0},{16,24},{24,16},{1,9},{9,1},{17,25},{25,17},{2,10},{10... | collective-permute-start | bytes 414728 | tf_op jit(solution)/shard_map/ppermute | solution.py:268
  22.3 16.0 %collective-permute-start.4 = (bf16[60,1152]{1,0:T(8,128)(2,1)S(1)}, bf16[60,1152]{1,0:T(8,128)(2,1)S(1)}, u32[]{:S(2)}, u32[]{:S(2)}) collective-permute-start(bf16[60,1152]{1,0:T(8,128)(2,1)S(1)} %get-tuple-element.35), channel_id=1, source_target_pairs={{0,16},{8,24},{16,0},{24,8},{1,17},{9,25},{17,1},{25,9},{2,18},{10... | collective-permute-start | bytes 414728 | tf_op jit(solution)/shard_map/ppermute | solution.py:268
  23.8 16.1 %collective-permute-start.5 = (bf16[60,1152]{1,0:T(8,128)(2,1)S(1)}, bf16[60,1152]{1,0:T(8,128)(2,1)S(1)}, u32[]{:S(2)}, u32[]{:S(2)}) collective-permute-start(bf16[60,1152]{1,0:T(8,128)(2,1)S(1)} %get-tuple-element.36), channel_id=1, source_target_pairs={{0,24},{8,16},{16,8},{24,0},{1,25},{9,17},{17,9},{25,1},{2,26},{10... | collective-permute-start | bytes 414728 | tf_op jit(solution)/shard_map/ppermute | solution.py:268
  29.5 12.0 %collective-permute-start.10 = (bf16[60,1152]{1,0:T(8,128)(2,1)S(1)}, bf16[60,1152]{1,0:T(8,128)(2,1)S(1)}, u32[]{:S(2)}, u32[]{:S(2)}) collective-permute-start(bf16[60,1152]{1,0:T(8,128)(2,1)S(1)} %get-tuple-element.39), channel_id=1, source_target_pairs={{0,16},{8,24},{16,0},{24,8},{1,17},{9,25},{17,1},{25,9},{2,18},{10... | collective-permute-start | bytes 414728 | tf_op jit(solution)/shard_map/ppermute | solution.py:268
  31.1 11.0 %collective-permute-start.11 = (bf16[60,1152]{1,0:T(8,128)(2,1)S(1)}, bf16[60,1152]{1,0:T(8,128)(2,1)S(1)}, u32[]{:S(2)}, u32[]{:S(2)}) collective-permute-start(bf16[60,1152]{1,0:T(8,128)(2,1)S(1)} %get-tuple-element.40), channel_id=1, source_target_pairs={{0,24},{8,16},{16,8},{24,0},{1,25},{9,17},{17,9},{25,1},{2,26},{10... | collective-permute-start | bytes 414728 | tf_op jit(solution)/shard_map/ppermute | solution.py:268
  32.6 11.0 %collective-permute-start.9 = (bf16[60,1152]{1,0:T(8,128)(2,1)S(1)}, bf16[60,1152]{1,0:T(8,128)(2,1)S(1)}, u32[]{:S(2)}, u32[]{:S(2)}) collective-permute-start(bf16[60,1152]{1,0:T(8,128)(2,1)S(1)} %get-tuple-element.38), channel_id=1, source_target_pairs={{0,8},{8,0},{16,24},{24,16},{1,9},{9,1},{17,25},{25,17},{2,10},{10... | collective-permute-start | bytes 414728 | tf_op jit(solution)/shard_map/ppermute | solution.py:268
  38.3 6.9 %collective-permute-start.15 = (bf16[60,1152]{1,0:T(8,128)(2,1)S(1)}, bf16[60,1152]{1,0:T(8,128)(2,1)S(1)}, u32[]{:S(2)}, u32[]{:S(2)}) collective-permute-start(bf16[60,1152]{1,0:T(8,128)(2,1)S(1)} %get-tuple-element.42), channel_id=1, source_target_pairs={{0,8},{8,0},{16,24},{24,16},{1,9},{9,1},{17,25},{25,17},{2,10},{10... | collective-permute-start | bytes 414728 | tf_op jit(solution)/shard_map/ppermute | solution.py:268
  39.9 9.2 %collective-permute-start.16 = (bf16[60,1152]{1,0:T(8,128)(2,1)S(1)}, bf16[60,1152]{1,0:T(8,128)(2,1)S(1)}, u32[]{:S(2)}, u32[]{:S(2)}) collective-permute-start(bf16[60,1152]{1,0:T(8,128)(2,1)S(1)} %get-tuple-element.43), channel_id=1, source_target_pairs={{0,16},{8,24},{16,0},{24,8},{1,17},{9,25},{17,1},{25,9},{2,18},{10... | collective-permute-start | bytes 414728 | tf_op jit(solution)/shard_map/ppermute | solution.py:268
  41.5 8.4 %collective-permute-start.17 = (bf16[60,1152]{1,0:T(8,128)(2,1)S(1)}, bf16[60,1152]{1,0:T(8,128)(2,1)S(1)}, u32[]{:S(2)}, u32[]{:S(2)}) collective-permute-start(bf16[60,1152]{1,0:T(8,128)(2,1)S(1)} %get-tuple-element.44), channel_id=1, source_target_pairs={{0,24},{8,16},{16,8},{24,0},{1,25},{9,17},{17,9},{25,1},{2,26},{10... | collective-permute-start | bytes 414728 | tf_op jit(solution)/shard_map/ppermute | solution.py:268
  42.1 9.5 %collective-permute-start.6 = (bf16[60,1152]{1,0:T(8,128)(2,1)S(1)}, bf16[60,1152]{1,0:T(8,128)(2,1)S(1)}, u32[]{:S(2)}, u32[]{:S(2)}) collective-permute-start(bf16[60,1152]{1,0:T(8,128)(2,1)S(1)} %shard_map.86.refs_0_), channel_id=1, source_target_pairs={{0,8},{8,0},{16,24},{24,16},{1,9},{9,1},{17,25},{25,17},{2,10},{10... | collective-permute-start | bytes 414728 | tf_op jit(solution)/shard_map/ppermute | solution.py:268
  43.6 11.8 %collective-permute-start.7 = (bf16[60,1152]{1,0:T(8,128)(2,1)S(1)}, bf16[60,1152]{1,0:T(8,128)(2,1)S(1)}, u32[]{:S(2)}, u32[]{:S(2)}) collective-permute-start(bf16[60,1152]{1,0:T(8,128)(2,1)S(1)} %shard_map.86.refs_0_), channel_id=1, source_target_pairs={{0,16},{8,24},{16,0},{24,8},{1,17},{9,25},{17,1},{25,9},{2,18},{10... | collective-permute-start | bytes 414728 | tf_op jit(solution)/shard_map/ppermute | solution.py:268
  45.3 10.9 %collective-permute-start.8 = (bf16[60,1152]{1,0:T(8,128)(2,1)S(1)}, bf16[60,1152]{1,0:T(8,128)(2,1)S(1)}, u32[]{:S(2)}, u32[]{:S(2)}) collective-permute-start(bf16[60,1152]{1,0:T(8,128)(2,1)S(1)} %shard_map.86.refs_0_), channel_id=1, source_target_pairs={{0,24},{8,16},{16,8},{24,0},{1,25},{9,17},{17,9},{25,1},{2,26},{10... | collective-permute-start | bytes 414728 | tf_op jit(solution)/shard_map/ppermute | solution.py:268
  49.1 8.8 %collective-permute-start.12 = (bf16[60,1152]{1,0:T(8,128)(2,1)S(1)}, bf16[60,1152]{1,0:T(8,128)(2,1)S(1)}, u32[]{:S(2)}, u32[]{:S(2)}) collective-permute-start(bf16[60,1152]{1,0:T(8,128)(2,1)S(1)} %shard_map.90.refs_0_), channel_id=1, source_target_pairs={{0,8},{8,0},{16,24},{24,16},{1,9},{9,1},{17,25},{25,17},{2,10},{10... | collective-permute-start | bytes 414728 | tf_op jit(solution)/shard_map/ppermute | solution.py:268
  49.9 10.5 %collective-permute-start.13 = (bf16[60,1152]{1,0:T(8,128)(2,1)S(1)}, bf16[60,1152]{1,0:T(8,128)(2,1)S(1)}, u32[]{:S(2)}, u32[]{:S(2)}) collective-permute-start(bf16[60,1152]{1,0:T(8,128)(2,1)S(1)} %shard_map.90.refs_0_), channel_id=1, source_target_pairs={{0,16},{8,24},{16,0},{24,8},{1,17},{9,25},{17,1},{25,9},{2,18},{10... | collective-permute-start | bytes 414728 | tf_op jit(solution)/shard_map/ppermute | solution.py:268
  51.5 9.9 %collective-permute-start.14 = (bf16[60,1152]{1,0:T(8,128)(2,1)S(1)}, bf16[60,1152]{1,0:T(8,128)(2,1)S(1)}, u32[]{:S(2)}, u32[]{:S(2)}) collective-permute-start(bf16[60,1152]{1,0:T(8,128)(2,1)S(1)} %shard_map.90.refs_0_), channel_id=1, source_target_pairs={{0,24},{8,16},{16,8},{24,0},{1,25},{9,17},{17,9},{25,1},{2,26},{10... | collective-permute-start | bytes 414728 | tf_op jit(solution)/shard_map/ppermute | solution.py:268
  55.4 15.4 %collective-permute-start.18 = (bf16[60,1152]{1,0:T(8,128)(2,1)S(1)}, bf16[60,1152]{1,0:T(8,128)(2,1)S(1)}, u32[]{:S(2)}, u32[]{:S(2)}) collective-permute-start(bf16[60,1152]{1,0:T(8,128)(2,1)S(1)} %shard_map.94.refs_0_), channel_id=1, source_target_pairs={{0,8},{8,0},{16,24},{24,16},{1,9},{9,1},{17,25},{25,17},{2,10},{10... | collective-permute-start | bytes 414728 | tf_op jit(solution)/shard_map/ppermute | solution.py:268
  56.2 14.6 %collective-permute-start.19 = (bf16[60,1152]{1,0:T(8,128)(2,1)S(1)}, bf16[60,1152]{1,0:T(8,128)(2,1)S(1)}, u32[]{:S(2)}, u32[]{:S(2)}) collective-permute-start(bf16[60,1152]{1,0:T(8,128)(2,1)S(1)} %shard_map.94.refs_0_), channel_id=1, source_target_pairs={{0,16},{8,24},{16,0},{24,8},{1,17},{9,25},{17,1},{25,9},{2,18},{10... | collective-permute-start | bytes 414728 | tf_op jit(solution)/shard_map/ppermute | solution.py:268
  57.9 12.9 %collective-permute-start.20 = (bf16[60,1152]{1,0:T(8,128)(2,1)S(1)}, bf16[60,1152]{1,0:T(8,128)(2,1)S(1)}, u32[]{:S(2)}, u32[]{:S(2)}) collective-permute-start(bf16[60,1152]{1,0:T(8,128)(2,1)S(1)} %shard_map.94.refs_0_), channel_id=1, source_target_pairs={{0,24},{8,16},{16,8},{24,0},{1,25},{9,17},{17,9},{25,1},{2,26},{10... | collective-permute-start | bytes 414728 | tf_op jit(solution)/shard_map/ppermute | solution.py:268
  75.7 5.4 %collective-permute-start.21 = (bf16[20,1280]{1,0:T(8,128)(2,1)S(1)}, bf16[20,1280]{1,0:T(8,128)(2,1)S(1)}, u32[]{:S(2)}, u32[]{:S(2)}) collective-permute-start(bf16[20,1280]{1,0:T(8,128)(2,1)S(1)} %get-tuple-element.46), channel_id=1, source_target_pairs={{0,2},{2,0},{4,6},{6,4},{1,3},{3,1},{5,7},{7,5},{8,10},{10,8},{12,... | collective-permute-start | bytes 153608 | tf_op jit(solution)/shard_map/ppermute | solution.py:268
  78.0 5.8 %collective-permute-start.22 = (bf16[20,1280]{1,0:T(8,128)(2,1)S(1)}, bf16[20,1280]{1,0:T(8,128)(2,1)S(1)}, u32[]{:S(2)}, u32[]{:S(2)}) collective-permute-start(bf16[20,1280]{1,0:T(8,128)(2,1)S(1)} %get-tuple-element.47), channel_id=1, source_target_pairs={{0,4},{2,6},{4,0},{6,2},{1,5},{3,7},{5,1},{7,3},{8,12},{10,14},{12... | collective-permute-start | bytes 153608 | tf_op jit(solution)/shard_map/ppermute | solution.py:268
  79.1 6.1 %collective-permute-start.23 = (bf16[20,1280]{1,0:T(8,128)(2,1)S(1)}, bf16[20,1280]{1,0:T(8,128)(2,1)S(1)}, u32[]{:S(2)}, u32[]{:S(2)}) collective-permute-start(bf16[20,1280]{1,0:T(8,128)(2,1)S(1)} %get-tuple-element.48), channel_id=1, source_target_pairs={{0,6},{2,4},{4,2},{6,0},{1,7},{3,5},{5,3},{7,1},{8,14},{10,12},{12... | collective-permute-start | bytes 153608 | tf_op jit(solution)/shard_map/ppermute | solution.py:268
  80.5 5.4 %collective-permute-start.24 = (bf16[160,1280]{1,0:T(8,128)(2,1)S(1)}, bf16[160,1280]{1,0:T(8,128)(2,1)S(1)}, u32[]{:S(2)}, u32[]{:S(2)}) collective-permute-start(bf16[160,1280]{1,0:T(8,128)(2,1)S(1)} %pad_maximum_fusion), channel_id=1, source_target_pairs={{0,1},{1,0},{2,3},{3,2},{4,5},{5,4},{6,7},{7,6},{8,9},{9,8},{10,11... | collective-permute-start | bytes 1228808 | tf_op jit(solution)/shard_map/ppermute | solution.py:268
  80.6 9.2 %collective-permute-start.27 = (bf16[240,1152]{1,0:T(8,128)(2,1)S(1)}, bf16[240,1152]{1,0:T(8,128)(2,1)}, u32[]{:S(2)}, u32[]{:S(2)}) collective-permute-start(bf16[240,1152]{1,0:T(8,128)(2,1)S(1)} %shard_map.87.d_gate_ref.d_up_ref.mine_ref), channel_id=1, source_target_pairs={{0,1},{1,0},{2,3},{3,2},{4,5},{5,4},{6,7},{7,6},{8,9},{9,8},{10,11... | collective-permute-start | bytes 1658888 | tf_op jit(solution)/shard_map/ppermute | solution.py:268
  81.1 14.6 %collective-permute-start.26 = (bf16[240,1152]{1,0:T(8,128)(2,1)S(1)}, bf16[240,1152]{1,0:T(8,128)(2,1)S(1)}, u32[]{:S(2)}, u32[]{:S(2)}) collective-permute-start(bf16[240,1152]{1,0:T(8,128)(2,1)S(1)} %shard_map.91.d_gate_ref.d_up_ref.mine_ref), channel_id=1, source_target_pairs={{0,1},{1,0},{2,3},{3,2},{4,5},{5,4},{6,7},{7,6},{8,9},{9,8},{10,11... | collective-permute-start | bytes 1658888 | tf_op jit(solution)/shard_map/ppermute | solution.py:268
  83.8 17.0 %collective-permute-start.25 = (bf16[240,1152]{1,0:T(8,128)(2,1)S(1)}, bf16[240,1152]{1,0:T(8,128)(2,1)S(1)}, u32[]{:S(2)}, u32[]{:S(2)}) collective-permute-start(bf16[240,1152]{1,0:T(8,128)(2,1)S(1)} %shard_map.95.d_gate_ref.d_up_ref.mine_ref), channel_id=1, source_target_pairs={{0,1},{1,0},{2,3},{3,2},{4,5},{5,4},{6,7},{7,6},{8,9},{9,8},{10,11... | collective-permute-start | bytes 1658888 | tf_op jit(solution)/shard_map/ppermute | solution.py:268

commit v2 on v1

--- a/solution.py
+++ b/solution.py
@@ -13,7 +13,7 @@
 TN = (((0,), (0,)), ((), ()))
 LANES = 128
 CHUNKS = 3
-VMEM_LIMIT = 48 * 1024 * 1024
+MIB = 1024 * 1024
 
 
 def pointwise(gate_sum, up_sum, dh_sum):
@@ -25,7 +25,9 @@
     return (hidden, d_gate, d_up)
 
 
-def call(kernel, grid, in_specs, out_specs, out_shape, flops, moved, scratch=(), aliases=None):
+def call(
+    kernel, grid, in_specs, out_specs, out_shape, flops, moved, scratch=(), aliases=None, limit=4
+):
     return pl.pallas_call(
         kernel,
         grid=grid,
@@ -35,7 +37,7 @@
         scratch_shapes=list(scratch),
         input_output_aliases=aliases or {},
         cost_estimate=pl.CostEstimate(flops=flops, bytes_accessed=moved, transcendentals=0),
-        compiler_params=pltpu.CompilerParams(vmem_limit_bytes=VMEM_LIMIT),
+        compiler_params=pltpu.CompilerParams(vmem_limit_bytes=limit * MIB),
     )
 
 
@@ -44,6 +46,8 @@
 
 
 SCALAR = pl.BlockSpec(memory_space=pltpu.SMEM)
+IN_VMEM = pl.BlockSpec(memory_space=pltpu.VMEM)
+TOKEN = jax.ShapeDtypeStruct((8, LANES), F32)
 
 
 def order_kernel(parts, rows, wa_ref, *refs):
@@ -68,19 +72,20 @@
     shape = (parts * rows, width)
     return call(
         functools.partial(order_kernel, parts, rows),
-        (1,),
-        [SCALAR] + [whole((2 * rows, width))] * parts,
-        [whole(shape)] * 2,
+        (),
+        [SCALAR] + [IN_VMEM] * parts,
+        [IN_VMEM] * 2,
         [jax.ShapeDtypeStruct(shape, BF16)] * 2,
         0,
         8 * shape[0] * width,
     )(wa, *pieces)
 
 
-def forward_kernel(parts, rows, x_ref, y_ref, gate_ref, up_ref, down_ref, own_ref, *send_refs):
-    gate = jnp.dot(x_ref[...], gate_ref[...], preferred_element_type=F32)
-    up = jnp.dot(x_ref[...], up_ref[...], preferred_element_type=F32)
-    dh = lax.dot_general(y_ref[...], down_ref[...], NT, preferred_element_type=F32)
+def forward_kernel(parts, rows, begin, x_ref, y_ref, gate_ref, up_ref, down_ref, own_ref, *send_refs):
+    there = pl.ds(begin, own_ref.shape[1])
+    gate = jnp.dot(x_ref[...], gate_ref[:, there], preferred_element_type=F32)
+    up = jnp.dot(x_ref[...], up_ref[:, there], preferred_element_type=F32)
+    dh = lax.dot_general(y_ref[...], down_ref[there, :], NT, preferred_element_type=F32)
     for slot in range(parts):
         cut = slice(slot * rows, (slot + 1) * rows)
         block = jnp.concatenate([gate[cut], up[cut], dh[cut]], axis=0)
@@ -90,21 +95,49 @@
             send_refs[slot - 1][...] = block.astype(BF16)
 
 
+def load_kernel(cuts, *refs):
+    count = (len(refs) - 1) // 2
+    sems = refs[-1]
+    copies = []
+    for at in range(count):
+        rows = refs[at].shape[0] // cuts
+        for cut in range(cuts):
+            part = pl.ds(cut * rows, rows)
+            copies.append(
+                pltpu.make_async_copy(
+                    refs[at].at[part], refs[count + at].at[part], sems.at[at, cut]
+                )
+            )
+    for copy in copies:
+        copy.start()
+    for copy in copies:
+        copy.wait()
+
+
+def load(*weights):
+    cuts = 4
+    return pl.pallas_call(
+        functools.partial(load_kernel, cuts),
+        in_specs=[pl.BlockSpec(memory_space=pl.ANY)] * len(weights),
+        out_specs=[IN_VMEM] * len(weights),
+        out_shape=[pltpu.VMEM(w.shape, w.dtype) for w in weights],
+        scratch_shapes=[pltpu.SemaphoreType.DMA((len(weights), cuts))],
+        cost_estimate=pl.CostEstimate(
+            flops=0, bytes_accessed=sum(2 * w.size for w in weights), transcendentals=0
+        ),
+        compiler_params=pltpu.CompilerParams(vmem_limit_bytes=34 * MIB),
+    )(*weights)
+
+
 def forward(parts, first, count, tile, x, y, gate_weight, up_weight, down_weight):
     group, width = x.shape
     rows = group // parts
     columns = count * tile
     return call(
-        functools.partial(forward_kernel, parts, rows),
-        (count,),
-        [
-            whole((group, width)),
-            whole((group, width)),
-            pl.BlockSpec((width, tile), lambda i: (0, first + i)),
-            pl.BlockSpec((width, tile), lambda i: (0, first + i)),
-            pl.BlockSpec((tile, width), lambda i: (first + i, 0)),
-        ],
-        [pl.BlockSpec((3 * rows, tile), lambda i: (0, i))] * parts,
+        functools.partial(forward_kernel, parts, rows, first * tile),
+        (),
+        [IN_VMEM] * 5,
+        [IN_VMEM] * parts,
         [jax.ShapeDtypeStruct((3 * rows, columns), F32)]
         + [jax.ShapeDtypeStruct((3 * rows, columns), BF16)] * (parts - 1),
         6 * group * width * columns,
@@ -126,9 +159,9 @@
     shape = own.shape
     return call(
         functools.partial(middle_kernel, shape[0] // 3),
-        (1,),
-        [whole(shape)] * (1 + len(received)),
-        whole(shape),
+        (),
+        [IN_VMEM] * (1 + len(received)),
+        IN_VMEM,
         jax.ShapeDtypeStruct(shape, BF16),
         20 * shape[0] * shape[1],
         12 * shape[0] * shape[1],
@@ -149,47 +182,106 @@
     shape = (3 * parts * rows, columns)
     return call(
         functools.partial(stack_kernel, rows),
-        (1,),
-        [whole(blocks[0].shape)] * parts,
-        whole(shape),
+        (),
+        [IN_VMEM] * parts,
+        IN_VMEM,
         jax.ShapeDtypeStruct(shape, BF16),
         0,
         4 * shape[0] * columns,
     )(*blocks)
 
 
-def input_grad_kernel(group, start_ref, d_gate_ref, d_up_ref, gate_ref, up_ref, out_ref):
-    @pl.when(pl.program_id(0) == 0)
-    def _():
-        out_ref[...] = start_ref[...]
-
-    out_ref[...] += lax.dot_general(
-        d_gate_ref[...], gate_ref[...], NT, preferred_element_type=F32
-    ) + lax.dot_general(d_up_ref[...], up_ref[...], NT, preferred_element_type=F32)
-
-
-def input_grad(first, count, tile, start, stacked, gate_weight, up_weight):
-    group = stacked.shape[0] // 3
+def input_grad_kernel(group, begin, after, stack_ref, gate_ref, up_ref, *refs):
+    there = pl.ds(begin, stack_ref.shape[1])
+    grad = lax.dot_general(
+        stack_ref[:group], gate_ref[:, there], NT, preferred_element_type=F32
+    ) + lax.dot_general(
+        stack_ref[group : 2 * group], up_ref[:, there], NT, preferred_element_type=F32
+    )
+    refs[-1][...] = grad + refs[0][...] if after else grad
+
+
+def input_grad(begin, stacked, gate_weight, up_weight, after):
+    group, columns = stacked.shape[0] // 3, stacked.shape[1]
     width = gate_weight.shape[0]
     return call(
-        functools.partial(input_grad_kernel, group),
-        (count,),
+        functools.partial(input_grad_kernel, group, begin, bool(after)),
+        (),
+        [IN_VMEM] * (3 + len(after)),
+        IN_VMEM,
+        jax.ShapeDtypeStruct((group, width), F32),
+        4 * group * width * columns,
+        4 * width * columns,
+    )(stacked, gate_weight, up_weight, *after)
+
+
+def factors_kernel(group, row_ref, x_ref, y_ref, other_ref, xt_ref, y_all_ref):
+    first = row_ref[0] == 0
+    x, y = x_ref[...], y_ref[...]
+    x_other, y_other = other_ref[:group], other_ref[group:]
+    y_all_ref[:group] = jnp.where(first, y, y_other)
+    y_all_ref[group:] = jnp.where(first, y_other, y)
+    x_all = jnp.concatenate([jnp.where(first, x, x_other), jnp.where(first, x_other, x)], axis=0)
+    xt_ref[...] = x_all.T
+
+
+def factors(row, x, y, other):
+    group, width = x.shape
+    return call(
+        functools.partial(factors_kernel, group),
+        (),
+        [SCALAR] + [IN_VMEM] * 3,
+        [IN_VMEM] * 2,
         [
-            whole((group, width)),
-            pl.BlockSpec((group, tile), lambda i: (0, i)),
-            pl.BlockSpec((group, tile), lambda i: (1, i)),
-            pl.BlockSpec((width, tile), lambda i: (0, first + i)),
-            pl.BlockSpec((width, tile), lambda i: (0, first + i)),
+            jax.ShapeDtypeStruct((width, 2 * group), BF16),
+            jax.ShapeDtypeStruct((2 * group, width), BF16),
         ],
-        whole((group, width)),
-        jax.ShapeDtypeStruct((group, width), F32),
-        4 * group * width * count * tile,
-        4 * width * count * tile,
-    )(start, stacked, stacked, gate_weight, up_weight)
+        0,
+        8 * group * width,
+    )(row, x, y, other)
+
+
+def join_kernel(first_ref, second_ref, out_ref):
+    out_ref[...] = jnp.concatenate(
+        [first_ref[...].astype(F32), second_ref[...].astype(F32)], axis=0
+    ).astype(BF16)
+
+
+def join(first, second):
+    shape = (first.shape[0] + second.shape[0], first.shape[1])
+    return call(
+        join_kernel,
+        (),
+        [IN_VMEM] * 2,
+        IN_VMEM,
+        jax.ShapeDtypeStruct(shape, BF16),
+        0,
+        4 * shape[0] * shape[1],
+    )(first, second)
+
+
+def total_kernel(own_ref, *refs):
+    total = own_ref[...]
+    for ref in refs[:-1]:
+        total = total + ref[...].astype(F32)
+    refs[-1][...] = total.astype(BF16)
+
+
+def total(own, received):
+    return call(
+        total_kernel,
+        (),
+        [IN_VMEM] * (1 + len(received)),
+        IN_VMEM,
+        jax.ShapeDtypeStruct(own.shape, BF16),
+        4 * own.size,
+        12 * own.size,
+    )(own, *received)
 
 
 def weight_grad_kernel(group, has_start, row_ref, xt_ref, y_ref, mine_ref, other_ref, *refs):
-    gate_ref, up_ref, down_ref, both = refs[3 * has_start :]
+    gate_ref, up_ref, down_ref, token_ref, both = refs[3 * has_start :]
+    token_ref[...] = jnp.zeros_like(token_ref)
     first = row_ref[0] == 0
     for at in range(3):
         cut = slice(at * group, (at + 1) * group)
@@ -222,16 +314,19 @@
             pl.BlockSpec((width, tile), lambda i: (0, first + i)),
             pl.BlockSpec((width, tile), lambda i: (0, first + i)),
             pl.BlockSpec((tile, width), lambda i: (first + i, 0)),
+            whole(TOKEN.shape),
         ],
         [
             jax.ShapeDtypeStruct((width, hidden_width), BF16),
             jax.ShapeDtypeStruct((width, hidden_width), BF16),
             jax.ShapeDtypeStruct((hidden_width, width), BF16),
+            TOKEN,
         ],
         12 * group * width * count * tile,
         6 * width * count * tile,
         scratch=[pltpu.VMEM((3, 2 * group, tile), BF16)],
         aliases={5 + i: i for i in range(len(start))},
+        limit=16,
     )(row, xt, y, mine, other, *start)
 
 
@@ -254,9 +349,9 @@
     rows, width = grad.shape[0] // parts, grad.shape[1]
     return call(
         functools.partial(last_kernel, parts, rows),
-        (1,),
-        [SCALAR, whole(grad.shape)],
-        [whole((rows, width))] * parts,
+        (),
+        [SCALAR, IN_VMEM],
+        [IN_VMEM] * parts,
         [jax.ShapeDtypeStruct((rows, width), F32)]
         + [jax.ShapeDtypeStruct((rows, width), BF16)] * (parts - 1),
         0,
@@ -278,7 +373,8 @@
     wa = lax.axis_index("wa").astype(jnp.int32).reshape(1)
     row = lax.axis_index("row").astype(jnp.int32).reshape(1)
 
-    both = jnp.concatenate([tokens, cotangent], axis=0)
+    both = join(tokens, cotangent)
+    gate_weight, up_weight, down_weight = load(gate_weight, up_weight, down_weight)
     pieces = [both] + [swap(both, "ha", n_ha, step) for step in range(1, n_ha)]
     x, y = order_rows(wa, pieces)
 
@@ -288,36 +384,26 @@
             n_wa, chunk * count, count, tile, x, y, gate_weight, up_weight, down_weight
         )
         blocks.append((own, [swap(s, "wa", n_wa, k + 1) for k, s in enumerate(sends)]))
-
-    xy = jnp.concatenate([x, y], axis=0)
-    xy_other = swap(xy, "row", n_row, 1)
-    first = row[0] == 0
-    x_low, x_high = jnp.where(first, xy[:group], xy_other[:group]), jnp.where(first, xy_other[:group], xy[:group])
-    y_low, y_high = jnp.where(first, xy[group:], xy_other[group:]), jnp.where(first, xy_other[group:], xy[group:])
-    xt = jnp.concatenate([x_low, x_high], axis=0).T
-    y_all = jnp.concatenate([y_low, y_high], axis=0)
+    xt, y_all = factors(row, x, y, swap(join(x, y), "row", n_row, 1))
 
     gathered = []
     for own, received in blocks:
         mine = middle(own, received)
         gathered.append([mine] + [swap(mine, "wa", n_wa, step) for step in range(1, n_wa)])
 
-    grad = jnp.zeros((group, width), F32)
-    stacks = []
+    grads, after = None, ()
     for chunk in range(CHUNKS):
         mine = stack(gathered[chunk])
-        stacks.append((mine, swap(mine, "row", n_row, 1)))
-        grad = input_grad(chunk * count, count, tile, grad, mine, gate_weight, up_weight)
-    own, *sends = last_pieces(n_ha, wa, grad)
-    for step, sent in enumerate(sends):
-        own = own + swap(sent, "ha", n_ha, step + 1).astype(F32)
-
-    grads = None
-    for chunk, (mine, other) in enumerate(stacks):
-        grads = weight_grad(
+        other = swap(mine, "row", n_row, 1)
+        grad = input_grad(chunk * columns, mine, gate_weight, up_weight, after)
+        if chunk == CHUNKS - 1:
+            own, *sends = last_pieces(n_ha, wa, grad)
+            received = [swap(sent, "ha", n_ha, k + 1) for k, sent in enumerate(sends)]
+        *grads, token = weight_grad(
             chunk * count, count, tile, hidden_width, row, xt, y_all, mine, other, grads
         )
-    return (own.astype(BF16), *grads)
+        after = (grad, token)
+    return (total(own, received), *grads)
 
 
 def plain_body(tokens, cotangent, gate_weight, up_weight, down_weight):

time: 106 us -> 110 us (1.038)
  local copies, waits for them, and re-layouts: 1.26 us -> 12.2 us
  waiting for transfers between devices: 17.7 us -> 26.3 us
  starting transfers between devices: 35.4 us -> 29 us
  Pallas kernels: 46.5 us -> 41.1 us
  other arithmetic: 4.22 us -> 0.01 us
    unnamed x0 -> x26, local copies, waits for them, and re-layouts: none -> 12.2 us
    ppermute x28, waiting for transfers between devices: 17.7 us -> 26.3 us  [swap(): return lax.ppermute(value, axis, [(at, at ^ step) for at in range(size)])]
    pallas_call x14 -> x19, Pallas kernels: 30.4 us -> 23.5 us  [the longest x1 8.73 us: load(): pl.pallas_call(functools.partial(load_kernel, cuts), in_specs=[pl.BlockSp...]
    ppermute x28, starting transfers between devices: 35.4 us -> 29 us  [swap(): return lax.ppermute(value, axis, [(at, at ^ step) for at in range(size)])]
    concatenate x3 -> x0, other arithmetic: 1.97 us -> none  [the longest x1 1.06 us: fast_body(): y_all = jnp.concatenate([y_low, y_high], axis=0)]
    pallas_call x3, Pallas kernels: 16.1 us -> 17.6 us  [weight_grad(): call(functools.partial(weight_grad_kernel, group, has_start), (count,), [...]
    transpose x1 -> x0, local copies, waits for them, and re-layouts: 1.24 us -> none  [fast_body(): xt = jnp.concatenate([x_low, x_high], axis=0).T]
  transfers between devices with their start and end apart: 28 -> 28, of which waited for: 9 -> 11; matrix products, arithmetic and copies ran while one was open for 4% -> 0% of each run, Pallas kernels for 29% -> 35%
where the time goes in v2:
time: 110 us; the launch traced here: 109 us
  Pallas kernels  41.1 us (37%)
  starting transfers between devices  29 us (26%)
  waiting for transfers between devices  26.3 us (24%)
  local copies, waits for them, and re-layouts  12.2 us (11%)
    ppermute x28, starting transfers between devices, swap(): return lax.ppermute(value, axis, [(at, at ^ step) for at in range(size)])  29 us
    ppermute x28, waiting for transfers between devices, swap(): return lax.ppermute(value, axis, [(at, at ^ step) for at in range(size)])  26.3 us
    pallas_call x3, Pallas kernels, weight_grad(): call(functools.partial(weight_grad_kernel, group, has_start), (count,), [...  17.6 us
    unnamed x26, local copies, waits for them, and re-layouts  12.2 us
    pallas_call x1, Pallas kernels, load(): pl.pallas_call(functools.partial(load_kernel, cuts), in_specs=[pl.BlockSp...  8.73 us
    pallas_call x3, Pallas kernels, input_grad(): call(functools.partial(input_grad_kernel, group, begin, bool(after)), (),...  5.69 us
    pallas_call x3, Pallas kernels, forward(): call(functools.partial(forward_kernel, parts, rows, first * tile), (), [I...  5.57 us
  transfers between devices with their start and end apart: 28, of which 11 were waited for; matrix products, arithmetic and copies ran while one was open for 0% of the time, Pallas kernels for 35%

profile of v2, /device:TPU:0, one launch (start us, length us, event | category | flops | bytes accessed | tf_op | source)
XLA Modules:
  0.0 109.5 jit_solution(6067600403197823846)
XLA Ops:
  0.6 0.8 copy-done.5
  1.5 0.8 copy-done.6
  2.3 3.1 %collective-permute-start = (bf16[40,1280]{1,0:T(8,128)(2,1)S(1)}, bf16[40,1280]{1,0:T(8,128)(2,1)S(1)}, u32[]{:S(2)}, u32[]{:S(2)}) collective-permute-start(bf16[40,1280]{1,0:T(8,128)(2,1)S(1)} %shard_map.84.refs_0_), channel_id=1, source_target_pairs={{0,2},{2,0},{4,6},{6,4},{1,3},{3,1},{5,7},{7,5},{8,10},{10,8},{12,... | collective-permute-start | bytes 307208 | tf_op jit(solution)/shard_map/ppermute | solution.py:363
  5.4 2.6 %collective-permute-start.1 = (bf16[40,1280]{1,0:T(8,128)(2,1)S(1)}, bf16[40,1280]{1,0:T(8,128)(2,1)S(1)}, u32[]{:S(2)}, u32[]{:S(2)}) collective-permute-start(bf16[40,1280]{1,0:T(8,128)(2,1)S(1)} %shard_map.84.refs_0_), channel_id=1, source_target_pairs={{0,4},{2,6},{4,0},{6,2},{1,5},{3,7},{5,1},{7,3},{8,12},{10,14},{12... | collective-permute-start | bytes 307208 | tf_op jit(solution)/shard_map/ppermute | solution.py:363
  8.0 8.7 %shard_map.86 = (bf16[1280,3456]{1,0:T(8,128)(2,1)S(1)}, bf16[1280,3456]{1,0:T(8,128)(2,1)S(1)}, bf16[3456,1280]{1,0:T(8,128)(2,1)S(1)}) custom-call(bf16[1280,3456]{1,0:T(8,128)(2,1)} %refs_0_.1, bf16[1280,3456]{1,0:T(8,128)(2,1)} %refs_1_.1, bf16[3456,1280]{1,0:T(8,128)(2,1)} %refs_2_.1), custom_call_target="tpu_custom_call" | custom-call | bytes 26542080 | tf_op jit(solution)/shard_map/pallas_call | solution.py:119
  16.8 0.0 collective-permute-done.refs_1_
  16.8 0.0 collective-permute-done.2.refs_3_
  16.8 0.2 shard_map.85
  17.0 1.9 %shard_map.93 = (f32[60,1152]{1,0:T(8,128)S(1)}, bf16[60,1152]{1,0:T(8,128)(2,1)S(1)}, bf16[60,1152]{1,0:T(8,128)(2,1)S(1)}, bf16[60,1152]{1,0:T(8,128)(2,1)S(1)}) custom-call(bf16[80,1280]{1,0:T(8,128)(2,1)S(1)} %get-tuple-element.38.x_ref.first_ref, bf16[80,1280]{1,0:T(8,128)(2,1)S(1)} %get-tuple-element.39.y_ref.second_ref, ...), custom_call_target="tpu_custom_call" | custom-call | flops 707788800 | bytes 8847360 | tf_op jit(solution)/shard_map/pallas_call | solution.py:136
  18.8 1.8 %collective-permute-start.15 = (bf16[60,1152]{1,0:T(8,128)(2,1)S(1)}, bf16[60,1152]{1,0:T(8,128)(2,1)S(1)}, u32[]{:S(2)}, u32[]{:S(2)}) collective-permute-start(bf16[60,1152]{1,0:T(8,128)(2,1)S(1)} %get-tuple-element.52), channel_id=1, source_target_pairs={{0,8},{8,0},{16,24},{24,16},{1,9},{9,1},{17,25},{25,17},{2,10},{10... | collective-permute-start | bytes 414728 | tf_op jit(solution)/shard_map/ppermute | solution.py:363
  20.6 1.5 %collective-permute-start.16 = (bf16[60,1152]{1,0:T(8,128)(2,1)S(1)}, bf16[60,1152]{1,0:T(8,128)(2,1)S(1)}, u32[]{:S(2)}, u32[]{:S(2)}) collective-permute-start(bf16[60,1152]{1,0:T(8,128)(2,1)S(1)} %get-tuple-element.53), channel_id=1, source_target_pairs={{0,16},{8,24},{16,0},{24,8},{1,17},{9,25},{17,1},{25,9},{2,18},{10... | collective-permute-start | bytes 414728 | tf_op jit(solution)/shard_map/ppermute | solution.py:363
  22.1 0.3 collective-permute-start.17
  22.4 1.9 %shard_map.90 = (f32[60,1152]{1,0:T(8,128)S(1)}, bf16[60,1152]{1,0:T(8,128)(2,1)S(1)}, bf16[60,1152]{1,0:T(8,128)(2,1)S(1)}, bf16[60,1152]{1,0:T(8,128)(2,1)S(1)}) custom-call(bf16[80,1280]{1,0:T(8,128)(2,1)S(1)} %get-tuple-element.38.x_ref.first_ref, bf16[80,1280]{1,0:T(8,128)(2,1)S(1)} %get-tuple-element.39.y_ref.second_ref, ...), custom_call_target="tpu_custom_call" | custom-call | flops 707788800 | bytes 8847360 | tf_op jit(solution)/shard_map/pallas_call | solution.py:136
  24.2 1.8 %collective-permute-start.9 = (bf16[60,1152]{1,0:T(8,128)(2,1)S(1)}, bf16[60,1152]{1,0:T(8,128)(2,1)S(1)}, u32[]{:S(2)}, u32[]{:S(2)}) collective-permute-start(bf16[60,1152]{1,0:T(8,128)(2,1)S(1)} %get-tuple-element.48), channel_id=1, source_target_pairs={{0,8},{8,0},{16,24},{24,16},{1,9},{9,1},{17,25},{25,17},{2,10},{10... | collective-permute-start | bytes 414728 | tf_op jit(solution)/shard_map/ppermute | solution.py:363
  26.0 1.9 %collective-permute-done.16.refs_1_ = bf16[60,1152]{1,0:T(8,128)(2,1)S(1)} collective-permute-done((bf16[60,1152]{1,0:T(8,128)(2,1)S(1)}, bf16[60,1152]{1,0:T(8,128)(2,1)S(1)}, u32[]{:S(2)}, u32[]{:S(2)}) %collective-permute-start.16) | collective-permute-done | bytes 138272 | tf_op jit(solution)/shard_map/ppermute | solution.py:363
  27.9 1.9 %collective-permute-done.17.refs_2_ = bf16[60,1152]{1,0:T(8,128)(2,1)S(1)} collective-permute-done((bf16[60,1152]{1,0:T(8,128)(2,1)S(1)}, bf16[60,1152]{1,0:T(8,128)(2,1)S(1)}, u32[]{:S(2)}, u32[]{:S(2)}) %collective-permute-start.17) | collective-permute-done | bytes 138272 | tf_op jit(solution)/shard_map/ppermute | solution.py:363
  29.8 0.1 shard_map.94.refs_0_
  29.9 1.5 %collective-permute-start.18 = (bf16[60,1152]{1,0:T(8,128)(2,1)S(1)}, bf16[60,1152]{1,0:T(8,128)(2,1)S(1)}, u32[]{:S(2)}, u32[]{:S(2)}) collective-permute-start(bf16[60,1152]{1,0:T(8,128)(2,1)S(1)} %shard_map.94.refs_0_), channel_id=1, source_target_pairs={{0,8},{8,0},{16,24},{24,16},{1,9},{9,1},{17,25},{25,17},{2,10},{10... | collective-permute-start | bytes 414728 | tf_op jit(solution)/shard_map/ppermute | solution.py:363
  31.4 0.4 collective-permute-start.19
  31.8 1.7 %collective-permute-start.20 = (bf16[60,1152]{1,0:T(8,128)(2,1)S(1)}, bf16[60,1152]{1,0:T(8,128)(2,1)S(1)}, u32[]{:S(2)}, u32[]{:S(2)}) collective-permute-start(bf16[60,1152]{1,0:T(8,128)(2,1)S(1)} %shard_map.94.refs_0_), channel_id=1, source_target_pairs={{0,24},{8,16},{16,8},{24,0},{1,25},{9,17},{17,9},{25,1},{2,26},{10... | collective-permute-start | bytes 414728 | tf_op jit(solution)/shard_map/ppermute | solution.py:363
  33.5 0.4 collective-permute-start.10
  33.9 2.4 %collective-permute-start.11 = (bf16[60,1152]{1,0:T(8,128)(2,1)S(1)}, bf16[60,1152]{1,0:T(8,128)(2,1)S(1)}, u32[]{:S(2)}, u32[]{:S(2)}) collective-permute-start(bf16[60,1152]{1,0:T(8,128)(2,1)S(1)} %get-tuple-element.50), channel_id=1, source_target_pairs={{0,24},{8,16},{16,8},{24,0},{1,25},{9,17},{17,9},{25,1},{2,26},{10... | collective-permute-start | bytes 414728 | tf_op jit(solution)/shard_map/ppermute | solution.py:363
  36.4 1.9 %shard_map.87 = (f32[60,1152]{1,0:T(8,128)S(1)}, bf16[60,1152]{1,0:T(8,128)(2,1)S(1)}, bf16[60,1152]{1,0:T(8,128)(2,1)S(1)}, bf16[60,1152]{1,0:T(8,128)(2,1)S(1)}) custom-call(bf16[80,1280]{1,0:T(8,128)(2,1)S(1)} %get-tuple-element.38.x_ref.first_ref, bf16[80,1280]{1,0:T(8,128)(2,1)S(1)} %get-tuple-element.39.y_ref.second_ref, ...), custom_call_target="tpu_custom_call" | custom-call | flops 707788800 | bytes 8847360 | tf_op jit(solution)/shard_map/pallas_call | solution.py:136
  38.2 0.0 collective-permute-done.18.refs_1_
  38.2 0.7 collective-permute-start.3
  38.9 4.5 %collective-permute-done.19.refs_2_ = bf16[60,1152]{1,0:T(8,128)(2,1)S(1)} collective-permute-done((bf16[60,1152]{1,0:T(8,128)(2,1)S(1)}, bf16[60,1152]{1,0:T(8,128)(2,1)S(1)}, u32[]{:S(2)}, u32[]{:S(2)}) %collective-permute-start.19) | collective-permute-done | bytes 138272 | tf_op jit(solution)/shard_map/ppermute | solution.py:363
  43.4 1.4 %collective-permute-start.4 = (bf16[60,1152]{1,0:T(8,128)(2,1)S(1)}, bf16[60,1152]{1,0:T(8,128)(2,1)S(1)}, u32[]{:S(2)}, u32[]{:S(2)}) collective-permute-start(bf16[60,1152]{1,0:T(8,128)(2,1)S(1)} %get-tuple-element.45), channel_id=1, source_target_pairs={{0,16},{8,24},{16,0},{24,8},{1,17},{9,25},{17,1},{25,9},{2,18},{10... | collective-permute-start | bytes 414728 | tf_op jit(solution)/shard_map/ppermute | solution.py:363
  44.8 0.0 collective-permute-start.5
  44.8 0.1 shard_map.95.stack_ref.mine_ref
  44.9 1.8 %collective-permute-done.10.refs_1_ = bf16[60,1152]{1,0:T(8,128)(2,1)S(1)} collective-permute-done((bf16[60,1152]{1,0:T(8,128)(2,1)S(1)}, bf16[60,1152]{1,0:T(8,128)(2,1)S(1)}, u32[]{:S(2)}, u32[]{:S(2)}) %collective-permute-start.10) | collective-permute-done | bytes 138272 | tf_op jit(solution)/shard_map/ppermute | solution.py:363
  46.7 0.1 shard_map.91.refs_0_
  46.8 0.7 collective-permute-start.12
  47.6 1.1 %collective-permute-start.13 = (bf16[60,1152]{1,0:T(8,128)(2,1)S(1)}, bf16[60,1152]{1,0:T(8,128)(2,1)S(1)}, u32[]{:S(2)}, u32[]{:S(2)}) collective-permute-start(bf16[60,1152]{1,0:T(8,128)(2,1)S(1)} %shard_map.91.refs_0_), channel_id=1, source_target_pairs={{0,16},{8,24},{16,0},{24,8},{1,17},{9,25},{17,1},{25,9},{2,18},{10... | collective-permute-start | bytes 414728 | tf_op jit(solution)/shard_map/ppermute | solution.py:363
  48.7 1.7 %collective-permute-start.14 = (bf16[60,1152]{1,0:T(8,128)(2,1)S(1)}, bf16[60,1152]{1,0:T(8,128)(2,1)S(1)}, u32[]{:S(2)}, u32[]{:S(2)}) collective-permute-start(bf16[60,1152]{1,0:T(8,128)(2,1)S(1)} %shard_map.91.refs_0_), channel_id=1, source_target_pairs={{0,24},{8,16},{16,8},{24,0},{1,25},{9,17},{17,9},{25,1},{2,26},{10... | collective-permute-start | bytes 414728 | tf_op jit(solution)/shard_map/ppermute | solution.py:363
  50.4 1.6 %collective-permute-done.5.refs_2_ = bf16[60,1152]{1,0:T(8,128)(2,1)S(1)} collective-permute-done((bf16[60,1152]{1,0:T(8,128)(2,1)S(1)}, bf16[60,1152]{1,0:T(8,128)(2,1)S(1)}, u32[]{:S(2)}, u32[]{:S(2)}) %collective-permute-start.5) | collective-permute-done | bytes 138272 | tf_op jit(solution)/shard_map/ppermute | solution.py:363
  52.0 0.1 shard_map.88.refs_0_
  52.2 0.1 collective-permute-start.6
  52.3 1.3 %collective-permute-done.12.refs_1_ = bf16[60,1152]{1,0:T(8,128)(2,1)S(1)} collective-permute-done((bf16[60,1152]{1,0:T(8,128)(2,1)S(1)}, bf16[60,1152]{1,0:T(8,128)(2,1)S(1)}, u32[]{:S(2)}, u32[]{:S(2)}) %collective-permute-start.12) | collective-permute-done | bytes 138272 | tf_op jit(solution)/shard_map/ppermute | solution.py:363
  53.5 3.2 %collective-permute-done.13.refs_2_ = bf16[60,1152]{1,0:T(8,128)(2,1)S(1)} collective-permute-done((bf16[60,1152]{1,0:T(8,128)(2,1)S(1)}, bf16[60,1152]{1,0:T(8,128)(2,1)S(1)}, u32[]{:S(2)}, u32[]{:S(2)}) %collective-permute-start.13) | collective-permute-done | bytes 138272 | tf_op jit(solution)/shard_map/ppermute | solution.py:363
  56.7 1.6 %collective-permute-done.14.refs_3_ = bf16[60,1152]{1,0:T(8,128)(2,1)S(1)} collective-permute-done((bf16[60,1152]{1,0:T(8,128)(2,1)S(1)}, bf16[60,1152]{1,0:T(8,128)(2,1)S(1)}, u32[]{:S(2)}, u32[]{:S(2)}) %collective-permute-start.14) | collective-permute-done | bytes 138272 | tf_op jit(solution)/shard_map/ppermute | solution.py:363
  58.4 0.1 shard_map.92.stack_ref.mine_ref
  58.4 0.1 collective-permute-start.23
  58.5 0.1 collective-permute-start.7
  58.6 0.9 collective-permute-done.6.refs_1_
  59.5 1.2 %collective-permute-start.8 = (bf16[60,1152]{1,0:T(8,128)(2,1)S(1)}, bf16[60,1152]{1,0:T(8,128)(2,1)S(1)}, u32[]{:S(2)}, u32[]{:S(2)}) collective-permute-start(bf16[60,1152]{1,0:T(8,128)(2,1)S(1)} %shard_map.88.refs_0_), channel_id=1, source_target_pairs={{0,24},{8,16},{16,8},{24,0},{1,25},{9,17},{17,9},{25,1},{2,26},{10... | collective-permute-start | bytes 414728 | tf_op jit(solution)/shard_map/ppermute | solution.py:363
  60.7 7.2 %collective-permute-done.7.refs_2_ = bf16[60,1152]{1,0:T(8,128)(2,1)S(1)} collective-permute-done((bf16[60,1152]{1,0:T(8,128)(2,1)S(1)}, bf16[60,1152]{1,0:T(8,128)(2,1)S(1)}, u32[]{:S(2)}, u32[]{:S(2)}) %collective-permute-start.7) | collective-permute-done | bytes 138272 | tf_op jit(solution)/shard_map/ppermute | solution.py:363
  68.0 0.1 shard_map.89.stack_ref.mine_ref
  68.0 0.1 collective-permute-start.27
  68.1 3.5 %copy-done.1 = bf16[1280,3456]{1,0:T(8,128)(2,1)S(1)} copy-done((bf16[1280,3456]{1,0:T(8,128)(2,1)S(1)}, bf16[1280,3456]{1,0:T(8,128)(2,1)}, u32[]{:S(2)}) %copy-start.1) | copy-done | bytes 8847384
  71.6 3.5 %copy-done.3 = bf16[1280,3456]{1,0:T(8,128)(2,1)S(1)} copy-done((bf16[1280,3456]{1,0:T(8,128)(2,1)S(1)}, bf16[1280,3456]{1,0:T(8,128)(2,1)}, u32[]{:S(2)}) %copy-start.3) | copy-done | bytes 8847384
  75.2 1.9 %shard_map.96.refs_0_ = f32[80,1280]{1,0:T(8,128)S(1)} custom-call(bf16[240,1152]{1,0:T(8,128)(2,1)S(1)} %shard_map.95.stack_ref.mine_ref, bf16[1280,3456]{1,0:T(8,128)(2,1)S(1)} %copy-done.1, bf16[1280,3456]{1,0:T(8,128)(2,1)S(1)} %copy-done.3), custom_call_target="tpu_custom_call" | custom-call | flops 471859200 | bytes 5898240 | tf_op jit(solution)/shard_map/pallas_call | solution.py:207
  77.1 1.8 %shard_map.98 = (bf16[1280,160]{1,0:T(8,128)(2,1)S(1)}, bf16[160,1280]{1,0:T(8,128)(2,1)S(1)}) custom-call(s32[1]{0:T(128)} %bitcast.1.row_ref, bf16[80,1280]{1,0:T(8,128)(2,1)S(1)} %get-tuple-element.38.x_ref.first_ref, bf16[80,1280]{1,0:T(8,128)(2,1)S(1)} %get-tuple-element.39.y_ref.second_ref, bf16[160,1280]{1,0:T(8,128)(2,1)} %collective-permute-done.21.other_ref), custom_call_target="tpu_custom_call" | custom-call | bytes 819200 | tf_op jit(solution)/shard_map/pallas_call | solution.py:230
  78.9 6.1 %shard_map.99 = (bf16[1280,3456]{1,0:T(8,128)(2,1)}, bf16[1280,3456]{1,0:T(8,128)(2,1)}, bf16[3456,1280]{1,0:T(8,128)(2,1)}, f32[8,128]{1,0:T(8,128)S(1)}) custom-call(s32[1]{0:T(128)} %bitcast.1.row_ref, bf16[1280,160]{1,0:T(8,128)(2,1)S(1)} %get-tuple-element.55.xt_ref, bf16[160,1280]{1,0:T(8,128)(2,1)S(1)} %get-tuple-element.56.y_ref, ...), custom_call_target="tpu_custom_call" | custom-call | flops 1415577600 | bytes 8847360 | tf_op jit(solution)/shard_map/pallas_call | solution.py:302
  85.0 3.5 %copy-done.4 = bf16[1280,3456]{1,0:T(8,128)(2,1)S(1)} copy-done((bf16[1280,3456]{1,0:T(8,128)(2,1)S(1)}, bf16[1280,3456]{1,0:T(8,128)(2,1)}, u32[]{:S(2)}) %copy-start.4) | copy-done | bytes 8847384
  88.5 1.9 %shard_map.100.refs_0_ = f32[80,1280]{1,0:T(8,128)S(1)} custom-call(bf16[240,1152]{1,0:T(8,128)(2,1)S(1)} %shard_map.92.stack_ref.mine_ref, bf16[1280,3456]{1,0:T(8,128)(2,1)S(1)} %bitcast.3, bf16[1280,3456]{1,0:T(8,128)(2,1)S(1)} %copy-done.4, f32[80,1280]{1,0:T(8,128)S(1)} %shard_map.96.refs_0_, f32[8,128]{1,0:T(8,128)S(1)} %get-tuple-element.57.refs_1_), custom_call_target="tpu_custom_call" | custom-call | flops 471859200 | bytes 5898240 | tf_op jit(solution)/shard_map/pallas_call | solution.py:207
  90.4 6.5 %shard_map.101 = (bf16[1280,3456]{1,0:T(8,128)(2,1)}, bf16[1280,3456]{1,0:T(8,128)(2,1)}, bf16[3456,1280]{1,0:T(8,128)(2,1)}, f32[8,128]{1,0:T(8,128)S(1)}) custom-call(s32[1]{0:T(128)} %bitcast.1.row_ref, bf16[1280,160]{1,0:T(8,128)(2,1)S(1)} %get-tuple-element.55.xt_ref, ...), custom_call_target="tpu_custom_call", output_to_operand_aliasing={{0}: (5, {}), {1}: (6, {}), {2}: (7, {})} | custom-call | flops 1415577600 | bytes 8847360 | tf_op jit(solution)/shard_map/pallas_call | solution.py:302
  96.9 1.9 %shard_map.102.grad_ref = f32[80,1280]{1,0:T(8,128)S(1)} custom-call(bf16[240,1152]{1,0:T(8,128)(2,1)S(1)} %shard_map.89.stack_ref.mine_ref, bf16[1280,3456]{1,0:T(8,128)(2,1)S(1)} %bitcast.3, bf16[1280,3456]{1,0:T(8,128)(2,1)S(1)} %bitcast.5, f32[80,1280]{1,0:T(8,128)S(1)} %shard_map.100.refs_0_, f32[8,128]{1,0:T(8,128)S(1)} %get-tuple-element.61.refs_1_), custom_call_target="tpu_custom_call" | custom-call | flops 471859200 | bytes 5898240 | tf_op jit(solution)/shard_map/pallas_call | solution.py:207
  98.8 0.2 shard_map.103
  99.0 0.4 collective-permute-start.24
  99.4 3.4 %collective-permute-start.25 = (bf16[20,1280]{1,0:T(8,128)(2,1)S(1)}, bf16[20,1280]{1,0:T(8,128)(2,1)S(1)}, u32[]{:S(2)}, u32[]{:S(2)}) collective-permute-start(bf16[20,1280]{1,0:T(8,128)(2,1)S(1)} %get-tuple-element.64), channel_id=1, source_target_pairs={{0,4},{2,6},{4,0},{6,2},{1,5},{3,7},{5,1},{7,3},{8,12},{10,14},{12... | collective-permute-start | bytes 153608 | tf_op jit(solution)/shard_map/ppermute | solution.py:363
  102.7 0.7 collective-permute-start.26
  103.4 5.0 %shard_map.105 = (bf16[1280,3456]{1,0:T(8,128)(2,1)}, bf16[1280,3456]{1,0:T(8,128)(2,1)}, bf16[3456,1280]{1,0:T(8,128)(2,1)}, f32[8,128]{1,0:T(8,128)}) custom-call(s32[1]{0:T(128)} %bitcast.1.row_ref, bf16[1280,160]{1,0:T(8,128)(2,1)S(1)} %get-tuple-element.55.xt_ref, ...), custom_call_target="tpu_custom_call", output_to_operand_aliasing={{0}: (5, {}), {1}: (6, {}), {2}: (7, {})} | custom-call | flops 1415577600 | bytes 8847360 | tf_op jit(solution)/shard_map/pallas_call | solution.py:302
  108.5 0.3 collective-permute-done.26.refs_2_
  108.8 0.7 shard_map.104
  (42 shorter events, 0.1 us)
Async XLA Ops:
  0.6 0.8 copy-start.5
  1.5 0.8 copy-start.6
  2.3 14.4 %collective-permute-start = (bf16[40,1280]{1,0:T(8,128)(2,1)S(1)}, bf16[40,1280]{1,0:T(8,128)(2,1)S(1)}, u32[]{:S(2)}, u32[]{:S(2)}) collective-permute-start(bf16[40,1280]{1,0:T(8,128)(2,1)S(1)} %shard_map.84.refs_0_), channel_id=1, source_target_pairs={{0,2},{2,0},{4,6},{6,4},{1,3},{3,1},{5,7},{7,5},{8,10},{10,8},{12,... | collective-permute-start | bytes 307208 | tf_op jit(solution)/shard_map/ppermute | solution.py:363
  5.4 11.4 %collective-permute-start.1 = (bf16[40,1280]{1,0:T(8,128)(2,1)S(1)}, bf16[40,1280]{1,0:T(8,128)(2,1)S(1)}, u32[]{:S(2)}, u32[]{:S(2)}) collective-permute-start(bf16[40,1280]{1,0:T(8,128)(2,1)S(1)} %shard_map.84.refs_0_), channel_id=1, source_target_pairs={{0,4},{2,6},{4,0},{6,2},{1,5},{3,7},{5,1},{7,3},{8,12},{10,14},{12... | collective-permute-start | bytes 307208 | tf_op jit(solution)/shard_map/ppermute | solution.py:363
  8.0 8.8 %collective-permute-start.2 = (bf16[40,1280]{1,0:T(8,128)(2,1)S(1)}, bf16[40,1280]{1,0:T(8,128)(2,1)S(1)}, u32[]{:S(2)}, u32[]{:S(2)}) collective-permute-start(bf16[40,1280]{1,0:T(8,128)(2,1)S(1)} %shard_map.84.refs_0_), channel_id=1, source_target_pairs={{0,6},{2,4},{4,2},{6,0},{1,7},{3,5},{5,3},{7,1},{8,14},{10,12},{12... | collective-permute-start | bytes 307208 | tf_op jit(solution)/shard_map/ppermute | solution.py:363
  16.7 19.6 %copy-start = (bf16[1280,3456]{1,0:T(8,128)(2,1)}, bf16[1280,3456]{1,0:T(8,128)(2,1)S(1)}, u32[]{:S(2)}) copy-start(bf16[1280,3456]{1,0:T(8,128)(2,1)S(1)} %get-tuple-element.40.gate_ref) | copy-start | bytes 26542084
  16.7 19.6 %copy-start.2 = (bf16[1280,3456]{1,0:T(8,128)(2,1)}, bf16[1280,3456]{1,0:T(8,128)(2,1)S(1)}, u32[]{:S(2)}) copy-start(bf16[1280,3456]{1,0:T(8,128)(2,1)S(1)} %get-tuple-element.41.up_ref) | copy-start | bytes 26542084
  18.8 7.2 %collective-permute-start.15 = (bf16[60,1152]{1,0:T(8,128)(2,1)S(1)}, bf16[60,1152]{1,0:T(8,128)(2,1)S(1)}, u32[]{:S(2)}, u32[]{:S(2)}) collective-permute-start(bf16[60,1152]{1,0:T(8,128)(2,1)S(1)} %get-tuple-element.52), channel_id=1, source_target_pairs={{0,8},{8,0},{16,24},{24,16},{1,9},{9,1},{17,25},{25,17},{2,10},{10... | collective-permute-start | bytes 414728 | tf_op jit(solution)/shard_map/ppermute | solution.py:363
  20.6 7.3 %collective-permute-start.16 = (bf16[60,1152]{1,0:T(8,128)(2,1)S(1)}, bf16[60,1152]{1,0:T(8,128)(2,1)S(1)}, u32[]{:S(2)}, u32[]{:S(2)}) collective-permute-start(bf16[60,1152]{1,0:T(8,128)(2,1)S(1)} %get-tuple-element.53), channel_id=1, source_target_pairs={{0,16},{8,24},{16,0},{24,8},{1,17},{9,25},{17,1},{25,9},{2,18},{10... | collective-permute-start | bytes 414728 | tf_op jit(solution)/shard_map/ppermute | solution.py:363
  22.1 7.7 %collective-permute-start.17 = (bf16[60,1152]{1,0:T(8,128)(2,1)S(1)}, bf16[60,1152]{1,0:T(8,128)(2,1)S(1)}, u32[]{:S(2)}, u32[]{:S(2)}) collective-permute-start(bf16[60,1152]{1,0:T(8,128)(2,1)S(1)} %get-tuple-element.54), channel_id=1, source_target_pairs={{0,24},{8,16},{16,8},{24,0},{1,25},{9,17},{17,9},{25,1},{2,26},{10... | collective-permute-start | bytes 414728 | tf_op jit(solution)/shard_map/ppermute | solution.py:363
  24.2 9.7 %collective-permute-start.9 = (bf16[60,1152]{1,0:T(8,128)(2,1)S(1)}, bf16[60,1152]{1,0:T(8,128)(2,1)S(1)}, u32[]{:S(2)}, u32[]{:S(2)}) collective-permute-start(bf16[60,1152]{1,0:T(8,128)(2,1)S(1)} %get-tuple-element.48), channel_id=1, source_target_pairs={{0,8},{8,0},{16,24},{24,16},{1,9},{9,1},{17,25},{25,17},{2,10},{10... | collective-permute-start | bytes 414728 | tf_op jit(solution)/shard_map/ppermute | solution.py:363
  29.9 8.3 %collective-permute-start.18 = (bf16[60,1152]{1,0:T(8,128)(2,1)S(1)}, bf16[60,1152]{1,0:T(8,128)(2,1)S(1)}, u32[]{:S(2)}, u32[]{:S(2)}) collective-permute-start(bf16[60,1152]{1,0:T(8,128)(2,1)S(1)} %shard_map.94.refs_0_), channel_id=1, source_target_pairs={{0,8},{8,0},{16,24},{24,16},{1,9},{9,1},{17,25},{25,17},{2,10},{10... | collective-permute-start | bytes 414728 | tf_op jit(solution)/shard_map/ppermute | solution.py:363
  31.4 12.0 %collective-permute-start.19 = (bf16[60,1152]{1,0:T(8,128)(2,1)S(1)}, bf16[60,1152]{1,0:T(8,128)(2,1)S(1)}, u32[]{:S(2)}, u32[]{:S(2)}) collective-permute-start(bf16[60,1152]{1,0:T(8,128)(2,1)S(1)} %shard_map.94.refs_0_), channel_id=1, source_target_pairs={{0,16},{8,24},{16,0},{24,8},{1,17},{9,25},{17,1},{25,9},{2,18},{10... | collective-permute-start | bytes 414728 | tf_op jit(solution)/shard_map/ppermute | solution.py:363
  31.8 13.0 %collective-permute-start.20 = (bf16[60,1152]{1,0:T(8,128)(2,1)S(1)}, bf16[60,1152]{1,0:T(8,128)(2,1)S(1)}, u32[]{:S(2)}, u32[]{:S(2)}) collective-permute-start(bf16[60,1152]{1,0:T(8,128)(2,1)S(1)} %shard_map.94.refs_0_), channel_id=1, source_target_pairs={{0,24},{8,16},{16,8},{24,0},{1,25},{9,17},{17,9},{25,1},{2,26},{10... | collective-permute-start | bytes 414728 | tf_op jit(solution)/shard_map/ppermute | solution.py:363
  33.5 13.2 %collective-permute-start.10 = (bf16[60,1152]{1,0:T(8,128)(2,1)S(1)}, bf16[60,1152]{1,0:T(8,128)(2,1)S(1)}, u32[]{:S(2)}, u32[]{:S(2)}) collective-permute-start(bf16[60,1152]{1,0:T(8,128)(2,1)S(1)} %get-tuple-element.49), channel_id=1, source_target_pairs={{0,16},{8,24},{16,0},{24,8},{1,17},{9,25},{17,1},{25,9},{2,18},{10... | collective-permute-start | bytes 414728 | tf_op jit(solution)/shard_map/ppermute | solution.py:363
  33.9 12.8 %collective-permute-start.11 = (bf16[60,1152]{1,0:T(8,128)(2,1)S(1)}, bf16[60,1152]{1,0:T(8,128)(2,1)S(1)}, u32[]{:S(2)}, u32[]{:S(2)}) collective-permute-start(bf16[60,1152]{1,0:T(8,128)(2,1)S(1)} %get-tuple-element.50), channel_id=1, source_target_pairs={{0,24},{8,16},{16,8},{24,0},{1,25},{9,17},{17,9},{25,1},{2,26},{10... | collective-permute-start | bytes 414728 | tf_op jit(solution)/shard_map/ppermute | solution.py:363
  38.2 9.4 %collective-permute-start.3 = (bf16[60,1152]{1,0:T(8,128)(2,1)S(1)}, bf16[60,1152]{1,0:T(8,128)(2,1)S(1)}, u32[]{:S(2)}, u32[]{:S(2)}) collective-permute-start(bf16[60,1152]{1,0:T(8,128)(2,1)S(1)} %get-tuple-element.44), channel_id=1, source_target_pairs={{0,8},{8,0},{16,24},{24,16},{1,9},{9,1},{17,25},{25,17},{2,10},{10... | collective-permute-start | bytes 414728 | tf_op jit(solution)/shard_map/ppermute | solution.py:363
  43.4 5.3 %collective-permute-start.4 = (bf16[60,1152]{1,0:T(8,128)(2,1)S(1)}, bf16[60,1152]{1,0:T(8,128)(2,1)S(1)}, u32[]{:S(2)}, u32[]{:S(2)}) collective-permute-start(bf16[60,1152]{1,0:T(8,128)(2,1)S(1)} %get-tuple-element.45), channel_id=1, source_target_pairs={{0,16},{8,24},{16,0},{24,8},{1,17},{9,25},{17,1},{25,9},{2,18},{10... | collective-permute-start | bytes 414728 | tf_op jit(solution)/shard_map/ppermute | solution.py:363
  44.8 7.2 %collective-permute-start.5 = (bf16[60,1152]{1,0:T(8,128)(2,1)S(1)}, bf16[60,1152]{1,0:T(8,128)(2,1)S(1)}, u32[]{:S(2)}, u32[]{:S(2)}) collective-permute-start(bf16[60,1152]{1,0:T(8,128)(2,1)S(1)} %get-tuple-element.46), channel_id=1, source_target_pairs={{0,24},{8,16},{16,8},{24,0},{1,25},{9,17},{17,9},{25,1},{2,26},{10... | collective-permute-start | bytes 414728 | tf_op jit(solution)/shard_map/ppermute | solution.py:363
  46.7 32.2 %collective-permute-start.22 = (bf16[240,1152]{1,0:T(8,128)(2,1)S(1)}, bf16[240,1152]{1,0:T(8,128)(2,1)}, u32[]{:S(2)}, u32[]{:S(2)}) collective-permute-start(bf16[240,1152]{1,0:T(8,128)(2,1)S(1)} %shard_map.95.stack_ref.mine_ref), channel_id=1, source_target_pairs={{0,1},{1,0},{2,3},{3,2},{4,5},{5,4},{6,7},{7,6},{8,9},{9,8},{10,11... | collective-permute-start | bytes 1658888 | tf_op jit(solution)/shard_map/ppermute | solution.py:363
  46.8 6.7 %collective-permute-start.12 = (bf16[60,1152]{1,0:T(8,128)(2,1)S(1)}, bf16[60,1152]{1,0:T(8,128)(2,1)S(1)}, u32[]{:S(2)}, u32[]{:S(2)}) collective-permute-start(bf16[60,1152]{1,0:T(8,128)(2,1)S(1)} %shard_map.91.refs_0_), channel_id=1, source_target_pairs={{0,8},{8,0},{16,24},{24,16},{1,9},{9,1},{17,25},{25,17},{2,10},{10... | collective-permute-start | bytes 414728 | tf_op jit(solution)/shard_map/ppermute | solution.py:363
  47.6 9.1 %collective-permute-start.13 = (bf16[60,1152]{1,0:T(8,128)(2,1)S(1)}, bf16[60,1152]{1,0:T(8,128)(2,1)S(1)}, u32[]{:S(2)}, u32[]{:S(2)}) collective-permute-start(bf16[60,1152]{1,0:T(8,128)(2,1)S(1)} %shard_map.91.refs_0_), channel_id=1, source_target_pairs={{0,16},{8,24},{16,0},{24,8},{1,17},{9,25},{17,1},{25,9},{2,18},{10... | collective-permute-start | bytes 414728 | tf_op jit(solution)/shard_map/ppermute | solution.py:363
  48.7 9.7 %collective-permute-start.14 = (bf16[60,1152]{1,0:T(8,128)(2,1)S(1)}, bf16[60,1152]{1,0:T(8,128)(2,1)S(1)}, u32[]{:S(2)}, u32[]{:S(2)}) collective-permute-start(bf16[60,1152]{1,0:T(8,128)(2,1)S(1)} %shard_map.91.refs_0_), channel_id=1, source_target_pairs={{0,24},{8,16},{16,8},{24,0},{1,25},{9,17},{17,9},{25,1},{2,26},{10... | collective-permute-start | bytes 414728 | tf_op jit(solution)/shard_map/ppermute | solution.py:363
  52.2 7.3 %collective-permute-start.6 = (bf16[60,1152]{1,0:T(8,128)(2,1)S(1)}, bf16[60,1152]{1,0:T(8,128)(2,1)S(1)}, u32[]{:S(2)}, u32[]{:S(2)}) collective-permute-start(bf16[60,1152]{1,0:T(8,128)(2,1)S(1)} %shard_map.88.refs_0_), channel_id=1, source_target_pairs={{0,8},{8,0},{16,24},{24,16},{1,9},{9,1},{17,25},{25,17},{2,10},{10... | collective-permute-start | bytes 414728 | tf_op jit(solution)/shard_map/ppermute | solution.py:363
  53.5 23.5 %collective-permute-start.21 = (bf16[160,1280]{1,0:T(8,128)(2,1)S(1)}, bf16[160,1280]{1,0:T(8,128)(2,1)}, u32[]{:S(2)}, u32[]{:S(2)}) collective-permute-start(bf16[160,1280]{1,0:T(8,128)(2,1)S(1)} %shard_map.97), channel_id=1, source_target_pairs={{0,1},{1,0},{2,3},{3,2},{4,5},{5,4},{6,7},{7,6},{8,9},{9,8},{10,11... | collective-permute-start | bytes 1228808 | tf_op jit(solution)/shard_map/ppermute | solution.py:363
  58.4 32.0 %collective-permute-start.23 = (bf16[240,1152]{1,0:T(8,128)(2,1)S(1)}, bf16[240,1152]{1,0:T(8,128)(2,1)}, u32[]{:S(2)}, u32[]{:S(2)}) collective-permute-start(bf16[240,1152]{1,0:T(8,128)(2,1)S(1)} %shard_map.92.stack_ref.mine_ref), channel_id=1, source_target_pairs={{0,1},{1,0},{2,3},{3,2},{4,5},{5,4},{6,7},{7,6},{8,9},{9,8},{10,11... | collective-permute-start | bytes 1658888 | tf_op jit(solution)/shard_map/ppermute | solution.py:363
  58.5 9.4 %collective-permute-start.7 = (bf16[60,1152]{1,0:T(8,128)(2,1)S(1)}, bf16[60,1152]{1,0:T(8,128)(2,1)S(1)}, u32[]{:S(2)}, u32[]{:S(2)}) collective-permute-start(bf16[60,1152]{1,0:T(8,128)(2,1)S(1)} %shard_map.88.refs_0_), channel_id=1, source_target_pairs={{0,16},{8,24},{16,0},{24,8},{1,17},{9,25},{17,1},{25,9},{2,18},{10... | collective-permute-start | bytes 414728 | tf_op jit(solution)/shard_map/ppermute | solution.py:363
  59.5 8.5 %collective-permute-start.8 = (bf16[60,1152]{1,0:T(8,128)(2,1)S(1)}, bf16[60,1152]{1,0:T(8,128)(2,1)S(1)}, u32[]{:S(2)}, u32[]{:S(2)}) collective-permute-start(bf16[60,1152]{1,0:T(8,128)(2,1)S(1)} %shard_map.88.refs_0_), channel_id=1, source_target_pairs={{0,24},{8,16},{16,8},{24,0},{1,25},{9,17},{17,9},{25,1},{2,26},{10... | collective-permute-start | bytes 414728 | tf_op jit(solution)/shard_map/ppermute | solution.py:363
  68.0 17.0 %slice-start = ((s8[8847360]{0:T(1024)(128)(4,1)}), s8[458752]{0:T(1024)(128)(4,1)S(1)}, s32[]{:S(2)}) async-start(s8[8847360]{0:T(1024)(128)(4,1)} %bitcast.2), calls=%async_computation | async-start | bytes 917504
  68.0 35.4 %collective-permute-start.27 = (bf16[240,1152]{1,0:T(8,128)(2,1)S(1)}, bf16[240,1152]{1,0:T(8,128)(2,1)S(1)}, u32[]{:S(2)}, u32[]{:S(2)}) collective-permute-start(bf16[240,1152]{1,0:T(8,128)(2,1)S(1)} %shard_map.89.stack_ref.mine_ref), channel_id=1, source_target_pairs={{0,1},{1,0},{2,3},{3,2},{4,5},{5,4},{6,7},{7,6},{8,9},{9,8},{10,11... | collective-permute-start | bytes 1658888 | tf_op jit(solution)/shard_map/ppermute | solution.py:363
  68.1 3.5 %copy-start.1 = (bf16[1280,3456]{1,0:T(8,128)(2,1)S(1)}, bf16[1280,3456]{1,0:T(8,128)(2,1)}, u32[]{:S(2)}) copy-start(bf16[1280,3456]{1,0:T(8,128)(2,1)} %copy-done) | copy-start | bytes 26542084
  71.6 3.5 %copy-start.3 = (bf16[1280,3456]{1,0:T(8,128)(2,1)S(1)}, bf16[1280,3456]{1,0:T(8,128)(2,1)}, u32[]{:S(2)}) copy-start(bf16[1280,3456]{1,0:T(8,128)(2,1)} %copy-done.2) | copy-start | bytes 26542084
  75.2 9.8 %slice-start.1 = ((s8[8847360]{0:T(1024)(128)(4,1)}), s8[4194304]{0:T(1024)(128)(4,1)S(1)}, s32[]{:S(2)}) async-start(s8[8847360]{0:T(1024)(128)(4,1)} %bitcast.2), calls=%async_computation.1 | async-start | bytes 8388608
  75.2 9.8 %slice-start.2 = ((s8[8847360]{0:T(1024)(128)(4,1)}), s8[4194304]{0:T(1024)(128)(4,1)S(1)}, s32[]{:S(2)}) async-start(s8[8847360]{0:T(1024)(128)(4,1)} %bitcast.2), calls=%async_computation.2 | async-start | bytes 8388608
  85.0 3.5 %copy-start.4 = (bf16[1280,3456]{1,0:T(8,128)(2,1)S(1)}, bf16[1280,3456]{1,0:T(8,128)(2,1)}, u32[]{:S(2)}) copy-start(bf16[1280,3456]{1,0:T(8,128)(2,1)} %copy-done.2) | copy-start | bytes 26542084
  88.5 8.4 %slice-start.3 = ((s8[8847360]{0:T(1024)(128)(4,1)}), s8[4194304]{0:T(1024)(128)(4,1)S(1)}, s32[]{:S(2)}) async-start(s8[8847360]{0:T(1024)(128)(4,1)} %bitcast.4), calls=%async_computation.3 | async-start | bytes 8388608
  88.5 8.4 %slice-start.4 = ((s8[8847360]{0:T(1024)(128)(4,1)}), s8[4194304]{0:T(1024)(128)(4,1)S(1)}, s32[]{:S(2)}) async-start(s8[8847360]{0:T(1024)(128)(4,1)} %bitcast.4), calls=%async_computation.4 | async-start | bytes 8388608
  90.4 6.5 %slice-start.5 = ((s8[8847360]{0:T(1024)(128)(4,1)}), s8[458752]{0:T(1024)(128)(4,1)S(1)}, s32[]{:S(2)}) async-start(s8[8847360]{0:T(1024)(128)(4,1)} %bitcast.4), calls=%async_computation.5 | async-start | bytes 917504
  99.0 9.5 %collective-permute-start.24 = (bf16[20,1280]{1,0:T(8,128)(2,1)S(1)}, bf16[20,1280]{1,0:T(8,128)(2,1)S(1)}, u32[]{:S(2)}, u32[]{:S(2)}) collective-permute-start(bf16[20,1280]{1,0:T(8,128)(2,1)S(1)} %get-tuple-element.63), channel_id=1, source_target_pairs={{0,2},{2,0},{4,6},{6,4},{1,3},{3,1},{5,7},{7,5},{8,10},{10,8},{12,... | collective-permute-start | bytes 153608 | tf_op jit(solution)/shard_map/ppermute | solution.py:363
  99.4 9.1 %collective-permute-start.25 = (bf16[20,1280]{1,0:T(8,128)(2,1)S(1)}, bf16[20,1280]{1,0:T(8,128)(2,1)S(1)}, u32[]{:S(2)}, u32[]{:S(2)}) collective-permute-start(bf16[20,1280]{1,0:T(8,128)(2,1)S(1)} %get-tuple-element.64), channel_id=1, source_target_pairs={{0,4},{2,6},{4,0},{6,2},{1,5},{3,7},{5,1},{7,3},{8,12},{10,14},{12... | collective-permute-start | bytes 153608 | tf_op jit(solution)/shard_map/ppermute | solution.py:363
  102.7 6.1 %collective-permute-start.26 = (bf16[20,1280]{1,0:T(8,128)(2,1)S(1)}, bf16[20,1280]{1,0:T(8,128)(2,1)S(1)}, u32[]{:S(2)}, u32[]{:S(2)}) collective-permute-start(bf16[20,1280]{1,0:T(8,128)(2,1)S(1)} %get-tuple-element.65), channel_id=1, source_target_pairs={{0,6},{2,4},{4,2},{6,0},{1,7},{3,5},{5,3},{7,1},{8,14},{10,12},{12... | collective-permute-start | bytes 153608 | tf_op jit(solution)/shard_map/ppermute | solution.py:363

commit v3 on v2

--- a/solution.py
+++ b/solution.py
@@ -12,7 +12,8 @@
 NT = (((1,), (1,)), ((), ()))
 TN = (((0,), (0,)), ((), ()))
 LANES = 128
-CHUNKS = 3
+CHUNKS = 4
+TILE = 256
 MIB = 1024 * 1024
 
 
@@ -45,15 +46,14 @@
     return pl.BlockSpec(shape, lambda i: (0,) * len(shape))
 
 
-SCALAR = pl.BlockSpec(memory_space=pltpu.SMEM)
 IN_VMEM = pl.BlockSpec(memory_space=pltpu.VMEM)
 TOKEN = jax.ShapeDtypeStruct((8, LANES), F32)
 
 
-def order_kernel(parts, rows, wa_ref, *refs):
+def order_kernel(parts, rows, *refs):
     pieces = [ref[...].astype(F32) for ref in refs[:parts]]
     x_ref, y_ref = refs[parts:]
-    wa = wa_ref[0]
+    wa = lax.axis_index("wa")
     xs, ys = [], []
     for slot in range(parts):
         at = wa ^ slot
@@ -66,33 +66,34 @@
     y_ref[...] = jnp.concatenate(ys, axis=0).astype(BF16)
 
 
-def order_rows(wa, pieces):
+def order_rows(pieces):
     parts = len(pieces)
     rows, width = pieces[0].shape[0] // 2, pieces[0].shape[1]
     shape = (parts * rows, width)
     return call(
         functools.partial(order_kernel, parts, rows),
         (),
-        [SCALAR] + [IN_VMEM] * parts,
+        [IN_VMEM] * parts,
         [IN_VMEM] * 2,
         [jax.ShapeDtypeStruct(shape, BF16)] * 2,
         0,
         8 * shape[0] * width,
-    )(wa, *pieces)
-
-
-def forward_kernel(parts, rows, begin, x_ref, y_ref, gate_ref, up_ref, down_ref, own_ref, *send_refs):
-    there = pl.ds(begin, own_ref.shape[1])
+    )(*pieces)
+
+
+def forward_kernel(rows, begin, near, far, after, x_ref, y_ref, gate_ref, up_ref, down_ref, *refs):
+    keep_ref, send_ref = refs[after:]
+    there = pl.ds(begin, keep_ref.shape[1])
     gate = jnp.dot(x_ref[...], gate_ref[:, there], preferred_element_type=F32)
     up = jnp.dot(x_ref[...], up_ref[:, there], preferred_element_type=F32)
     dh = lax.dot_general(y_ref[...], down_ref[there, :], NT, preferred_element_type=F32)
-    for slot in range(parts):
-        cut = slice(slot * rows, (slot + 1) * rows)
-        block = jnp.concatenate([gate[cut], up[cut], dh[cut]], axis=0)
-        if slot == 0:
-            own_ref[...] = block
-        else:
-            send_refs[slot - 1][...] = block.astype(BF16)
+
+    def slots(*which):
+        cuts = [slice(slot * rows, (slot + 1) * rows) for slot in which]
+        return jnp.concatenate([part[cut] for cut in cuts for part in (gate, up, dh)], axis=0)
+
+    keep_ref[...] = slots(0, far)
+    send_ref[...] = slots(near, near ^ far).astype(BF16)
 
 
 def load_kernel(cuts, *refs):
@@ -129,20 +130,41 @@
     )(*weights)
 
 
-def forward(parts, first, count, tile, x, y, gate_weight, up_weight, down_weight):
+def forward(begin, columns, near, far, x, y, gate_weight, up_weight, down_weight, after):
     group, width = x.shape
-    rows = group // parts
-    columns = count * tile
-    return call(
-        functools.partial(forward_kernel, parts, rows, first * tile),
-        (),
-        [IN_VMEM] * 5,
-        [IN_VMEM] * parts,
-        [jax.ShapeDtypeStruct((3 * rows, columns), F32)]
-        + [jax.ShapeDtypeStruct((3 * rows, columns), BF16)] * (parts - 1),
+    rows = group // 4
+    return call(
+        functools.partial(forward_kernel, rows, begin, near, far, len(after)),
+        (),
+        [IN_VMEM] * (5 + len(after)),
+        [IN_VMEM] * 2,
+        [
+            jax.ShapeDtypeStruct((6 * rows, columns), F32),
+            jax.ShapeDtypeStruct((6 * rows, columns), BF16),
+        ],
         6 * group * width * columns,
         6 * width * columns,
-    )(x, y, gate_weight, up_weight, down_weight)
+    )(x, y, gate_weight, up_weight, down_weight, *after)
+
+
+def halve_kernel(keep_ref, received_ref, _, own_ref, send_ref):
+    total = keep_ref[...] + received_ref[...].astype(F32)
+    half = own_ref.shape[0]
+    own_ref[...] = total[:half]
+    send_ref[...] = total[half:].astype(BF16)
+
+
+def halve(keep, received, after):
+    shape = (keep.shape[0] // 2, keep.shape[1])
+    return call(
+        halve_kernel,
+        (),
+        [IN_VMEM] * 3,
+        [IN_VMEM] * 2,
+        [jax.ShapeDtypeStruct(shape, F32), jax.ShapeDtypeStruct(shape, BF16)],
+        2 * keep.size,
+        9 * keep.size,
+    )(keep, received, after)
 
 
 def middle_kernel(rows, own_ref, *refs):
@@ -168,37 +190,36 @@
     )(own, *received)
 
 
-def stack_kernel(rows, *refs):
-    blocks = [ref[...].astype(F32) for ref in refs[:-1]]
-    cuts = [
-        block[at * rows : (at + 1) * rows] for at in range(3) for block in blocks
-    ]
-    refs[-1][...] = jnp.concatenate(cuts, axis=0).astype(BF16)
-
-
-def stack(blocks):
-    parts = len(blocks)
-    rows, columns = blocks[0].shape[0] // 3, blocks[0].shape[1]
-    shape = (3 * parts * rows, columns)
-    return call(
-        functools.partial(stack_kernel, rows),
-        (),
-        [IN_VMEM] * parts,
+def stack_kernel(rows, near, far, mine_ref, other_ref, out_ref):
+    mine, other = mine_ref[...].astype(F32), other_ref[...].astype(F32)
+    slots = {0: mine[: 3 * rows], near: mine[3 * rows :]}
+    slots |= {far: other[: 3 * rows], near ^ far: other[3 * rows :]}
+    cuts = [slots[slot][at * rows : (at + 1) * rows] for at in range(3) for slot in range(4)]
+    out_ref[...] = jnp.concatenate(cuts, axis=0).astype(BF16)
+
+
+def stack(near, far, mine, other):
+    rows, columns = mine.shape[0] // 6, mine.shape[1]
+    shape = (12 * rows, columns)
+    return call(
+        functools.partial(stack_kernel, rows, near, far),
+        (),
+        [IN_VMEM] * 2,
         IN_VMEM,
         jax.ShapeDtypeStruct(shape, BF16),
         0,
         4 * shape[0] * columns,
-    )(*blocks)
-
-
-def input_grad_kernel(group, begin, after, stack_ref, gate_ref, up_ref, *refs):
+    )(mine, other)
+
+
+def input_grad_kernel(group, begin, has_start, stack_ref, gate_ref, up_ref, *refs):
     there = pl.ds(begin, stack_ref.shape[1])
     grad = lax.dot_general(
         stack_ref[:group], gate_ref[:, there], NT, preferred_element_type=F32
     ) + lax.dot_general(
         stack_ref[group : 2 * group], up_ref[:, there], NT, preferred_element_type=F32
     )
-    refs[-1][...] = grad + refs[0][...] if after else grad
+    refs[-1][...] = grad + refs[0][...] if has_start else grad
 
 
 def input_grad(begin, stacked, gate_weight, up_weight, after):
@@ -215,8 +236,8 @@
     )(stacked, gate_weight, up_weight, *after)
 
 
-def factors_kernel(group, row_ref, x_ref, y_ref, other_ref, xt_ref, y_all_ref):
-    first = row_ref[0] == 0
+def factors_kernel(group, x_ref, y_ref, other_ref, xt_ref, y_all_ref):
+    first = lax.axis_index("row") == 0
     x, y = x_ref[...], y_ref[...]
     x_other, y_other = other_ref[:group], other_ref[group:]
     y_all_ref[:group] = jnp.where(first, y, y_other)
@@ -225,12 +246,12 @@
     xt_ref[...] = x_all.T
 
 
-def factors(row, x, y, other):
+def factors(x, y, other):
     group, width = x.shape
     return call(
         functools.partial(factors_kernel, group),
         (),
-        [SCALAR] + [IN_VMEM] * 3,
+        [IN_VMEM] * 3,
         [IN_VMEM] * 2,
         [
             jax.ShapeDtypeStruct((width, 2 * group), BF16),
@@ -238,7 +259,7 @@
         ],
         0,
         8 * group * width,
-    )(row, x, y, other)
+    )(x, y, other)
 
 
 def join_kernel(first_ref, second_ref, out_ref):
@@ -247,13 +268,13 @@
     ).astype(BF16)
 
 
-def join(first, second):
+def join(first, second, from_hbm=False):
     shape = (first.shape[0] + second.shape[0], first.shape[1])
     return call(
         join_kernel,
-        (),
-        [IN_VMEM] * 2,
-        IN_VMEM,
+        (1,) if from_hbm else (),
+        [whole(first.shape), whole(second.shape)] if from_hbm else [IN_VMEM] * 2,
+        whole(shape) if from_hbm else IN_VMEM,
         jax.ShapeDtypeStruct(shape, BF16),
         0,
         4 * shape[0] * shape[1],
@@ -279,61 +300,73 @@
     )(own, *received)
 
 
-def weight_grad_kernel(group, has_start, row_ref, xt_ref, y_ref, mine_ref, other_ref, *refs):
-    gate_ref, up_ref, down_ref, token_ref, both = refs[3 * has_start :]
-    token_ref[...] = jnp.zeros_like(token_ref)
-    first = row_ref[0] == 0
+def weight_grad_kernel(group, begin, skip, xt_ref, y_ref, mine_ref, other_ref, *refs):
+    *outs, token_ref, both, gate, up, down, sems = refs[skip:]
+    columns = mine_ref.shape[1]
+    first = lax.axis_index("row") == 0
     for at in range(3):
         cut = slice(at * group, (at + 1) * group)
         both[at, :group] = jnp.where(first, mine_ref[cut], other_ref[cut])
         both[at, group:] = jnp.where(first, other_ref[cut], mine_ref[cut])
-    gate_ref[...] = jnp.dot(xt_ref[...], both[0], preferred_element_type=F32).astype(BF16)
-    up_ref[...] = jnp.dot(xt_ref[...], both[1], preferred_element_type=F32).astype(BF16)
-    down_ref[...] = lax.dot_general(
-        both[2], y_ref[...], TN, preferred_element_type=F32
-    ).astype(BF16)
-
-
-def weight_grad(first, count, tile, hidden_width, row, xt, y, mine, other, start):
+    copies = []
+
+    def send(at, source, target):
+        copies.append(pltpu.make_async_copy(source, target, sems.at[at, len(copies) // 3]))
+        copies[-1].start()
+
+    for start in range(0, columns, TILE):
+        size = min(TILE, columns - start)
+        here, there = pl.ds(start, size), pl.ds(begin + start, size)
+        gate[:, here] = jnp.dot(
+            xt_ref[...], both[0, :, here], preferred_element_type=F32
+        ).astype(BF16)
+        send(0, gate.at[:, here], outs[0].at[:, there])
+        up[:, here] = jnp.dot(
+            xt_ref[...], both[1, :, here], preferred_element_type=F32
+        ).astype(BF16)
+        send(1, up.at[:, here], outs[1].at[:, there])
+        down[here, :] = lax.dot_general(
+            both[2, :, here], y_ref[...], TN, preferred_element_type=F32
+        ).astype(BF16)
+        send(2, down.at[here], outs[2].at[there])
+    token_ref[...] = jnp.zeros_like(token_ref)
+    for copy in copies:
+        copy.wait()
+
+
+def weight_grad(begin, hidden_width, xt, y, mine, other, grads, after):
     width = xt.shape[0]
-    group = mine.shape[0] // 3
-    has_start = start is not None
-    start = start or ()
-    return call(
-        functools.partial(weight_grad_kernel, group, has_start),
-        (count,),
-        [
-            SCALAR,
-            whole((width, 2 * group)),
-            whole((2 * group, width)),
-            pl.BlockSpec((3 * group, tile), lambda i: (0, i)),
-            pl.BlockSpec((3 * group, tile), lambda i: (0, i)),
-        ]
-        + [pl.BlockSpec(memory_space=pl.ANY)] * len(start),
-        [
-            pl.BlockSpec((width, tile), lambda i: (0, first + i)),
-            pl.BlockSpec((width, tile), lambda i: (0, first + i)),
-            pl.BlockSpec((tile, width), lambda i: (first + i, 0)),
-            whole(TOKEN.shape),
-        ],
+    group, columns = mine.shape[0] // 3, mine.shape[1]
+    in_hbm = pl.BlockSpec(memory_space=pl.ANY)
+    return call(
+        functools.partial(weight_grad_kernel, group, begin, len(grads) + len(after)),
+        (),
+        [IN_VMEM] * 4 + [in_hbm] * len(grads) + [IN_VMEM] * len(after),
+        [in_hbm] * 3 + [IN_VMEM],
         [
             jax.ShapeDtypeStruct((width, hidden_width), BF16),
             jax.ShapeDtypeStruct((width, hidden_width), BF16),
             jax.ShapeDtypeStruct((hidden_width, width), BF16),
             TOKEN,
         ],
-        12 * group * width * count * tile,
-        6 * width * count * tile,
-        scratch=[pltpu.VMEM((3, 2 * group, tile), BF16)],
-        aliases={5 + i: i for i in range(len(start))},
+        12 * group * width * columns,
+        6 * width * columns,
+        scratch=[
+            pltpu.VMEM((3, 2 * group, columns), BF16),
+            pltpu.VMEM((width, columns), BF16),
+            pltpu.VMEM((width, columns), BF16),
+            pltpu.VMEM((columns, width), BF16),
+            pltpu.SemaphoreType.DMA((3, pl.cdiv(columns, TILE))),
+        ],
+        aliases={4 + i: i for i in range(len(grads))},
         limit=16,
-    )(row, xt, y, mine, other, *start)
-
-
-def last_kernel(parts, rows, wa_ref, grad_ref, own_ref, *send_refs):
+    )(xt, y, mine, other, *grads, *after)
+
+
+def last_kernel(parts, rows, grad_ref, own_ref, *send_refs):
     grad = grad_ref[...]
     cuts = [grad[slot * rows : (slot + 1) * rows] for slot in range(parts)]
-    wa = wa_ref[0]
+    wa = lax.axis_index("wa")
     for step in range(parts):
         at = wa ^ step
         piece = cuts[0]
@@ -345,18 +378,18 @@
             send_refs[step - 1][...] = piece.astype(BF16)
 
 
-def last_pieces(parts, wa, grad):
+def last_pieces(parts, grad):
     rows, width = grad.shape[0] // parts, grad.shape[1]
     return call(
         functools.partial(last_kernel, parts, rows),
         (),
-        [SCALAR, IN_VMEM],
+        [IN_VMEM],
         [IN_VMEM] * parts,
         [jax.ShapeDtypeStruct((rows, width), F32)]
         + [jax.ShapeDtypeStruct((rows, width), BF16)] * (parts - 1),
         0,
         8 * grad.shape[0] * width,
-    )(wa, grad)
+    )(grad)
 
 
 def swap(value, axis, size, step):
@@ -364,45 +397,49 @@
 
 
 def fast_body(n_wa, n_ha, n_row, tokens, cotangent, gate_weight, up_weight, down_weight):
-    rows, width = tokens.shape
     hidden_width = gate_weight.shape[1]
-    columns = hidden_width // CHUNKS
-    tile = max(t for t in range(LANES, 513, LANES) if columns % t == 0)
-    count = columns // tile
-    group = n_ha * rows
-    wa = lax.axis_index("wa").astype(jnp.int32).reshape(1)
-    row = lax.axis_index("row").astype(jnp.int32).reshape(1)
-
-    both = join(tokens, cotangent)
+    tiles = hidden_width // LANES
+    ends = [-(-tiles * (at + 1) // CHUNKS) * LANES for at in range(CHUNKS)]
+    chunks = [(begin, end - begin) for begin, end in zip([0] + ends, ends)]
+    axes = [((1, 2), (2, 1))[at % 2] for at in range(CHUNKS)]
+
+    both = join(tokens, cotangent, from_hbm=True)
     gate_weight, up_weight, down_weight = load(gate_weight, up_weight, down_weight)
     pieces = [both] + [swap(both, "ha", n_ha, step) for step in range(1, n_ha)]
-    x, y = order_rows(wa, pieces)
-
-    blocks = []
-    for chunk in range(CHUNKS):
-        own, *sends = forward(
-            n_wa, chunk * count, count, tile, x, y, gate_weight, up_weight, down_weight
+    x, y = order_rows(pieces)
+
+    sums, after = [], ()
+    for (begin, columns), (near, far) in zip(chunks, axes):
+        keep, send = forward(
+            begin, columns, near, far, x, y, gate_weight, up_weight, down_weight, after
         )
-        blocks.append((own, [swap(s, "wa", n_wa, k + 1) for k, s in enumerate(sends)]))
-    xt, y_all = factors(row, x, y, swap(join(x, y), "row", n_row, 1))
-
-    gathered = []
-    for own, received in blocks:
-        mine = middle(own, received)
-        gathered.append([mine] + [swap(mine, "wa", n_wa, step) for step in range(1, n_wa)])
-
-    grads, after = None, ()
-    for chunk in range(CHUNKS):
-        mine = stack(gathered[chunk])
-        other = swap(mine, "row", n_row, 1)
-        grad = input_grad(chunk * columns, mine, gate_weight, up_weight, after)
-        if chunk == CHUNKS - 1:
-            own, *sends = last_pieces(n_ha, wa, grad)
-            received = [swap(sent, "ha", n_ha, k + 1) for k, sent in enumerate(sends)]
-        *grads, token = weight_grad(
-            chunk * count, count, tile, hidden_width, row, xt, y_all, mine, other, grads
+        sums.append((keep, swap(send, "wa", n_wa, near)))
+        after = (send,)
+    sums = [halve(keep, received, send) for keep, received in sums]
+    sums = [(own, swap(send, "wa", n_wa, far)) for (own, send), (_, far) in zip(sums, axes)]
+    xt, y_all = factors(x, y, swap(join(x, y), "row", n_row, 1))
+    mine = [middle(own, [received]) for own, received in sums]
+    mine = [join(m, swap(m, "wa", n_wa, near)) for m, (near, _) in zip(mine, axes)]
+    mine = [(m, swap(m, "wa", n_wa, far)) for m, (_, far) in zip(mine, axes)]
+    mine = [stack(*axis, *m) for axis, m in zip(axes, mine)]
+    other = [swap(m, "row", n_row, 1) for m in mine]
+
+    grad, grads, token = (), (), ()
+    for at, (begin, columns) in enumerate(chunks):
+        grad = (input_grad(begin, mine[at], gate_weight, up_weight, grad + token),)
+        if at < CHUNKS - 2:
+            *grads, token = weight_grad(
+                begin, hidden_width, xt, y_all, mine[at], other[at], grads, ()
+            )
+            token = (token,)
+        else:
+            token = ()
+    own, *sends = last_pieces(n_ha, grad[0])
+    received = [swap(sent, "ha", n_ha, k + 1) for k, sent in enumerate(sends)]
+    for at in range(CHUNKS - 2, CHUNKS):
+        *grads, _ = weight_grad(
+            chunks[at][0], hidden_width, xt, y_all, mine[at], other[at], grads, (own,)
         )
-        after = (grad, token)
     return (total(own, received), *grads)
 
 
@@ -443,7 +480,8 @@
             n_wa == n_ha == 4
             and n_row == 2
             and width % LANES == 0
-            and hidden_width % (LANES * CHUNKS) == 0
+            and hidden_width % LANES == 0
+            and hidden_width >= LANES * CHUNKS
             and (tokens.shape[0] * n_ha) % 16 == 0
         )
         if fits:

time: 110 us -> 95.7 us (0.87)
  local copies, waits for them, and re-layouts: 12.2 us -> 1.65 us
  Pallas kernels: 41.1 us -> 37.3 us
    unnamed x26 -> x4, local copies, waits for them, and re-layouts: 12.2 us -> 1.65 us
    pallas_call x14 -> x25, Pallas kernels: 25.6 us -> 21.8 us  [the longest x4 14.6 us: weight_grad(): call(functools.partial(weight_grad_kernel, group, begin, len(grads) + len...]
    ppermute x28 -> x27, starting transfers between devices: 29 us -> 29.4 us  [swap(): return lax.ppermute(value, axis, [(at, at ^ step) for at in range(size)])]
    pallas_call x3 -> x4, Pallas kernels: 5.69 us -> 5.85 us  [input_grad(): call(functools.partial(input_grad_kernel, group, begin, bool(after)), (),...]
    ppermute x28 -> x27, waiting for transfers between devices: 26.3 us -> 26.1 us  [swap(): return lax.ppermute(value, axis, [(at, at ^ step) for at in range(size)])]
  transfers between devices with their start and end apart: 28 -> 27, of which waited for: 11 -> 7; matrix products, arithmetic and copies ran while one was open for 0% -> 0% of each run, Pallas kernels for 35% -> 37%
where the time goes in v3:
time: 95.7 us; the launch traced here: 95.5 us
  Pallas kernels  37.3 us (39%)
  starting transfers between devices  29.4 us (31%)
  waiting for transfers between devices  26.1 us (27%)
  local copies, waits for them, and re-layouts  1.65 us (2%)
    ppermute x27, starting transfers between devices, swap(): return lax.ppermute(value, axis, [(at, at ^ step) for at in range(size)])  29.4 us
    ppermute x27, waiting for transfers between devices, swap(): return lax.ppermute(value, axis, [(at, at ^ step) for at in range(size)])  26.1 us
    pallas_call x4, Pallas kernels, weight_grad(): call(functools.partial(weight_grad_kernel, group, begin, len(grads) + len...  14.6 us
    pallas_call x1, Pallas kernels, load(): pl.pallas_call(functools.partial(load_kernel, cuts), in_specs=[pl.BlockSp...  8.73 us
    pallas_call x4, Pallas kernels, forward(): call(functools.partial(forward_kernel, rows, begin, near, far, len(after)...  5.95 us
    pallas_call x4, Pallas kernels, input_grad(): call(functools.partial(input_grad_kernel, group, begin, bool(after)), (),...  5.85 us
  transfers between devices with their start and end apart: 27, of which 7 were waited for; matrix products, arithmetic and copies ran while one was open for 0% of the time, Pallas kernels for 37%

profile of v3, /device:TPU:0, one launch (start us, length us, event | category | flops | bytes accessed | tf_op | source)
XLA Modules:
  0.0 95.5 jit_solution(17450813329844949920)
XLA Ops:
  0.6 0.8 copy-done
  1.5 0.8 copy-done.1
  2.3 3.1 %collective-permute-start = (bf16[40,1280]{1,0:T(8,128)(2,1)S(1)}, bf16[40,1280]{1,0:T(8,128)(2,1)S(1)}, u32[]{:S(2)}, u32[]{:S(2)}) collective-permute-start(bf16[40,1280]{1,0:T(8,128)(2,1)S(1)} %shard_map.84.refs_0_), channel_id=1, source_target_pairs={{0,2},{2,0},{4,6},{6,4},{1,3},{3,1},{5,7},{7,5},{8,10},{10,8},{12,... | collective-permute-start | bytes 307208 | tf_op jit(solution)/shard_map/ppermute | solution.py:396
  5.4 2.6 %collective-permute-start.1 = (bf16[40,1280]{1,0:T(8,128)(2,1)S(1)}, bf16[40,1280]{1,0:T(8,128)(2,1)S(1)}, u32[]{:S(2)}, u32[]{:S(2)}) collective-permute-start(bf16[40,1280]{1,0:T(8,128)(2,1)S(1)} %shard_map.84.refs_0_), channel_id=1, source_target_pairs={{0,4},{2,6},{4,0},{6,2},{1,5},{3,7},{5,1},{7,3},{8,12},{10,14},{12... | collective-permute-start | bytes 307208 | tf_op jit(solution)/shard_map/ppermute | solution.py:396
  8.0 8.7 %shard_map.86 = (bf16[1280,3456]{1,0:T(8,128)(2,1)S(1)}, bf16[1280,3456]{1,0:T(8,128)(2,1)S(1)}, bf16[3456,1280]{1,0:T(8,128)(2,1)S(1)}) custom-call(bf16[1280,3456]{1,0:T(8,128)(2,1)} %refs_0_.1, bf16[1280,3456]{1,0:T(8,128)(2,1)} %refs_1_.1, bf16[3456,1280]{1,0:T(8,128)(2,1)} %refs_2_.1), custom_call_target="tpu_custom_call" | custom-call | bytes 26542080 | tf_op jit(solution)/shard_map/pallas_call | solution.py:120
  16.8 0.2 shard_map.85
  17.0 1.5 %shard_map.87 = (f32[120,896]{1,0:T(8,128)S(1)}, bf16[120,896]{1,0:T(8,128)(2,1)S(1)}) custom-call(bf16[80,1280]{1,0:T(8,128)(2,1)S(1)} %get-tuple-element.45.x_ref.first_ref, bf16[80,1280]{1,0:T(8,128)(2,1)S(1)} %get-tuple-element.46.y_ref.second_ref, bf16[1280,3456]{1,0:T(8,128)(2,1)S(1)} %get-tuple-element.47.gate_ref, ...), custom_call_target="tpu_custom_call" | custom-call | flops 550502400 | bytes 6881280 | tf_op jit(solution)/shard_map/pallas_call | solution.py:136
  18.5 1.8 %collective-permute-start.15 = (bf16[120,896]{1,0:T(8,128)(2,1)S(1)}, bf16[120,896]{1,0:T(8,128)(2,1)S(1)}, u32[]{:S(2)}, u32[]{:S(2)}) collective-permute-start(bf16[120,896]{1,0:T(8,128)(2,1)S(1)} %get-tuple-element.50.refs_0_), channel_id=1, source_target_pairs={{0,8},{8,0},{16,24},{24,16},{1,9},{9,1},{17,25},{25,17},{2,10},{10... | collective-permute-start | bytes 645128 | tf_op jit(solution)/shard_map/ppermute | solution.py:396
  20.2 1.5 %shard_map.88 = (f32[120,896]{1,0:T(8,128)S(1)}, bf16[120,896]{1,0:T(8,128)(2,1)S(1)}) custom-call(bf16[80,1280]{1,0:T(8,128)(2,1)S(1)} %get-tuple-element.45.x_ref.first_ref, bf16[80,1280]{1,0:T(8,128)(2,1)S(1)} %get-tuple-element.46.y_ref.second_ref, bf16[1280,3456]{1,0:T(8,128)(2,1)S(1)} %get-tuple-element.47.gate_ref, ...), custom_call_target="tpu_custom_call" | custom-call | flops 550502400 | bytes 6881280 | tf_op jit(solution)/shard_map/pallas_call | solution.py:136
  21.8 1.6 %collective-permute-start.11 = (bf16[120,896]{1,0:T(8,128)(2,1)S(1)}, bf16[120,896]{1,0:T(8,128)(2,1)S(1)}, u32[]{:S(2)}, u32[]{:S(2)}) collective-permute-start(bf16[120,896]{1,0:T(8,128)(2,1)S(1)} %get-tuple-element.51.refs_0_), channel_id=1, source_target_pairs={{0,16},{8,24},{16,0},{24,8},{1,17},{9,25},{17,1},{25,9},{2,18},{10... | collective-permute-start | bytes 645128 | tf_op jit(solution)/shard_map/ppermute | solution.py:396
  23.4 1.5 %shard_map.89 = (f32[120,896]{1,0:T(8,128)S(1)}, bf16[120,896]{1,0:T(8,128)(2,1)S(1)}) custom-call(bf16[80,1280]{1,0:T(8,128)(2,1)S(1)} %get-tuple-element.45.x_ref.first_ref, bf16[80,1280]{1,0:T(8,128)(2,1)S(1)} %get-tuple-element.46.y_ref.second_ref, bf16[1280,3456]{1,0:T(8,128)(2,1)S(1)} %get-tuple-element.47.gate_ref, ...), custom_call_target="tpu_custom_call" | custom-call | flops 550502400 | bytes 6881280 | tf_op jit(solution)/shard_map/pallas_call | solution.py:136
  24.9 1.4 %shard_map.90 = (f32[120,768]{1,0:T(8,128)S(1)}, bf16[120,768]{1,0:T(8,128)(2,1)S(1)}) custom-call(bf16[80,1280]{1,0:T(8,128)(2,1)S(1)} %get-tuple-element.45.x_ref.first_ref, bf16[80,1280]{1,0:T(8,128)(2,1)S(1)} %get-tuple-element.46.y_ref.second_ref, bf16[1280,3456]{1,0:T(8,128)(2,1)S(1)} %get-tuple-element.47.gate_ref, ...), custom_call_target="tpu_custom_call" | custom-call | flops 471859200 | bytes 5898240 | tf_op jit(solution)/shard_map/pallas_call | solution.py:136
  26.3 0.1 shard_map.103
  26.4 0.6 collective-permute-start.16
  26.9 1.2 %collective-permute-start.7 = (bf16[120,896]{1,0:T(8,128)(2,1)S(1)}, bf16[120,896]{1,0:T(8,128)(2,1)S(1)}, u32[]{:S(2)}, u32[]{:S(2)}) collective-permute-start(bf16[120,896]{1,0:T(8,128)(2,1)S(1)} %get-tuple-element.52.refs_0_), channel_id=1, source_target_pairs={{0,8},{8,0},{16,24},{24,16},{1,9},{9,1},{17,25},{25,17},{2,10},{10... | collective-permute-start | bytes 645128 | tf_op jit(solution)/shard_map/ppermute | solution.py:396
  28.2 3.1 %collective-permute-done.16.refs_0_ = bf16[60,896]{1,0:T(8,128)(2,1)S(1)} collective-permute-done((bf16[60,896]{1,0:T(8,128)(2,1)S(1)}, bf16[60,896]{1,0:T(8,128)(2,1)S(1)}, u32[]{:S(2)}, u32[]{:S(2)}) %collective-permute-start.16) | collective-permute-done | bytes 107552 | tf_op jit(solution)/shard_map/ppermute | solution.py:396
  31.2 0.1 shard_map.104.first_ref
  31.3 0.6 collective-permute-start.17
  31.9 0.1 shard_map.99
  32.0 1.6 %collective-permute-start.12 = (bf16[60,896]{1,0:T(8,128)(2,1)S(1)}, bf16[60,896]{1,0:T(8,128)(2,1)S(1)}, u32[]{:S(2)}, u32[]{:S(2)}) collective-permute-start(bf16[60,896]{1,0:T(8,128)(2,1)S(1)} %get-tuple-element.62), channel_id=1, source_target_pairs={{0,8},{8,0},{16,24},{24,16},{1,9},{9,1},{17,25},{25,17},{2,10},{10... | collective-permute-start | bytes 322568 | tf_op jit(solution)/shard_map/ppermute | solution.py:396
  33.5 3.0 %collective-permute-done.17.second_ref = bf16[60,896]{1,0:T(8,128)(2,1)S(1)} collective-permute-done((bf16[60,896]{1,0:T(8,128)(2,1)S(1)}, bf16[60,896]{1,0:T(8,128)(2,1)S(1)}, u32[]{:S(2)}, u32[]{:S(2)}) %collective-permute-start.17) | collective-permute-done | bytes 107552 | tf_op jit(solution)/shard_map/ppermute | solution.py:396
  36.5 1.6 %collective-permute-start.18 = (bf16[120,896]{1,0:T(8,128)(2,1)S(1)}, bf16[120,896]{1,0:T(8,128)(2,1)S(1)}, u32[]{:S(2)}, u32[]{:S(2)}) collective-permute-start(bf16[120,896]{1,0:T(8,128)(2,1)S(1)} %shard_map.105.mine_ref), channel_id=1, source_target_pairs={{0,16},{8,24},{16,0},{24,8},{1,17},{9,25},{17,1},{25,9},{2,18},{10... | collective-permute-start | bytes 645128 | tf_op jit(solution)/shard_map/ppermute | solution.py:396
  38.1 0.1 shard_map.100.first_ref
  38.2 1.2 %collective-permute-start.13 = (bf16[60,896]{1,0:T(8,128)(2,1)S(1)}, bf16[60,896]{1,0:T(8,128)(2,1)S(1)}, u32[]{:S(2)}, u32[]{:S(2)}) collective-permute-start(bf16[60,896]{1,0:T(8,128)(2,1)S(1)} %shard_map.100.first_ref), channel_id=1, source_target_pairs={{0,16},{8,24},{16,0},{24,8},{1,17},{9,25},{17,1},{25,9},{2,18},{10... | collective-permute-start | bytes 322568 | tf_op jit(solution)/shard_map/ppermute | solution.py:396
  39.4 0.9 collective-permute-start.3
  40.3 0.1 shard_map.95
  40.4 1.2 %collective-permute-start.8 = (bf16[60,896]{1,0:T(8,128)(2,1)S(1)}, bf16[60,896]{1,0:T(8,128)(2,1)S(1)}, u32[]{:S(2)}, u32[]{:S(2)}) collective-permute-start(bf16[60,896]{1,0:T(8,128)(2,1)S(1)} %get-tuple-element.59), channel_id=1, source_target_pairs={{0,16},{8,24},{16,0},{24,8},{1,17},{9,25},{17,1},{25,9},{2,18},{10... | collective-permute-start | bytes 322568 | tf_op jit(solution)/shard_map/ppermute | solution.py:396
  41.5 5.5 %collective-permute-done.13.second_ref = bf16[60,896]{1,0:T(8,128)(2,1)S(1)} collective-permute-done((bf16[60,896]{1,0:T(8,128)(2,1)S(1)}, bf16[60,896]{1,0:T(8,128)(2,1)S(1)}, u32[]{:S(2)}, u32[]{:S(2)}) %collective-permute-start.13) | collective-permute-done | bytes 107552 | tf_op jit(solution)/shard_map/ppermute | solution.py:396
  47.1 0.8 collective-permute-start.14
  47.9 2.4 %collective-permute-done.8.refs_0_ = bf16[60,896]{1,0:T(8,128)(2,1)S(1)} collective-permute-done((bf16[60,896]{1,0:T(8,128)(2,1)S(1)}, bf16[60,896]{1,0:T(8,128)(2,1)S(1)}, u32[]{:S(2)}, u32[]{:S(2)}) %collective-permute-start.8) | collective-permute-done | bytes 107552 | tf_op jit(solution)/shard_map/ppermute | solution.py:396
  50.3 0.1 shard_map.96.first_ref
  50.4 0.8 collective-permute-start.9
  51.1 0.1 collective-permute-start.19
  51.2 0.1 shard_map.106.stack_ref.mine_ref
  51.3 0.6 collective-permute-start.20
  51.9 0.1 shard_map.91
  51.9 1.4 %collective-permute-start.4 = (bf16[60,768]{1,0:T(8,128)(2,1)S(1)}, bf16[60,768]{1,0:T(8,128)(2,1)S(1)}, u32[]{:S(2)}, u32[]{:S(2)}) collective-permute-start(bf16[60,768]{1,0:T(8,128)(2,1)S(1)} %get-tuple-element.56), channel_id=1, source_target_pairs={{0,8},{8,0},{16,24},{24,16},{1,9},{9,1},{17,25},{25,17},{2,10},{10... | collective-permute-start | bytes 276488 | tf_op jit(solution)/shard_map/ppermute | solution.py:396
  53.3 2.6 %collective-permute-done.9.second_ref = bf16[60,896]{1,0:T(8,128)(2,1)S(1)} collective-permute-done((bf16[60,896]{1,0:T(8,128)(2,1)S(1)}, bf16[60,896]{1,0:T(8,128)(2,1)S(1)}, u32[]{:S(2)}, u32[]{:S(2)}) %collective-permute-start.9) | collective-permute-done | bytes 107552 | tf_op jit(solution)/shard_map/ppermute | solution.py:396
  55.9 2.1 %collective-permute-start.10 = (bf16[120,896]{1,0:T(8,128)(2,1)S(1)}, bf16[120,896]{1,0:T(8,128)(2,1)S(1)}, u32[]{:S(2)}, u32[]{:S(2)}) collective-permute-start(bf16[120,896]{1,0:T(8,128)(2,1)S(1)} %shard_map.97.mine_ref), channel_id=1, source_target_pairs={{0,16},{8,24},{16,0},{24,8},{1,17},{9,25},{17,1},{25,9},{2,18},{10... | collective-permute-start | bytes 645128 | tf_op jit(solution)/shard_map/ppermute | solution.py:396
  58.1 0.1 shard_map.92.first_ref
  58.1 1.1 %collective-permute-start.5 = (bf16[60,768]{1,0:T(8,128)(2,1)S(1)}, bf16[60,768]{1,0:T(8,128)(2,1)S(1)}, u32[]{:S(2)}, u32[]{:S(2)}) collective-permute-start(bf16[60,768]{1,0:T(8,128)(2,1)S(1)} %shard_map.92.first_ref), channel_id=1, source_target_pairs={{0,16},{8,24},{16,0},{24,8},{1,17},{9,25},{17,1},{25,9},{2,18},{10... | collective-permute-start | bytes 276488 | tf_op jit(solution)/shard_map/ppermute | solution.py:396
  59.2 0.1 shard_map.102.stack_ref.mine_ref
  59.3 0.1 collective-permute-start.21
  59.3 4.5 %collective-permute-done.5.second_ref = bf16[60,768]{1,0:T(8,128)(2,1)S(1)} collective-permute-done((bf16[60,768]{1,0:T(8,128)(2,1)S(1)}, bf16[60,768]{1,0:T(8,128)(2,1)S(1)}, u32[]{:S(2)}, u32[]{:S(2)}) %collective-permute-start.5) | collective-permute-done | bytes 92192 | tf_op jit(solution)/shard_map/ppermute | solution.py:396
  63.9 0.2 collective-permute-start.6
  64.1 0.1 shard_map.98.stack_ref.mine_ref
  64.2 0.1 collective-permute-start.26
  64.2 0.3 shard_map.109
  64.5 5.0 %collective-permute-done.6.other_ref = bf16[120,768]{1,0:T(8,128)(2,1)S(1)} collective-permute-done((bf16[120,768]{1,0:T(8,128)(2,1)S(1)}, bf16[120,768]{1,0:T(8,128)(2,1)S(1)}, u32[]{:S(2)}, u32[]{:S(2)}) %collective-permute-start.6) | collective-permute-done | bytes 184352 | tf_op jit(solution)/shard_map/ppermute | solution.py:396
  69.5 0.1 shard_map.94.stack_ref.mine_ref
  69.6 0.1 collective-permute-start.25
  69.7 1.5 %shard_map.107.refs_0_ = f32[80,1280]{1,0:T(8,128)S(1)} custom-call(bf16[240,896]{1,0:T(8,128)(2,1)S(1)} %shard_map.106.stack_ref.mine_ref, bf16[1280,3456]{1,0:T(8,128)(2,1)S(1)} %get-tuple-element.47.gate_ref, bf16[1280,3456]{1,0:T(8,128)(2,1)S(1)} %get-tuple-element.48.up_ref), custom_call_target="tpu_custom_call" | custom-call | flops 367001600 | bytes 4587520 | tf_op jit(solution)/shard_map/pallas_call | solution.py:228
  71.2 3.4 %shard_map.110 = (bf16[1280,3456]{1,0:T(8,128)(2,1)}, bf16[1280,3456]{1,0:T(8,128)(2,1)}, bf16[3456,1280]{1,0:T(8,128)(2,1)}, f32[8,128]{1,0:T(8,128)S(1)}) custom-call(bf16[1280,160]{1,0:T(8,128)(2,1)S(1)} %get-tuple-element.66.xt_ref, bf16[160,1280]{1,0:T(8,128)(2,1)S(1)} %get-tuple-element.67.y_ref, bf16[240,896]{1,0:T(8,128)(2,1)S(1)} %shard_map.106.stack_ref.mine_ref, ...), custom_call_target="tpu_custom_call" | custom-call | flops 1101004800 | bytes 6881280 | tf_op jit(solution)/shard_map/pallas_call | solution.py:341
  74.6 1.5 %shard_map.111.refs_0_ = f32[80,1280]{1,0:T(8,128)S(1)} custom-call(bf16[240,896]{1,0:T(8,128)(2,1)S(1)} %shard_map.102.stack_ref.mine_ref, bf16[1280,3456]{1,0:T(8,128)(2,1)S(1)} %get-tuple-element.47.gate_ref, bf16[1280,3456]{1,0:T(8,128)(2,1)S(1)} %get-tuple-element.48.up_ref, f32[80,1280]{1,0:T(8,128)S(1)} %shard_map.107.refs_0_, ...), custom_call_target="tpu_custom_call" | custom-call | flops 367001600 | bytes 4587520 | tf_op jit(solution)/shard_map/pallas_call | solution.py:228
  76.2 3.4 %shard_map.112 = (bf16[1280,3456]{1,0:T(8,128)(2,1)}, bf16[1280,3456]{1,0:T(8,128)(2,1)}, bf16[3456,1280]{1,0:T(8,128)(2,1)}, f32[8,128]{1,0:T(8,128)S(1)}) custom-call(bf16[1280,160]{1,0:T(8,128)(2,1)S(1)} %get-tuple-element.66.xt_ref, bf16[160,1280]{1,0:T(8,128)(2,1)S(1)} %get-tuple-element.67.y_ref, ...), custom_call_target="tpu_custom_call", output_to_operand_aliasing={{0}: (4, {}), {1}: (5, {}), {2}: (6, {})} | custom-call | flops 1101004800 | bytes 6881280 | tf_op jit(solution)/shard_map/pallas_call | solution.py:341
  79.6 1.5 %shard_map.113.refs_0_ = f32[80,1280]{1,0:T(8,128)S(1)} custom-call(bf16[240,896]{1,0:T(8,128)(2,1)S(1)} %shard_map.98.stack_ref.mine_ref, bf16[1280,3456]{1,0:T(8,128)(2,1)S(1)} %get-tuple-element.47.gate_ref, bf16[1280,3456]{1,0:T(8,128)(2,1)S(1)} %get-tuple-element.48.up_ref, f32[80,1280]{1,0:T(8,128)S(1)} %shard_map.111.refs_0_, ...), custom_call_target="tpu_custom_call" | custom-call | flops 367001600 | bytes 4587520 | tf_op jit(solution)/shard_map/pallas_call | solution.py:228
  81.1 1.3 %shard_map.114.grad_ref = f32[80,1280]{1,0:T(8,128)S(1)} custom-call(bf16[240,768]{1,0:T(8,128)(2,1)S(1)} %shard_map.94.stack_ref.mine_ref, bf16[1280,3456]{1,0:T(8,128)(2,1)S(1)} %get-tuple-element.47.gate_ref, bf16[1280,3456]{1,0:T(8,128)(2,1)S(1)} %get-tuple-element.48.up_ref, f32[80,1280]{1,0:T(8,128)S(1)} %shard_map.113.refs_0_), custom_call_target="tpu_custom_call" | custom-call | flops 314572800 | bytes 3932160 | tf_op jit(solution)/shard_map/pallas_call | solution.py:228
  82.4 0.2 shard_map.115
  82.6 0.7 collective-permute-start.22
  83.3 3.4 %collective-permute-start.23 = (bf16[20,1280]{1,0:T(8,128)(2,1)S(1)}, bf16[20,1280]{1,0:T(8,128)(2,1)S(1)}, u32[]{:S(2)}, u32[]{:S(2)}) collective-permute-start(bf16[20,1280]{1,0:T(8,128)(2,1)S(1)} %get-tuple-element.75), channel_id=1, source_target_pairs={{0,4},{2,6},{4,0},{6,2},{1,5},{3,7},{5,1},{7,3},{8,12},{10,14},{12... | collective-permute-start | bytes 153608 | tf_op jit(solution)/shard_map/ppermute | solution.py:396
  86.8 0.3 collective-permute-start.24
  87.1 4.0 %shard_map.117 = (bf16[1280,3456]{1,0:T(8,128)(2,1)}, bf16[1280,3456]{1,0:T(8,128)(2,1)}, bf16[3456,1280]{1,0:T(8,128)(2,1)}, f32[8,128]{1,0:T(8,128)}) custom-call(bf16[1280,160]{1,0:T(8,128)(2,1)S(1)} %get-tuple-element.66.xt_ref, bf16[160,1280]{1,0:T(8,128)(2,1)S(1)} %get-tuple-element.67.y_ref, ...), custom_call_target="tpu_custom_call", output_to_operand_aliasing={{0}: (4, {}), {1}: (5, {}), {2}: (6, {})} | custom-call | flops 1101004800 | bytes 6881280 | tf_op jit(solution)/shard_map/pallas_call | solution.py:341
  91.1 3.7 %shard_map.118 = (bf16[1280,3456]{1,0:T(8,128)(2,1)}, bf16[1280,3456]{1,0:T(8,128)(2,1)}, bf16[3456,1280]{1,0:T(8,128)(2,1)}, f32[8,128]{1,0:T(8,128)}) custom-call(bf16[1280,160]{1,0:T(8,128)(2,1)S(1)} %get-tuple-element.66.xt_ref, bf16[160,1280]{1,0:T(8,128)(2,1)S(1)} %get-tuple-element.67.y_ref, ...), custom_call_target="tpu_custom_call", output_to_operand_aliasing={{0}: (4, {}), {1}: (5, {}), {2}: (6, {})} | custom-call | flops 943718400 | bytes 5898240 | tf_op jit(solution)/shard_map/pallas_call | solution.py:341
  94.8 0.7 shard_map.116
  (29 shorter events, 0.3 us)
Async XLA Ops:
  0.6 0.8 copy-start
  1.5 0.8 copy-start.1
  2.3 14.4 %collective-permute-start = (bf16[40,1280]{1,0:T(8,128)(2,1)S(1)}, bf16[40,1280]{1,0:T(8,128)(2,1)S(1)}, u32[]{:S(2)}, u32[]{:S(2)}) collective-permute-start(bf16[40,1280]{1,0:T(8,128)(2,1)S(1)} %shard_map.84.refs_0_), channel_id=1, source_target_pairs={{0,2},{2,0},{4,6},{6,4},{1,3},{3,1},{5,7},{7,5},{8,10},{10,8},{12,... | collective-permute-start | bytes 307208 | tf_op jit(solution)/shard_map/ppermute | solution.py:396
  5.4 11.3 %collective-permute-start.1 = (bf16[40,1280]{1,0:T(8,128)(2,1)S(1)}, bf16[40,1280]{1,0:T(8,128)(2,1)S(1)}, u32[]{:S(2)}, u32[]{:S(2)}) collective-permute-start(bf16[40,1280]{1,0:T(8,128)(2,1)S(1)} %shard_map.84.refs_0_), channel_id=1, source_target_pairs={{0,4},{2,6},{4,0},{6,2},{1,5},{3,7},{5,1},{7,3},{8,12},{10,14},{12... | collective-permute-start | bytes 307208 | tf_op jit(solution)/shard_map/ppermute | solution.py:396
  8.0 8.8 %collective-permute-start.2 = (bf16[40,1280]{1,0:T(8,128)(2,1)S(1)}, bf16[40,1280]{1,0:T(8,128)(2,1)S(1)}, u32[]{:S(2)}, u32[]{:S(2)}) collective-permute-start(bf16[40,1280]{1,0:T(8,128)(2,1)S(1)} %shard_map.84.refs_0_), channel_id=1, source_target_pairs={{0,6},{2,4},{4,2},{6,0},{1,7},{3,5},{5,3},{7,1},{8,14},{10,12},{12... | collective-permute-start | bytes 307208 | tf_op jit(solution)/shard_map/ppermute | solution.py:396
  18.5 7.8 %collective-permute-start.15 = (bf16[120,896]{1,0:T(8,128)(2,1)S(1)}, bf16[120,896]{1,0:T(8,128)(2,1)S(1)}, u32[]{:S(2)}, u32[]{:S(2)}) collective-permute-start(bf16[120,896]{1,0:T(8,128)(2,1)S(1)} %get-tuple-element.50.refs_0_), channel_id=1, source_target_pairs={{0,8},{8,0},{16,24},{24,16},{1,9},{9,1},{17,25},{25,17},{2,10},{10... | collective-permute-start | bytes 645128 | tf_op jit(solution)/shard_map/ppermute | solution.py:396
  21.8 10.1 %collective-permute-start.11 = (bf16[120,896]{1,0:T(8,128)(2,1)S(1)}, bf16[120,896]{1,0:T(8,128)(2,1)S(1)}, u32[]{:S(2)}, u32[]{:S(2)}) collective-permute-start(bf16[120,896]{1,0:T(8,128)(2,1)S(1)} %get-tuple-element.51.refs_0_), channel_id=1, source_target_pairs={{0,16},{8,24},{16,0},{24,8},{1,17},{9,25},{17,1},{25,9},{2,18},{10... | collective-permute-start | bytes 645128 | tf_op jit(solution)/shard_map/ppermute | solution.py:396
  26.4 4.9 %collective-permute-start.16 = (bf16[60,896]{1,0:T(8,128)(2,1)S(1)}, bf16[60,896]{1,0:T(8,128)(2,1)S(1)}, u32[]{:S(2)}, u32[]{:S(2)}) collective-permute-start(bf16[60,896]{1,0:T(8,128)(2,1)S(1)} %get-tuple-element.65), channel_id=1, source_target_pairs={{0,16},{8,24},{16,0},{24,8},{1,17},{9,25},{17,1},{25,9},{2,18},{10... | collective-permute-start | bytes 322568 | tf_op jit(solution)/shard_map/ppermute | solution.py:396
  26.9 13.4 %collective-permute-start.7 = (bf16[120,896]{1,0:T(8,128)(2,1)S(1)}, bf16[120,896]{1,0:T(8,128)(2,1)S(1)}, u32[]{:S(2)}, u32[]{:S(2)}) collective-permute-start(bf16[120,896]{1,0:T(8,128)(2,1)S(1)} %get-tuple-element.52.refs_0_), channel_id=1, source_target_pairs={{0,8},{8,0},{16,24},{24,16},{1,9},{9,1},{17,25},{25,17},{2,10},{10... | collective-permute-start | bytes 645128 | tf_op jit(solution)/shard_map/ppermute | solution.py:396
  31.3 5.2 %collective-permute-start.17 = (bf16[60,896]{1,0:T(8,128)(2,1)S(1)}, bf16[60,896]{1,0:T(8,128)(2,1)S(1)}, u32[]{:S(2)}, u32[]{:S(2)}) collective-permute-start(bf16[60,896]{1,0:T(8,128)(2,1)S(1)} %shard_map.104.first_ref), channel_id=1, source_target_pairs={{0,8},{8,0},{16,24},{24,16},{1,9},{9,1},{17,25},{25,17},{2,10},{10... | collective-permute-start | bytes 322568 | tf_op jit(solution)/shard_map/ppermute | solution.py:396
  32.0 6.2 %collective-permute-start.12 = (bf16[60,896]{1,0:T(8,128)(2,1)S(1)}, bf16[60,896]{1,0:T(8,128)(2,1)S(1)}, u32[]{:S(2)}, u32[]{:S(2)}) collective-permute-start(bf16[60,896]{1,0:T(8,128)(2,1)S(1)} %get-tuple-element.62), channel_id=1, source_target_pairs={{0,8},{8,0},{16,24},{24,16},{1,9},{9,1},{17,25},{25,17},{2,10},{10... | collective-permute-start | bytes 322568 | tf_op jit(solution)/shard_map/ppermute | solution.py:396
  36.5 14.7 %collective-permute-start.18 = (bf16[120,896]{1,0:T(8,128)(2,1)S(1)}, bf16[120,896]{1,0:T(8,128)(2,1)S(1)}, u32[]{:S(2)}, u32[]{:S(2)}) collective-permute-start(bf16[120,896]{1,0:T(8,128)(2,1)S(1)} %shard_map.105.mine_ref), channel_id=1, source_target_pairs={{0,16},{8,24},{16,0},{24,8},{1,17},{9,25},{17,1},{25,9},{2,18},{10... | collective-permute-start | bytes 645128 | tf_op jit(solution)/shard_map/ppermute | solution.py:396
  38.2 8.9 %collective-permute-start.13 = (bf16[60,896]{1,0:T(8,128)(2,1)S(1)}, bf16[60,896]{1,0:T(8,128)(2,1)S(1)}, u32[]{:S(2)}, u32[]{:S(2)}) collective-permute-start(bf16[60,896]{1,0:T(8,128)(2,1)S(1)} %shard_map.100.first_ref), channel_id=1, source_target_pairs={{0,16},{8,24},{16,0},{24,8},{1,17},{9,25},{17,1},{25,9},{2,18},{10... | collective-permute-start | bytes 322568 | tf_op jit(solution)/shard_map/ppermute | solution.py:396
  39.4 12.5 %collective-permute-start.3 = (bf16[120,768]{1,0:T(8,128)(2,1)S(1)}, bf16[120,768]{1,0:T(8,128)(2,1)S(1)}, u32[]{:S(2)}, u32[]{:S(2)}) collective-permute-start(bf16[120,768]{1,0:T(8,128)(2,1)S(1)} %get-tuple-element.54._), channel_id=1, source_target_pairs={{0,16},{8,24},{16,0},{24,8},{1,17},{9,25},{17,1},{25,9},{2,18},{10... | collective-permute-start | bytes 552968 | tf_op jit(solution)/shard_map/ppermute | solution.py:396
  40.4 9.9 %collective-permute-start.8 = (bf16[60,896]{1,0:T(8,128)(2,1)S(1)}, bf16[60,896]{1,0:T(8,128)(2,1)S(1)}, u32[]{:S(2)}, u32[]{:S(2)}) collective-permute-start(bf16[60,896]{1,0:T(8,128)(2,1)S(1)} %get-tuple-element.59), channel_id=1, source_target_pairs={{0,16},{8,24},{16,0},{24,8},{1,17},{9,25},{17,1},{25,9},{2,18},{10... | collective-permute-start | bytes 322568 | tf_op jit(solution)/shard_map/ppermute | solution.py:396
  47.1 12.1 %collective-permute-start.14 = (bf16[120,896]{1,0:T(8,128)(2,1)S(1)}, bf16[120,896]{1,0:T(8,128)(2,1)S(1)}, u32[]{:S(2)}, u32[]{:S(2)}) collective-permute-start(bf16[120,896]{1,0:T(8,128)(2,1)S(1)} %shard_map.101.mine_ref), channel_id=1, source_target_pairs={{0,8},{8,0},{16,24},{24,16},{1,9},{9,1},{17,25},{25,17},{2,10},{10... | collective-permute-start | bytes 645128 | tf_op jit(solution)/shard_map/ppermute | solution.py:396
  50.4 5.5 %collective-permute-start.9 = (bf16[60,896]{1,0:T(8,128)(2,1)S(1)}, bf16[60,896]{1,0:T(8,128)(2,1)S(1)}, u32[]{:S(2)}, u32[]{:S(2)}) collective-permute-start(bf16[60,896]{1,0:T(8,128)(2,1)S(1)} %shard_map.96.first_ref), channel_id=1, source_target_pairs={{0,8},{8,0},{16,24},{24,16},{1,9},{9,1},{17,25},{25,17},{2,10},{10... | collective-permute-start | bytes 322568 | tf_op jit(solution)/shard_map/ppermute | solution.py:396
  51.1 13.1 %collective-permute-start.19 = (bf16[160,1280]{1,0:T(8,128)(2,1)S(1)}, bf16[160,1280]{1,0:T(8,128)(2,1)S(1)}, u32[]{:S(2)}, u32[]{:S(2)}) collective-permute-start(bf16[160,1280]{1,0:T(8,128)(2,1)S(1)} %shard_map.108), channel_id=1, source_target_pairs={{0,1},{1,0},{2,3},{3,2},{4,5},{5,4},{6,7},{7,6},{8,9},{9,8},{10,11... | collective-permute-start | bytes 1228808 | tf_op jit(solution)/shard_map/ppermute | solution.py:396
  51.3 19.9 %collective-permute-start.20 = (bf16[240,896]{1,0:T(8,128)(2,1)S(1)}, bf16[240,896]{1,0:T(8,128)(2,1)S(1)}, u32[]{:S(2)}, u32[]{:S(2)}) collective-permute-start(bf16[240,896]{1,0:T(8,128)(2,1)S(1)} %shard_map.106.stack_ref.mine_ref), channel_id=1, source_target_pairs={{0,1},{1,0},{2,3},{3,2},{4,5},{5,4},{6,7},{7,6},{8,9},{9,8},{10,11... | collective-permute-start | bytes 1290248 | tf_op jit(solution)/shard_map/ppermute | solution.py:396
  51.9 6.2 %collective-permute-start.4 = (bf16[60,768]{1,0:T(8,128)(2,1)S(1)}, bf16[60,768]{1,0:T(8,128)(2,1)S(1)}, u32[]{:S(2)}, u32[]{:S(2)}) collective-permute-start(bf16[60,768]{1,0:T(8,128)(2,1)S(1)} %get-tuple-element.56), channel_id=1, source_target_pairs={{0,8},{8,0},{16,24},{24,16},{1,9},{9,1},{17,25},{25,17},{2,10},{10... | collective-permute-start | bytes 276488 | tf_op jit(solution)/shard_map/ppermute | solution.py:396
  55.9 8.2 %collective-permute-start.10 = (bf16[120,896]{1,0:T(8,128)(2,1)S(1)}, bf16[120,896]{1,0:T(8,128)(2,1)S(1)}, u32[]{:S(2)}, u32[]{:S(2)}) collective-permute-start(bf16[120,896]{1,0:T(8,128)(2,1)S(1)} %shard_map.97.mine_ref), channel_id=1, source_target_pairs={{0,16},{8,24},{16,0},{24,8},{1,17},{9,25},{17,1},{25,9},{2,18},{10... | collective-permute-start | bytes 645128 | tf_op jit(solution)/shard_map/ppermute | solution.py:396
  58.1 5.8 %collective-permute-start.5 = (bf16[60,768]{1,0:T(8,128)(2,1)S(1)}, bf16[60,768]{1,0:T(8,128)(2,1)S(1)}, u32[]{:S(2)}, u32[]{:S(2)}) collective-permute-start(bf16[60,768]{1,0:T(8,128)(2,1)S(1)} %shard_map.92.first_ref), channel_id=1, source_target_pairs={{0,16},{8,24},{16,0},{24,8},{1,17},{9,25},{17,1},{25,9},{2,18},{10... | collective-permute-start | bytes 276488 | tf_op jit(solution)/shard_map/ppermute | solution.py:396
  59.3 16.9 %collective-permute-start.21 = (bf16[240,896]{1,0:T(8,128)(2,1)S(1)}, bf16[240,896]{1,0:T(8,128)(2,1)S(1)}, u32[]{:S(2)}, u32[]{:S(2)}) collective-permute-start(bf16[240,896]{1,0:T(8,128)(2,1)S(1)} %shard_map.102.stack_ref.mine_ref), channel_id=1, source_target_pairs={{0,1},{1,0},{2,3},{3,2},{4,5},{5,4},{6,7},{7,6},{8,9},{9,8},{10,11... | collective-permute-start | bytes 1290248 | tf_op jit(solution)/shard_map/ppermute | solution.py:396
  63.9 5.6 %collective-permute-start.6 = (bf16[120,768]{1,0:T(8,128)(2,1)S(1)}, bf16[120,768]{1,0:T(8,128)(2,1)S(1)}, u32[]{:S(2)}, u32[]{:S(2)}) collective-permute-start(bf16[120,768]{1,0:T(8,128)(2,1)S(1)} %shard_map.93.mine_ref), channel_id=1, source_target_pairs={{0,8},{8,0},{16,24},{24,16},{1,9},{9,1},{17,25},{25,17},{2,10},{10... | collective-permute-start | bytes 552968 | tf_op jit(solution)/shard_map/ppermute | solution.py:396
  64.2 22.9 %collective-permute-start.26 = (bf16[240,896]{1,0:T(8,128)(2,1)S(1)}, bf16[240,896]{1,0:T(8,128)(2,1)S(1)}, u32[]{:S(2)}, u32[]{:S(2)}) collective-permute-start(bf16[240,896]{1,0:T(8,128)(2,1)S(1)} %shard_map.98.stack_ref.mine_ref), channel_id=1, source_target_pairs={{0,1},{1,0},{2,3},{3,2},{4,5},{5,4},{6,7},{7,6},{8,9},{9,8},{10,11... | collective-permute-start | bytes 1290248 | tf_op jit(solution)/shard_map/ppermute | solution.py:396
  69.6 21.5 %collective-permute-start.25 = (bf16[240,768]{1,0:T(8,128)(2,1)S(1)}, bf16[240,768]{1,0:T(8,128)(2,1)S(1)}, u32[]{:S(2)}, u32[]{:S(2)}) collective-permute-start(bf16[240,768]{1,0:T(8,128)(2,1)S(1)} %shard_map.94.stack_ref.mine_ref), channel_id=1, source_target_pairs={{0,1},{1,0},{2,3},{3,2},{4,5},{5,4},{6,7},{7,6},{8,9},{9,8},{10,11... | collective-permute-start | bytes 1105928 | tf_op jit(solution)/shard_map/ppermute | solution.py:396
  82.6 12.2 %collective-permute-start.22 = (bf16[20,1280]{1,0:T(8,128)(2,1)S(1)}, bf16[20,1280]{1,0:T(8,128)(2,1)S(1)}, u32[]{:S(2)}, u32[]{:S(2)}) collective-permute-start(bf16[20,1280]{1,0:T(8,128)(2,1)S(1)} %get-tuple-element.74), channel_id=1, source_target_pairs={{0,2},{2,0},{4,6},{6,4},{1,3},{3,1},{5,7},{7,5},{8,10},{10,8},{12,... | collective-permute-start | bytes 153608 | tf_op jit(solution)/shard_map/ppermute | solution.py:396
  83.3 11.5 %collective-permute-start.23 = (bf16[20,1280]{1,0:T(8,128)(2,1)S(1)}, bf16[20,1280]{1,0:T(8,128)(2,1)S(1)}, u32[]{:S(2)}, u32[]{:S(2)}) collective-permute-start(bf16[20,1280]{1,0:T(8,128)(2,1)S(1)} %get-tuple-element.75), channel_id=1, source_target_pairs={{0,4},{2,6},{4,0},{6,2},{1,5},{3,7},{5,1},{7,3},{8,12},{10,14},{12... | collective-permute-start | bytes 153608 | tf_op jit(solution)/shard_map/ppermute | solution.py:396
  86.8 8.1 %collective-permute-start.24 = (bf16[20,1280]{1,0:T(8,128)(2,1)S(1)}, bf16[20,1280]{1,0:T(8,128)(2,1)S(1)}, u32[]{:S(2)}, u32[]{:S(2)}) collective-permute-start(bf16[20,1280]{1,0:T(8,128)(2,1)S(1)} %get-tuple-element.76), channel_id=1, source_target_pairs={{0,6},{2,4},{4,2},{6,0},{1,7},{3,5},{5,3},{7,1},{8,14},{10,12},{12... | collective-permute-start | bytes 153608 | tf_op jit(solution)/shard_map/ppermute | solution.py:396

commit v4 on v0

v4 whole, which is shorter than its diff:
```python
import functools

import jax
import jax.numpy as jnp
from jax import lax
from jax.experimental import pallas as pl
from jax.experimental.pallas import tpu as pltpu
from jax.sharding import PartitionSpec as P

BF16 = jnp.bfloat16
F32 = jnp.float32
NT = (((1,), (1,)), ((), ()))
TN = (((0,), (0,)), ((), ()))
LANES = 128
CHUNKS = 4
TILE = 256
CUTS = 4
MIB = 1024 * 1024
IN_VMEM = pl.BlockSpec(memory_space=pltpu.VMEM)
IN_HBM = pl.BlockSpec(memory_space=pl.ANY)


def shaped(rows, columns, dtype=BF16):
    return jax.ShapeDtypeStruct((rows, columns), dtype)


def joined(*blocks):
    return jnp.concatenate([block.astype(F32) for block in blocks], axis=0)


def pointwise(gate_sum, up_sum, dh_sum):
    sig = jax.nn.sigmoid(gate_sum)
    active = gate_sum * sig
    hidden = (active * up_sum).astype(BF16)
    d_up = (dh_sum * active).astype(BF16)
    d_gate = (dh_sum * up_sum * sig * (1.0 + gate_sum * (1.0 - sig))).astype(BF16)
    return (hidden, d_gate, d_up)


class Line:
    def __init__(self):
        self.token = ()

    def call(self, kernel, args, out_shape, in_specs=None, out_specs=None, scratch=(), limit=4):
        count, outs, tokens = len(args), len(out_shape), len(self.token)

        def body(*refs):
            rest = refs[count + tokens :]
            rest[outs][...] = jnp.zeros_like(rest[outs])
            kernel(*refs[:count], *rest[:outs], *rest[outs + 1 :])

        *results, token = pl.pallas_call(
            body,
            in_specs=(in_specs or [IN_VMEM] * count) + [IN_VMEM] * tokens,
            out_specs=(out_specs or [IN_VMEM] * outs) + [IN_VMEM],
            out_shape=[*out_shape, shaped(8, LANES, F32)],
            scratch_shapes=list(scratch),
            cost_estimate=pl.CostEstimate(flops=1, bytes_accessed=1, transcendentals=0),
            compiler_params=pltpu.CompilerParams(vmem_limit_bytes=limit * MIB),
        )(*args, *self.token)
        self.token = (token,)
        return results


def load_kernel(*refs):
    count = len(refs) // 2
    sems = refs[-1]
    copies = []
    for cut in range(CUTS):
        for at, (source, target) in enumerate(zip(refs[:count], refs[count:-1])):
            rows = source.shape[0] // CUTS
            part = pl.ds(cut * rows, rows)
            copies.append(
                pltpu.make_async_copy(source.at[part], target.at[part], sems.at[at, cut])
            )
    for copy in copies:
        copy.start()
    for copy in copies:
        copy.wait()


def load(line, *weights):
    return line.call(
        load_kernel,
        weights,
        [pltpu.VMEM(weight.shape, BF16) for weight in weights],
        in_specs=[IN_HBM] * len(weights),
        scratch=[pltpu.SemaphoreType.DMA((len(weights), CUTS))],
        limit=34,
    )


def order_kernel(*refs):
    *piece_refs, out_ref = refs
    pieces = [ref[...].astype(F32) for ref in piece_refs]
    rows = pieces[0].shape[0] // 2
    wa = lax.axis_index("wa")
    slots = []
    for slot in range(len(pieces)):
        at = wa ^ slot
        piece = pieces[0]
        for other in range(1, len(pieces)):
            piece = jnp.where(at == other, pieces[other], piece)
        slots.append(piece)
    out_ref[...] = joined(
        *(slot[:rows] for slot in slots), *(slot[rows:] for slot in slots)
    ).astype(BF16)


def order_rows(line, pieces):
    rows, width = pieces[0].shape
    return line.call(order_kernel, pieces, [shaped(4 * rows, width)])[0]


def forward_kernel(begin, near, far, xy_ref, gate_ref, up_ref, down_ref, *refs):
    keep_ref, send_ref = refs
    group = xy_ref.shape[0] // 2
    rows = group // 4
    x, y = xy_ref[:group], xy_ref[group:]
    there = pl.ds(begin, keep_ref.shape[1])
    gate = jnp.dot(x, gate_ref[:, there], preferred_element_type=F32)
    up = jnp.dot(x, up_ref[:, there], preferred_element_type=F32)
    dh = lax.dot_general(y, down_ref[there], NT, preferred_element_type=F32)

    def slots(*which):
        cuts = [slice(slot * rows, (slot + 1) * rows) for slot in which]
        return joined(*(part[cut] for cut in cuts for part in (gate, up, dh)))

    keep_ref[...] = slots(0, far)
    send_ref[...] = slots(near, near ^ far).astype(BF16)


def forward(line, begin, columns, axes, xy, gate_weight, up_weight, down_weight):
    rows = 6 * (xy.shape[0] // 8)
    return line.call(
        functools.partial(forward_kernel, begin, *axes),
        (xy, gate_weight, up_weight, down_weight),
        [shaped(rows, columns, F32), shaped(rows, columns)],
    )


def halve_kernel(keep_ref, received_ref, own_ref, send_ref):
    total = keep_ref[...] + received_ref[...].astype(F32)
    half = own_ref.shape[0]
    own_ref[...] = total[:half]
    send_ref[...] = total[half:].astype(BF16)


def halve(line, keep, received):
    shape = (keep.shape[0] // 2, keep.shape[1])
    return line.call(halve_kernel, (keep, received), [shaped(*shape, F32), shaped(*shape)])


def middle_kernel(own_ref, received_ref, out_ref):
    total = own_ref[...] + received_ref[...].astype(F32)
    rows = total.shape[0] // 3
    hidden, d_gate, d_up = pointwise(total[:rows], total[rows : 2 * rows], total[2 * rows :])
    out_ref[...] = joined(d_gate, d_up, hidden).astype(BF16)


def middle(line, own, received):
    return line.call(middle_kernel, (own, received), [shaped(*own.shape)])[0]


def join_kernel(first_ref, second_ref, out_ref):
    out_ref[...] = joined(first_ref[...], second_ref[...]).astype(BF16)


def join(line, first, second):
    rows = first.shape[0] + second.shape[0]
    return line.call(join_kernel, (first, second), [shaped(rows, first.shape[1])])[0]


def stack_kernel(axes, *refs):
    out_ref = refs[-1]
    begin = 0
    for at, (near, far) in enumerate(axes):
        mine, other = refs[2 * at][...].astype(F32), refs[2 * at + 1][...].astype(F32)
        columns = mine.shape[1]
        half, rows = mine.shape[0] // 2, mine.shape[0] // 6
        slots = {0: mine[:half], near: mine[half:]}
        slots |= {far: other[:half], near ^ far: other[half:]}
        cuts = [slots[slot][k * rows : (k + 1) * rows] for k in range(3) for slot in range(4)]
        out_ref[:, begin : begin + columns] = joined(*cuts).astype(BF16)
        begin += columns


def stack(line, axes, blocks):
    rows = 2 * blocks[0][0].shape[0]
    columns = sum(mine.shape[1] for mine, _ in blocks)
    return line.call(
        functools.partial(stack_kernel, axes),
        [block for pair in blocks for block in pair],
        [shaped(rows, columns)],
    )[0]


def input_grad_kernel(begin, stack_ref, gate_ref, up_ref, *refs):
    there = pl.ds(begin, stack_ref.shape[1])
    group = stack_ref.shape[0] // 3
    grad = lax.dot_general(
        stack_ref[:group], gate_ref[:, there], NT, preferred_element_type=F32
    ) + lax.dot_general(
        stack_ref[group : 2 * group], up_ref[:, there], NT, preferred_element_type=F32
    )
    refs[-1][...] = grad + refs[0][...] if len(refs) > 1 else grad


def input_grad(line, begin, stacked, gate_weight, up_weight, start):
    shape = (stacked.shape[0] // 3, gate_weight.shape[0])
    return line.call(
        functools.partial(input_grad_kernel, begin),
        (stacked, gate_weight, up_weight, *start),
        [shaped(*shape, F32)],
    )


def factors_kernel(mine_ref, other_ref, xt_ref, y_all_ref):
    group = mine_ref.shape[0] // 2
    first = lax.axis_index("row") == 0
    x, y = mine_ref[:group], mine_ref[group:]
    x_other, y_other = other_ref[:group], other_ref[group:]
    y_all_ref[:group] = jnp.where(first, y, y_other)
    y_all_ref[group:] = jnp.where(first, y_other, y)
    x_all = jnp.concatenate([jnp.where(first, x, x_other), jnp.where(first, x_other, x)], axis=0)
    xt_ref[...] = x_all.T


def factors(line, xy, other):
    rows, width = xy.shape
    return line.call(factors_kernel, (xy, other), [shaped(width, rows), shaped(rows, width)])


def weight_grad_kernel(parts, xt_ref, y_ref, *refs):
    mine_refs, other_refs = refs[:parts], refs[parts : 2 * parts]
    *outs, both, gate, up, down, sems = refs[2 * parts :]
    group = y_ref.shape[0] // 2
    first = lax.axis_index("row") == 0
    copies = []

    def send(at, source, target):
        copies.append(pltpu.make_async_copy(source, target, sems.at[at, len(copies) // 3]))
        copies[-1].start()

    begin = 0
    for mine_ref, other_ref in zip(mine_refs, other_refs):
        columns = mine_ref.shape[1]
        for start in range(0, columns, TILE):
            size = min(TILE, columns - start)
            source, here = pl.ds(start, size), pl.ds(begin + start, size)
            for at in range(3):
                cut = slice(at * group, (at + 1) * group)
                mine, other = mine_ref[cut, source], other_ref[cut, source]
                both[at, :group, here] = jnp.where(first, mine, other)
                both[at, group:, here] = jnp.where(first, other, mine)
            gate[:, here] = jnp.dot(
                xt_ref[...], both[0, :, here], preferred_element_type=F32
            ).astype(BF16)
            send(0, gate.at[:, here], outs[0].at[:, here])
            up[:, here] = jnp.dot(
                xt_ref[...], both[1, :, here], preferred_element_type=F32
            ).astype(BF16)
            send(1, up.at[:, here], outs[1].at[:, here])
            down[here, :] = lax.dot_general(
                both[2, :, here], y_ref[...], TN, preferred_element_type=F32
            ).astype(BF16)
            send(2, down.at[here], outs[2].at[here])
        begin += columns
    for copy in copies:
        copy.wait()


def weight_grad(line, xt, y, mine, other):
    width = xt.shape[0]
    hidden_width = sum(m.shape[1] for m in mine)
    shapes = [(width, hidden_width), (width, hidden_width), (hidden_width, width)]
    steps = sum(pl.cdiv(m.shape[1], TILE) for m in mine)
    return line.call(
        functools.partial(weight_grad_kernel, len(mine)),
        (xt, y, *mine, *other),
        [shaped(*shape) for shape in shapes],
        out_specs=[IN_HBM] * 3,
        scratch=[
            pltpu.VMEM((3, y.shape[0], hidden_width), BF16),
            *(pltpu.VMEM(shape, BF16) for shape in shapes),
            pltpu.SemaphoreType.DMA((3, steps)),
        ],
        limit=40,
    )


def last_kernel(grad_ref, *out_refs):
    grad = grad_ref[...]
    rows = out_refs[0].shape[0]
    cuts = [grad[slot * rows : (slot + 1) * rows] for slot in range(len(out_refs))]
    wa = lax.axis_index("wa")
    for step, out_ref in enumerate(out_refs):
        at = wa ^ step
        piece = cuts[0]
        for slot in range(1, len(cuts)):
            piece = jnp.where(at == slot, cuts[slot], piece)
        out_ref[...] = piece.astype(out_ref.dtype)


def last_pieces(line, parts, grad):
    shape = (grad.shape[0] // parts, grad.shape[1])
    return line.call(
        last_kernel, (grad,), [shaped(*shape, F32)] + [shaped(*shape)] * (parts - 1)
    )


def total_kernel(own_ref, *refs):
    total = own_ref[...]
    for ref in refs[:-1]:
        total = total + ref[...].astype(F32)
    refs[-1][...] = total.astype(BF16)


def total(line, own, received):
    return line.call(total_kernel, (own, *received), [shaped(*own.shape)])[0]


def swap(value, axis, size, step):
    return lax.ppermute(value, axis, [(at, at ^ step) for at in range(size)])


def fast_body(n_wa, n_ha, n_row, tokens, cotangent, gate_weight, up_weight, down_weight):
    hidden_width = gate_weight.shape[1]
    tiles = hidden_width // LANES
    ends = [-(-tiles * (at + 1) // CHUNKS) * LANES for at in range(CHUNKS)]
    chunks = [(begin, end - begin) for begin, end in zip([0] + ends, ends)]
    axes = [((1, 2), (2, 1))[at % 2] for at in range(CHUNKS)]
    line = Line()

    both = jnp.concatenate([tokens, cotangent], axis=0)
    pieces = [both] + [swap(both, "ha", n_ha, step) for step in range(1, n_ha)]
    gate_weight, up_weight, down_weight = load(Line(), gate_weight, up_weight, down_weight)
    xy = order_rows(line, pieces)
    xy_other = swap(xy, "row", n_row, 1)

    kept, got = [], []
    for (begin, columns), axis in zip(chunks, axes):
        keep, send = forward(
            line, begin, columns, axis, xy, gate_weight, up_weight, down_weight
        )
        kept.append(keep)
        got.append(swap(send, "wa", n_wa, axis[0]))
    for at, (_, far) in enumerate(axes):
        kept[at], send = halve(line, kept[at], got[at])
        got[at] = swap(send, "wa", n_wa, far)
    order = [pair + 1 - at for pair in range(0, CHUNKS, 2) for at in range(2)]
    for at in order:
        kept[at] = middle(line, kept[at], got[at])
        got[at] = swap(kept[at], "wa", n_wa, axes[at][0])
    xt, y_all = factors(line, xy, xy_other)
    for at, (_, far) in enumerate(axes):
        kept[at] = join(line, kept[at], got[at])
        got[at] = swap(kept[at], "wa", n_wa, far)

    mine, other, grad = [], [], ()
    for at in range(0, CHUNKS, 2):
        pair = slice(at, at + 2)
        mine.append(stack(line, axes[pair], list(zip(kept, got))[pair]))
        other.append(swap(mine[-1], "row", n_row, 1))
        grad = input_grad(line, chunks[at][0], mine[-1], gate_weight, up_weight, grad)
    own, *sends = last_pieces(line, n_ha, grad[0])
    received = [swap(sent, "ha", n_ha, k + 1) for k, sent in enumerate(sends)]
    grads = weight_grad(line, xt, y_all, mine, other)
    return (total(line, own, received), *grads)


def plain_body(tokens, cotangent, gate_weight, up_weight, down_weight):
    hidden_width = gate_weight.shape[1]
    x = lax.all_gather(tokens, "ha", axis=0, tiled=True)
    y = lax.all_gather(cotangent, "ha", axis=0, tiled=True)
    gate_part = jnp.dot(x, gate_weight, preferred_element_type=F32)
    up_part = jnp.dot(x, up_weight, preferred_element_type=F32)
    dh_part = lax.dot_general(y, down_weight, NT, preferred_element_type=F32)
    summed = lax.psum(jnp.concatenate([gate_part, up_part, dh_part], axis=1), "wa")
    hidden, d_gate, d_up = pointwise(
        summed[:, :hidden_width],
        summed[:, hidden_width : 2 * hidden_width],
        summed[:, 2 * hidden_width :],
    )
    partial = lax.dot_general(
        d_gate, gate_weight, NT, preferred_element_type=F32
    ) + lax.dot_general(d_up, up_weight, NT, preferred_element_type=F32)
    grad_tokens = lax.psum_scatter(partial, "ha", scatter_dimension=0, tiled=True)
    grads = (
        lax.dot_general(x, d_gate, TN, preferred_element_type=F32),
        lax.dot_general(x, d_up, TN, preferred_element_type=F32),
        lax.dot_general(hidden, y, TN, preferred_element_type=F32),
    )
    return (
        grad_tokens.astype(BF16),
        *(lax.psum(g.astype(BF16), "row").astype(BF16) for g in grads),
    )


def solution(mesh):
    n_wa, n_ha, n_row = (mesh.shape[name] for name in ("wa", "ha", "row"))

    def body(tokens, cotangent, gate_weight, up_weight, down_weight):
        width, hidden_width = gate_weight.shape
        fits = (
            n_wa == n_ha == 4
            and n_row == 2
            and width % LANES == 0
            and hidden_width % LANES == 0
            and hidden_width >= LANES * CHUNKS
            and (tokens.shape[0] * n_ha) % 16 == 0
        )
        if fits:
            return fast_body(
                n_wa, n_ha, n_row, tokens, cotangent, gate_weight, up_weight, down_weight
            )
        return plain_body(tokens, cotangent, gate_weight, up_weight, down_weight)

    return jax.shard_map(
        body,
        mesh=mesh,
        in_specs=(
            P(("row", "ha"), "wa"),
            P(("row", "ha"), "wa"),
            P("wa", "ha"),
            P("wa", "ha"),
            P("ha", "wa"),
        ),
        out_specs=(P(("row", "ha"), "wa"), P("wa", "ha"), P("wa", "ha"), P("ha", "wa")),
        check_vma=False,
    )
```

time: 288 us -> 73.5 us (0.26)
  waiting for transfers between devices: 139 us -> 11.9 us
  blocking collectives: 49 us -> 0 us
  matrix products: 41.3 us -> 0 us
  local copies, waits for them, and re-layouts: 36.1 us -> 0 us
  Pallas kernels: 0 us -> 32.5 us
  starting transfers between devices: 2.11 us -> 27.2 us
  between operations: 14.9 us -> 0.84 us
  other arithmetic: 4.37 us -> 0.88 us
    psum x2 -> x0, waiting for transfers between devices: 139 us -> none  [the longest x1 91 us: body(): lax.psum(jnp.concatenate([gate_part, up_part, dh_part], axis=1), 'wa')]
    dot_general x8 -> x0, matrix products: 41.3 us -> none  [the longest x1 7.36 us: body(): lax.dot_general(d_up, up_weight, contract_last, preferred_element_type=jn...]
    unnamed x24 -> x0, local copies, waits for them, and re-layouts: 35.5 us -> none
    pallas_call x0 -> x26, Pallas kernels: none -> 32.5 us  [call(): pl.pallas_call(body, in_specs=(in_specs or [IN_VMEM] * count) + [IN_VMEM]...]
    all_gather x2 -> x0, blocking collectives: 30.5 us -> none  [the longest x1 15.8 us: body(): lax.all_gather(tokens, 'ha', axis=0, tiled=True)]
    ppermute x0 -> x25, starting transfers between devices: none -> 27.2 us  [swap(): return lax.ppermute(value, axis, [(at, at ^ step) for at in range(size)])]
    unnamed x1 -> x0, blocking collectives: 18.5 us -> none
    ppermute x0 -> x25, waiting for transfers between devices: none -> 11.9 us  [swap(): return lax.ppermute(value, axis, [(at, at ^ step) for at in range(size)])]
  transfers between devices with their start and end apart: 3 -> 25, of which waited for: 3 -> 11; matrix products, arithmetic and copies ran while one was open for 12% -> 0% of each run, Pallas kernels for 0% -> 41%
where the time goes in v4:
time: 73.5 us; the launch traced here: 73.3 us
  Pallas kernels  32.5 us (44%)
  starting transfers between devices  27.2 us (37%)
  waiting for transfers between devices  11.9 us (16%)
  other arithmetic  0.88 us (1%)
  between operations  0.84 us (1%)
    pallas_call x26, Pallas kernels, call(): pl.pallas_call(body, in_specs=(in_specs or [IN_VMEM] * count) + [IN_VMEM]...  32.5 us
    ppermute x25, starting transfers between devices, swap(): return lax.ppermute(value, axis, [(at, at ^ step) for at in range(size)])  27.2 us
    ppermute x25, waiting for transfers between devices, swap(): return lax.ppermute(value, axis, [(at, at ^ step) for at in range(size)])  11.9 us
  transfers between devices with their start and end apart: 25, of which 11 were waited for; matrix products, arithmetic and copies ran while one was open for 0% of the time, Pallas kernels for 41%

profile of v4, /device:TPU:0, one launch (start us, length us, event | category | flops | bytes accessed | tf_op | source)
XLA Modules:
  0.0 73.3 jit_solution(13778154149045853453)
XLA Ops:
  0.6 0.9 %pad_maximum_fusion.refs_0_ = bf16[40,1280]{1,0:T(8,128)(2,1)S(1)} fusion(bf16[20,1280]{1,0:T(8,128)(2,1)} %param.6, bf16[20,1280]{1,0:T(8,128)(2,1)} %param.5), kind=kLoop, calls=%fused_computation | loop fusion | flops 204800 | bytes 204800 | tf_op jit(solution)/shard_map/concatenate | solution.py:335
  1.5 5.1 %collective-permute-start.2 = (bf16[40,1280]{1,0:T(8,128)(2,1)S(1)}, bf16[40,1280]{1,0:T(8,128)(2,1)S(1)}, u32[]{:S(2)}, u32[]{:S(2)}) collective-permute-start(bf16[40,1280]{1,0:T(8,128)(2,1)S(1)} %pad_maximum_fusion.refs_0_), channel_id=1, source_target_pairs={{0,6},{2,4},{4,2},{6,0},{1,7},{3,5},{5,3},{7,1},{8,14},{10,12},{12... | collective-permute-start | bytes 307208 | tf_op jit(solution)/shard_map/ppermute | solution.py:324
  6.6 0.0 collective-permute-start.1
  6.6 0.6 collective-permute-start
  7.3 9.3 %shard_map.85 = (bf16[1280,3456]{1,0:T(8,128)(2,1)S(1)}, bf16[1280,3456]{1,0:T(8,128)(2,1)S(1)}, bf16[3456,1280]{1,0:T(8,128)(2,1)S(1)}, f32[8,128]{1,0:T(8,128)}) custom-call(bf16[1280,3456]{1,0:T(8,128)(2,1)} %refs_0_.1, bf16[1280,3456]{1,0:T(8,128)(2,1)} %refs_1_.1, bf16[3456,1280]{1,0:T(8,128)(2,1)} %refs_2_.1), custom_call_target="tpu_custom_call" | custom-call | flops 1 | bytes 1 | tf_op jit(solution)/shard_map/pallas_call | solution.py:52
  16.6 0.0 collective-permute-done.1.refs_2_
  16.6 0.0 collective-permute-done.refs_1_
  16.6 0.2 shard_map.84
  16.8 1.5 %shard_map.86 = (f32[120,896]{1,0:T(8,128)S(1)}, bf16[120,896]{1,0:T(8,128)(2,1)S(1)}, f32[8,128]{1,0:T(8,128)S(1)}) custom-call(bf16[160,1280]{1,0:T(8,128)(2,1)S(1)} %get-tuple-element.70.refs_0_, bf16[1280,3456]{1,0:T(8,128)(2,1)S(1)} %get-tuple-element.71.refs_1_, bf16[1280,3456]{1,0:T(8,128)(2,1)S(1)} %get-tuple-element.72.refs_2_, ...), custom_call_target="tpu_custom_call" | custom-call | flops 1 | bytes 1 | tf_op jit(solution)/shard_map/pallas_call | solution.py:52
  18.3 1.7 %collective-permute-start.5 = (bf16[120,896]{1,0:T(8,128)(2,1)S(1)}, bf16[120,896]{1,0:T(8,128)(2,1)S(1)}, u32[]{:S(2)}, u32[]{:S(2)}) collective-permute-start(bf16[120,896]{1,0:T(8,128)(2,1)S(1)} %get-tuple-element.82), channel_id=1, source_target_pairs={{0,8},{8,0},{16,24},{24,16},{1,9},{9,1},{17,25},{25,17},{2,10},{10... | collective-permute-start | bytes 645128 | tf_op jit(solution)/shard_map/ppermute | solution.py:324
  20.0 1.5 %shard_map.87 = (f32[120,896]{1,0:T(8,128)S(1)}, bf16[120,896]{1,0:T(8,128)(2,1)S(1)}, f32[8,128]{1,0:T(8,128)S(1)}) custom-call(bf16[160,1280]{1,0:T(8,128)(2,1)S(1)} %get-tuple-element.70.refs_0_, bf16[1280,3456]{1,0:T(8,128)(2,1)S(1)} %get-tuple-element.71.refs_1_, bf16[1280,3456]{1,0:T(8,128)(2,1)S(1)} %get-tuple-element.72.refs_2_, ...), custom_call_target="tpu_custom_call" | custom-call | flops 1 | bytes 1 | tf_op jit(solution)/shard_map/pallas_call | solution.py:52
  21.5 1.6 %collective-permute-start.4 = (bf16[120,896]{1,0:T(8,128)(2,1)S(1)}, bf16[120,896]{1,0:T(8,128)(2,1)S(1)}, u32[]{:S(2)}, u32[]{:S(2)}) collective-permute-start(bf16[120,896]{1,0:T(8,128)(2,1)S(1)} %get-tuple-element.80), channel_id=1, source_target_pairs={{0,16},{8,24},{16,0},{24,8},{1,17},{9,25},{17,1},{25,9},{2,18},{10... | collective-permute-start | bytes 645128 | tf_op jit(solution)/shard_map/ppermute | solution.py:324
  23.1 0.0 collective-permute-start.14
  23.1 1.5 %shard_map.88 = (f32[120,896]{1,0:T(8,128)S(1)}, bf16[120,896]{1,0:T(8,128)(2,1)S(1)}, f32[8,128]{1,0:T(8,128)S(1)}) custom-call(bf16[160,1280]{1,0:T(8,128)(2,1)S(1)} %get-tuple-element.70.refs_0_, bf16[1280,3456]{1,0:T(8,128)(2,1)S(1)} %get-tuple-element.71.refs_1_, bf16[1280,3456]{1,0:T(8,128)(2,1)S(1)} %get-tuple-element.72.refs_2_, ...), custom_call_target="tpu_custom_call" | custom-call | flops 1 | bytes 1 | tf_op jit(solution)/shard_map/pallas_call | solution.py:52
  24.6 0.6 collective-permute-start.3
  25.2 1.4 %shard_map.89 = (f32[120,768]{1,0:T(8,128)S(1)}, bf16[120,768]{1,0:T(8,128)(2,1)S(1)}, f32[8,128]{1,0:T(8,128)S(1)}) custom-call(bf16[160,1280]{1,0:T(8,128)(2,1)S(1)} %get-tuple-element.70.refs_0_, bf16[1280,3456]{1,0:T(8,128)(2,1)S(1)} %get-tuple-element.71.refs_1_, bf16[1280,3456]{1,0:T(8,128)(2,1)S(1)} %get-tuple-element.72.refs_2_, ...), custom_call_target="tpu_custom_call" | custom-call | flops 1 | bytes 1 | tf_op jit(solution)/shard_map/pallas_call | solution.py:52
  26.6 0.4 collective-permute-start.7
  27.0 0.0 collective-permute-done.5.refs_1_
  27.0 0.1 shard_map.90
  27.1 0.6 collective-permute-done.4.refs_1_
  27.6 0.1 shard_map.91
  27.7 1.2 %collective-permute-start.10 = (bf16[60,896]{1,0:T(8,128)(2,1)S(1)}, bf16[60,896]{1,0:T(8,128)(2,1)S(1)}, u32[]{:S(2)}, u32[]{:S(2)}) collective-permute-start(bf16[60,896]{1,0:T(8,128)(2,1)S(1)} %get-tuple-element.97), channel_id=1, source_target_pairs={{0,8},{8,0},{16,24},{24,16},{1,9},{9,1},{17,25},{25,17},{2,10},{10... | collective-permute-start | bytes 322568 | tf_op jit(solution)/shard_map/ppermute | solution.py:324
  28.8 1.5 %collective-permute-start.9 = (bf16[60,896]{1,0:T(8,128)(2,1)S(1)}, bf16[60,896]{1,0:T(8,128)(2,1)S(1)}, u32[]{:S(2)}, u32[]{:S(2)}) collective-permute-start(bf16[60,896]{1,0:T(8,128)(2,1)S(1)} %get-tuple-element.95), channel_id=1, source_target_pairs={{0,16},{8,24},{16,0},{24,8},{1,17},{9,25},{17,1},{25,9},{2,18},{10... | collective-permute-start | bytes 322568 | tf_op jit(solution)/shard_map/ppermute | solution.py:324
  30.4 2.4 %collective-permute-done.3.refs_1_ = bf16[120,896]{1,0:T(8,128)(2,1)S(1)} collective-permute-done((bf16[120,896]{1,0:T(8,128)(2,1)S(1)}, bf16[120,896]{1,0:T(8,128)(2,1)S(1)}, u32[]{:S(2)}, u32[]{:S(2)}) %collective-permute-start.3) | collective-permute-done | bytes 215072 | tf_op jit(solution)/shard_map/ppermute | solution.py:324
  32.7 0.1 shard_map.92
  32.8 0.6 collective-permute-start.6
  33.4 0.7 collective-permute-done.7.refs_1_
  34.1 0.1 shard_map.93
  34.2 1.6 %collective-permute-start.8 = (bf16[60,768]{1,0:T(8,128)(2,1)S(1)}, bf16[60,768]{1,0:T(8,128)(2,1)S(1)}, u32[]{:S(2)}, u32[]{:S(2)}) collective-permute-start(bf16[60,768]{1,0:T(8,128)(2,1)S(1)} %get-tuple-element.93), channel_id=1, source_target_pairs={{0,8},{8,0},{16,24},{24,16},{1,9},{9,1},{17,25},{25,17},{2,10},{10... | collective-permute-start | bytes 276488 | tf_op jit(solution)/shard_map/ppermute | solution.py:324
  35.7 0.0 collective-permute-done.10.refs_1_
  35.7 0.1 shard_map.94
  35.8 0.8 %collective-permute-done.9.refs_1_ = bf16[60,896]{1,0:T(8,128)(2,1)S(1)} collective-permute-done((bf16[60,896]{1,0:T(8,128)(2,1)S(1)}, bf16[60,896]{1,0:T(8,128)(2,1)S(1)}, u32[]{:S(2)}, u32[]{:S(2)}) %collective-permute-start.9) | collective-permute-done | bytes 107552 | tf_op jit(solution)/shard_map/ppermute | solution.py:324
  36.6 0.1 shard_map.95
  36.6 1.6 %collective-permute-start.13 = (bf16[60,896]{1,0:T(8,128)(2,1)S(1)}, bf16[60,896]{1,0:T(8,128)(2,1)S(1)}, u32[]{:S(2)}, u32[]{:S(2)}) collective-permute-start(bf16[60,896]{1,0:T(8,128)(2,1)S(1)} %get-tuple-element.104.refs_0_), channel_id=1, source_target_pairs={{0,8},{8,0},{16,24},{24,16},{1,9},{9,1},{17,25},{25,17},{2,10},{10... | collective-permute-start | bytes 322568 | tf_op jit(solution)/shard_map/ppermute | solution.py:324
  38.2 0.5 collective-permute-start.12
  38.7 1.0 %collective-permute-done.8.refs_1_ = bf16[60,768]{1,0:T(8,128)(2,1)S(1)} collective-permute-done((bf16[60,768]{1,0:T(8,128)(2,1)S(1)}, bf16[60,768]{1,0:T(8,128)(2,1)S(1)}, u32[]{:S(2)}, u32[]{:S(2)}) %collective-permute-start.8) | collective-permute-done | bytes 92192 | tf_op jit(solution)/shard_map/ppermute | solution.py:324
  39.7 0.1 shard_map.96
  39.8 0.0 collective-permute-done.6.refs_1_
  39.8 0.1 shard_map.97
  39.9 1.6 %collective-permute-start.11 = (bf16[60,896]{1,0:T(8,128)(2,1)S(1)}, bf16[60,896]{1,0:T(8,128)(2,1)S(1)}, u32[]{:S(2)}, u32[]{:S(2)}) collective-permute-start(bf16[60,896]{1,0:T(8,128)(2,1)S(1)} %get-tuple-element.102.refs_0_), channel_id=1, source_target_pairs={{0,8},{8,0},{16,24},{24,16},{1,9},{9,1},{17,25},{25,17},{2,10},{10... | collective-permute-start | bytes 322568 | tf_op jit(solution)/shard_map/ppermute | solution.py:324
  41.4 0.5 collective-permute-start.16
  41.9 0.3 shard_map.98
  42.2 0.3 collective-permute-done.13.refs_1_
  42.6 1.4 %collective-permute-done.12.refs_1_ = bf16[60,896]{1,0:T(8,128)(2,1)S(1)} collective-permute-done((bf16[60,896]{1,0:T(8,128)(2,1)S(1)}, bf16[60,896]{1,0:T(8,128)(2,1)S(1)}, u32[]{:S(2)}, u32[]{:S(2)}) %collective-permute-start.12) | collective-permute-done | bytes 107552 | tf_op jit(solution)/shard_map/ppermute | solution.py:324
  44.0 0.6 collective-permute-start.19
  44.6 0.4 collective-permute-start.18
  44.9 1.0 %collective-permute-done.11.refs_1_ = bf16[60,896]{1,0:T(8,128)(2,1)S(1)} collective-permute-done((bf16[60,896]{1,0:T(8,128)(2,1)S(1)}, bf16[60,896]{1,0:T(8,128)(2,1)S(1)}, u32[]{:S(2)}, u32[]{:S(2)}) %collective-permute-start.11) | collective-permute-done | bytes 107552 | tf_op jit(solution)/shard_map/ppermute | solution.py:324
  46.0 1.0 %collective-permute-start.15 = (bf16[120,896]{1,0:T(8,128)(2,1)S(1)}, bf16[120,896]{1,0:T(8,128)(2,1)S(1)}, u32[]{:S(2)}, u32[]{:S(2)}) collective-permute-start(bf16[120,896]{1,0:T(8,128)(2,1)S(1)} %get-tuple-element.109.refs_0_), channel_id=1, source_target_pairs={{0,16},{8,24},{16,0},{24,8},{1,17},{9,25},{17,1},{25,9},{2,18},{10... | collective-permute-start | bytes 645128 | tf_op jit(solution)/shard_map/ppermute | solution.py:324
  46.9 0.2 collective-permute-done.16.refs_1_
  47.1 1.2 %collective-permute-start.17 = (bf16[120,768]{1,0:T(8,128)(2,1)S(1)}, bf16[120,768]{1,0:T(8,128)(2,1)S(1)}, u32[]{:S(2)}, u32[]{:S(2)}) collective-permute-start(bf16[120,768]{1,0:T(8,128)(2,1)S(1)} %get-tuple-element.112.refs_2_), channel_id=1, source_target_pairs={{0,8},{8,0},{16,24},{24,16},{1,9},{9,1},{17,25},{25,17},{2,10},{10... | collective-permute-start | bytes 552968 | tf_op jit(solution)/shard_map/ppermute | solution.py:324
  48.3 2.7 %collective-permute-done.19.refs_3_ = bf16[120,896]{1,0:T(8,128)(2,1)S(1)} collective-permute-done((bf16[120,896]{1,0:T(8,128)(2,1)S(1)}, bf16[120,896]{1,0:T(8,128)(2,1)S(1)}, u32[]{:S(2)}, u32[]{:S(2)}) %collective-permute-start.19) | collective-permute-done | bytes 215072 | tf_op jit(solution)/shard_map/ppermute | solution.py:324
  51.1 0.8 %collective-permute-done.18.refs_1_ = bf16[120,896]{1,0:T(8,128)(2,1)S(1)} collective-permute-done((bf16[120,896]{1,0:T(8,128)(2,1)S(1)}, bf16[120,896]{1,0:T(8,128)(2,1)S(1)}, u32[]{:S(2)}, u32[]{:S(2)}) %collective-permute-start.18) | collective-permute-done | bytes 215072 | tf_op jit(solution)/shard_map/ppermute | solution.py:324
  51.9 0.1 shard_map.103
  52.0 0.1 collective-permute-start.23
  52.1 2.9 %shard_map.104 = (f32[80,1280]{1,0:T(8,128)S(1)}, f32[8,128]{1,0:T(8,128)S(1)}) custom-call(bf16[240,1792]{1,0:T(8,128)(2,1)S(1)} %get-tuple-element.116.refs_0_.refs_2_, bf16[1280,3456]{1,0:T(8,128)(2,1)S(1)} %get-tuple-element.71.refs_1_, bf16[1280,3456]{1,0:T(8,128)(2,1)S(1)} %get-tuple-element.72.refs_2_, f32[8,128]{1,0:T(8,128)S(1)} %get-tuple-element.117.refs_3_), custom_call_target="tpu_custom_call" | custom-call | flops 1 | bytes 1 | tf_op jit(solution)/shard_map/pallas_call | solution.py:52
  55.0 0.1 shard_map.105
  55.1 0.6 collective-permute-start.24
  55.7 2.7 %shard_map.106 = (f32[80,1280]{1,0:T(8,128)S(1)}, f32[8,128]{1,0:T(8,128)S(1)}) custom-call(bf16[240,1664]{1,0:T(8,128)(2,1)S(1)} %get-tuple-element.119.refs_0_.refs_3_, bf16[1280,3456]{1,0:T(8,128)(2,1)S(1)} %get-tuple-element.71.refs_1_, bf16[1280,3456]{1,0:T(8,128)(2,1)S(1)} %get-tuple-element.72.refs_2_, f32[80,1280]{1,0:T(8,128)S(1)} %get-tuple-element.120.refs_3_, ...), custom_call_target="tpu_custom_call" | custom-call | flops 1 | bytes 1 | tf_op jit(solution)/shard_map/pallas_call | solution.py:52
  58.4 0.2 shard_map.107
  58.5 1.3 %collective-permute-start.20 = (bf16[20,1280]{1,0:T(8,128)(2,1)S(1)}, bf16[20,1280]{1,0:T(8,128)(2,1)S(1)}, u32[]{:S(2)}, u32[]{:S(2)}) collective-permute-start(bf16[20,1280]{1,0:T(8,128)(2,1)S(1)} %get-tuple-element.125), channel_id=1, source_target_pairs={{0,2},{2,0},{4,6},{6,4},{1,3},{3,1},{5,7},{7,5},{8,10},{10,8},{12,... | collective-permute-start | bytes 153608 | tf_op jit(solution)/shard_map/ppermute | solution.py:324
  59.8 2.9 %collective-permute-start.21 = (bf16[20,1280]{1,0:T(8,128)(2,1)S(1)}, bf16[20,1280]{1,0:T(8,128)(2,1)S(1)}, u32[]{:S(2)}, u32[]{:S(2)}) collective-permute-start(bf16[20,1280]{1,0:T(8,128)(2,1)S(1)} %get-tuple-element.126), channel_id=1, source_target_pairs={{0,4},{2,6},{4,0},{6,2},{1,5},{3,7},{5,1},{7,3},{8,12},{10,14},{12... | collective-permute-start | bytes 153608 | tf_op jit(solution)/shard_map/ppermute | solution.py:324
  62.8 0.2 collective-permute-start.22
  63.0 9.6 %shard_map.108 = (bf16[1280,3456]{1,0:T(8,128)(2,1)}, bf16[1280,3456]{1,0:T(8,128)(2,1)}, bf16[3456,1280]{1,0:T(8,128)(2,1)}, f32[8,128]{1,0:T(8,128)S(1)}) custom-call(bf16[1280,160]{1,0:T(8,128)(2,1)S(1)} %get-tuple-element.128.refs_0_, bf16[160,1280]{1,0:T(8,128)(2,1)S(1)} %get-tuple-element.129.refs_1_, ...), custom_call_target="tpu_custom_call" | custom-call | flops 1 | bytes 1 | tf_op jit(solution)/shard_map/pallas_call | solution.py:52
  72.6 0.7 shard_map.109
  (13 shorter events, 0.2 us)
Async XLA Ops:
  1.5 15.1 %collective-permute-start.2 = (bf16[40,1280]{1,0:T(8,128)(2,1)S(1)}, bf16[40,1280]{1,0:T(8,128)(2,1)S(1)}, u32[]{:S(2)}, u32[]{:S(2)}) collective-permute-start(bf16[40,1280]{1,0:T(8,128)(2,1)S(1)} %pad_maximum_fusion.refs_0_), channel_id=1, source_target_pairs={{0,6},{2,4},{4,2},{6,0},{1,7},{3,5},{5,3},{7,1},{8,14},{10,12},{12... | collective-permute-start | bytes 307208 | tf_op jit(solution)/shard_map/ppermute | solution.py:324
  6.6 10.0 %collective-permute-start.1 = (bf16[40,1280]{1,0:T(8,128)(2,1)S(1)}, bf16[40,1280]{1,0:T(8,128)(2,1)S(1)}, u32[]{:S(2)}, u32[]{:S(2)}) collective-permute-start(bf16[40,1280]{1,0:T(8,128)(2,1)S(1)} %pad_maximum_fusion.refs_0_), channel_id=1, source_target_pairs={{0,4},{2,6},{4,0},{6,2},{1,5},{3,7},{5,1},{7,3},{8,12},{10,14},{12... | collective-permute-start | bytes 307208 | tf_op jit(solution)/shard_map/ppermute | solution.py:324
  6.6 10.0 %collective-permute-start = (bf16[40,1280]{1,0:T(8,128)(2,1)S(1)}, bf16[40,1280]{1,0:T(8,128)(2,1)S(1)}, u32[]{:S(2)}, u32[]{:S(2)}) collective-permute-start(bf16[40,1280]{1,0:T(8,128)(2,1)S(1)} %pad_maximum_fusion.refs_0_), channel_id=1, source_target_pairs={{0,2},{2,0},{4,6},{6,4},{1,3},{3,1},{5,7},{7,5},{8,10},{10,8},{12,... | collective-permute-start | bytes 307208 | tf_op jit(solution)/shard_map/ppermute | solution.py:324
  18.3 8.7 %collective-permute-start.5 = (bf16[120,896]{1,0:T(8,128)(2,1)S(1)}, bf16[120,896]{1,0:T(8,128)(2,1)S(1)}, u32[]{:S(2)}, u32[]{:S(2)}) collective-permute-start(bf16[120,896]{1,0:T(8,128)(2,1)S(1)} %get-tuple-element.82), channel_id=1, source_target_pairs={{0,8},{8,0},{16,24},{24,16},{1,9},{9,1},{17,25},{25,17},{2,10},{10... | collective-permute-start | bytes 645128 | tf_op jit(solution)/shard_map/ppermute | solution.py:324
  21.5 6.1 %collective-permute-start.4 = (bf16[120,896]{1,0:T(8,128)(2,1)S(1)}, bf16[120,896]{1,0:T(8,128)(2,1)S(1)}, u32[]{:S(2)}, u32[]{:S(2)}) collective-permute-start(bf16[120,896]{1,0:T(8,128)(2,1)S(1)} %get-tuple-element.80), channel_id=1, source_target_pairs={{0,16},{8,24},{16,0},{24,8},{1,17},{9,25},{17,1},{25,9},{2,18},{10... | collective-permute-start | bytes 645128 | tf_op jit(solution)/shard_map/ppermute | solution.py:324
  23.1 18.8 %collective-permute-start.14 = (bf16[160,1280]{1,0:T(8,128)(2,1)S(1)}, bf16[160,1280]{1,0:T(8,128)(2,1)S(1)}, u32[]{:S(2)}, u32[]{:S(2)}) collective-permute-start(bf16[160,1280]{1,0:T(8,128)(2,1)S(1)} %get-tuple-element.70.refs_0_), channel_id=1, source_target_pairs={{0,1},{1,0},{2,3},{3,2},{4,5},{5,4},{6,7},{7,6},{8,9},{9,8},{10,11... | collective-permute-start | bytes 1228808 | tf_op jit(solution)/shard_map/ppermute | solution.py:324
  24.6 8.2 %collective-permute-start.3 = (bf16[120,896]{1,0:T(8,128)(2,1)S(1)}, bf16[120,896]{1,0:T(8,128)(2,1)S(1)}, u32[]{:S(2)}, u32[]{:S(2)}) collective-permute-start(bf16[120,896]{1,0:T(8,128)(2,1)S(1)} %get-tuple-element.78), channel_id=1, source_target_pairs={{0,8},{8,0},{16,24},{24,16},{1,9},{9,1},{17,25},{25,17},{2,10},{10... | collective-permute-start | bytes 645128 | tf_op jit(solution)/shard_map/ppermute | solution.py:324
  26.6 7.5 %collective-permute-start.7 = (bf16[120,768]{1,0:T(8,128)(2,1)S(1)}, bf16[120,768]{1,0:T(8,128)(2,1)S(1)}, u32[]{:S(2)}, u32[]{:S(2)}) collective-permute-start(bf16[120,768]{1,0:T(8,128)(2,1)S(1)} %get-tuple-element.90), channel_id=1, source_target_pairs={{0,16},{8,24},{16,0},{24,8},{1,17},{9,25},{17,1},{25,9},{2,18},{10... | collective-permute-start | bytes 552968 | tf_op jit(solution)/shard_map/ppermute | solution.py:324
  27.7 8.0 %collective-permute-start.10 = (bf16[60,896]{1,0:T(8,128)(2,1)S(1)}, bf16[60,896]{1,0:T(8,128)(2,1)S(1)}, u32[]{:S(2)}, u32[]{:S(2)}) collective-permute-start(bf16[60,896]{1,0:T(8,128)(2,1)S(1)} %get-tuple-element.97), channel_id=1, source_target_pairs={{0,8},{8,0},{16,24},{24,16},{1,9},{9,1},{17,25},{25,17},{2,10},{10... | collective-permute-start | bytes 322568 | tf_op jit(solution)/shard_map/ppermute | solution.py:324
  28.8 7.7 %collective-permute-start.9 = (bf16[60,896]{1,0:T(8,128)(2,1)S(1)}, bf16[60,896]{1,0:T(8,128)(2,1)S(1)}, u32[]{:S(2)}, u32[]{:S(2)}) collective-permute-start(bf16[60,896]{1,0:T(8,128)(2,1)S(1)} %get-tuple-element.95), channel_id=1, source_target_pairs={{0,16},{8,24},{16,0},{24,8},{1,17},{9,25},{17,1},{25,9},{2,18},{10... | collective-permute-start | bytes 322568 | tf_op jit(solution)/shard_map/ppermute | solution.py:324
  32.8 6.9 %collective-permute-start.6 = (bf16[60,896]{1,0:T(8,128)(2,1)S(1)}, bf16[60,896]{1,0:T(8,128)(2,1)S(1)}, u32[]{:S(2)}, u32[]{:S(2)}) collective-permute-start(bf16[60,896]{1,0:T(8,128)(2,1)S(1)} %get-tuple-element.88), channel_id=1, source_target_pairs={{0,16},{8,24},{16,0},{24,8},{1,17},{9,25},{17,1},{25,9},{2,18},{10... | collective-permute-start | bytes 322568 | tf_op jit(solution)/shard_map/ppermute | solution.py:324
  34.2 5.5 %collective-permute-start.8 = (bf16[60,768]{1,0:T(8,128)(2,1)S(1)}, bf16[60,768]{1,0:T(8,128)(2,1)S(1)}, u32[]{:S(2)}, u32[]{:S(2)}) collective-permute-start(bf16[60,768]{1,0:T(8,128)(2,1)S(1)} %get-tuple-element.93), channel_id=1, source_target_pairs={{0,8},{8,0},{16,24},{24,16},{1,9},{9,1},{17,25},{25,17},{2,10},{10... | collective-permute-start | bytes 276488 | tf_op jit(solution)/shard_map/ppermute | solution.py:324
  36.6 5.9 %collective-permute-start.13 = (bf16[60,896]{1,0:T(8,128)(2,1)S(1)}, bf16[60,896]{1,0:T(8,128)(2,1)S(1)}, u32[]{:S(2)}, u32[]{:S(2)}) collective-permute-start(bf16[60,896]{1,0:T(8,128)(2,1)S(1)} %get-tuple-element.104.refs_0_), channel_id=1, source_target_pairs={{0,8},{8,0},{16,24},{24,16},{1,9},{9,1},{17,25},{25,17},{2,10},{10... | collective-permute-start | bytes 322568 | tf_op jit(solution)/shard_map/ppermute | solution.py:324
  38.2 5.8 %collective-permute-start.12 = (bf16[60,896]{1,0:T(8,128)(2,1)S(1)}, bf16[60,896]{1,0:T(8,128)(2,1)S(1)}, u32[]{:S(2)}, u32[]{:S(2)}) collective-permute-start(bf16[60,896]{1,0:T(8,128)(2,1)S(1)} %get-tuple-element.103.refs_0_), channel_id=1, source_target_pairs={{0,16},{8,24},{16,0},{24,8},{1,17},{9,25},{17,1},{25,9},{2,18},{10... | collective-permute-start | bytes 322568 | tf_op jit(solution)/shard_map/ppermute | solution.py:324
  39.9 6.1 %collective-permute-start.11 = (bf16[60,896]{1,0:T(8,128)(2,1)S(1)}, bf16[60,896]{1,0:T(8,128)(2,1)S(1)}, u32[]{:S(2)}, u32[]{:S(2)}) collective-permute-start(bf16[60,896]{1,0:T(8,128)(2,1)S(1)} %get-tuple-element.102.refs_0_), channel_id=1, source_target_pairs={{0,8},{8,0},{16,24},{24,16},{1,9},{9,1},{17,25},{25,17},{2,10},{10... | collective-permute-start | bytes 322568 | tf_op jit(solution)/shard_map/ppermute | solution.py:324
  41.4 5.7 %collective-permute-start.16 = (bf16[60,768]{1,0:T(8,128)(2,1)S(1)}, bf16[60,768]{1,0:T(8,128)(2,1)S(1)}, u32[]{:S(2)}, u32[]{:S(2)}) collective-permute-start(bf16[60,768]{1,0:T(8,128)(2,1)S(1)} %get-tuple-element.110.refs_0_), channel_id=1, source_target_pairs={{0,16},{8,24},{16,0},{24,8},{1,17},{9,25},{17,1},{25,9},{2,18},{10... | collective-permute-start | bytes 276488 | tf_op jit(solution)/shard_map/ppermute | solution.py:324
  44.0 7.1 %collective-permute-start.19 = (bf16[120,896]{1,0:T(8,128)(2,1)S(1)}, bf16[120,896]{1,0:T(8,128)(2,1)S(1)}, u32[]{:S(2)}, u32[]{:S(2)}) collective-permute-start(bf16[120,896]{1,0:T(8,128)(2,1)S(1)} %get-tuple-element.114.refs_2_), channel_id=1, source_target_pairs={{0,8},{8,0},{16,24},{24,16},{1,9},{9,1},{17,25},{25,17},{2,10},{10... | collective-permute-start | bytes 645128 | tf_op jit(solution)/shard_map/ppermute | solution.py:324
  44.6 7.3 %collective-permute-start.18 = (bf16[120,896]{1,0:T(8,128)(2,1)S(1)}, bf16[120,896]{1,0:T(8,128)(2,1)S(1)}, u32[]{:S(2)}, u32[]{:S(2)}) collective-permute-start(bf16[120,896]{1,0:T(8,128)(2,1)S(1)} %get-tuple-element.113.refs_0_), channel_id=1, source_target_pairs={{0,16},{8,24},{16,0},{24,8},{1,17},{9,25},{17,1},{25,9},{2,18},{10... | collective-permute-start | bytes 645128 | tf_op jit(solution)/shard_map/ppermute | solution.py:324
  46.0 9.0 %collective-permute-start.15 = (bf16[120,896]{1,0:T(8,128)(2,1)S(1)}, bf16[120,896]{1,0:T(8,128)(2,1)S(1)}, u32[]{:S(2)}, u32[]{:S(2)}) collective-permute-start(bf16[120,896]{1,0:T(8,128)(2,1)S(1)} %get-tuple-element.109.refs_0_), channel_id=1, source_target_pairs={{0,16},{8,24},{16,0},{24,8},{1,17},{9,25},{17,1},{25,9},{2,18},{10... | collective-permute-start | bytes 645128 | tf_op jit(solution)/shard_map/ppermute | solution.py:324
  47.1 7.9 %collective-permute-start.17 = (bf16[120,768]{1,0:T(8,128)(2,1)S(1)}, bf16[120,768]{1,0:T(8,128)(2,1)S(1)}, u32[]{:S(2)}, u32[]{:S(2)}) collective-permute-start(bf16[120,768]{1,0:T(8,128)(2,1)S(1)} %get-tuple-element.112.refs_2_), channel_id=1, source_target_pairs={{0,8},{8,0},{16,24},{24,16},{1,9},{9,1},{17,25},{25,17},{2,10},{10... | collective-permute-start | bytes 552968 | tf_op jit(solution)/shard_map/ppermute | solution.py:324
  52.0 10.9 %collective-permute-start.23 = (bf16[240,1792]{1,0:T(8,128)(2,1)S(1)}, bf16[240,1792]{1,0:T(8,128)(2,1)S(1)}, u32[]{:S(2)}, u32[]{:S(2)}) collective-permute-start(bf16[240,1792]{1,0:T(8,128)(2,1)S(1)} %get-tuple-element.116.refs_0_.refs_2_), channel_id=1, source_target_pairs={{0,1},{1,0},{2,3},{3,2},{4,5},{5,4},{6,7},{7,6},{8,9},{9,8},{10,11... | collective-permute-start | bytes 2580488 | tf_op jit(solution)/shard_map/ppermute | solution.py:324
  55.1 7.9 %collective-permute-start.24 = (bf16[240,1664]{1,0:T(8,128)(2,1)S(1)}, bf16[240,1664]{1,0:T(8,128)(2,1)S(1)}, u32[]{:S(2)}, u32[]{:S(2)}) collective-permute-start(bf16[240,1664]{1,0:T(8,128)(2,1)S(1)} %get-tuple-element.119.refs_0_.refs_3_), channel_id=1, source_target_pairs={{0,1},{1,0},{2,3},{3,2},{4,5},{5,4},{6,7},{7,6},{8,9},{9,8},{10,11... | collective-permute-start | bytes 2396168 | tf_op jit(solution)/shard_map/ppermute | solution.py:324
  58.5 14.1 %collective-permute-start.20 = (bf16[20,1280]{1,0:T(8,128)(2,1)S(1)}, bf16[20,1280]{1,0:T(8,128)(2,1)S(1)}, u32[]{:S(2)}, u32[]{:S(2)}) collective-permute-start(bf16[20,1280]{1,0:T(8,128)(2,1)S(1)} %get-tuple-element.125), channel_id=1, source_target_pairs={{0,2},{2,0},{4,6},{6,4},{1,3},{3,1},{5,7},{7,5},{8,10},{10,8},{12,... | collective-permute-start | bytes 153608 | tf_op jit(solution)/shard_map/ppermute | solution.py:324
  59.8 12.8 %collective-permute-start.21 = (bf16[20,1280]{1,0:T(8,128)(2,1)S(1)}, bf16[20,1280]{1,0:T(8,128)(2,1)S(1)}, u32[]{:S(2)}, u32[]{:S(2)}) collective-permute-start(bf16[20,1280]{1,0:T(8,128)(2,1)S(1)} %get-tuple-element.126), channel_id=1, source_target_pairs={{0,4},{2,6},{4,0},{6,2},{1,5},{3,7},{5,1},{7,3},{8,12},{10,14},{12... | collective-permute-start | bytes 153608 | tf_op jit(solution)/shard_map/ppermute | solution.py:324
  62.8 9.9 %collective-permute-start.22 = (bf16[20,1280]{1,0:T(8,128)(2,1)S(1)}, bf16[20,1280]{1,0:T(8,128)(2,1)S(1)}, u32[]{:S(2)}, u32[]{:S(2)}) collective-permute-start(bf16[20,1280]{1,0:T(8,128)(2,1)S(1)} %get-tuple-element.127), channel_id=1, source_target_pairs={{0,6},{2,4},{4,2},{6,0},{1,7},{3,5},{5,3},{7,1},{8,14},{10,12},{12... | collective-permute-start | bytes 153608 | tf_op jit(solution)/shard_map/ppermute | solution.py:324

commit v5 on v4

--- a/solution.py
+++ b/solution.py
@@ -41,7 +41,17 @@
     def __init__(self):
         self.token = ()
 
-    def call(self, kernel, args, out_shape, in_specs=None, out_specs=None, scratch=(), limit=4):
+    def call(
+        self,
+        kernel,
+        args,
+        out_shape,
+        in_specs=None,
+        out_specs=None,
+        scratch=(),
+        aliases=None,
+        limit=4,
+    ):
         count, outs, tokens = len(args), len(out_shape), len(self.token)
 
         def body(*refs):
@@ -55,38 +65,42 @@
             out_specs=(out_specs or [IN_VMEM] * outs) + [IN_VMEM],
             out_shape=[*out_shape, shaped(8, LANES, F32)],
             scratch_shapes=list(scratch),
+            input_output_aliases=aliases or {},
             cost_estimate=pl.CostEstimate(flops=1, bytes_accessed=1, transcendentals=0),
             compiler_params=pltpu.CompilerParams(vmem_limit_bytes=limit * MIB),
+            name=getattr(kernel, "func", kernel).__name__,
         )(*args, *self.token)
         self.token = (token,)
         return results
 
 
-def load_kernel(*refs):
-    count = len(refs) // 2
-    sems = refs[-1]
+def copy_rows(sems, source, target, begin=0):
+    rows = target.shape[0] // CUTS
     copies = []
     for cut in range(CUTS):
-        for at, (source, target) in enumerate(zip(refs[:count], refs[count:-1])):
-            rows = source.shape[0] // CUTS
-            part = pl.ds(cut * rows, rows)
-            copies.append(
-                pltpu.make_async_copy(source.at[part], target.at[part], sems.at[at, cut])
-            )
-    for copy in copies:
-        copy.start()
+        there, here = pl.ds(begin + cut * rows, rows), pl.ds(cut * rows, rows)
+        copies.append(pltpu.make_async_copy(source.at[there], target.at[here], sems.at[cut]))
+        copies[-1].start()
+    return copies
+
+
+def load_kernel(gate_ref, up_ref, down_ref, gate_out, up_out, down_out, sems):
+    copies = copy_rows(sems.at[0], gate_ref, gate_out)
+    copies += copy_rows(sems.at[1], up_ref, up_out)
+    copies += copy_rows(sems.at[2], down_ref, down_out)
     for copy in copies:
         copy.wait()
 
 
-def load(line, *weights):
+def load(line, gate_weight, up_weight, down_weight, rows):
+    shapes = [gate_weight.shape, up_weight.shape, (rows, down_weight.shape[1])]
     return line.call(
         load_kernel,
-        weights,
-        [pltpu.VMEM(weight.shape, BF16) for weight in weights],
-        in_specs=[IN_HBM] * len(weights),
-        scratch=[pltpu.SemaphoreType.DMA((len(weights), CUTS))],
-        limit=34,
+        (gate_weight, up_weight, down_weight),
+        [pltpu.VMEM(shape, BF16) for shape in shapes],
+        in_specs=[IN_HBM] * 3,
+        scratch=[pltpu.SemaphoreType.DMA((3, CUTS))],
+        limit=30,
     )
 
 
@@ -112,15 +126,24 @@
     return line.call(order_kernel, pieces, [shaped(4 * rows, width)])[0]
 
 
-def forward_kernel(begin, near, far, xy_ref, gate_ref, up_ref, down_ref, *refs):
-    keep_ref, send_ref = refs
+def forward_kernel(begin, down_begin, near, far, later, *refs):
+    xy_ref, gate_ref, up_ref, down_ref, *refs = refs
+    copies = []
+    if later is not None:
+        all_ref, keep_ref, send_ref, later_ref, sems = refs
+        copies = copy_rows(sems, all_ref, later_ref, later)
+    else:
+        keep_ref, send_ref = refs
+    columns = keep_ref.shape[1]
     group = xy_ref.shape[0] // 2
     rows = group // 4
     x, y = xy_ref[:group], xy_ref[group:]
-    there = pl.ds(begin, keep_ref.shape[1])
+    there = pl.ds(begin, columns)
     gate = jnp.dot(x, gate_ref[:, there], preferred_element_type=F32)
     up = jnp.dot(x, up_ref[:, there], preferred_element_type=F32)
-    dh = lax.dot_general(y, down_ref[there], NT, preferred_element_type=F32)
+    dh = lax.dot_general(
+        y, down_ref[pl.ds(down_begin, columns)], NT, preferred_element_type=F32
+    )
 
     def slots(*which):
         cuts = [slice(slot * rows, (slot + 1) * rows) for slot in which]
@@ -128,14 +151,27 @@
 
     keep_ref[...] = slots(0, far)
     send_ref[...] = slots(near, near ^ far).astype(BF16)
-
-
-def forward(line, begin, columns, axes, xy, gate_weight, up_weight, down_weight):
+    for copy in copies:
+        copy.wait()
+
+
+def forward(line, begin, columns, axes, xy, gate, up, down, down_begin, rest=None):
     rows = 6 * (xy.shape[0] // 8)
-    return line.call(
-        functools.partial(forward_kernel, begin, *axes),
-        (xy, gate_weight, up_weight, down_weight),
-        [shaped(rows, columns, F32), shaped(rows, columns)],
+    args, specs = [xy, gate, up, down], [IN_VMEM] * 4
+    shapes = [shaped(rows, columns, F32), shaped(rows, columns)]
+    later = None
+    if rest is not None:
+        weight, later = rest
+        args.append(weight)
+        specs.append(IN_HBM)
+        shapes.append(pltpu.VMEM((weight.shape[0] - later, weight.shape[1]), BF16))
+    return line.call(
+        functools.partial(forward_kernel, begin, down_begin, *axes, later),
+        args,
+        shapes,
+        in_specs=specs,
+        scratch=[pltpu.SemaphoreType.DMA((CUTS,))] if rest is not None else [],
+        limit=25 if rest is not None else 4,
     )
 
 
@@ -334,15 +370,22 @@
 
     both = jnp.concatenate([tokens, cotangent], axis=0)
     pieces = [both] + [swap(both, "ha", n_ha, step) for step in range(1, n_ha)]
-    gate_weight, up_weight, down_weight = load(Line(), gate_weight, up_weight, down_weight)
+    half = chunks[CHUNKS // 2][0]
+    gate, up, down = load(Line(), gate_weight, up_weight, down_weight, half)
     xy = order_rows(line, pieces)
     xy_other = swap(xy, "row", n_row, 1)
 
     kept, got = [], []
-    for (begin, columns), axis in zip(chunks, axes):
-        keep, send = forward(
-            line, begin, columns, axis, xy, gate_weight, up_weight, down_weight
-        )
+    later = None
+    for at, ((begin, columns), axis) in enumerate(zip(chunks, axes)):
+        if at == 0:
+            keep, send, later = forward(
+                line, begin, columns, axis, xy, gate, up, down, begin, (down_weight, half)
+            )
+        elif begin < half:
+            keep, send = forward(line, begin, columns, axis, xy, gate, up, down, begin)
+        else:
+            keep, send = forward(line, begin, columns, axis, xy, gate, up, later, begin - half)
         kept.append(keep)
         got.append(swap(send, "wa", n_wa, axis[0]))
     for at, (_, far) in enumerate(axes):
@@ -362,7 +405,7 @@
         pair = slice(at, at + 2)
         mine.append(stack(line, axes[pair], list(zip(kept, got))[pair]))
         other.append(swap(mine[-1], "row", n_row, 1))
-        grad = input_grad(line, chunks[at][0], mine[-1], gate_weight, up_weight, grad)
+        grad = input_grad(line, chunks[at][0], mine[-1], gate, up, grad)
     own, *sends = last_pieces(line, n_ha, grad[0])
     received = [swap(sent, "ha", n_ha, k + 1) for k, sent in enumerate(sends)]
     grads = weight_grad(line, xt, y_all, mine, other)
@@ -408,6 +451,7 @@
             and width % LANES == 0
             and hidden_width % LANES == 0
             and hidden_width >= LANES * CHUNKS
+            and width % (16 * CUTS) == 0
             and (tokens.shape[0] * n_ha) % 16 == 0
         )
         if fits:

time: 73.5 us -> 73.1 us (level)
  transfers between devices with their start and end apart: 25 -> 25, of which waited for: 11 -> 11; matrix products, arithmetic and copies ran while one was open for 0% -> 0% of each run, Pallas kernels for 41% -> 40%
where the time goes in v5:
time: 73.1 us; the launch traced here: 72.9 us
  Pallas kernels  32.1 us (44%)
  starting transfers between devices  27.2 us (37%)
  waiting for transfers between devices  11.9 us (16%)
  other arithmetic  0.88 us (1%)
  between operations  0.84 us (1%)
    pallas_call x26, Pallas kernels, call(): pl.pallas_call(body, in_specs=(in_specs or [IN_VMEM] * count) + [IN_VMEM]...  32.1 us
    ppermute x25, starting transfers between devices, swap(): return lax.ppermute(value, axis, [(at, at ^ step) for at in range(size)])  27.2 us
    ppermute x25, waiting for transfers between devices, swap(): return lax.ppermute(value, axis, [(at, at ^ step) for at in range(size)])  11.9 us
  transfers between devices with their start and end apart: 25, of which 11 were waited for; matrix products, arithmetic and copies ran while one was open for 0% of the time, Pallas kernels for 40%

profile of v5, /device:TPU:0, one launch (start us, length us, event | category | flops | bytes accessed | tf_op | source)
XLA Modules:
  0.0 72.9 jit_solution(7484206462159682035)
XLA Ops:
  0.6 0.9 %pad_maximum_fusion.refs_0_ = bf16[40,1280]{1,0:T(8,128)(2,1)S(1)} fusion(bf16[20,1280]{1,0:T(8,128)(2,1)} %param.6, bf16[20,1280]{1,0:T(8,128)(2,1)} %param.5), kind=kLoop, calls=%fused_computation | loop fusion | flops 204800 | bytes 204800 | tf_op jit(solution)/shard_map/concatenate | solution.py:371
  1.5 5.1 %collective-permute-start.2 = (bf16[40,1280]{1,0:T(8,128)(2,1)S(1)}, bf16[40,1280]{1,0:T(8,128)(2,1)S(1)}, u32[]{:S(2)}, u32[]{:S(2)}) collective-permute-start(bf16[40,1280]{1,0:T(8,128)(2,1)S(1)} %pad_maximum_fusion.refs_0_), channel_id=1, source_target_pairs={{0,6},{2,4},{4,2},{6,0},{1,7},{3,5},{5,3},{7,1},{8,14},{10,12},{12... | collective-permute-start | bytes 307208 | tf_op jit(solution)/shard_map/ppermute | solution.py:360
  6.6 0.0 collective-permute-start.1
  6.6 0.6 collective-permute-start
  7.3 8.0 %load_kernel.1 = (bf16[1280,3456]{1,0:T(8,128)(2,1)S(1)}, bf16[1280,3456]{1,0:T(8,128)(2,1)S(1)}, bf16[1792,1280]{1,0:T(8,128)(2,1)S(1)}, f32[8,128]{1,0:T(8,128)}) custom-call(bf16[1280,3456]{1,0:T(8,128)(2,1)} %refs_0_.1, bf16[1280,3456]{1,0:T(8,128)(2,1)} %refs_1_.1, bf16[3456,1280]{1,0:T(8,128)(2,1)} %refs_4_.1), custom_call_target="tpu_custom_call" | custom-call | flops 1 | bytes 1 | tf_op jit(solution)/shard_map/load_kernel/pallas_call | solution.py:62
  15.3 0.0 collective-permute-done.1.refs_2_
  15.3 0.0 collective-permute-done.refs_1_
  15.4 0.2 order_kernel.1
  15.5 2.4 %forward_kernel.4 = (f32[120,896]{1,0:T(8,128)S(1)}, bf16[120,896]{1,0:T(8,128)(2,1)S(1)}, bf16[1664,1280]{1,0:T(8,128)(2,1)S(1)}, f32[8,128]{1,0:T(8,128)S(1)}) custom-call(bf16[160,1280]{1,0:T(8,128)(2,1)S(1)} %get-tuple-element.71.refs_0_, bf16[1280,3456]{1,0:T(8,128)(2,1)S(1)} %get-tuple-element.72.refs_1_, ...), custom_call_target="tpu_custom_call" | custom-call | flops 1 | bytes 1 | tf_op jit(solution)/shard_map/forward_kernel/pallas_call | solution.py:62
  17.9 1.7 %collective-permute-start.5 = (bf16[120,896]{1,0:T(8,128)(2,1)S(1)}, bf16[120,896]{1,0:T(8,128)(2,1)S(1)}, u32[]{:S(2)}, u32[]{:S(2)}) collective-permute-start(bf16[120,896]{1,0:T(8,128)(2,1)S(1)} %get-tuple-element.84), channel_id=1, source_target_pairs={{0,8},{8,0},{16,24},{24,16},{1,9},{9,1},{17,25},{25,17},{2,10},{10... | collective-permute-start | bytes 645128 | tf_op jit(solution)/shard_map/ppermute | solution.py:360
  19.6 1.5 %forward_kernel.5 = (f32[120,896]{1,0:T(8,128)S(1)}, bf16[120,896]{1,0:T(8,128)(2,1)S(1)}, f32[8,128]{1,0:T(8,128)S(1)}) custom-call(bf16[160,1280]{1,0:T(8,128)(2,1)S(1)} %get-tuple-element.71.refs_0_, bf16[1280,3456]{1,0:T(8,128)(2,1)S(1)} %get-tuple-element.72.refs_1_, bf16[1280,3456]{1,0:T(8,128)(2,1)S(1)} %get-tuple-element.73.refs_2_, ...), custom_call_target="tpu_custom_call" | custom-call | flops 1 | bytes 1 | tf_op jit(solution)/shard_map/forward_kernel/pallas_call | solution.py:62
  21.1 1.6 %collective-permute-start.4 = (bf16[120,896]{1,0:T(8,128)(2,1)S(1)}, bf16[120,896]{1,0:T(8,128)(2,1)S(1)}, u32[]{:S(2)}, u32[]{:S(2)}) collective-permute-start(bf16[120,896]{1,0:T(8,128)(2,1)S(1)} %get-tuple-element.82), channel_id=1, source_target_pairs={{0,16},{8,24},{16,0},{24,8},{1,17},{9,25},{17,1},{25,9},{2,18},{10... | collective-permute-start | bytes 645128 | tf_op jit(solution)/shard_map/ppermute | solution.py:360
  22.7 0.0 collective-permute-start.14
  22.7 1.5 %forward_kernel.6 = (f32[120,896]{1,0:T(8,128)S(1)}, bf16[120,896]{1,0:T(8,128)(2,1)S(1)}, f32[8,128]{1,0:T(8,128)S(1)}) custom-call(bf16[160,1280]{1,0:T(8,128)(2,1)S(1)} %get-tuple-element.71.refs_0_, bf16[1280,3456]{1,0:T(8,128)(2,1)S(1)} %get-tuple-element.72.refs_1_, bf16[1280,3456]{1,0:T(8,128)(2,1)S(1)} %get-tuple-element.73.refs_2_, ...), custom_call_target="tpu_custom_call" | custom-call | flops 1 | bytes 1 | tf_op jit(solution)/shard_map/forward_kernel/pallas_call | solution.py:62
  24.2 0.6 collective-permute-start.3
  24.8 1.4 %forward_kernel.7 = (f32[120,768]{1,0:T(8,128)S(1)}, bf16[120,768]{1,0:T(8,128)(2,1)S(1)}, f32[8,128]{1,0:T(8,128)S(1)}) custom-call(bf16[160,1280]{1,0:T(8,128)(2,1)S(1)} %get-tuple-element.71.refs_0_, bf16[1280,3456]{1,0:T(8,128)(2,1)S(1)} %get-tuple-element.72.refs_1_, bf16[1280,3456]{1,0:T(8,128)(2,1)S(1)} %get-tuple-element.73.refs_2_, ...), custom_call_target="tpu_custom_call" | custom-call | flops 1 | bytes 1 | tf_op jit(solution)/shard_map/forward_kernel/pallas_call | solution.py:62
  26.2 0.4 collective-permute-start.7
  26.6 0.1 halve_kernel.4
  26.7 0.5 collective-permute-done.4.refs_1_
  27.2 0.1 halve_kernel.5
  27.3 1.2 %collective-permute-start.10 = (bf16[60,896]{1,0:T(8,128)(2,1)S(1)}, bf16[60,896]{1,0:T(8,128)(2,1)S(1)}, u32[]{:S(2)}, u32[]{:S(2)}) collective-permute-start(bf16[60,896]{1,0:T(8,128)(2,1)S(1)} %get-tuple-element.99), channel_id=1, source_target_pairs={{0,8},{8,0},{16,24},{24,16},{1,9},{9,1},{17,25},{25,17},{2,10},{10... | collective-permute-start | bytes 322568 | tf_op jit(solution)/shard_map/ppermute | solution.py:360
  28.5 1.5 %collective-permute-start.9 = (bf16[60,896]{1,0:T(8,128)(2,1)S(1)}, bf16[60,896]{1,0:T(8,128)(2,1)S(1)}, u32[]{:S(2)}, u32[]{:S(2)}) collective-permute-start(bf16[60,896]{1,0:T(8,128)(2,1)S(1)} %get-tuple-element.97), channel_id=1, source_target_pairs={{0,16},{8,24},{16,0},{24,8},{1,17},{9,25},{17,1},{25,9},{2,18},{10... | collective-permute-start | bytes 322568 | tf_op jit(solution)/shard_map/ppermute | solution.py:360
  30.0 2.4 %collective-permute-done.3.refs_1_ = bf16[120,896]{1,0:T(8,128)(2,1)S(1)} collective-permute-done((bf16[120,896]{1,0:T(8,128)(2,1)S(1)}, bf16[120,896]{1,0:T(8,128)(2,1)S(1)}, u32[]{:S(2)}, u32[]{:S(2)}) %collective-permute-start.3) | collective-permute-done | bytes 215072 | tf_op jit(solution)/shard_map/ppermute | solution.py:360
  32.4 0.1 halve_kernel.6
  32.4 0.6 collective-permute-start.6
  33.0 0.7 collective-permute-done.7.refs_1_
  33.7 0.1 halve_kernel.7
  33.8 1.6 %collective-permute-start.8 = (bf16[60,768]{1,0:T(8,128)(2,1)S(1)}, bf16[60,768]{1,0:T(8,128)(2,1)S(1)}, u32[]{:S(2)}, u32[]{:S(2)}) collective-permute-start(bf16[60,768]{1,0:T(8,128)(2,1)S(1)} %get-tuple-element.95), channel_id=1, source_target_pairs={{0,8},{8,0},{16,24},{24,16},{1,9},{9,1},{17,25},{25,17},{2,10},{10... | collective-permute-start | bytes 276488 | tf_op jit(solution)/shard_map/ppermute | solution.py:360
  35.3 0.0 collective-permute-done.10.refs_1_
  35.3 0.1 middle_kernel.4
  35.4 0.8 %collective-permute-done.9.refs_1_ = bf16[60,896]{1,0:T(8,128)(2,1)S(1)} collective-permute-done((bf16[60,896]{1,0:T(8,128)(2,1)S(1)}, bf16[60,896]{1,0:T(8,128)(2,1)S(1)}, u32[]{:S(2)}, u32[]{:S(2)}) %collective-permute-start.9) | collective-permute-done | bytes 107552 | tf_op jit(solution)/shard_map/ppermute | solution.py:360
  36.2 0.1 middle_kernel.5
  36.3 1.6 %collective-permute-start.13 = (bf16[60,896]{1,0:T(8,128)(2,1)S(1)}, bf16[60,896]{1,0:T(8,128)(2,1)S(1)}, u32[]{:S(2)}, u32[]{:S(2)}) collective-permute-start(bf16[60,896]{1,0:T(8,128)(2,1)S(1)} %get-tuple-element.106.refs_0_), channel_id=1, source_target_pairs={{0,8},{8,0},{16,24},{24,16},{1,9},{9,1},{17,25},{25,17},{2,10},{10... | collective-permute-start | bytes 322568 | tf_op jit(solution)/shard_map/ppermute | solution.py:360
  37.8 0.5 collective-permute-start.12
  38.3 1.0 %collective-permute-done.8.refs_1_ = bf16[60,768]{1,0:T(8,128)(2,1)S(1)} collective-permute-done((bf16[60,768]{1,0:T(8,128)(2,1)S(1)}, bf16[60,768]{1,0:T(8,128)(2,1)S(1)}, u32[]{:S(2)}, u32[]{:S(2)}) %collective-permute-start.8) | collective-permute-done | bytes 92192 | tf_op jit(solution)/shard_map/ppermute | solution.py:360
  39.3 0.1 middle_kernel.6
  39.4 0.1 middle_kernel.7
  39.5 1.6 %collective-permute-start.11 = (bf16[60,896]{1,0:T(8,128)(2,1)S(1)}, bf16[60,896]{1,0:T(8,128)(2,1)S(1)}, u32[]{:S(2)}, u32[]{:S(2)}) collective-permute-start(bf16[60,896]{1,0:T(8,128)(2,1)S(1)} %get-tuple-element.104.refs_0_), channel_id=1, source_target_pairs={{0,8},{8,0},{16,24},{24,16},{1,9},{9,1},{17,25},{25,17},{2,10},{10... | collective-permute-start | bytes 322568 | tf_op jit(solution)/shard_map/ppermute | solution.py:360
  41.0 0.5 collective-permute-start.16
  41.5 0.0 collective-permute-done.14.refs_1_
  41.5 0.3 factors_kernel.1
  41.8 0.4 collective-permute-done.13.refs_1_
  42.2 1.4 %collective-permute-done.12.refs_1_ = bf16[60,896]{1,0:T(8,128)(2,1)S(1)} collective-permute-done((bf16[60,896]{1,0:T(8,128)(2,1)S(1)}, bf16[60,896]{1,0:T(8,128)(2,1)S(1)}, u32[]{:S(2)}, u32[]{:S(2)}) %collective-permute-start.12) | collective-permute-done | bytes 107552 | tf_op jit(solution)/shard_map/ppermute | solution.py:360
  43.6 0.6 collective-permute-start.19
  44.2 0.3 collective-permute-start.18
  44.6 1.0 %collective-permute-done.11.refs_1_ = bf16[60,896]{1,0:T(8,128)(2,1)S(1)} collective-permute-done((bf16[60,896]{1,0:T(8,128)(2,1)S(1)}, bf16[60,896]{1,0:T(8,128)(2,1)S(1)}, u32[]{:S(2)}, u32[]{:S(2)}) %collective-permute-start.11) | collective-permute-done | bytes 107552 | tf_op jit(solution)/shard_map/ppermute | solution.py:360
  45.6 1.0 %collective-permute-start.15 = (bf16[120,896]{1,0:T(8,128)(2,1)S(1)}, bf16[120,896]{1,0:T(8,128)(2,1)S(1)}, u32[]{:S(2)}, u32[]{:S(2)}) collective-permute-start(bf16[120,896]{1,0:T(8,128)(2,1)S(1)} %get-tuple-element.111.refs_0_), channel_id=1, source_target_pairs={{0,16},{8,24},{16,0},{24,8},{1,17},{9,25},{17,1},{25,9},{2,18},{10... | collective-permute-start | bytes 645128 | tf_op jit(solution)/shard_map/ppermute | solution.py:360
  46.6 0.1 collective-permute-done.16.refs_1_
  46.7 1.3 %collective-permute-start.17 = (bf16[120,768]{1,0:T(8,128)(2,1)S(1)}, bf16[120,768]{1,0:T(8,128)(2,1)S(1)}, u32[]{:S(2)}, u32[]{:S(2)}) collective-permute-start(bf16[120,768]{1,0:T(8,128)(2,1)S(1)} %get-tuple-element.114.refs_2_), channel_id=1, source_target_pairs={{0,8},{8,0},{16,24},{24,16},{1,9},{9,1},{17,25},{25,17},{2,10},{10... | collective-permute-start | bytes 552968 | tf_op jit(solution)/shard_map/ppermute | solution.py:360
  48.0 2.7 %collective-permute-done.19.refs_3_ = bf16[120,896]{1,0:T(8,128)(2,1)S(1)} collective-permute-done((bf16[120,896]{1,0:T(8,128)(2,1)S(1)}, bf16[120,896]{1,0:T(8,128)(2,1)S(1)}, u32[]{:S(2)}, u32[]{:S(2)}) %collective-permute-start.19) | collective-permute-done | bytes 215072 | tf_op jit(solution)/shard_map/ppermute | solution.py:360
  50.7 0.8 %collective-permute-done.18.refs_1_ = bf16[120,896]{1,0:T(8,128)(2,1)S(1)} collective-permute-done((bf16[120,896]{1,0:T(8,128)(2,1)S(1)}, bf16[120,896]{1,0:T(8,128)(2,1)S(1)}, u32[]{:S(2)}, u32[]{:S(2)}) %collective-permute-start.18) | collective-permute-done | bytes 215072 | tf_op jit(solution)/shard_map/ppermute | solution.py:360
  51.5 0.1 stack_kernel.2
  51.7 0.1 collective-permute-start.23
  51.7 2.9 %input_grad_kernel.2 = (f32[80,1280]{1,0:T(8,128)S(1)}, f32[8,128]{1,0:T(8,128)S(1)}) custom-call(bf16[240,1792]{1,0:T(8,128)(2,1)S(1)} %get-tuple-element.118.refs_0_.refs_2_, bf16[1280,3456]{1,0:T(8,128)(2,1)S(1)} %get-tuple-element.72.refs_1_, bf16[1280,3456]{1,0:T(8,128)(2,1)S(1)} %get-tuple-element.73.refs_2_, f32[8,128]{1,0:T(8,128)S(1)} %get-tuple-element.119.refs_3_), custom_call_target="tpu_custom_call" | custom-call | flops 1 | bytes 1 | tf_op jit(solution)/shard_map/input_grad_kernel/pallas_call | solution.py:62
  54.6 0.0 collective-permute-done.17.refs_3_
  54.6 0.1 stack_kernel.3
  54.7 0.6 collective-permute-start.24
  55.3 2.7 %input_grad_kernel.3 = (f32[80,1280]{1,0:T(8,128)S(1)}, f32[8,128]{1,0:T(8,128)S(1)}) custom-call(bf16[240,1664]{1,0:T(8,128)(2,1)S(1)} %get-tuple-element.121.refs_0_.refs_3_, bf16[1280,3456]{1,0:T(8,128)(2,1)S(1)} %get-tuple-element.72.refs_1_, bf16[1280,3456]{1,0:T(8,128)(2,1)S(1)} %get-tuple-element.73.refs_2_, ...), custom_call_target="tpu_custom_call" | custom-call | flops 1 | bytes 1 | tf_op jit(solution)/shard_map/input_grad_kernel/pallas_call | solution.py:62
  58.0 0.2 last_kernel.1
  58.2 1.3 %collective-permute-start.20 = (bf16[20,1280]{1,0:T(8,128)(2,1)S(1)}, bf16[20,1280]{1,0:T(8,128)(2,1)S(1)}, u32[]{:S(2)}, u32[]{:S(2)}) collective-permute-start(bf16[20,1280]{1,0:T(8,128)(2,1)S(1)} %get-tuple-element.127), channel_id=1, source_target_pairs={{0,2},{2,0},{4,6},{6,4},{1,3},{3,1},{5,7},{7,5},{8,10},{10,8},{12,... | collective-permute-start | bytes 153608 | tf_op jit(solution)/shard_map/ppermute | solution.py:360
  59.5 2.9 %collective-permute-start.21 = (bf16[20,1280]{1,0:T(8,128)(2,1)S(1)}, bf16[20,1280]{1,0:T(8,128)(2,1)S(1)}, u32[]{:S(2)}, u32[]{:S(2)}) collective-permute-start(bf16[20,1280]{1,0:T(8,128)(2,1)S(1)} %get-tuple-element.128), channel_id=1, source_target_pairs={{0,4},{2,6},{4,0},{6,2},{1,5},{3,7},{5,1},{7,3},{8,12},{10,14},{12... | collective-permute-start | bytes 153608 | tf_op jit(solution)/shard_map/ppermute | solution.py:360
  62.4 0.2 collective-permute-start.22
  62.6 9.6 %weight_grad_kernel.1 = (bf16[1280,3456]{1,0:T(8,128)(2,1)}, bf16[1280,3456]{1,0:T(8,128)(2,1)}, bf16[3456,1280]{1,0:T(8,128)(2,1)}, f32[8,128]{1,0:T(8,128)S(1)}) custom-call(bf16[1280,160]{1,0:T(8,128)(2,1)S(1)} %get-tuple-element.130.refs_0_, bf16[160,1280]{1,0:T(8,128)(2,1)S(1)} %get-tuple-element.131.refs_1_, ...), custom_call_target="tpu_custom_call" | custom-call | flops 1 | bytes 1 | tf_op jit(solution)/shard_map/weight_grad_kernel/pallas_call | solution.py:62
  72.3 0.7 total_kernel.1
  (13 shorter events, 0.2 us)
Async XLA Ops:
  1.5 13.8 %collective-permute-start.2 = (bf16[40,1280]{1,0:T(8,128)(2,1)S(1)}, bf16[40,1280]{1,0:T(8,128)(2,1)S(1)}, u32[]{:S(2)}, u32[]{:S(2)}) collective-permute-start(bf16[40,1280]{1,0:T(8,128)(2,1)S(1)} %pad_maximum_fusion.refs_0_), channel_id=1, source_target_pairs={{0,6},{2,4},{4,2},{6,0},{1,7},{3,5},{5,3},{7,1},{8,14},{10,12},{12... | collective-permute-start | bytes 307208 | tf_op jit(solution)/shard_map/ppermute | solution.py:360
  6.6 8.7 %collective-permute-start.1 = (bf16[40,1280]{1,0:T(8,128)(2,1)S(1)}, bf16[40,1280]{1,0:T(8,128)(2,1)S(1)}, u32[]{:S(2)}, u32[]{:S(2)}) collective-permute-start(bf16[40,1280]{1,0:T(8,128)(2,1)S(1)} %pad_maximum_fusion.refs_0_), channel_id=1, source_target_pairs={{0,4},{2,6},{4,0},{6,2},{1,5},{3,7},{5,1},{7,3},{8,12},{10,14},{12... | collective-permute-start | bytes 307208 | tf_op jit(solution)/shard_map/ppermute | solution.py:360
  6.6 8.7 %collective-permute-start = (bf16[40,1280]{1,0:T(8,128)(2,1)S(1)}, bf16[40,1280]{1,0:T(8,128)(2,1)S(1)}, u32[]{:S(2)}, u32[]{:S(2)}) collective-permute-start(bf16[40,1280]{1,0:T(8,128)(2,1)S(1)} %pad_maximum_fusion.refs_0_), channel_id=1, source_target_pairs={{0,2},{2,0},{4,6},{6,4},{1,3},{3,1},{5,7},{7,5},{8,10},{10,8},{12,... | collective-permute-start | bytes 307208 | tf_op jit(solution)/shard_map/ppermute | solution.py:360
  17.9 8.7 %collective-permute-start.5 = (bf16[120,896]{1,0:T(8,128)(2,1)S(1)}, bf16[120,896]{1,0:T(8,128)(2,1)S(1)}, u32[]{:S(2)}, u32[]{:S(2)}) collective-permute-start(bf16[120,896]{1,0:T(8,128)(2,1)S(1)} %get-tuple-element.84), channel_id=1, source_target_pairs={{0,8},{8,0},{16,24},{24,16},{1,9},{9,1},{17,25},{25,17},{2,10},{10... | collective-permute-start | bytes 645128 | tf_op jit(solution)/shard_map/ppermute | solution.py:360
  21.1 6.1 %collective-permute-start.4 = (bf16[120,896]{1,0:T(8,128)(2,1)S(1)}, bf16[120,896]{1,0:T(8,128)(2,1)S(1)}, u32[]{:S(2)}, u32[]{:S(2)}) collective-permute-start(bf16[120,896]{1,0:T(8,128)(2,1)S(1)} %get-tuple-element.82), channel_id=1, source_target_pairs={{0,16},{8,24},{16,0},{24,8},{1,17},{9,25},{17,1},{25,9},{2,18},{10... | collective-permute-start | bytes 645128 | tf_op jit(solution)/shard_map/ppermute | solution.py:360
  22.7 18.8 %collective-permute-start.14 = (bf16[160,1280]{1,0:T(8,128)(2,1)S(1)}, bf16[160,1280]{1,0:T(8,128)(2,1)S(1)}, u32[]{:S(2)}, u32[]{:S(2)}) collective-permute-start(bf16[160,1280]{1,0:T(8,128)(2,1)S(1)} %get-tuple-element.71.refs_0_), channel_id=1, source_target_pairs={{0,1},{1,0},{2,3},{3,2},{4,5},{5,4},{6,7},{7,6},{8,9},{9,8},{10,11... | collective-permute-start | bytes 1228808 | tf_op jit(solution)/shard_map/ppermute | solution.py:360
  24.2 8.2 %collective-permute-start.3 = (bf16[120,896]{1,0:T(8,128)(2,1)S(1)}, bf16[120,896]{1,0:T(8,128)(2,1)S(1)}, u32[]{:S(2)}, u32[]{:S(2)}) collective-permute-start(bf16[120,896]{1,0:T(8,128)(2,1)S(1)} %get-tuple-element.80), channel_id=1, source_target_pairs={{0,8},{8,0},{16,24},{24,16},{1,9},{9,1},{17,25},{25,17},{2,10},{10... | collective-permute-start | bytes 645128 | tf_op jit(solution)/shard_map/ppermute | solution.py:360
  26.2 7.5 %collective-permute-start.7 = (bf16[120,768]{1,0:T(8,128)(2,1)S(1)}, bf16[120,768]{1,0:T(8,128)(2,1)S(1)}, u32[]{:S(2)}, u32[]{:S(2)}) collective-permute-start(bf16[120,768]{1,0:T(8,128)(2,1)S(1)} %get-tuple-element.92), channel_id=1, source_target_pairs={{0,16},{8,24},{16,0},{24,8},{1,17},{9,25},{17,1},{25,9},{2,18},{10... | collective-permute-start | bytes 552968 | tf_op jit(solution)/shard_map/ppermute | solution.py:360
  27.3 8.0 %collective-permute-start.10 = (bf16[60,896]{1,0:T(8,128)(2,1)S(1)}, bf16[60,896]{1,0:T(8,128)(2,1)S(1)}, u32[]{:S(2)}, u32[]{:S(2)}) collective-permute-start(bf16[60,896]{1,0:T(8,128)(2,1)S(1)} %get-tuple-element.99), channel_id=1, source_target_pairs={{0,8},{8,0},{16,24},{24,16},{1,9},{9,1},{17,25},{25,17},{2,10},{10... | collective-permute-start | bytes 322568 | tf_op jit(solution)/shard_map/ppermute | solution.py:360
  28.5 7.7 %collective-permute-start.9 = (bf16[60,896]{1,0:T(8,128)(2,1)S(1)}, bf16[60,896]{1,0:T(8,128)(2,1)S(1)}, u32[]{:S(2)}, u32[]{:S(2)}) collective-permute-start(bf16[60,896]{1,0:T(8,128)(2,1)S(1)} %get-tuple-element.97), channel_id=1, source_target_pairs={{0,16},{8,24},{16,0},{24,8},{1,17},{9,25},{17,1},{25,9},{2,18},{10... | collective-permute-start | bytes 322568 | tf_op jit(solution)/shard_map/ppermute | solution.py:360
  32.4 6.9 %collective-permute-start.6 = (bf16[60,896]{1,0:T(8,128)(2,1)S(1)}, bf16[60,896]{1,0:T(8,128)(2,1)S(1)}, u32[]{:S(2)}, u32[]{:S(2)}) collective-permute-start(bf16[60,896]{1,0:T(8,128)(2,1)S(1)} %get-tuple-element.90), channel_id=1, source_target_pairs={{0,16},{8,24},{16,0},{24,8},{1,17},{9,25},{17,1},{25,9},{2,18},{10... | collective-permute-start | bytes 322568 | tf_op jit(solution)/shard_map/ppermute | solution.py:360
  33.8 5.5 %collective-permute-start.8 = (bf16[60,768]{1,0:T(8,128)(2,1)S(1)}, bf16[60,768]{1,0:T(8,128)(2,1)S(1)}, u32[]{:S(2)}, u32[]{:S(2)}) collective-permute-start(bf16[60,768]{1,0:T(8,128)(2,1)S(1)} %get-tuple-element.95), channel_id=1, source_target_pairs={{0,8},{8,0},{16,24},{24,16},{1,9},{9,1},{17,25},{25,17},{2,10},{10... | collective-permute-start | bytes 276488 | tf_op jit(solution)/shard_map/ppermute | solution.py:360
  36.3 5.9 %collective-permute-start.13 = (bf16[60,896]{1,0:T(8,128)(2,1)S(1)}, bf16[60,896]{1,0:T(8,128)(2,1)S(1)}, u32[]{:S(2)}, u32[]{:S(2)}) collective-permute-start(bf16[60,896]{1,0:T(8,128)(2,1)S(1)} %get-tuple-element.106.refs_0_), channel_id=1, source_target_pairs={{0,8},{8,0},{16,24},{24,16},{1,9},{9,1},{17,25},{25,17},{2,10},{10... | collective-permute-start | bytes 322568 | tf_op jit(solution)/shard_map/ppermute | solution.py:360
  37.8 5.8 %collective-permute-start.12 = (bf16[60,896]{1,0:T(8,128)(2,1)S(1)}, bf16[60,896]{1,0:T(8,128)(2,1)S(1)}, u32[]{:S(2)}, u32[]{:S(2)}) collective-permute-start(bf16[60,896]{1,0:T(8,128)(2,1)S(1)} %get-tuple-element.105.refs_0_), channel_id=1, source_target_pairs={{0,16},{8,24},{16,0},{24,8},{1,17},{9,25},{17,1},{25,9},{2,18},{10... | collective-permute-start | bytes 322568 | tf_op jit(solution)/shard_map/ppermute | solution.py:360
  39.5 6.1 %collective-permute-start.11 = (bf16[60,896]{1,0:T(8,128)(2,1)S(1)}, bf16[60,896]{1,0:T(8,128)(2,1)S(1)}, u32[]{:S(2)}, u32[]{:S(2)}) collective-permute-start(bf16[60,896]{1,0:T(8,128)(2,1)S(1)} %get-tuple-element.104.refs_0_), channel_id=1, source_target_pairs={{0,8},{8,0},{16,24},{24,16},{1,9},{9,1},{17,25},{25,17},{2,10},{10... | collective-permute-start | bytes 322568 | tf_op jit(solution)/shard_map/ppermute | solution.py:360
  41.0 5.7 %collective-permute-start.16 = (bf16[60,768]{1,0:T(8,128)(2,1)S(1)}, bf16[60,768]{1,0:T(8,128)(2,1)S(1)}, u32[]{:S(2)}, u32[]{:S(2)}) collective-permute-start(bf16[60,768]{1,0:T(8,128)(2,1)S(1)} %get-tuple-element.112.refs_0_), channel_id=1, source_target_pairs={{0,16},{8,24},{16,0},{24,8},{1,17},{9,25},{17,1},{25,9},{2,18},{10... | collective-permute-start | bytes 276488 | tf_op jit(solution)/shard_map/ppermute | solution.py:360
  43.6 7.1 %collective-permute-start.19 = (bf16[120,896]{1,0:T(8,128)(2,1)S(1)}, bf16[120,896]{1,0:T(8,128)(2,1)S(1)}, u32[]{:S(2)}, u32[]{:S(2)}) collective-permute-start(bf16[120,896]{1,0:T(8,128)(2,1)S(1)} %get-tuple-element.116.refs_2_), channel_id=1, source_target_pairs={{0,8},{8,0},{16,24},{24,16},{1,9},{9,1},{17,25},{25,17},{2,10},{10... | collective-permute-start | bytes 645128 | tf_op jit(solution)/shard_map/ppermute | solution.py:360
  44.2 7.3 %collective-permute-start.18 = (bf16[120,896]{1,0:T(8,128)(2,1)S(1)}, bf16[120,896]{1,0:T(8,128)(2,1)S(1)}, u32[]{:S(2)}, u32[]{:S(2)}) collective-permute-start(bf16[120,896]{1,0:T(8,128)(2,1)S(1)} %get-tuple-element.115.refs_0_), channel_id=1, source_target_pairs={{0,16},{8,24},{16,0},{24,8},{1,17},{9,25},{17,1},{25,9},{2,18},{10... | collective-permute-start | bytes 645128 | tf_op jit(solution)/shard_map/ppermute | solution.py:360
  45.6 9.0 %collective-permute-start.15 = (bf16[120,896]{1,0:T(8,128)(2,1)S(1)}, bf16[120,896]{1,0:T(8,128)(2,1)S(1)}, u32[]{:S(2)}, u32[]{:S(2)}) collective-permute-start(bf16[120,896]{1,0:T(8,128)(2,1)S(1)} %get-tuple-element.111.refs_0_), channel_id=1, source_target_pairs={{0,16},{8,24},{16,0},{24,8},{1,17},{9,25},{17,1},{25,9},{2,18},{10... | collective-permute-start | bytes 645128 | tf_op jit(solution)/shard_map/ppermute | solution.py:360
  46.7 7.9 %collective-permute-start.17 = (bf16[120,768]{1,0:T(8,128)(2,1)S(1)}, bf16[120,768]{1,0:T(8,128)(2,1)S(1)}, u32[]{:S(2)}, u32[]{:S(2)}) collective-permute-start(bf16[120,768]{1,0:T(8,128)(2,1)S(1)} %get-tuple-element.114.refs_2_), channel_id=1, source_target_pairs={{0,8},{8,0},{16,24},{24,16},{1,9},{9,1},{17,25},{25,17},{2,10},{10... | collective-permute-start | bytes 552968 | tf_op jit(solution)/shard_map/ppermute | solution.py:360
  51.7 10.9 %collective-permute-start.23 = (bf16[240,1792]{1,0:T(8,128)(2,1)S(1)}, bf16[240,1792]{1,0:T(8,128)(2,1)S(1)}, u32[]{:S(2)}, u32[]{:S(2)}) collective-permute-start(bf16[240,1792]{1,0:T(8,128)(2,1)S(1)} %get-tuple-element.118.refs_0_.refs_2_), channel_id=1, source_target_pairs={{0,1},{1,0},{2,3},{3,2},{4,5},{5,4},{6,7},{7,6},{8,9},{9,8},{10,11... | collective-permute-start | bytes 2580488 | tf_op jit(solution)/shard_map/ppermute | solution.py:360
  54.7 7.9 %collective-permute-start.24 = (bf16[240,1664]{1,0:T(8,128)(2,1)S(1)}, bf16[240,1664]{1,0:T(8,128)(2,1)S(1)}, u32[]{:S(2)}, u32[]{:S(2)}) collective-permute-start(bf16[240,1664]{1,0:T(8,128)(2,1)S(1)} %get-tuple-element.121.refs_0_.refs_3_), channel_id=1, source_target_pairs={{0,1},{1,0},{2,3},{3,2},{4,5},{5,4},{6,7},{7,6},{8,9},{9,8},{10,11... | collective-permute-start | bytes 2396168 | tf_op jit(solution)/shard_map/ppermute | solution.py:360
  58.2 14.1 %collective-permute-start.20 = (bf16[20,1280]{1,0:T(8,128)(2,1)S(1)}, bf16[20,1280]{1,0:T(8,128)(2,1)S(1)}, u32[]{:S(2)}, u32[]{:S(2)}) collective-permute-start(bf16[20,1280]{1,0:T(8,128)(2,1)S(1)} %get-tuple-element.127), channel_id=1, source_target_pairs={{0,2},{2,0},{4,6},{6,4},{1,3},{3,1},{5,7},{7,5},{8,10},{10,8},{12,... | collective-permute-start | bytes 153608 | tf_op jit(solution)/shard_map/ppermute | solution.py:360
  59.5 12.8 %collective-permute-start.21 = (bf16[20,1280]{1,0:T(8,128)(2,1)S(1)}, bf16[20,1280]{1,0:T(8,128)(2,1)S(1)}, u32[]{:S(2)}, u32[]{:S(2)}) collective-permute-start(bf16[20,1280]{1,0:T(8,128)(2,1)S(1)} %get-tuple-element.128), channel_id=1, source_target_pairs={{0,4},{2,6},{4,0},{6,2},{1,5},{3,7},{5,1},{7,3},{8,12},{10,14},{12... | collective-permute-start | bytes 153608 | tf_op jit(solution)/shard_map/ppermute | solution.py:360
  62.4 9.9 %collective-permute-start.22 = (bf16[20,1280]{1,0:T(8,128)(2,1)S(1)}, bf16[20,1280]{1,0:T(8,128)(2,1)S(1)}, u32[]{:S(2)}, u32[]{:S(2)}) collective-permute-start(bf16[20,1280]{1,0:T(8,128)(2,1)S(1)} %get-tuple-element.129), channel_id=1, source_target_pairs={{0,6},{2,4},{4,2},{6,0},{1,7},{3,5},{5,3},{7,1},{8,14},{10,12},{12... | collective-permute-start | bytes 153608 | tf_op jit(solution)/shard_map/ppermute | solution.py:360

commit v6 on v5

--- a/solution.py
+++ b/solution.py
@@ -126,7 +126,7 @@
     return line.call(order_kernel, pieces, [shaped(4 * rows, width)])[0]
 
 
-def forward_kernel(begin, down_begin, near, far, later, *refs):
+def forward_kernel(begin, near, far, later, *refs):
     xy_ref, gate_ref, up_ref, down_ref, *refs = refs
     copies = []
     if later is not None:
@@ -141,9 +141,7 @@
     there = pl.ds(begin, columns)
     gate = jnp.dot(x, gate_ref[:, there], preferred_element_type=F32)
     up = jnp.dot(x, up_ref[:, there], preferred_element_type=F32)
-    dh = lax.dot_general(
-        y, down_ref[pl.ds(down_begin, columns)], NT, preferred_element_type=F32
-    )
+    dh = lax.dot_general(y, down_ref[...], NT, preferred_element_type=F32)
 
     def slots(*which):
         cuts = [slice(slot * rows, (slot + 1) * rows) for slot in which]
@@ -155,18 +153,18 @@
         copy.wait()
 
 
-def forward(line, begin, columns, axes, xy, gate, up, down, down_begin, rest=None):
+def forward(line, begin, columns, axes, xy, gate, up, down, rest=None):
     rows = 6 * (xy.shape[0] // 8)
     args, specs = [xy, gate, up, down], [IN_VMEM] * 4
     shapes = [shaped(rows, columns, F32), shaped(rows, columns)]
     later = None
     if rest is not None:
-        weight, later = rest
+        weight, later, size = rest
         args.append(weight)
         specs.append(IN_HBM)
-        shapes.append(pltpu.VMEM((weight.shape[0] - later, weight.shape[1]), BF16))
-    return line.call(
-        functools.partial(forward_kernel, begin, down_begin, *axes, later),
+        shapes.append(pltpu.VMEM((size, weight.shape[1]), BF16))
+    return line.call(
+        functools.partial(forward_kernel, begin, *axes, later),
         args,
         shapes,
         in_specs=specs,
@@ -370,36 +368,32 @@
 
     both = jnp.concatenate([tokens, cotangent], axis=0)
     pieces = [both] + [swap(both, "ha", n_ha, step) for step in range(1, n_ha)]
-    half = chunks[CHUNKS // 2][0]
-    gate, up, down = load(Line(), gate_weight, up_weight, down_weight, half)
+    gate, up, down = load(Line(), gate_weight, up_weight, down_weight, chunks[0][1])
     xy = order_rows(line, pieces)
     xy_other = swap(xy, "row", n_row, 1)
 
     kept, got = [], []
-    later = None
     for at, ((begin, columns), axis) in enumerate(zip(chunks, axes)):
-        if at == 0:
-            keep, send, later = forward(
-                line, begin, columns, axis, xy, gate, up, down, begin, (down_weight, half)
-            )
-        elif begin < half:
-            keep, send = forward(line, begin, columns, axis, xy, gate, up, down, begin)
-        else:
-            keep, send = forward(line, begin, columns, axis, xy, gate, up, later, begin - half)
+        rest = (down_weight, *chunks[at + 1]) if at + 1 < CHUNKS else None
+        keep, send, *down_next = forward(
+            line, begin, columns, axis, xy, gate, up, down, rest
+        )
+        down = down_next[0] if down_next else None
         kept.append(keep)
         got.append(swap(send, "wa", n_wa, axis[0]))
     for at, (_, far) in enumerate(axes):
         kept[at], send = halve(line, kept[at], got[at])
         got[at] = swap(send, "wa", n_wa, far)
-    order = [pair + 1 - at for pair in range(0, CHUNKS, 2) for at in range(2)]
+    order = [1, 0, 3, 2]
     for at in order:
         kept[at] = middle(line, kept[at], got[at])
         got[at] = swap(kept[at], "wa", n_wa, axes[at][0])
-    xt, y_all = factors(line, xy, xy_other)
-    for at, (_, far) in enumerate(axes):
+    for at in [1, 0, 3, 2]:
+        far = axes[at][1]
         kept[at] = join(line, kept[at], got[at])
         got[at] = swap(kept[at], "wa", n_wa, far)
 
+    xt, y_all = factors(line, xy, xy_other)
     mine, other, grad = [], [], ()
     for at in range(0, CHUNKS, 2):
         pair = slice(at, at + 2)

time: 73.1 us -> 71.1 us (0.973)
  waiting for transfers between devices: 11.9 us -> 9.22 us
  starting transfers between devices: 27.2 us -> 28 us
    ppermute x25, waiting for transfers between devices: 11.9 us -> 9.22 us  [swap(): return lax.ppermute(value, axis, [(at, at ^ step) for at in range(size)])]
    ppermute x25, starting transfers between devices: 27.2 us -> 28 us  [swap(): return lax.ppermute(value, axis, [(at, at ^ step) for at in range(size)])]
  transfers between devices with their start and end apart: 25 -> 25, of which waited for: 11 -> 9; matrix products, arithmetic and copies ran while one was open for 0% -> 0% of each run, Pallas kernels for 40% -> 41%
where the time goes in v6:
time: 71.1 us; the launch traced here: 70.8 us
  Pallas kernels  31.9 us (45%)
  starting transfers between devices  28 us (39%)
  waiting for transfers between devices  9.22 us (13%)
  other arithmetic  0.88 us (1%)
  between operations  0.86 us (1%)
    pallas_call x26, Pallas kernels, call(): pl.pallas_call(body, in_specs=(in_specs or [IN_VMEM] * count) + [IN_VMEM]...  31.9 us
    ppermute x25, starting transfers between devices, swap(): return lax.ppermute(value, axis, [(at, at ^ step) for at in range(size)])  28 us
    ppermute x25, waiting for transfers between devices, swap(): return lax.ppermute(value, axis, [(at, at ^ step) for at in range(size)])  9.22 us
  transfers between devices with their start and end apart: 25, of which 9 were waited for; matrix products, arithmetic and copies ran while one was open for 0% of the time, Pallas kernels for 41%

profile of v6, /device:TPU:0, one launch (start us, length us, event | category | flops | bytes accessed | tf_op | source)
XLA Modules:
  0.0 70.8 jit_solution(6073551613394081569)
XLA Ops:
  0.6 0.9 %pad_maximum_fusion.refs_0_ = bf16[40,1280]{1,0:T(8,128)(2,1)S(1)} fusion(bf16[20,1280]{1,0:T(8,128)(2,1)} %param.6, bf16[20,1280]{1,0:T(8,128)(2,1)} %param.5), kind=kLoop, calls=%fused_computation | loop fusion | flops 204800 | bytes 204800 | tf_op jit(solution)/shard_map/concatenate | solution.py:369
  1.5 5.1 %collective-permute-start.2 = (bf16[40,1280]{1,0:T(8,128)(2,1)S(1)}, bf16[40,1280]{1,0:T(8,128)(2,1)S(1)}, u32[]{:S(2)}, u32[]{:S(2)}) collective-permute-start(bf16[40,1280]{1,0:T(8,128)(2,1)S(1)} %pad_maximum_fusion.refs_0_), channel_id=1, source_target_pairs={{0,6},{2,4},{4,2},{6,0},{1,7},{3,5},{5,3},{7,1},{8,14},{10,12},{12... | collective-permute-start | bytes 307208 | tf_op jit(solution)/shard_map/ppermute | solution.py:358
  6.6 0.6 collective-permute-start
  7.3 7.4 %load_kernel.1 = (bf16[1280,3456]{1,0:T(8,128)(2,1)S(1)}, bf16[1280,3456]{1,0:T(8,128)(2,1)S(1)}, bf16[896,1280]{1,0:T(8,128)(2,1)S(1)}, f32[8,128]{1,0:T(8,128)}) custom-call(bf16[1280,3456]{1,0:T(8,128)(2,1)} %refs_0_.1, bf16[1280,3456]{1,0:T(8,128)(2,1)} %refs_1_.1, bf16[3456,1280]{1,0:T(8,128)(2,1)} %refs_4_.5), custom_call_target="tpu_custom_call" | custom-call | flops 1 | bytes 1 | tf_op jit(solution)/shard_map/load_kernel/pallas_call | solution.py:62
  14.6 0.6 collective-permute-done.1.refs_2_
  15.3 0.2 order_kernel.1
  15.4 1.9 %forward_kernel.4 = (f32[120,896]{1,0:T(8,128)S(1)}, bf16[120,896]{1,0:T(8,128)(2,1)S(1)}, bf16[896,1280]{1,0:T(8,128)(2,1)S(1)}, f32[8,128]{1,0:T(8,128)S(1)}) custom-call(bf16[160,1280]{1,0:T(8,128)(2,1)S(1)} %get-tuple-element.73.refs_0_, bf16[1280,3456]{1,0:T(8,128)(2,1)S(1)} %get-tuple-element.74.refs_1_, ...), custom_call_target="tpu_custom_call" | custom-call | flops 1 | bytes 1 | tf_op jit(solution)/shard_map/forward_kernel/pallas_call | solution.py:62
  17.3 1.6 %collective-permute-start.5 = (bf16[120,896]{1,0:T(8,128)(2,1)S(1)}, bf16[120,896]{1,0:T(8,128)(2,1)S(1)}, u32[]{:S(2)}, u32[]{:S(2)}) collective-permute-start(bf16[120,896]{1,0:T(8,128)(2,1)S(1)} %get-tuple-element.87), channel_id=1, source_target_pairs={{0,8},{8,0},{16,24},{24,16},{1,9},{9,1},{17,25},{25,17},{2,10},{10... | collective-permute-start | bytes 645128 | tf_op jit(solution)/shard_map/ppermute | solution.py:358
  18.9 2.1 %forward_kernel.5 = (f32[120,896]{1,0:T(8,128)S(1)}, bf16[120,896]{1,0:T(8,128)(2,1)S(1)}, bf16[896,1280]{1,0:T(8,128)(2,1)S(1)}, f32[8,128]{1,0:T(8,128)S(1)}) custom-call(bf16[160,1280]{1,0:T(8,128)(2,1)S(1)} %get-tuple-element.73.refs_0_, bf16[1280,3456]{1,0:T(8,128)(2,1)S(1)} %get-tuple-element.74.refs_1_, ...), custom_call_target="tpu_custom_call" | custom-call | flops 1 | bytes 1 | tf_op jit(solution)/shard_map/forward_kernel/pallas_call | solution.py:62
  21.0 1.6 %collective-permute-start.4 = (bf16[120,896]{1,0:T(8,128)(2,1)S(1)}, bf16[120,896]{1,0:T(8,128)(2,1)S(1)}, u32[]{:S(2)}, u32[]{:S(2)}) collective-permute-start(bf16[120,896]{1,0:T(8,128)(2,1)S(1)} %get-tuple-element.85), channel_id=1, source_target_pairs={{0,16},{8,24},{16,0},{24,8},{1,17},{9,25},{17,1},{25,9},{2,18},{10... | collective-permute-start | bytes 645128 | tf_op jit(solution)/shard_map/ppermute | solution.py:358
  22.6 1.8 %forward_kernel.6 = (f32[120,896]{1,0:T(8,128)S(1)}, bf16[120,896]{1,0:T(8,128)(2,1)S(1)}, bf16[768,1280]{1,0:T(8,128)(2,1)S(1)}, f32[8,128]{1,0:T(8,128)S(1)}) custom-call(bf16[160,1280]{1,0:T(8,128)(2,1)S(1)} %get-tuple-element.73.refs_0_, bf16[1280,3456]{1,0:T(8,128)(2,1)S(1)} %get-tuple-element.74.refs_1_, ...), custom_call_target="tpu_custom_call" | custom-call | flops 1 | bytes 1 | tf_op jit(solution)/shard_map/forward_kernel/pallas_call | solution.py:62
  24.4 0.6 collective-permute-start.3
  25.0 1.4 %forward_kernel.7 = (f32[120,768]{1,0:T(8,128)S(1)}, bf16[120,768]{1,0:T(8,128)(2,1)S(1)}, f32[8,128]{1,0:T(8,128)S(1)}) custom-call(bf16[160,1280]{1,0:T(8,128)(2,1)S(1)} %get-tuple-element.73.refs_0_, bf16[1280,3456]{1,0:T(8,128)(2,1)S(1)} %get-tuple-element.74.refs_1_, bf16[1280,3456]{1,0:T(8,128)(2,1)S(1)} %get-tuple-element.75.refs_2_, ...), custom_call_target="tpu_custom_call" | custom-call | flops 1 | bytes 1 | tf_op jit(solution)/shard_map/forward_kernel/pallas_call | solution.py:62
  26.4 0.6 collective-permute-start.7
  27.0 0.0 collective-permute-done.5.refs_1_
  27.0 0.1 halve_kernel.4
  27.0 0.1 collective-permute-done.4.refs_1_
  27.1 0.1 halve_kernel.5
  27.2 1.5 %collective-permute-start.10 = (bf16[60,896]{1,0:T(8,128)(2,1)S(1)}, bf16[60,896]{1,0:T(8,128)(2,1)S(1)}, u32[]{:S(2)}, u32[]{:S(2)}) collective-permute-start(bf16[60,896]{1,0:T(8,128)(2,1)S(1)} %get-tuple-element.103), channel_id=1, source_target_pairs={{0,8},{8,0},{16,24},{24,16},{1,9},{9,1},{17,25},{25,17},{2,10},{10... | collective-permute-start | bytes 322568 | tf_op jit(solution)/shard_map/ppermute | solution.py:358
  28.7 1.5 %collective-permute-start.9 = (bf16[60,896]{1,0:T(8,128)(2,1)S(1)}, bf16[60,896]{1,0:T(8,128)(2,1)S(1)}, u32[]{:S(2)}, u32[]{:S(2)}) collective-permute-start(bf16[60,896]{1,0:T(8,128)(2,1)S(1)} %get-tuple-element.101), channel_id=1, source_target_pairs={{0,16},{8,24},{16,0},{24,8},{1,17},{9,25},{17,1},{25,9},{2,18},{10... | collective-permute-start | bytes 322568 | tf_op jit(solution)/shard_map/ppermute | solution.py:358
  30.2 0.0 collective-permute-start.19
  30.2 1.3 %collective-permute-done.3.refs_1_ = bf16[120,896]{1,0:T(8,128)(2,1)S(1)} collective-permute-done((bf16[120,896]{1,0:T(8,128)(2,1)S(1)}, bf16[120,896]{1,0:T(8,128)(2,1)S(1)}, u32[]{:S(2)}, u32[]{:S(2)}) %collective-permute-start.3) | collective-permute-done | bytes 215072 | tf_op jit(solution)/shard_map/ppermute | solution.py:358
  31.5 0.1 halve_kernel.6
  31.6 0.6 collective-permute-start.6
  32.2 0.3 collective-permute-done.7.refs_1_
  32.5 0.1 halve_kernel.7
  32.6 1.6 %collective-permute-start.8 = (bf16[60,768]{1,0:T(8,128)(2,1)S(1)}, bf16[60,768]{1,0:T(8,128)(2,1)S(1)}, u32[]{:S(2)}, u32[]{:S(2)}) collective-permute-start(bf16[60,768]{1,0:T(8,128)(2,1)S(1)} %get-tuple-element.99), channel_id=1, source_target_pairs={{0,8},{8,0},{16,24},{24,16},{1,9},{9,1},{17,25},{25,17},{2,10},{10... | collective-permute-start | bytes 276488 | tf_op jit(solution)/shard_map/ppermute | solution.py:358
  34.2 0.1 middle_kernel.4
  34.2 0.6 collective-permute-start.14
  34.8 0.0 collective-permute-done.9.refs_1_
  34.8 0.1 middle_kernel.5
  34.9 1.4 %collective-permute-start.13 = (bf16[60,896]{1,0:T(8,128)(2,1)S(1)}, bf16[60,896]{1,0:T(8,128)(2,1)S(1)}, u32[]{:S(2)}, u32[]{:S(2)}) collective-permute-start(bf16[60,896]{1,0:T(8,128)(2,1)S(1)} %get-tuple-element.110.refs_0_), channel_id=1, source_target_pairs={{0,8},{8,0},{16,24},{24,16},{1,9},{9,1},{17,25},{25,17},{2,10},{10... | collective-permute-start | bytes 322568 | tf_op jit(solution)/shard_map/ppermute | solution.py:358
  36.3 1.9 %collective-permute-done.8.refs_1_ = bf16[60,768]{1,0:T(8,128)(2,1)S(1)} collective-permute-done((bf16[60,768]{1,0:T(8,128)(2,1)S(1)}, bf16[60,768]{1,0:T(8,128)(2,1)S(1)}, u32[]{:S(2)}, u32[]{:S(2)}) %collective-permute-start.8) | collective-permute-done | bytes 92192 | tf_op jit(solution)/shard_map/ppermute | solution.py:358
  38.2 0.1 middle_kernel.6
  38.3 0.1 middle_kernel.7
  38.4 1.2 %collective-permute-start.11 = (bf16[60,896]{1,0:T(8,128)(2,1)S(1)}, bf16[60,896]{1,0:T(8,128)(2,1)S(1)}, u32[]{:S(2)}, u32[]{:S(2)}) collective-permute-start(bf16[60,896]{1,0:T(8,128)(2,1)S(1)} %get-tuple-element.108.refs_0_), channel_id=1, source_target_pairs={{0,8},{8,0},{16,24},{24,16},{1,9},{9,1},{17,25},{25,17},{2,10},{10... | collective-permute-start | bytes 322568 | tf_op jit(solution)/shard_map/ppermute | solution.py:358
  39.6 0.6 collective-permute-start.12
  40.2 0.0 collective-permute-done.14.refs_1_
  40.2 0.7 %collective-permute-done.13.refs_1_ = bf16[60,896]{1,0:T(8,128)(2,1)S(1)} collective-permute-done((bf16[60,896]{1,0:T(8,128)(2,1)S(1)}, bf16[60,896]{1,0:T(8,128)(2,1)S(1)}, u32[]{:S(2)}, u32[]{:S(2)}) %collective-permute-start.13) | collective-permute-done | bytes 107552 | tf_op jit(solution)/shard_map/ppermute | solution.py:358
  41.0 0.9 %collective-permute-start.17 = (bf16[120,896]{1,0:T(8,128)(2,1)S(1)}, bf16[120,896]{1,0:T(8,128)(2,1)S(1)}, u32[]{:S(2)}, u32[]{:S(2)}) collective-permute-start(bf16[120,896]{1,0:T(8,128)(2,1)S(1)} %get-tuple-element.118.refs_0_), channel_id=1, source_target_pairs={{0,16},{8,24},{16,0},{24,8},{1,17},{9,25},{17,1},{25,9},{2,18},{10... | collective-permute-start | bytes 645128 | tf_op jit(solution)/shard_map/ppermute | solution.py:358
  41.9 1.3 %collective-permute-start.18 = (bf16[120,896]{1,0:T(8,128)(2,1)S(1)}, bf16[120,896]{1,0:T(8,128)(2,1)S(1)}, u32[]{:S(2)}, u32[]{:S(2)}) collective-permute-start(bf16[120,896]{1,0:T(8,128)(2,1)S(1)} %get-tuple-element.119.refs_2_), channel_id=1, source_target_pairs={{0,8},{8,0},{16,24},{24,16},{1,9},{9,1},{17,25},{25,17},{2,10},{10... | collective-permute-start | bytes 645128 | tf_op jit(solution)/shard_map/ppermute | solution.py:358
  43.2 2.1 %collective-permute-done.12.refs_1_ = bf16[60,768]{1,0:T(8,128)(2,1)S(1)} collective-permute-done((bf16[60,768]{1,0:T(8,128)(2,1)S(1)}, bf16[60,768]{1,0:T(8,128)(2,1)S(1)}, u32[]{:S(2)}, u32[]{:S(2)}) %collective-permute-start.12) | collective-permute-done | bytes 92192 | tf_op jit(solution)/shard_map/ppermute | solution.py:358
  45.3 0.0 collective-permute-done.11.refs_1_
  45.4 0.7 collective-permute-start.15
  46.1 1.0 %collective-permute-start.16 = (bf16[120,768]{1,0:T(8,128)(2,1)S(1)}, bf16[120,768]{1,0:T(8,128)(2,1)S(1)}, u32[]{:S(2)}, u32[]{:S(2)}) collective-permute-start(bf16[120,768]{1,0:T(8,128)(2,1)S(1)} %get-tuple-element.117.refs_2_), channel_id=1, source_target_pairs={{0,8},{8,0},{16,24},{24,16},{1,9},{9,1},{17,25},{25,17},{2,10},{10... | collective-permute-start | bytes 552968 | tf_op jit(solution)/shard_map/ppermute | solution.py:358
  47.1 0.3 factors_kernel.1
  47.4 1.9 %collective-permute-done.17.refs_1_ = bf16[120,896]{1,0:T(8,128)(2,1)S(1)} collective-permute-done((bf16[120,896]{1,0:T(8,128)(2,1)S(1)}, bf16[120,896]{1,0:T(8,128)(2,1)S(1)}, u32[]{:S(2)}, u32[]{:S(2)}) %collective-permute-start.17) | collective-permute-done | bytes 215072 | tf_op jit(solution)/shard_map/ppermute | solution.py:358
  49.3 0.1 collective-permute-done.18.refs_3_
  49.4 0.1 stack_kernel.2
  49.5 0.1 collective-permute-start.23
  49.6 2.9 %input_grad_kernel.2 = (f32[80,1280]{1,0:T(8,128)S(1)}, f32[8,128]{1,0:T(8,128)S(1)}) custom-call(bf16[240,1792]{1,0:T(8,128)(2,1)S(1)} %get-tuple-element.122.refs_0_.refs_2_, bf16[1280,3456]{1,0:T(8,128)(2,1)S(1)} %get-tuple-element.74.refs_1_, bf16[1280,3456]{1,0:T(8,128)(2,1)S(1)} %get-tuple-element.75.refs_2_, f32[8,128]{1,0:T(8,128)S(1)} %get-tuple-element.123.refs_3_), custom_call_target="tpu_custom_call" | custom-call | flops 1 | bytes 1 | tf_op jit(solution)/shard_map/input_grad_kernel/pallas_call | solution.py:62
  52.5 0.0 collective-permute-done.16.refs_3_
  52.5 0.1 stack_kernel.3
  52.6 0.6 collective-permute-start.24
  53.2 2.7 %input_grad_kernel.3 = (f32[80,1280]{1,0:T(8,128)S(1)}, f32[8,128]{1,0:T(8,128)S(1)}) custom-call(bf16[240,1664]{1,0:T(8,128)(2,1)S(1)} %get-tuple-element.125.refs_0_.refs_3_, bf16[1280,3456]{1,0:T(8,128)(2,1)S(1)} %get-tuple-element.74.refs_1_, bf16[1280,3456]{1,0:T(8,128)(2,1)S(1)} %get-tuple-element.75.refs_2_, ...), custom_call_target="tpu_custom_call" | custom-call | flops 1 | bytes 1 | tf_op jit(solution)/shard_map/input_grad_kernel/pallas_call | solution.py:62
  55.9 0.2 last_kernel.1
  56.0 1.0 %collective-permute-start.20 = (bf16[20,1280]{1,0:T(8,128)(2,1)S(1)}, bf16[20,1280]{1,0:T(8,128)(2,1)S(1)}, u32[]{:S(2)}, u32[]{:S(2)}) collective-permute-start(bf16[20,1280]{1,0:T(8,128)(2,1)S(1)} %get-tuple-element.131), channel_id=1, source_target_pairs={{0,2},{2,0},{4,6},{6,4},{1,3},{3,1},{5,7},{7,5},{8,10},{10,8},{12,... | collective-permute-start | bytes 153608 | tf_op jit(solution)/shard_map/ppermute | solution.py:358
  57.0 2.6 %collective-permute-start.21 = (bf16[20,1280]{1,0:T(8,128)(2,1)S(1)}, bf16[20,1280]{1,0:T(8,128)(2,1)S(1)}, u32[]{:S(2)}, u32[]{:S(2)}) collective-permute-start(bf16[20,1280]{1,0:T(8,128)(2,1)S(1)} %get-tuple-element.132), channel_id=1, source_target_pairs={{0,4},{2,6},{4,0},{6,2},{1,5},{3,7},{5,1},{7,3},{8,12},{10,14},{12... | collective-permute-start | bytes 153608 | tf_op jit(solution)/shard_map/ppermute | solution.py:358
  59.7 0.8 %collective-permute-start.22 = (bf16[20,1280]{1,0:T(8,128)(2,1)S(1)}, bf16[20,1280]{1,0:T(8,128)(2,1)S(1)}, u32[]{:S(2)}, u32[]{:S(2)}) collective-permute-start(bf16[20,1280]{1,0:T(8,128)(2,1)S(1)} %get-tuple-element.133), channel_id=1, source_target_pairs={{0,6},{2,4},{4,2},{6,0},{1,7},{3,5},{5,3},{7,1},{8,14},{10,12},{12... | collective-permute-start | bytes 153608 | tf_op jit(solution)/shard_map/ppermute | solution.py:358
  60.5 0.0 collective-permute-done.24.refs_5_
  60.5 0.0 collective-permute-done.23.refs_4_
  60.5 9.6 %weight_grad_kernel.1 = (bf16[1280,3456]{1,0:T(8,128)(2,1)}, bf16[1280,3456]{1,0:T(8,128)(2,1)}, bf16[3456,1280]{1,0:T(8,128)(2,1)}, f32[8,128]{1,0:T(8,128)S(1)}) custom-call(bf16[1280,160]{1,0:T(8,128)(2,1)S(1)} %get-tuple-element.134.refs_0_, bf16[160,1280]{1,0:T(8,128)(2,1)S(1)} %get-tuple-element.135.refs_1_, ...), custom_call_target="tpu_custom_call" | custom-call | flops 1 | bytes 1 | tf_op jit(solution)/shard_map/weight_grad_kernel/pallas_call | solution.py:62
  70.1 0.0 collective-permute-done.20.refs_1_
  70.1 0.7 total_kernel.1
  (13 shorter events, 0.2 us)
Async XLA Ops:
  1.5 13.1 %collective-permute-start.2 = (bf16[40,1280]{1,0:T(8,128)(2,1)S(1)}, bf16[40,1280]{1,0:T(8,128)(2,1)S(1)}, u32[]{:S(2)}, u32[]{:S(2)}) collective-permute-start(bf16[40,1280]{1,0:T(8,128)(2,1)S(1)} %pad_maximum_fusion.refs_0_), channel_id=1, source_target_pairs={{0,6},{2,4},{4,2},{6,0},{1,7},{3,5},{5,3},{7,1},{8,14},{10,12},{12... | collective-permute-start | bytes 307208 | tf_op jit(solution)/shard_map/ppermute | solution.py:358
  6.6 8.6 %collective-permute-start.1 = (bf16[40,1280]{1,0:T(8,128)(2,1)S(1)}, bf16[40,1280]{1,0:T(8,128)(2,1)S(1)}, u32[]{:S(2)}, u32[]{:S(2)}) collective-permute-start(bf16[40,1280]{1,0:T(8,128)(2,1)S(1)} %pad_maximum_fusion.refs_0_), channel_id=1, source_target_pairs={{0,4},{2,6},{4,0},{6,2},{1,5},{3,7},{5,1},{7,3},{8,12},{10,14},{12... | collective-permute-start | bytes 307208 | tf_op jit(solution)/shard_map/ppermute | solution.py:358
  6.6 8.6 %collective-permute-start = (bf16[40,1280]{1,0:T(8,128)(2,1)S(1)}, bf16[40,1280]{1,0:T(8,128)(2,1)S(1)}, u32[]{:S(2)}, u32[]{:S(2)}) collective-permute-start(bf16[40,1280]{1,0:T(8,128)(2,1)S(1)} %pad_maximum_fusion.refs_0_), channel_id=1, source_target_pairs={{0,2},{2,0},{4,6},{6,4},{1,3},{3,1},{5,7},{7,5},{8,10},{10,8},{12,... | collective-permute-start | bytes 307208 | tf_op jit(solution)/shard_map/ppermute | solution.py:358
  17.3 9.6 %collective-permute-start.5 = (bf16[120,896]{1,0:T(8,128)(2,1)S(1)}, bf16[120,896]{1,0:T(8,128)(2,1)S(1)}, u32[]{:S(2)}, u32[]{:S(2)}) collective-permute-start(bf16[120,896]{1,0:T(8,128)(2,1)S(1)} %get-tuple-element.87), channel_id=1, source_target_pairs={{0,8},{8,0},{16,24},{24,16},{1,9},{9,1},{17,25},{25,17},{2,10},{10... | collective-permute-start | bytes 645128 | tf_op jit(solution)/shard_map/ppermute | solution.py:358
  21.0 6.1 %collective-permute-start.4 = (bf16[120,896]{1,0:T(8,128)(2,1)S(1)}, bf16[120,896]{1,0:T(8,128)(2,1)S(1)}, u32[]{:S(2)}, u32[]{:S(2)}) collective-permute-start(bf16[120,896]{1,0:T(8,128)(2,1)S(1)} %get-tuple-element.85), channel_id=1, source_target_pairs={{0,16},{8,24},{16,0},{24,8},{1,17},{9,25},{17,1},{25,9},{2,18},{10... | collective-permute-start | bytes 645128 | tf_op jit(solution)/shard_map/ppermute | solution.py:358
  24.4 7.1 %collective-permute-start.3 = (bf16[120,896]{1,0:T(8,128)(2,1)S(1)}, bf16[120,896]{1,0:T(8,128)(2,1)S(1)}, u32[]{:S(2)}, u32[]{:S(2)}) collective-permute-start(bf16[120,896]{1,0:T(8,128)(2,1)S(1)} %get-tuple-element.83), channel_id=1, source_target_pairs={{0,8},{8,0},{16,24},{24,16},{1,9},{9,1},{17,25},{25,17},{2,10},{10... | collective-permute-start | bytes 645128 | tf_op jit(solution)/shard_map/ppermute | solution.py:358
  26.4 6.1 %collective-permute-start.7 = (bf16[120,768]{1,0:T(8,128)(2,1)S(1)}, bf16[120,768]{1,0:T(8,128)(2,1)S(1)}, u32[]{:S(2)}, u32[]{:S(2)}) collective-permute-start(bf16[120,768]{1,0:T(8,128)(2,1)S(1)} %get-tuple-element.96), channel_id=1, source_target_pairs={{0,16},{8,24},{16,0},{24,8},{1,17},{9,25},{17,1},{25,9},{2,18},{10... | collective-permute-start | bytes 552968 | tf_op jit(solution)/shard_map/ppermute | solution.py:358
  27.2 7.0 %collective-permute-start.10 = (bf16[60,896]{1,0:T(8,128)(2,1)S(1)}, bf16[60,896]{1,0:T(8,128)(2,1)S(1)}, u32[]{:S(2)}, u32[]{:S(2)}) collective-permute-start(bf16[60,896]{1,0:T(8,128)(2,1)S(1)} %get-tuple-element.103), channel_id=1, source_target_pairs={{0,8},{8,0},{16,24},{24,16},{1,9},{9,1},{17,25},{25,17},{2,10},{10... | collective-permute-start | bytes 322568 | tf_op jit(solution)/shard_map/ppermute | solution.py:358
  28.7 6.1 %collective-permute-start.9 = (bf16[60,896]{1,0:T(8,128)(2,1)S(1)}, bf16[60,896]{1,0:T(8,128)(2,1)S(1)}, u32[]{:S(2)}, u32[]{:S(2)}) collective-permute-start(bf16[60,896]{1,0:T(8,128)(2,1)S(1)} %get-tuple-element.101), channel_id=1, source_target_pairs={{0,16},{8,24},{16,0},{24,8},{1,17},{9,25},{17,1},{25,9},{2,18},{10... | collective-permute-start | bytes 322568 | tf_op jit(solution)/shard_map/ppermute | solution.py:358
  30.2 16.9 %collective-permute-start.19 = (bf16[160,1280]{1,0:T(8,128)(2,1)S(1)}, bf16[160,1280]{1,0:T(8,128)(2,1)S(1)}, u32[]{:S(2)}, u32[]{:S(2)}) collective-permute-start(bf16[160,1280]{1,0:T(8,128)(2,1)S(1)} %get-tuple-element.73.refs_0_), channel_id=1, source_target_pairs={{0,1},{1,0},{2,3},{3,2},{4,5},{5,4},{6,7},{7,6},{8,9},{9,8},{10,11... | collective-permute-start | bytes 1228808 | tf_op jit(solution)/shard_map/ppermute | solution.py:358
  31.6 6.7 %collective-permute-start.6 = (bf16[60,896]{1,0:T(8,128)(2,1)S(1)}, bf16[60,896]{1,0:T(8,128)(2,1)S(1)}, u32[]{:S(2)}, u32[]{:S(2)}) collective-permute-start(bf16[60,896]{1,0:T(8,128)(2,1)S(1)} %get-tuple-element.94), channel_id=1, source_target_pairs={{0,16},{8,24},{16,0},{24,8},{1,17},{9,25},{17,1},{25,9},{2,18},{10... | collective-permute-start | bytes 322568 | tf_op jit(solution)/shard_map/ppermute | solution.py:358
  32.6 5.6 %collective-permute-start.8 = (bf16[60,768]{1,0:T(8,128)(2,1)S(1)}, bf16[60,768]{1,0:T(8,128)(2,1)S(1)}, u32[]{:S(2)}, u32[]{:S(2)}) collective-permute-start(bf16[60,768]{1,0:T(8,128)(2,1)S(1)} %get-tuple-element.99), channel_id=1, source_target_pairs={{0,8},{8,0},{16,24},{24,16},{1,9},{9,1},{17,25},{25,17},{2,10},{10... | collective-permute-start | bytes 276488 | tf_op jit(solution)/shard_map/ppermute | solution.py:358
  34.2 5.9 %collective-permute-start.14 = (bf16[60,896]{1,0:T(8,128)(2,1)S(1)}, bf16[60,896]{1,0:T(8,128)(2,1)S(1)}, u32[]{:S(2)}, u32[]{:S(2)}) collective-permute-start(bf16[60,896]{1,0:T(8,128)(2,1)S(1)} %get-tuple-element.111.refs_0_), channel_id=1, source_target_pairs={{0,16},{8,24},{16,0},{24,8},{1,17},{9,25},{17,1},{25,9},{2,18},{10... | collective-permute-start | bytes 322568 | tf_op jit(solution)/shard_map/ppermute | solution.py:358
  34.9 6.1 %collective-permute-start.13 = (bf16[60,896]{1,0:T(8,128)(2,1)S(1)}, bf16[60,896]{1,0:T(8,128)(2,1)S(1)}, u32[]{:S(2)}, u32[]{:S(2)}) collective-permute-start(bf16[60,896]{1,0:T(8,128)(2,1)S(1)} %get-tuple-element.110.refs_0_), channel_id=1, source_target_pairs={{0,8},{8,0},{16,24},{24,16},{1,9},{9,1},{17,25},{25,17},{2,10},{10... | collective-permute-start | bytes 322568 | tf_op jit(solution)/shard_map/ppermute | solution.py:358
  38.4 7.0 %collective-permute-start.11 = (bf16[60,896]{1,0:T(8,128)(2,1)S(1)}, bf16[60,896]{1,0:T(8,128)(2,1)S(1)}, u32[]{:S(2)}, u32[]{:S(2)}) collective-permute-start(bf16[60,896]{1,0:T(8,128)(2,1)S(1)} %get-tuple-element.108.refs_0_), channel_id=1, source_target_pairs={{0,8},{8,0},{16,24},{24,16},{1,9},{9,1},{17,25},{25,17},{2,10},{10... | collective-permute-start | bytes 322568 | tf_op jit(solution)/shard_map/ppermute | solution.py:358
  39.6 5.7 %collective-permute-start.12 = (bf16[60,768]{1,0:T(8,128)(2,1)S(1)}, bf16[60,768]{1,0:T(8,128)(2,1)S(1)}, u32[]{:S(2)}, u32[]{:S(2)}) collective-permute-start(bf16[60,768]{1,0:T(8,128)(2,1)S(1)} %get-tuple-element.109.refs_0_), channel_id=1, source_target_pairs={{0,16},{8,24},{16,0},{24,8},{1,17},{9,25},{17,1},{25,9},{2,18},{10... | collective-permute-start | bytes 276488 | tf_op jit(solution)/shard_map/ppermute | solution.py:358
  41.0 8.3 %collective-permute-start.17 = (bf16[120,896]{1,0:T(8,128)(2,1)S(1)}, bf16[120,896]{1,0:T(8,128)(2,1)S(1)}, u32[]{:S(2)}, u32[]{:S(2)}) collective-permute-start(bf16[120,896]{1,0:T(8,128)(2,1)S(1)} %get-tuple-element.118.refs_0_), channel_id=1, source_target_pairs={{0,16},{8,24},{16,0},{24,8},{1,17},{9,25},{17,1},{25,9},{2,18},{10... | collective-permute-start | bytes 645128 | tf_op jit(solution)/shard_map/ppermute | solution.py:358
  41.9 7.5 %collective-permute-start.18 = (bf16[120,896]{1,0:T(8,128)(2,1)S(1)}, bf16[120,896]{1,0:T(8,128)(2,1)S(1)}, u32[]{:S(2)}, u32[]{:S(2)}) collective-permute-start(bf16[120,896]{1,0:T(8,128)(2,1)S(1)} %get-tuple-element.119.refs_2_), channel_id=1, source_target_pairs={{0,8},{8,0},{16,24},{24,16},{1,9},{9,1},{17,25},{25,17},{2,10},{10... | collective-permute-start | bytes 645128 | tf_op jit(solution)/shard_map/ppermute | solution.py:358
  45.4 7.1 %collective-permute-start.15 = (bf16[120,896]{1,0:T(8,128)(2,1)S(1)}, bf16[120,896]{1,0:T(8,128)(2,1)S(1)}, u32[]{:S(2)}, u32[]{:S(2)}) collective-permute-start(bf16[120,896]{1,0:T(8,128)(2,1)S(1)} %get-tuple-element.116.refs_0_), channel_id=1, source_target_pairs={{0,16},{8,24},{16,0},{24,8},{1,17},{9,25},{17,1},{25,9},{2,18},{10... | collective-permute-start | bytes 645128 | tf_op jit(solution)/shard_map/ppermute | solution.py:358
  46.1 6.4 %collective-permute-start.16 = (bf16[120,768]{1,0:T(8,128)(2,1)S(1)}, bf16[120,768]{1,0:T(8,128)(2,1)S(1)}, u32[]{:S(2)}, u32[]{:S(2)}) collective-permute-start(bf16[120,768]{1,0:T(8,128)(2,1)S(1)} %get-tuple-element.117.refs_2_), channel_id=1, source_target_pairs={{0,8},{8,0},{16,24},{24,16},{1,9},{9,1},{17,25},{25,17},{2,10},{10... | collective-permute-start | bytes 552968 | tf_op jit(solution)/shard_map/ppermute | solution.py:358
  49.5 11.0 %collective-permute-start.23 = (bf16[240,1792]{1,0:T(8,128)(2,1)S(1)}, bf16[240,1792]{1,0:T(8,128)(2,1)S(1)}, u32[]{:S(2)}, u32[]{:S(2)}) collective-permute-start(bf16[240,1792]{1,0:T(8,128)(2,1)S(1)} %get-tuple-element.122.refs_0_.refs_2_), channel_id=1, source_target_pairs={{0,1},{1,0},{2,3},{3,2},{4,5},{5,4},{6,7},{7,6},{8,9},{9,8},{10,11... | collective-permute-start | bytes 2580488 | tf_op jit(solution)/shard_map/ppermute | solution.py:358
  52.6 7.9 %collective-permute-start.24 = (bf16[240,1664]{1,0:T(8,128)(2,1)S(1)}, bf16[240,1664]{1,0:T(8,128)(2,1)S(1)}, u32[]{:S(2)}, u32[]{:S(2)}) collective-permute-start(bf16[240,1664]{1,0:T(8,128)(2,1)S(1)} %get-tuple-element.125.refs_0_.refs_3_), channel_id=1, source_target_pairs={{0,1},{1,0},{2,3},{3,2},{4,5},{5,4},{6,7},{7,6},{8,9},{9,8},{10,11... | collective-permute-start | bytes 2396168 | tf_op jit(solution)/shard_map/ppermute | solution.py:358
  56.0 14.1 %collective-permute-start.20 = (bf16[20,1280]{1,0:T(8,128)(2,1)S(1)}, bf16[20,1280]{1,0:T(8,128)(2,1)S(1)}, u32[]{:S(2)}, u32[]{:S(2)}) collective-permute-start(bf16[20,1280]{1,0:T(8,128)(2,1)S(1)} %get-tuple-element.131), channel_id=1, source_target_pairs={{0,2},{2,0},{4,6},{6,4},{1,3},{3,1},{5,7},{7,5},{8,10},{10,8},{12,... | collective-permute-start | bytes 153608 | tf_op jit(solution)/shard_map/ppermute | solution.py:358
  57.0 13.1 %collective-permute-start.21 = (bf16[20,1280]{1,0:T(8,128)(2,1)S(1)}, bf16[20,1280]{1,0:T(8,128)(2,1)S(1)}, u32[]{:S(2)}, u32[]{:S(2)}) collective-permute-start(bf16[20,1280]{1,0:T(8,128)(2,1)S(1)} %get-tuple-element.132), channel_id=1, source_target_pairs={{0,4},{2,6},{4,0},{6,2},{1,5},{3,7},{5,1},{7,3},{8,12},{10,14},{12... | collective-permute-start | bytes 153608 | tf_op jit(solution)/shard_map/ppermute | solution.py:358
  59.7 10.5 %collective-permute-start.22 = (bf16[20,1280]{1,0:T(8,128)(2,1)S(1)}, bf16[20,1280]{1,0:T(8,128)(2,1)S(1)}, u32[]{:S(2)}, u32[]{:S(2)}) collective-permute-start(bf16[20,1280]{1,0:T(8,128)(2,1)S(1)} %get-tuple-element.133), channel_id=1, source_target_pairs={{0,6},{2,4},{4,2},{6,0},{1,7},{3,5},{5,3},{7,1},{8,14},{10,12},{12... | collective-permute-start | bytes 153608 | tf_op jit(solution)/shard_map/ppermute | solution.py:358

commit v7 on v6

--- a/solution.py
+++ b/solution.py
@@ -84,22 +84,20 @@
     return copies
 
 
-def load_kernel(gate_ref, up_ref, down_ref, gate_out, up_out, down_out, sems):
+def load_kernel(gate_ref, up_ref, gate_out, up_out, sems):
     copies = copy_rows(sems.at[0], gate_ref, gate_out)
     copies += copy_rows(sems.at[1], up_ref, up_out)
-    copies += copy_rows(sems.at[2], down_ref, down_out)
     for copy in copies:
         copy.wait()
 
 
-def load(line, gate_weight, up_weight, down_weight, rows):
-    shapes = [gate_weight.shape, up_weight.shape, (rows, down_weight.shape[1])]
+def load(line, *weights):
     return line.call(
         load_kernel,
-        (gate_weight, up_weight, down_weight),
-        [pltpu.VMEM(shape, BF16) for shape in shapes],
-        in_specs=[IN_HBM] * 3,
-        scratch=[pltpu.SemaphoreType.DMA((3, CUTS))],
+        weights,
+        [pltpu.VMEM(weight.shape, BF16) for weight in weights],
+        in_specs=[IN_HBM] * len(weights),
+        scratch=[pltpu.SemaphoreType.DMA((len(weights), CUTS))],
         limit=30,
     )
 
@@ -126,22 +124,14 @@
     return line.call(order_kernel, pieces, [shaped(4 * rows, width)])[0]
 
 
-def forward_kernel(begin, near, far, later, *refs):
-    xy_ref, gate_ref, up_ref, down_ref, *refs = refs
-    copies = []
-    if later is not None:
-        all_ref, keep_ref, send_ref, later_ref, sems = refs
-        copies = copy_rows(sems, all_ref, later_ref, later)
-    else:
-        keep_ref, send_ref = refs
-    columns = keep_ref.shape[1]
+def forward_kernel(begin, near, far, xy_ref, gate_ref, up_ref, down_ref, keep_ref, send_ref):
+    there = pl.ds(begin, keep_ref.shape[1])
     group = xy_ref.shape[0] // 2
     rows = group // 4
     x, y = xy_ref[:group], xy_ref[group:]
-    there = pl.ds(begin, columns)
     gate = jnp.dot(x, gate_ref[:, there], preferred_element_type=F32)
     up = jnp.dot(x, up_ref[:, there], preferred_element_type=F32)
-    dh = lax.dot_general(y, down_ref[...], NT, preferred_element_type=F32)
+    dh = lax.dot_general(y, down_ref[there], NT, preferred_element_type=F32)
 
     def slots(*which):
         cuts = [slice(slot * rows, (slot + 1) * rows) for slot in which]
@@ -149,27 +139,14 @@
 
     keep_ref[...] = slots(0, far)
     send_ref[...] = slots(near, near ^ far).astype(BF16)
-    for copy in copies:
-        copy.wait()
-
-
-def forward(line, begin, columns, axes, xy, gate, up, down, rest=None):
+
+
+def forward(line, begin, columns, axes, xy, gate, up, down):
     rows = 6 * (xy.shape[0] // 8)
-    args, specs = [xy, gate, up, down], [IN_VMEM] * 4
-    shapes = [shaped(rows, columns, F32), shaped(rows, columns)]
-    later = None
-    if rest is not None:
-        weight, later, size = rest
-        args.append(weight)
-        specs.append(IN_HBM)
-        shapes.append(pltpu.VMEM((size, weight.shape[1]), BF16))
-    return line.call(
-        functools.partial(forward_kernel, begin, *axes, later),
-        args,
-        shapes,
-        in_specs=specs,
-        scratch=[pltpu.SemaphoreType.DMA((CUTS,))] if rest is not None else [],
-        limit=25 if rest is not None else 4,
+    return line.call(
+        functools.partial(forward_kernel, begin, *axes),
+        (xy, gate, up, down),
+        [shaped(rows, columns, F32), shaped(rows, columns)],
     )
 
 
@@ -368,17 +345,13 @@
 
     both = jnp.concatenate([tokens, cotangent], axis=0)
     pieces = [both] + [swap(both, "ha", n_ha, step) for step in range(1, n_ha)]
-    gate, up, down = load(Line(), gate_weight, up_weight, down_weight, chunks[0][1])
+    gate, up = load(Line(), gate_weight, up_weight)
     xy = order_rows(line, pieces)
     xy_other = swap(xy, "row", n_row, 1)
 
     kept, got = [], []
     for at, ((begin, columns), axis) in enumerate(zip(chunks, axes)):
-        rest = (down_weight, *chunks[at + 1]) if at + 1 < CHUNKS else None
-        keep, send, *down_next = forward(
-            line, begin, columns, axis, xy, gate, up, down, rest
-        )
-        down = down_next[0] if down_next else None
+        keep, send = forward(line, begin, columns, axis, xy, gate, up, down_weight)
         kept.append(keep)
         got.append(swap(send, "wa", n_wa, axis[0]))
     for at, (_, far) in enumerate(axes):

time: 71.1 us -> 69.9 us (0.983)
  Pallas kernels: 31.9 us -> 30 us
  starting transfers between devices: 28 us -> 29.7 us
  waiting for transfers between devices: 9.22 us -> 8.04 us
    pallas_call x26, Pallas kernels: 31.9 us -> 30 us  [call(): pl.pallas_call(body, in_specs=(in_specs or [IN_VMEM] * count) + [IN_VMEM]...]
    ppermute x25, starting transfers between devices: 28 us -> 29.7 us  [swap(): return lax.ppermute(value, axis, [(at, at ^ step) for at in range(size)])]
    ppermute x25, waiting for transfers between devices: 9.22 us -> 8.04 us  [swap(): return lax.ppermute(value, axis, [(at, at ^ step) for at in range(size)])]
  transfers between devices with their start and end apart: 25 -> 25, of which waited for: 9 -> 9; matrix products, arithmetic and copies ran while one was open for 0% -> 0% of each run, Pallas kernels for 41% -> 40%
where the time goes in v7:
time: 69.9 us; the launch traced here: 69.7 us
  Pallas kernels  30 us (43%)
  starting transfers between devices  29.7 us (42%)
  waiting for transfers between devices  8.04 us (12%)
  other arithmetic  1.03 us (1%)
  between operations  0.89 us (1%)
    pallas_call x26, Pallas kernels, call(): pl.pallas_call(body, in_specs=(in_specs or [IN_VMEM] * count) + [IN_VMEM]...  30 us
    ppermute x25, starting transfers between devices, swap(): return lax.ppermute(value, axis, [(at, at ^ step) for at in range(size)])  29.7 us
    ppermute x25, waiting for transfers between devices, swap(): return lax.ppermute(value, axis, [(at, at ^ step) for at in range(size)])  8.04 us
  transfers between devices with their start and end apart: 25, of which 9 were waited for; matrix products, arithmetic and copies ran while one was open for 0% of the time, Pallas kernels for 40%

profile of v7, /device:TPU:0, one launch (start us, length us, event | category | flops | bytes accessed | tf_op | source)
XLA Modules:
  0.0 69.7 jit_solution(2512413714467607879)
XLA Ops:
  0.6 0.0 slice-start
  0.6 1.0 %pad_maximum_fusion.refs_0_ = bf16[40,1280]{1,0:T(8,128)(2,1)S(1)} fusion(bf16[20,1280]{1,0:T(8,128)(2,1)} %param.6, bf16[20,1280]{1,0:T(8,128)(2,1)} %param.5), kind=kLoop, calls=%fused_computation | loop fusion | flops 204800 | bytes 204800 | tf_op jit(solution)/shard_map/concatenate | solution.py:346
  1.7 0.0 slice-start.1
  1.7 5.1 %collective-permute-start.2 = (bf16[40,1280]{1,0:T(8,128)(2,1)S(1)}, bf16[40,1280]{1,0:T(8,128)(2,1)S(1)}, u32[]{:S(2)}, u32[]{:S(2)}) collective-permute-start(bf16[40,1280]{1,0:T(8,128)(2,1)S(1)} %pad_maximum_fusion.refs_0_), channel_id=1, source_target_pairs={{0,6},{2,4},{4,2},{6,0},{1,7},{3,5},{5,3},{7,1},{8,14},{10,12},{12... | collective-permute-start | bytes 307208 | tf_op jit(solution)/shard_map/ppermute | solution.py:335
  6.8 0.6 collective-permute-start
  7.5 6.8 %load_kernel.1 = (bf16[1280,3456]{1,0:T(8,128)(2,1)S(1)}, bf16[1280,3456]{1,0:T(8,128)(2,1)S(1)}, f32[8,128]{1,0:T(8,128)}) custom-call(bf16[1280,3456]{1,0:T(8,128)(2,1)} %refs_0_.1, bf16[1280,3456]{1,0:T(8,128)(2,1)} %refs_1_.1), custom_call_target="tpu_custom_call" | custom-call | flops 1 | bytes 1 | tf_op jit(solution)/shard_map/load_kernel/pallas_call | solution.py:62
  14.3 1.2 %collective-permute-done.1.refs_2_ = bf16[40,1280]{1,0:T(8,128)(2,1)S(1)} collective-permute-done((bf16[40,1280]{1,0:T(8,128)(2,1)S(1)}, bf16[40,1280]{1,0:T(8,128)(2,1)S(1)}, u32[]{:S(2)}, u32[]{:S(2)}) %collective-permute-start.1) | collective-permute-done | bytes 102432 | tf_op jit(solution)/shard_map/ppermute | solution.py:335
  15.4 0.0 collective-permute-done.refs_1_
  15.4 0.2 order_kernel.1
  15.7 1.5 %forward_kernel.4 = (f32[120,896]{1,0:T(8,128)S(1)}, bf16[120,896]{1,0:T(8,128)(2,1)S(1)}, f32[8,128]{1,0:T(8,128)S(1)}) custom-call(bf16[160,1280]{1,0:T(8,128)(2,1)S(1)} %get-tuple-element.69.refs_0_, bf16[1280,3456]{1,0:T(8,128)(2,1)S(1)} %get-tuple-element.70.refs_1_, bf16[1280,3456]{1,0:T(8,128)(2,1)S(1)} %get-tuple-element.71.refs_2_, ...), custom_call_target="tpu_custom_call" | custom-call | flops 1 | bytes 1 | tf_op jit(solution)/shard_map/forward_kernel/pallas_call | solution.py:62
  17.2 1.6 %collective-permute-start.5 = (bf16[120,896]{1,0:T(8,128)(2,1)S(1)}, bf16[120,896]{1,0:T(8,128)(2,1)S(1)}, u32[]{:S(2)}, u32[]{:S(2)}) collective-permute-start(bf16[120,896]{1,0:T(8,128)(2,1)S(1)} %get-tuple-element.80), channel_id=1, source_target_pairs={{0,8},{8,0},{16,24},{24,16},{1,9},{9,1},{17,25},{25,17},{2,10},{10... | collective-permute-start | bytes 645128 | tf_op jit(solution)/shard_map/ppermute | solution.py:335
  18.7 1.5 %forward_kernel.5 = (f32[120,896]{1,0:T(8,128)S(1)}, bf16[120,896]{1,0:T(8,128)(2,1)S(1)}, f32[8,128]{1,0:T(8,128)S(1)}) custom-call(bf16[160,1280]{1,0:T(8,128)(2,1)S(1)} %get-tuple-element.69.refs_0_, bf16[1280,3456]{1,0:T(8,128)(2,1)S(1)} %get-tuple-element.70.refs_1_, bf16[1280,3456]{1,0:T(8,128)(2,1)S(1)} %get-tuple-element.71.refs_2_, ...), custom_call_target="tpu_custom_call" | custom-call | flops 1 | bytes 1 | tf_op jit(solution)/shard_map/forward_kernel/pallas_call | solution.py:62
  20.2 1.6 %collective-permute-start.4 = (bf16[120,896]{1,0:T(8,128)(2,1)S(1)}, bf16[120,896]{1,0:T(8,128)(2,1)S(1)}, u32[]{:S(2)}, u32[]{:S(2)}) collective-permute-start(bf16[120,896]{1,0:T(8,128)(2,1)S(1)} %get-tuple-element.78), channel_id=1, source_target_pairs={{0,16},{8,24},{16,0},{24,8},{1,17},{9,25},{17,1},{25,9},{2,18},{10... | collective-permute-start | bytes 645128 | tf_op jit(solution)/shard_map/ppermute | solution.py:335
  21.8 1.5 %forward_kernel.6 = (f32[120,896]{1,0:T(8,128)S(1)}, bf16[120,896]{1,0:T(8,128)(2,1)S(1)}, f32[8,128]{1,0:T(8,128)S(1)}) custom-call(bf16[160,1280]{1,0:T(8,128)(2,1)S(1)} %get-tuple-element.69.refs_0_, bf16[1280,3456]{1,0:T(8,128)(2,1)S(1)} %get-tuple-element.70.refs_1_, bf16[1280,3456]{1,0:T(8,128)(2,1)S(1)} %get-tuple-element.71.refs_2_, ...), custom_call_target="tpu_custom_call" | custom-call | flops 1 | bytes 1 | tf_op jit(solution)/shard_map/forward_kernel/pallas_call | solution.py:62
  23.3 0.6 collective-permute-start.3
  23.9 1.4 %forward_kernel.7 = (f32[120,768]{1,0:T(8,128)S(1)}, bf16[120,768]{1,0:T(8,128)(2,1)S(1)}, f32[8,128]{1,0:T(8,128)S(1)}) custom-call(bf16[160,1280]{1,0:T(8,128)(2,1)S(1)} %get-tuple-element.69.refs_0_, bf16[1280,3456]{1,0:T(8,128)(2,1)S(1)} %get-tuple-element.70.refs_1_, bf16[1280,3456]{1,0:T(8,128)(2,1)S(1)} %get-tuple-element.71.refs_2_, ...), custom_call_target="tpu_custom_call" | custom-call | flops 1 | bytes 1 | tf_op jit(solution)/shard_map/forward_kernel/pallas_call | solution.py:62
  25.3 0.6 collective-permute-start.7
  25.9 0.1 halve_kernel.4
  26.0 0.4 collective-permute-done.4.refs_1_
  26.4 0.1 halve_kernel.5
  26.5 1.2 %collective-permute-start.10 = (bf16[60,896]{1,0:T(8,128)(2,1)S(1)}, bf16[60,896]{1,0:T(8,128)(2,1)S(1)}, u32[]{:S(2)}, u32[]{:S(2)}) collective-permute-start(bf16[60,896]{1,0:T(8,128)(2,1)S(1)} %get-tuple-element.95), channel_id=1, source_target_pairs={{0,8},{8,0},{16,24},{24,16},{1,9},{9,1},{17,25},{25,17},{2,10},{10... | collective-permute-start | bytes 322568 | tf_op jit(solution)/shard_map/ppermute | solution.py:335
  27.6 1.5 %collective-permute-start.9 = (bf16[60,896]{1,0:T(8,128)(2,1)S(1)}, bf16[60,896]{1,0:T(8,128)(2,1)S(1)}, u32[]{:S(2)}, u32[]{:S(2)}) collective-permute-start(bf16[60,896]{1,0:T(8,128)(2,1)S(1)} %get-tuple-element.93), channel_id=1, source_target_pairs={{0,16},{8,24},{16,0},{24,8},{1,17},{9,25},{17,1},{25,9},{2,18},{10... | collective-permute-start | bytes 322568 | tf_op jit(solution)/shard_map/ppermute | solution.py:335
  29.1 1.4 %collective-permute-done.3.refs_1_ = bf16[120,896]{1,0:T(8,128)(2,1)S(1)} collective-permute-done((bf16[120,896]{1,0:T(8,128)(2,1)S(1)}, bf16[120,896]{1,0:T(8,128)(2,1)S(1)}, u32[]{:S(2)}, u32[]{:S(2)}) %collective-permute-start.3) | collective-permute-done | bytes 215072 | tf_op jit(solution)/shard_map/ppermute | solution.py:335
  30.5 0.1 halve_kernel.6
  30.6 0.6 collective-permute-start.6
  31.1 0.4 collective-permute-done.7.refs_1_
  31.6 0.1 halve_kernel.7
  31.6 1.5 %collective-permute-start.8 = (bf16[60,768]{1,0:T(8,128)(2,1)S(1)}, bf16[60,768]{1,0:T(8,128)(2,1)S(1)}, u32[]{:S(2)}, u32[]{:S(2)}) collective-permute-start(bf16[60,768]{1,0:T(8,128)(2,1)S(1)} %get-tuple-element.91), channel_id=1, source_target_pairs={{0,8},{8,0},{16,24},{24,16},{1,9},{9,1},{17,25},{25,17},{2,10},{10... | collective-permute-start | bytes 276488 | tf_op jit(solution)/shard_map/ppermute | solution.py:335
  33.1 0.0 collective-permute-done.10.refs_1_
  33.1 0.1 middle_kernel.4
  33.2 0.8 %collective-permute-start.14 = (bf16[60,896]{1,0:T(8,128)(2,1)S(1)}, bf16[60,896]{1,0:T(8,128)(2,1)S(1)}, u32[]{:S(2)}, u32[]{:S(2)}) collective-permute-start(bf16[60,896]{1,0:T(8,128)(2,1)S(1)} %get-tuple-element.103.refs_0_), channel_id=1, source_target_pairs={{0,16},{8,24},{16,0},{24,8},{1,17},{9,25},{17,1},{25,9},{2,18},{10... | collective-permute-start | bytes 322568 | tf_op jit(solution)/shard_map/ppermute | solution.py:335
  33.9 0.1 middle_kernel.5
  34.0 1.6 %collective-permute-start.13 = (bf16[60,896]{1,0:T(8,128)(2,1)S(1)}, bf16[60,896]{1,0:T(8,128)(2,1)S(1)}, u32[]{:S(2)}, u32[]{:S(2)}) collective-permute-start(bf16[60,896]{1,0:T(8,128)(2,1)S(1)} %get-tuple-element.102.refs_0_), channel_id=1, source_target_pairs={{0,8},{8,0},{16,24},{24,16},{1,9},{9,1},{17,25},{25,17},{2,10},{10... | collective-permute-start | bytes 322568 | tf_op jit(solution)/shard_map/ppermute | solution.py:335
  35.6 1.1 %collective-permute-done.8.refs_1_ = bf16[60,768]{1,0:T(8,128)(2,1)S(1)} collective-permute-done((bf16[60,768]{1,0:T(8,128)(2,1)S(1)}, bf16[60,768]{1,0:T(8,128)(2,1)S(1)}, u32[]{:S(2)}, u32[]{:S(2)}) %collective-permute-start.8) | collective-permute-done | bytes 92192 | tf_op jit(solution)/shard_map/ppermute | solution.py:335
  36.8 0.1 middle_kernel.6
  36.8 0.0 collective-permute-done.6.refs_1_
  36.8 0.1 middle_kernel.7
  36.9 1.8 %collective-permute-start.11 = (bf16[60,896]{1,0:T(8,128)(2,1)S(1)}, bf16[60,896]{1,0:T(8,128)(2,1)S(1)}, u32[]{:S(2)}, u32[]{:S(2)}) collective-permute-start(bf16[60,896]{1,0:T(8,128)(2,1)S(1)} %get-tuple-element.100.refs_0_), channel_id=1, source_target_pairs={{0,8},{8,0},{16,24},{24,16},{1,9},{9,1},{17,25},{25,17},{2,10},{10... | collective-permute-start | bytes 322568 | tf_op jit(solution)/shard_map/ppermute | solution.py:335
  38.7 0.9 %collective-permute-start.12 = (bf16[60,768]{1,0:T(8,128)(2,1)S(1)}, bf16[60,768]{1,0:T(8,128)(2,1)S(1)}, u32[]{:S(2)}, u32[]{:S(2)}) collective-permute-start(bf16[60,768]{1,0:T(8,128)(2,1)S(1)} %get-tuple-element.101.refs_0_), channel_id=1, source_target_pairs={{0,16},{8,24},{16,0},{24,8},{1,17},{9,25},{17,1},{25,9},{2,18},{10... | collective-permute-start | bytes 276488 | tf_op jit(solution)/shard_map/ppermute | solution.py:335
  39.6 0.0 collective-permute-done.14.refs_1_
  39.7 0.3 collective-permute-done.13.refs_1_
  40.0 1.0 %collective-permute-start.17 = (bf16[120,896]{1,0:T(8,128)(2,1)S(1)}, bf16[120,896]{1,0:T(8,128)(2,1)S(1)}, u32[]{:S(2)}, u32[]{:S(2)}) collective-permute-start(bf16[120,896]{1,0:T(8,128)(2,1)S(1)} %get-tuple-element.110.refs_0_), channel_id=1, source_target_pairs={{0,16},{8,24},{16,0},{24,8},{1,17},{9,25},{17,1},{25,9},{2,18},{10... | collective-permute-start | bytes 645128 | tf_op jit(solution)/shard_map/ppermute | solution.py:335
  41.0 1.7 %collective-permute-start.18 = (bf16[120,896]{1,0:T(8,128)(2,1)S(1)}, bf16[120,896]{1,0:T(8,128)(2,1)S(1)}, u32[]{:S(2)}, u32[]{:S(2)}) collective-permute-start(bf16[120,896]{1,0:T(8,128)(2,1)S(1)} %get-tuple-element.111.refs_2_), channel_id=1, source_target_pairs={{0,8},{8,0},{16,24},{24,16},{1,9},{9,1},{17,25},{25,17},{2,10},{10... | collective-permute-start | bytes 645128 | tf_op jit(solution)/shard_map/ppermute | solution.py:335
  42.7 1.7 %collective-permute-done.12.refs_1_ = bf16[60,768]{1,0:T(8,128)(2,1)S(1)} collective-permute-done((bf16[60,768]{1,0:T(8,128)(2,1)S(1)}, bf16[60,768]{1,0:T(8,128)(2,1)S(1)}, u32[]{:S(2)}, u32[]{:S(2)}) %collective-permute-start.12) | collective-permute-done | bytes 92192 | tf_op jit(solution)/shard_map/ppermute | solution.py:335
  44.5 0.0 collective-permute-done.11.refs_1_
  44.5 1.0 %collective-permute-start.15 = (bf16[120,896]{1,0:T(8,128)(2,1)S(1)}, bf16[120,896]{1,0:T(8,128)(2,1)S(1)}, u32[]{:S(2)}, u32[]{:S(2)}) collective-permute-start(bf16[120,896]{1,0:T(8,128)(2,1)S(1)} %get-tuple-element.108.refs_0_), channel_id=1, source_target_pairs={{0,16},{8,24},{16,0},{24,8},{1,17},{9,25},{17,1},{25,9},{2,18},{10... | collective-permute-start | bytes 645128 | tf_op jit(solution)/shard_map/ppermute | solution.py:335
  45.5 1.1 %collective-permute-start.16 = (bf16[120,768]{1,0:T(8,128)(2,1)S(1)}, bf16[120,768]{1,0:T(8,128)(2,1)S(1)}, u32[]{:S(2)}, u32[]{:S(2)}) collective-permute-start(bf16[120,768]{1,0:T(8,128)(2,1)S(1)} %get-tuple-element.109.refs_2_), channel_id=1, source_target_pairs={{0,8},{8,0},{16,24},{24,16},{1,9},{9,1},{17,25},{25,17},{2,10},{10... | collective-permute-start | bytes 552968 | tf_op jit(solution)/shard_map/ppermute | solution.py:335
  46.6 0.3 factors_kernel.1
  46.9 1.4 %collective-permute-done.17.refs_1_ = bf16[120,896]{1,0:T(8,128)(2,1)S(1)} collective-permute-done((bf16[120,896]{1,0:T(8,128)(2,1)S(1)}, bf16[120,896]{1,0:T(8,128)(2,1)S(1)}, u32[]{:S(2)}, u32[]{:S(2)}) %collective-permute-start.17) | collective-permute-done | bytes 215072 | tf_op jit(solution)/shard_map/ppermute | solution.py:335
  48.3 0.1 collective-permute-done.18.refs_3_
  48.4 0.1 stack_kernel.2
  48.5 0.1 collective-permute-start.23
  48.6 2.9 %input_grad_kernel.2 = (f32[80,1280]{1,0:T(8,128)S(1)}, f32[8,128]{1,0:T(8,128)S(1)}) custom-call(bf16[240,1792]{1,0:T(8,128)(2,1)S(1)} %get-tuple-element.114.refs_0_.refs_2_, bf16[1280,3456]{1,0:T(8,128)(2,1)S(1)} %get-tuple-element.70.refs_1_, bf16[1280,3456]{1,0:T(8,128)(2,1)S(1)} %get-tuple-element.71.refs_2_, f32[8,128]{1,0:T(8,128)S(1)} %get-tuple-element.115.refs_3_), custom_call_target="tpu_custom_call" | custom-call | flops 1 | bytes 1 | tf_op jit(solution)/shard_map/input_grad_kernel/pallas_call | solution.py:62
  51.4 0.0 collective-permute-done.15.refs_1_
  51.4 0.1 stack_kernel.3
  51.6 0.6 collective-permute-start.24
  52.1 2.7 %input_grad_kernel.3 = (f32[80,1280]{1,0:T(8,128)S(1)}, f32[8,128]{1,0:T(8,128)S(1)}) custom-call(bf16[240,1664]{1,0:T(8,128)(2,1)S(1)} %get-tuple-element.117.refs_0_.refs_3_, bf16[1280,3456]{1,0:T(8,128)(2,1)S(1)} %get-tuple-element.70.refs_1_, bf16[1280,3456]{1,0:T(8,128)(2,1)S(1)} %get-tuple-element.71.refs_2_, ...), custom_call_target="tpu_custom_call" | custom-call | flops 1 | bytes 1 | tf_op jit(solution)/shard_map/input_grad_kernel/pallas_call | solution.py:62
  54.8 0.2 last_kernel.1
  55.0 0.4 collective-permute-start.20
  55.4 2.6 %collective-permute-start.21 = (bf16[20,1280]{1,0:T(8,128)(2,1)S(1)}, bf16[20,1280]{1,0:T(8,128)(2,1)S(1)}, u32[]{:S(2)}, u32[]{:S(2)}) collective-permute-start(bf16[20,1280]{1,0:T(8,128)(2,1)S(1)} %get-tuple-element.124), channel_id=1, source_target_pairs={{0,4},{2,6},{4,0},{6,2},{1,5},{3,7},{5,1},{7,3},{8,12},{10,14},{12... | collective-permute-start | bytes 153608 | tf_op jit(solution)/shard_map/ppermute | solution.py:335
  58.0 1.4 %collective-permute-start.22 = (bf16[20,1280]{1,0:T(8,128)(2,1)S(1)}, bf16[20,1280]{1,0:T(8,128)(2,1)S(1)}, u32[]{:S(2)}, u32[]{:S(2)}) collective-permute-start(bf16[20,1280]{1,0:T(8,128)(2,1)S(1)} %get-tuple-element.125), channel_id=1, source_target_pairs={{0,6},{2,4},{4,2},{6,0},{1,7},{3,5},{5,3},{7,1},{8,14},{10,12},{12... | collective-permute-start | bytes 153608 | tf_op jit(solution)/shard_map/ppermute | solution.py:335
  59.4 9.6 %weight_grad_kernel.1 = (bf16[1280,3456]{1,0:T(8,128)(2,1)}, bf16[1280,3456]{1,0:T(8,128)(2,1)}, bf16[3456,1280]{1,0:T(8,128)(2,1)}, f32[8,128]{1,0:T(8,128)S(1)}) custom-call(bf16[1280,160]{1,0:T(8,128)(2,1)S(1)} %get-tuple-element.126.refs_0_, bf16[160,1280]{1,0:T(8,128)(2,1)S(1)} %get-tuple-element.127.refs_1_, ...), custom_call_target="tpu_custom_call" | custom-call | flops 1 | bytes 1 | tf_op jit(solution)/shard_map/weight_grad_kernel/pallas_call | solution.py:62
  69.0 0.0 collective-permute-done.20.refs_1_
  69.1 0.7 total_kernel.1
  (20 shorter events, 0.2 us)
Async XLA Ops:
  0.6 15.0 %slice-start = ((s8[8847360]{0:T(1024)(128)(4,1)}), s8[4194304]{0:T(1024)(128)(4,1)S(1)}, s32[]{:S(2)}) async-start(s8[8847360]{0:T(1024)(128)(4,1)} %bitcast), calls=%async_computation | async-start | bytes 8388608
  1.7 14.0 %slice-start.1 = ((s8[8847360]{0:T(1024)(128)(4,1)}), s8[4194304]{0:T(1024)(128)(4,1)S(1)}, s32[]{:S(2)}) async-start(s8[8847360]{0:T(1024)(128)(4,1)} %bitcast), calls=%async_computation.1 | async-start | bytes 8388608
  1.7 14.0 %slice-start.2 = ((s8[8847360]{0:T(1024)(128)(4,1)}), s8[458752]{0:T(1024)(128)(4,1)S(1)}, s32[]{:S(2)}) async-start(s8[8847360]{0:T(1024)(128)(4,1)} %bitcast), calls=%async_computation.2 | async-start | bytes 917504
  1.7 12.5 %collective-permute-start.2 = (bf16[40,1280]{1,0:T(8,128)(2,1)S(1)}, bf16[40,1280]{1,0:T(8,128)(2,1)S(1)}, u32[]{:S(2)}, u32[]{:S(2)}) collective-permute-start(bf16[40,1280]{1,0:T(8,128)(2,1)S(1)} %pad_maximum_fusion.refs_0_), channel_id=1, source_target_pairs={{0,6},{2,4},{4,2},{6,0},{1,7},{3,5},{5,3},{7,1},{8,14},{10,12},{12... | collective-permute-start | bytes 307208 | tf_op jit(solution)/shard_map/ppermute | solution.py:335
  6.8 8.6 %collective-permute-start.1 = (bf16[40,1280]{1,0:T(8,128)(2,1)S(1)}, bf16[40,1280]{1,0:T(8,128)(2,1)S(1)}, u32[]{:S(2)}, u32[]{:S(2)}) collective-permute-start(bf16[40,1280]{1,0:T(8,128)(2,1)S(1)} %pad_maximum_fusion.refs_0_), channel_id=1, source_target_pairs={{0,4},{2,6},{4,0},{6,2},{1,5},{3,7},{5,1},{7,3},{8,12},{10,14},{12... | collective-permute-start | bytes 307208 | tf_op jit(solution)/shard_map/ppermute | solution.py:335
  6.8 8.6 %collective-permute-start = (bf16[40,1280]{1,0:T(8,128)(2,1)S(1)}, bf16[40,1280]{1,0:T(8,128)(2,1)S(1)}, u32[]{:S(2)}, u32[]{:S(2)}) collective-permute-start(bf16[40,1280]{1,0:T(8,128)(2,1)S(1)} %pad_maximum_fusion.refs_0_), channel_id=1, source_target_pairs={{0,2},{2,0},{4,6},{6,4},{1,3},{3,1},{5,7},{7,5},{8,10},{10,8},{12,... | collective-permute-start | bytes 307208 | tf_op jit(solution)/shard_map/ppermute | solution.py:335
  17.2 8.8 %collective-permute-start.5 = (bf16[120,896]{1,0:T(8,128)(2,1)S(1)}, bf16[120,896]{1,0:T(8,128)(2,1)S(1)}, u32[]{:S(2)}, u32[]{:S(2)}) collective-permute-start(bf16[120,896]{1,0:T(8,128)(2,1)S(1)} %get-tuple-element.80), channel_id=1, source_target_pairs={{0,8},{8,0},{16,24},{24,16},{1,9},{9,1},{17,25},{25,17},{2,10},{10... | collective-permute-start | bytes 645128 | tf_op jit(solution)/shard_map/ppermute | solution.py:335
  20.2 6.2 %collective-permute-start.4 = (bf16[120,896]{1,0:T(8,128)(2,1)S(1)}, bf16[120,896]{1,0:T(8,128)(2,1)S(1)}, u32[]{:S(2)}, u32[]{:S(2)}) collective-permute-start(bf16[120,896]{1,0:T(8,128)(2,1)S(1)} %get-tuple-element.78), channel_id=1, source_target_pairs={{0,16},{8,24},{16,0},{24,8},{1,17},{9,25},{17,1},{25,9},{2,18},{10... | collective-permute-start | bytes 645128 | tf_op jit(solution)/shard_map/ppermute | solution.py:335
  23.3 7.2 %collective-permute-start.3 = (bf16[120,896]{1,0:T(8,128)(2,1)S(1)}, bf16[120,896]{1,0:T(8,128)(2,1)S(1)}, u32[]{:S(2)}, u32[]{:S(2)}) collective-permute-start(bf16[120,896]{1,0:T(8,128)(2,1)S(1)} %get-tuple-element.76), channel_id=1, source_target_pairs={{0,8},{8,0},{16,24},{24,16},{1,9},{9,1},{17,25},{25,17},{2,10},{10... | collective-permute-start | bytes 645128 | tf_op jit(solution)/shard_map/ppermute | solution.py:335
  25.3 6.2 %collective-permute-start.7 = (bf16[120,768]{1,0:T(8,128)(2,1)S(1)}, bf16[120,768]{1,0:T(8,128)(2,1)S(1)}, u32[]{:S(2)}, u32[]{:S(2)}) collective-permute-start(bf16[120,768]{1,0:T(8,128)(2,1)S(1)} %get-tuple-element.88), channel_id=1, source_target_pairs={{0,16},{8,24},{16,0},{24,8},{1,17},{9,25},{17,1},{25,9},{2,18},{10... | collective-permute-start | bytes 552968 | tf_op jit(solution)/shard_map/ppermute | solution.py:335
  26.5 6.6 %collective-permute-start.10 = (bf16[60,896]{1,0:T(8,128)(2,1)S(1)}, bf16[60,896]{1,0:T(8,128)(2,1)S(1)}, u32[]{:S(2)}, u32[]{:S(2)}) collective-permute-start(bf16[60,896]{1,0:T(8,128)(2,1)S(1)} %get-tuple-element.95), channel_id=1, source_target_pairs={{0,8},{8,0},{16,24},{24,16},{1,9},{9,1},{17,25},{25,17},{2,10},{10... | collective-permute-start | bytes 322568 | tf_op jit(solution)/shard_map/ppermute | solution.py:335
  27.6 6.3 %collective-permute-start.9 = (bf16[60,896]{1,0:T(8,128)(2,1)S(1)}, bf16[60,896]{1,0:T(8,128)(2,1)S(1)}, u32[]{:S(2)}, u32[]{:S(2)}) collective-permute-start(bf16[60,896]{1,0:T(8,128)(2,1)S(1)} %get-tuple-element.93), channel_id=1, source_target_pairs={{0,16},{8,24},{16,0},{24,8},{1,17},{9,25},{17,1},{25,9},{2,18},{10... | collective-permute-start | bytes 322568 | tf_op jit(solution)/shard_map/ppermute | solution.py:335
  29.1 17.5 %collective-permute-start.19 = (bf16[160,1280]{1,0:T(8,128)(2,1)S(1)}, bf16[160,1280]{1,0:T(8,128)(2,1)S(1)}, u32[]{:S(2)}, u32[]{:S(2)}) collective-permute-start(bf16[160,1280]{1,0:T(8,128)(2,1)S(1)} %get-tuple-element.69.refs_0_), channel_id=1, source_target_pairs={{0,1},{1,0},{2,3},{3,2},{4,5},{5,4},{6,7},{7,6},{8,9},{9,8},{10,11... | collective-permute-start | bytes 1228808 | tf_op jit(solution)/shard_map/ppermute | solution.py:335
  30.6 6.3 %collective-permute-start.6 = (bf16[60,896]{1,0:T(8,128)(2,1)S(1)}, bf16[60,896]{1,0:T(8,128)(2,1)S(1)}, u32[]{:S(2)}, u32[]{:S(2)}) collective-permute-start(bf16[60,896]{1,0:T(8,128)(2,1)S(1)} %get-tuple-element.86), channel_id=1, source_target_pairs={{0,16},{8,24},{16,0},{24,8},{1,17},{9,25},{17,1},{25,9},{2,18},{10... | collective-permute-start | bytes 322568 | tf_op jit(solution)/shard_map/ppermute | solution.py:335
  31.6 5.1 %collective-permute-start.8 = (bf16[60,768]{1,0:T(8,128)(2,1)S(1)}, bf16[60,768]{1,0:T(8,128)(2,1)S(1)}, u32[]{:S(2)}, u32[]{:S(2)}) collective-permute-start(bf16[60,768]{1,0:T(8,128)(2,1)S(1)} %get-tuple-element.91), channel_id=1, source_target_pairs={{0,8},{8,0},{16,24},{24,16},{1,9},{9,1},{17,25},{25,17},{2,10},{10... | collective-permute-start | bytes 276488 | tf_op jit(solution)/shard_map/ppermute | solution.py:335
  33.2 6.5 %collective-permute-start.14 = (bf16[60,896]{1,0:T(8,128)(2,1)S(1)}, bf16[60,896]{1,0:T(8,128)(2,1)S(1)}, u32[]{:S(2)}, u32[]{:S(2)}) collective-permute-start(bf16[60,896]{1,0:T(8,128)(2,1)S(1)} %get-tuple-element.103.refs_0_), channel_id=1, source_target_pairs={{0,16},{8,24},{16,0},{24,8},{1,17},{9,25},{17,1},{25,9},{2,18},{10... | collective-permute-start | bytes 322568 | tf_op jit(solution)/shard_map/ppermute | solution.py:335
  34.0 6.0 %collective-permute-start.13 = (bf16[60,896]{1,0:T(8,128)(2,1)S(1)}, bf16[60,896]{1,0:T(8,128)(2,1)S(1)}, u32[]{:S(2)}, u32[]{:S(2)}) collective-permute-start(bf16[60,896]{1,0:T(8,128)(2,1)S(1)} %get-tuple-element.102.refs_0_), channel_id=1, source_target_pairs={{0,8},{8,0},{16,24},{24,16},{1,9},{9,1},{17,25},{25,17},{2,10},{10... | collective-permute-start | bytes 322568 | tf_op jit(solution)/shard_map/ppermute | solution.py:335
  36.9 7.5 %collective-permute-start.11 = (bf16[60,896]{1,0:T(8,128)(2,1)S(1)}, bf16[60,896]{1,0:T(8,128)(2,1)S(1)}, u32[]{:S(2)}, u32[]{:S(2)}) collective-permute-start(bf16[60,896]{1,0:T(8,128)(2,1)S(1)} %get-tuple-element.100.refs_0_), channel_id=1, source_target_pairs={{0,8},{8,0},{16,24},{24,16},{1,9},{9,1},{17,25},{25,17},{2,10},{10... | collective-permute-start | bytes 322568 | tf_op jit(solution)/shard_map/ppermute | solution.py:335
  38.7 5.7 %collective-permute-start.12 = (bf16[60,768]{1,0:T(8,128)(2,1)S(1)}, bf16[60,768]{1,0:T(8,128)(2,1)S(1)}, u32[]{:S(2)}, u32[]{:S(2)}) collective-permute-start(bf16[60,768]{1,0:T(8,128)(2,1)S(1)} %get-tuple-element.101.refs_0_), channel_id=1, source_target_pairs={{0,16},{8,24},{16,0},{24,8},{1,17},{9,25},{17,1},{25,9},{2,18},{10... | collective-permute-start | bytes 276488 | tf_op jit(solution)/shard_map/ppermute | solution.py:335
  40.0 8.3 %collective-permute-start.17 = (bf16[120,896]{1,0:T(8,128)(2,1)S(1)}, bf16[120,896]{1,0:T(8,128)(2,1)S(1)}, u32[]{:S(2)}, u32[]{:S(2)}) collective-permute-start(bf16[120,896]{1,0:T(8,128)(2,1)S(1)} %get-tuple-element.110.refs_0_), channel_id=1, source_target_pairs={{0,16},{8,24},{16,0},{24,8},{1,17},{9,25},{17,1},{25,9},{2,18},{10... | collective-permute-start | bytes 645128 | tf_op jit(solution)/shard_map/ppermute | solution.py:335
  41.0 7.3 %collective-permute-start.18 = (bf16[120,896]{1,0:T(8,128)(2,1)S(1)}, bf16[120,896]{1,0:T(8,128)(2,1)S(1)}, u32[]{:S(2)}, u32[]{:S(2)}) collective-permute-start(bf16[120,896]{1,0:T(8,128)(2,1)S(1)} %get-tuple-element.111.refs_2_), channel_id=1, source_target_pairs={{0,8},{8,0},{16,24},{24,16},{1,9},{9,1},{17,25},{25,17},{2,10},{10... | collective-permute-start | bytes 645128 | tf_op jit(solution)/shard_map/ppermute | solution.py:335
  44.5 6.9 %collective-permute-start.15 = (bf16[120,896]{1,0:T(8,128)(2,1)S(1)}, bf16[120,896]{1,0:T(8,128)(2,1)S(1)}, u32[]{:S(2)}, u32[]{:S(2)}) collective-permute-start(bf16[120,896]{1,0:T(8,128)(2,1)S(1)} %get-tuple-element.108.refs_0_), channel_id=1, source_target_pairs={{0,16},{8,24},{16,0},{24,8},{1,17},{9,25},{17,1},{25,9},{2,18},{10... | collective-permute-start | bytes 645128 | tf_op jit(solution)/shard_map/ppermute | solution.py:335
  45.5 5.9 %collective-permute-start.16 = (bf16[120,768]{1,0:T(8,128)(2,1)S(1)}, bf16[120,768]{1,0:T(8,128)(2,1)S(1)}, u32[]{:S(2)}, u32[]{:S(2)}) collective-permute-start(bf16[120,768]{1,0:T(8,128)(2,1)S(1)} %get-tuple-element.109.refs_2_), channel_id=1, source_target_pairs={{0,8},{8,0},{16,24},{24,16},{1,9},{9,1},{17,25},{25,17},{2,10},{10... | collective-permute-start | bytes 552968 | tf_op jit(solution)/shard_map/ppermute | solution.py:335
  48.5 11.0 %collective-permute-start.23 = (bf16[240,1792]{1,0:T(8,128)(2,1)S(1)}, bf16[240,1792]{1,0:T(8,128)(2,1)S(1)}, u32[]{:S(2)}, u32[]{:S(2)}) collective-permute-start(bf16[240,1792]{1,0:T(8,128)(2,1)S(1)} %get-tuple-element.114.refs_0_.refs_2_), channel_id=1, source_target_pairs={{0,1},{1,0},{2,3},{3,2},{4,5},{5,4},{6,7},{7,6},{8,9},{9,8},{10,11... | collective-permute-start | bytes 2580488 | tf_op jit(solution)/shard_map/ppermute | solution.py:335
  51.6 7.9 %collective-permute-start.24 = (bf16[240,1664]{1,0:T(8,128)(2,1)S(1)}, bf16[240,1664]{1,0:T(8,128)(2,1)S(1)}, u32[]{:S(2)}, u32[]{:S(2)}) collective-permute-start(bf16[240,1664]{1,0:T(8,128)(2,1)S(1)} %get-tuple-element.117.refs_0_.refs_3_), channel_id=1, source_target_pairs={{0,1},{1,0},{2,3},{3,2},{4,5},{5,4},{6,7},{7,6},{8,9},{9,8},{10,11... | collective-permute-start | bytes 2396168 | tf_op jit(solution)/shard_map/ppermute | solution.py:335
  55.0 14.1 %collective-permute-start.20 = (bf16[20,1280]{1,0:T(8,128)(2,1)S(1)}, bf16[20,1280]{1,0:T(8,128)(2,1)S(1)}, u32[]{:S(2)}, u32[]{:S(2)}) collective-permute-start(bf16[20,1280]{1,0:T(8,128)(2,1)S(1)} %get-tuple-element.123), channel_id=1, source_target_pairs={{0,2},{2,0},{4,6},{6,4},{1,3},{3,1},{5,7},{7,5},{8,10},{10,8},{12,... | collective-permute-start | bytes 153608 | tf_op jit(solution)/shard_map/ppermute | solution.py:335
  55.4 13.7 %collective-permute-start.21 = (bf16[20,1280]{1,0:T(8,128)(2,1)S(1)}, bf16[20,1280]{1,0:T(8,128)(2,1)S(1)}, u32[]{:S(2)}, u32[]{:S(2)}) collective-permute-start(bf16[20,1280]{1,0:T(8,128)(2,1)S(1)} %get-tuple-element.124), channel_id=1, source_target_pairs={{0,4},{2,6},{4,0},{6,2},{1,5},{3,7},{5,1},{7,3},{8,12},{10,14},{12... | collective-permute-start | bytes 153608 | tf_op jit(solution)/shard_map/ppermute | solution.py:335
  58.0 11.1 %collective-permute-start.22 = (bf16[20,1280]{1,0:T(8,128)(2,1)S(1)}, bf16[20,1280]{1,0:T(8,128)(2,1)S(1)}, u32[]{:S(2)}, u32[]{:S(2)}) collective-permute-start(bf16[20,1280]{1,0:T(8,128)(2,1)S(1)} %get-tuple-element.125), channel_id=1, source_target_pairs={{0,6},{2,4},{4,2},{6,0},{1,7},{3,5},{5,3},{7,1},{8,14},{10,12},{12... | collective-permute-start | bytes 153608 | tf_op jit(solution)/shard_map/ppermute | solution.py:335

commit v8 on v7

--- a/solution.py
+++ b/solution.py
@@ -194,11 +194,12 @@
         cuts = [slots[slot][k * rows : (k + 1) * rows] for k in range(3) for slot in range(4)]
         out_ref[:, begin : begin + columns] = joined(*cuts).astype(BF16)
         begin += columns
-
-
-def stack(line, axes, blocks):
+    if begin < out_ref.shape[1]:
+        out_ref[:, begin:] = jnp.zeros((out_ref.shape[0], out_ref.shape[1] - begin), BF16)
+
+
+def stack(line, axes, blocks, columns):
     rows = 2 * blocks[0][0].shape[0]
-    columns = sum(mine.shape[1] for mine, _ in blocks)
     return line.call(
         functools.partial(stack_kernel, axes),
         [block for pair in blocks for block in pair],
@@ -206,24 +207,27 @@
     )[0]
 
 
-def input_grad_kernel(begin, stack_ref, gate_ref, up_ref, *refs):
-    there = pl.ds(begin, stack_ref.shape[1])
-    group = stack_ref.shape[0] // 3
-    grad = lax.dot_general(
-        stack_ref[:group], gate_ref[:, there], NT, preferred_element_type=F32
+def input_grad_kernel(begin, mine_ref, gate_ref, up_ref, grad_ref):
+    grad_ref[...] = input_grad_part(begin, mine_ref, gate_ref, up_ref, 0, grad_ref.shape[1])
+
+
+def input_grad_part(begin, mine_ref, gate_ref, up_ref, start, size):
+    group = mine_ref.shape[0] // 3
+    columns = min(mine_ref.shape[1], gate_ref.shape[1] - begin)
+    here, there, used = pl.ds(start, size), pl.ds(begin, columns), pl.ds(0, columns)
+    return lax.dot_general(
+        mine_ref[:group, used], gate_ref[here, there], NT, preferred_element_type=F32
     ) + lax.dot_general(
-        stack_ref[group : 2 * group], up_ref[:, there], NT, preferred_element_type=F32
-    )
-    refs[-1][...] = grad + refs[0][...] if len(refs) > 1 else grad
-
-
-def input_grad(line, begin, stacked, gate_weight, up_weight, start):
-    shape = (stacked.shape[0] // 3, gate_weight.shape[0])
+        mine_ref[group : 2 * group, used], up_ref[here, there], NT, preferred_element_type=F32
+    )
+
+
+def input_grad(line, begin, mine, gate, up):
     return line.call(
         functools.partial(input_grad_kernel, begin),
-        (stacked, gate_weight, up_weight, *start),
-        [shaped(*shape, F32)],
-    )
+        (mine, gate, up),
+        [shaped(mine.shape[0] // 3, gate.shape[0], F32)],
+    )[0]
 
 
 def factors_kernel(mine_ref, other_ref, xt_ref, y_all_ref):
@@ -242,61 +246,103 @@
     return line.call(factors_kernel, (xy, other), [shaped(width, rows), shaped(rows, width)])
 
 
-def weight_grad_kernel(parts, xt_ref, y_ref, *refs):
-    mine_refs, other_refs = refs[:parts], refs[parts : 2 * parts]
-    *outs, both, gate, up, down, sems = refs[2 * parts :]
-    group = y_ref.shape[0] // 2
-    first = lax.axis_index("row") == 0
-    copies = []
-
-    def send(at, source, target):
-        copies.append(pltpu.make_async_copy(source, target, sems.at[at, len(copies) // 3]))
-        copies[-1].start()
-
-    begin = 0
-    for mine_ref, other_ref in zip(mine_refs, other_refs):
-        columns = mine_ref.shape[1]
-        for start in range(0, columns, TILE):
-            size = min(TILE, columns - start)
-            source, here = pl.ds(start, size), pl.ds(begin + start, size)
-            for at in range(3):
-                cut = slice(at * group, (at + 1) * group)
-                mine, other = mine_ref[cut, source], other_ref[cut, source]
-                both[at, :group, here] = jnp.where(first, mine, other)
-                both[at, group:, here] = jnp.where(first, other, mine)
-            gate[:, here] = jnp.dot(
-                xt_ref[...], both[0, :, here], preferred_element_type=F32
+class Writer:
+    def __init__(self, begin, xt_ref, y_ref, mine_ref, other_ref, outs, scratch):
+        self.begin, self.xt_ref, self.y_ref, self.outs = begin, xt_ref, y_ref, outs
+        self.both, self.gate, self.up, self.down, self.sems = scratch
+        self.mine_ref, self.other_ref = mine_ref, other_ref
+        columns = min(mine_ref.shape[1], outs[0].shape[1] - begin)
+        self.tiles = [(at, min(TILE, columns - at)) for at in range(0, columns, TILE)]
+        self.copies = []
+
+    def send(self, at, source, target):
+        step = len(self.copies) // 3
+        self.copies.append(pltpu.make_async_copy(source, target, self.sems.at[at, step]))
+        self.copies[-1].start()
+
+    def tile(self, start, size):
+        group = self.y_ref.shape[0] // 2
+        first = lax.axis_index("row") == 0
+        here, there = pl.ds(start, size), pl.ds(self.begin + start, size)
+        for at in range(3):
+            cut = slice(at * group, (at + 1) * group)
+            mine, other = self.mine_ref[cut, here], self.other_ref[cut, here]
+            self.both[at, :group, here] = jnp.where(first, mine, other)
+            self.both[at, group:, here] = jnp.where(first, other, mine)
+        for at, grad in enumerate((self.gate, self.up)):
+            grad[:, here] = jnp.dot(
+                self.xt_ref[...], self.both[at, :, here], preferred_element_type=F32
             ).astype(BF16)
-            send(0, gate.at[:, here], outs[0].at[:, here])
-            up[:, here] = jnp.dot(
-                xt_ref[...], both[1, :, here], preferred_element_type=F32
-            ).astype(BF16)
-            send(1, up.at[:, here], outs[1].at[:, here])
-            down[here, :] = lax.dot_general(
-                both[2, :, here], y_ref[...], TN, preferred_element_type=F32
-            ).astype(BF16)
-            send(2, down.at[here], outs[2].at[here])
-        begin += columns
-    for copy in copies:
-        copy.wait()
-
-
-def weight_grad(line, xt, y, mine, other):
-    width = xt.shape[0]
-    hidden_width = sum(m.shape[1] for m in mine)
-    shapes = [(width, hidden_width), (width, hidden_width), (hidden_width, width)]
-    steps = sum(pl.cdiv(m.shape[1], TILE) for m in mine)
-    return line.call(
-        functools.partial(weight_grad_kernel, len(mine)),
-        (xt, y, *mine, *other),
-        [shaped(*shape) for shape in shapes],
+            self.send(at, grad.at[:, here], self.outs[at].at[:, there])
+        self.down[here, :] = lax.dot_general(
+            self.both[2, :, here], self.y_ref[...], TN, preferred_element_type=F32
+        ).astype(BF16)
+        self.send(2, self.down.at[here], self.outs[2].at[there])
+
+    def wait(self):
+        for copy in self.copies:
+            copy.wait()
+
+
+def first_grads_kernel(begins, *refs):
+    xt_ref, y_ref, mine_ref, other_ref, start_ref, last_ref, gate_ref, up_ref, *refs = refs
+    *outs, grad_ref = refs[:4]
+    writer = Writer(begins[0], xt_ref, y_ref, mine_ref, other_ref, outs, refs[4:])
+    width = grad_ref.shape[1]
+    pieces = [(at, min(TILE, width - at)) for at in range(0, width, TILE)]
+    for step in range(max(len(pieces), len(writer.tiles))):
+        if step < len(writer.tiles):
+            writer.tile(*writer.tiles[step])
+        if step < len(pieces):
+            here = pl.ds(*pieces[step])
+            grad_ref[:, here] = start_ref[:, here] + input_grad_part(
+                begins[1], last_ref, gate_ref, up_ref, *pieces[step]
+            )
+    writer.wait()
+
+
+def grad_shapes(width, hidden_width):
+    return [(width, hidden_width), (width, hidden_width), (hidden_width, width)]
+
+
+def writer_scratch(width, rows, columns):
+    return [
+        pltpu.VMEM((3, rows, columns), BF16),
+        *(pltpu.VMEM(shape, BF16) for shape in grad_shapes(width, columns)),
+        pltpu.SemaphoreType.DMA((3, pl.cdiv(columns, TILE))),
+    ]
+
+
+def first_grads(line, begins, xt, y, mine, other, start, last, gate_weight, up_weight):
+    width, hidden_width = gate_weight.shape
+    shapes = [shaped(*shape) for shape in grad_shapes(width, hidden_width)]
+    return line.call(
+        functools.partial(first_grads_kernel, begins),
+        (xt, y, mine, other, start, last, gate_weight, up_weight),
+        shapes + [shaped(*start.shape, F32)],
+        out_specs=[IN_HBM] * 3 + [IN_VMEM],
+        scratch=writer_scratch(width, y.shape[0], mine.shape[1]),
+        limit=24,
+    )
+
+
+def weight_grad_kernel(begin, xt_ref, y_ref, mine_ref, other_ref, *refs):
+    writer = Writer(begin, xt_ref, y_ref, mine_ref, other_ref, refs[3:6], refs[6:])
+    for tile in writer.tiles:
+        writer.tile(*tile)
+    writer.wait()
+
+
+def weight_grad(line, begin, xt, y, mine, other, grads):
+    return line.call(
+        functools.partial(weight_grad_kernel, begin),
+        (xt, y, mine, other, *grads),
+        [shaped(*grad.shape) for grad in grads],
+        in_specs=[IN_VMEM] * 4 + [IN_HBM] * 3,
         out_specs=[IN_HBM] * 3,
-        scratch=[
-            pltpu.VMEM((3, y.shape[0], hidden_width), BF16),
-            *(pltpu.VMEM(shape, BF16) for shape in shapes),
-            pltpu.SemaphoreType.DMA((3, steps)),
-        ],
-        limit=40,
+        scratch=writer_scratch(xt.shape[0], y.shape[0], mine.shape[1]),
+        aliases={4 + at: at for at in range(3)},
+        limit=24,
     )
 
 
@@ -367,15 +413,20 @@
         got[at] = swap(kept[at], "wa", n_wa, far)
 
     xt, y_all = factors(line, xy, xy_other)
-    mine, other, grad = [], [], ()
+    mine, other = [], []
+    widths = [sum(c for _, c in chunks[at : at + 2]) for at in range(0, CHUNKS, 2)]
+    widest = max(widths)
+    begins = [chunks[at][0] for at in range(0, CHUNKS, 2)]
     for at in range(0, CHUNKS, 2):
         pair = slice(at, at + 2)
-        mine.append(stack(line, axes[pair], list(zip(kept, got))[pair]))
+        mine.append(stack(line, axes[pair], list(zip(kept, got))[pair], widest))
         other.append(swap(mine[-1], "row", n_row, 1))
-        grad = input_grad(line, chunks[at][0], mine[-1], gate, up, grad)
-    own, *sends = last_pieces(line, n_ha, grad[0])
+        if at == 0:
+            grad = input_grad(line, begins[0], mine[0], gate, up)
+    *grads, grad = first_grads(line, begins, xt, y_all, mine[0], other[0], grad, mine[1], gate, up)
+    own, *sends = last_pieces(line, n_ha, grad)
     received = [swap(sent, "ha", n_ha, k + 1) for k, sent in enumerate(sends)]
-    grads = weight_grad(line, xt, y_all, mine, other)
+    grads = weight_grad(line, begins[1], xt, y_all, mine[1], other[1], grads)
     return (total(line, own, received), *grads)
 
 

time: 69.9 us -> 71.3 us (1.020)
  starting transfers between devices: 29.7 us -> 32.1 us
  waiting for transfers between devices: 8.04 us -> 6.44 us
    ppermute x25, starting transfers between devices: 29.7 us -> 32.1 us  [swap(): return lax.ppermute(value, axis, [(at, at ^ step) for at in range(size)])]
    ppermute x25, waiting for transfers between devices: 8.04 us -> 6.44 us  [swap(): return lax.ppermute(value, axis, [(at, at ^ step) for at in range(size)])]
  transfers between devices with their start and end apart: 25 -> 25, of which waited for: 9 -> 8; matrix products, arithmetic and copies ran while one was open for 0% -> 0% of each run, Pallas kernels for 40% -> 40%
where the time goes in v8:
time: 71.3 us; the launch traced here: 71.1 us
  starting transfers between devices  32.1 us (45%)
  Pallas kernels  30.7 us (43%)
  waiting for transfers between devices  6.44 us (9%)
  other arithmetic  1.03 us (1%)
  between operations  0.88 us (1%)
    ppermute x25, starting transfers between devices, swap(): return lax.ppermute(value, axis, [(at, at ^ step) for at in range(size)])  32.1 us
    pallas_call x26, Pallas kernels, call(): pl.pallas_call(body, in_specs=(in_specs or [IN_VMEM] * count) + [IN_VMEM]...  30.7 us
    ppermute x25, waiting for transfers between devices, swap(): return lax.ppermute(value, axis, [(at, at ^ step) for at in range(size)])  6.44 us
  transfers between devices with their start and end apart: 25, of which 8 were waited for; matrix products, arithmetic and copies ran while one was open for 0% of the time, Pallas kernels for 40%

profile of v8, /device:TPU:0, one launch (start us, length us, event | category | flops | bytes accessed | tf_op | source)
XLA Modules:
  0.0 71.1 jit_solution(10019015454487774828)
XLA Ops:
  0.6 0.0 slice-start
  0.6 1.0 %pad_maximum_fusion.refs_0_ = bf16[40,1280]{1,0:T(8,128)(2,1)S(1)} fusion(bf16[20,1280]{1,0:T(8,128)(2,1)} %param.6, bf16[20,1280]{1,0:T(8,128)(2,1)} %param.5), kind=kLoop, calls=%fused_computation | loop fusion | flops 204800 | bytes 204800 | tf_op jit(solution)/shard_map/concatenate | solution.py:392
  1.7 0.0 slice-start.1
  1.7 0.0 slice-start.2
  1.7 3.1 %collective-permute-start = (bf16[40,1280]{1,0:T(8,128)(2,1)S(1)}, bf16[40,1280]{1,0:T(8,128)(2,1)S(1)}, u32[]{:S(2)}, u32[]{:S(2)}) collective-permute-start(bf16[40,1280]{1,0:T(8,128)(2,1)S(1)} %pad_maximum_fusion.refs_0_), channel_id=1, source_target_pairs={{0,2},{2,0},{4,6},{6,4},{1,3},{3,1},{5,7},{7,5},{8,10},{10,8},{12,... | collective-permute-start | bytes 307208 | tf_op jit(solution)/shard_map/ppermute | solution.py:381
  4.8 2.6 %collective-permute-start.1 = (bf16[40,1280]{1,0:T(8,128)(2,1)S(1)}, bf16[40,1280]{1,0:T(8,128)(2,1)S(1)}, u32[]{:S(2)}, u32[]{:S(2)}) collective-permute-start(bf16[40,1280]{1,0:T(8,128)(2,1)S(1)} %pad_maximum_fusion.refs_0_), channel_id=1, source_target_pairs={{0,4},{2,6},{4,0},{6,2},{1,5},{3,7},{5,1},{7,3},{8,12},{10,14},{12... | collective-permute-start | bytes 307208 | tf_op jit(solution)/shard_map/ppermute | solution.py:381
  7.4 0.0 collective-permute-start.2
  7.4 6.8 %load_kernel.1 = (bf16[1280,3456]{1,0:T(8,128)(2,1)S(1)}, bf16[1280,3456]{1,0:T(8,128)(2,1)S(1)}, f32[8,128]{1,0:T(8,128)}) custom-call(bf16[1280,3456]{1,0:T(8,128)(2,1)} %refs_0_.1, bf16[1280,3456]{1,0:T(8,128)(2,1)} %refs_1_.1), custom_call_target="tpu_custom_call" | custom-call | flops 1 | bytes 1 | tf_op jit(solution)/shard_map/load_kernel/pallas_call | solution.py:62
  14.2 0.0 collective-permute-done.refs_1_
  14.2 1.3 %collective-permute-done.1.refs_2_ = bf16[40,1280]{1,0:T(8,128)(2,1)S(1)} collective-permute-done((bf16[40,1280]{1,0:T(8,128)(2,1)S(1)}, bf16[40,1280]{1,0:T(8,128)(2,1)S(1)}, u32[]{:S(2)}, u32[]{:S(2)}) %collective-permute-start.1) | collective-permute-done | bytes 102432 | tf_op jit(solution)/shard_map/ppermute | solution.py:381
  15.5 0.0 collective-permute-done.2.refs_3_
  15.5 0.2 order_kernel.1
  15.7 1.5 %forward_kernel.4 = (f32[120,896]{1,0:T(8,128)S(1)}, bf16[120,896]{1,0:T(8,128)(2,1)S(1)}, f32[8,128]{1,0:T(8,128)S(1)}) custom-call(bf16[160,1280]{1,0:T(8,128)(2,1)S(1)} %get-tuple-element.72.refs_0_, bf16[1280,3456]{1,0:T(8,128)(2,1)S(1)} %get-tuple-element.73.refs_1_.refs_6_, bf16[1280,3456]{1,0:T(8,128)(2,1)S(1)} %get-tuple-element.74.refs_2_.refs_7_, ...), custom_call_target="tpu_custom_call" | custom-call | flops 1 | bytes 1 | tf_op jit(solution)/shard_map/forward_kernel/pallas_call | solution.py:62
  17.3 1.6 %collective-permute-start.6 = (bf16[120,896]{1,0:T(8,128)(2,1)S(1)}, bf16[120,896]{1,0:T(8,128)(2,1)S(1)}, u32[]{:S(2)}, u32[]{:S(2)}) collective-permute-start(bf16[120,896]{1,0:T(8,128)(2,1)S(1)} %get-tuple-element.83), channel_id=1, source_target_pairs={{0,8},{8,0},{16,24},{24,16},{1,9},{9,1},{17,25},{25,17},{2,10},{10... | collective-permute-start | bytes 645128 | tf_op jit(solution)/shard_map/ppermute | solution.py:381
  18.8 1.5 %forward_kernel.5 = (f32[120,896]{1,0:T(8,128)S(1)}, bf16[120,896]{1,0:T(8,128)(2,1)S(1)}, f32[8,128]{1,0:T(8,128)S(1)}) custom-call(bf16[160,1280]{1,0:T(8,128)(2,1)S(1)} %get-tuple-element.72.refs_0_, bf16[1280,3456]{1,0:T(8,128)(2,1)S(1)} %get-tuple-element.73.refs_1_.refs_6_, bf16[1280,3456]{1,0:T(8,128)(2,1)S(1)} %get-tuple-element.74.refs_2_.refs_7_, ...), custom_call_target="tpu_custom_call" | custom-call | flops 1 | bytes 1 | tf_op jit(solution)/shard_map/forward_kernel/pallas_call | solution.py:62
  20.3 1.6 %collective-permute-start.5 = (bf16[120,896]{1,0:T(8,128)(2,1)S(1)}, bf16[120,896]{1,0:T(8,128)(2,1)S(1)}, u32[]{:S(2)}, u32[]{:S(2)}) collective-permute-start(bf16[120,896]{1,0:T(8,128)(2,1)S(1)} %get-tuple-element.81), channel_id=1, source_target_pairs={{0,16},{8,24},{16,0},{24,8},{1,17},{9,25},{17,1},{25,9},{2,18},{10... | collective-permute-start | bytes 645128 | tf_op jit(solution)/shard_map/ppermute | solution.py:381
  21.9 1.5 %forward_kernel.6 = (f32[120,896]{1,0:T(8,128)S(1)}, bf16[120,896]{1,0:T(8,128)(2,1)S(1)}, f32[8,128]{1,0:T(8,128)S(1)}) custom-call(bf16[160,1280]{1,0:T(8,128)(2,1)S(1)} %get-tuple-element.72.refs_0_, bf16[1280,3456]{1,0:T(8,128)(2,1)S(1)} %get-tuple-element.73.refs_1_.refs_6_, bf16[1280,3456]{1,0:T(8,128)(2,1)S(1)} %get-tuple-element.74.refs_2_.refs_7_, ...), custom_call_target="tpu_custom_call" | custom-call | flops 1 | bytes 1 | tf_op jit(solution)/shard_map/forward_kernel/pallas_call | solution.py:62
  23.4 0.6 collective-permute-start.4
  24.0 1.4 %forward_kernel.7 = (f32[120,768]{1,0:T(8,128)S(1)}, bf16[120,768]{1,0:T(8,128)(2,1)S(1)}, f32[8,128]{1,0:T(8,128)S(1)}) custom-call(bf16[160,1280]{1,0:T(8,128)(2,1)S(1)} %get-tuple-element.72.refs_0_, bf16[1280,3456]{1,0:T(8,128)(2,1)S(1)} %get-tuple-element.73.refs_1_.refs_6_, bf16[1280,3456]{1,0:T(8,128)(2,1)S(1)} %get-tuple-element.74.refs_2_.refs_7_, ...), custom_call_target="tpu_custom_call" | custom-call | flops 1 | bytes 1 | tf_op jit(solution)/shard_map/forward_kernel/pallas_call | solution.py:62
  25.4 0.6 collective-permute-start.8
  26.0 0.0 collective-permute-done.6.refs_1_
  26.0 0.1 halve_kernel.4
  26.1 1.3 %collective-permute-done.5.refs_1_ = bf16[120,896]{1,0:T(8,128)(2,1)S(1)} collective-permute-done((bf16[120,896]{1,0:T(8,128)(2,1)S(1)}, bf16[120,896]{1,0:T(8,128)(2,1)S(1)}, u32[]{:S(2)}, u32[]{:S(2)}) %collective-permute-start.5) | collective-permute-done | bytes 215072 | tf_op jit(solution)/shard_map/ppermute | solution.py:381
  27.4 0.1 halve_kernel.5
  27.4 0.3 collective-permute-start.11
  27.7 2.3 %collective-permute-start.10 = (bf16[60,896]{1,0:T(8,128)(2,1)S(1)}, bf16[60,896]{1,0:T(8,128)(2,1)S(1)}, u32[]{:S(2)}, u32[]{:S(2)}) collective-permute-start(bf16[60,896]{1,0:T(8,128)(2,1)S(1)} %get-tuple-element.96), channel_id=1, source_target_pairs={{0,16},{8,24},{16,0},{24,8},{1,17},{9,25},{17,1},{25,9},{2,18},{10... | collective-permute-start | bytes 322568 | tf_op jit(solution)/shard_map/ppermute | solution.py:381
  30.1 0.0 collective-permute-start.3
  30.1 0.0 collective-permute-done.4.refs_1_
  30.1 0.1 halve_kernel.6
  30.1 0.9 %collective-permute-start.7 = (bf16[60,896]{1,0:T(8,128)(2,1)S(1)}, bf16[60,896]{1,0:T(8,128)(2,1)S(1)}, u32[]{:S(2)}, u32[]{:S(2)}) collective-permute-start(bf16[60,896]{1,0:T(8,128)(2,1)S(1)} %get-tuple-element.89), channel_id=1, source_target_pairs={{0,16},{8,24},{16,0},{24,8},{1,17},{9,25},{17,1},{25,9},{2,18},{10... | collective-permute-start | bytes 322568 | tf_op jit(solution)/shard_map/ppermute | solution.py:381
  31.0 0.5 collective-permute-done.8.refs_1_
  31.5 1.2 %collective-permute-start.9 = (bf16[60,768]{1,0:T(8,128)(2,1)S(1)}, bf16[60,768]{1,0:T(8,128)(2,1)S(1)}, u32[]{:S(2)}, u32[]{:S(2)}) collective-permute-start(bf16[60,768]{1,0:T(8,128)(2,1)S(1)} %get-tuple-element.94), channel_id=1, source_target_pairs={{0,8},{8,0},{16,24},{24,16},{1,9},{9,1},{17,25},{25,17},{2,10},{10... | collective-permute-start | bytes 276488 | tf_op jit(solution)/shard_map/ppermute | solution.py:381
  32.7 0.0 collective-permute-done.11.refs_1_
  32.7 0.1 middle_kernel.4
  32.7 2.2 %collective-permute-start.15 = (bf16[60,896]{1,0:T(8,128)(2,1)S(1)}, bf16[60,896]{1,0:T(8,128)(2,1)S(1)}, u32[]{:S(2)}, u32[]{:S(2)}) collective-permute-start(bf16[60,896]{1,0:T(8,128)(2,1)S(1)} %get-tuple-element.106.refs_0_), channel_id=1, source_target_pairs={{0,16},{8,24},{16,0},{24,8},{1,17},{9,25},{17,1},{25,9},{2,18},{10... | collective-permute-start | bytes 322568 | tf_op jit(solution)/shard_map/ppermute | solution.py:381
  34.9 0.0 collective-permute-done.10.refs_1_
  34.9 0.1 middle_kernel.5
  35.0 0.7 collective-permute-start.14
  35.7 0.5 collective-permute-done.9.refs_1_
  36.2 0.1 middle_kernel.6
  36.3 0.1 middle_kernel.7
  36.3 1.9 %collective-permute-start.12 = (bf16[60,896]{1,0:T(8,128)(2,1)S(1)}, bf16[60,896]{1,0:T(8,128)(2,1)S(1)}, u32[]{:S(2)}, u32[]{:S(2)}) collective-permute-start(bf16[60,896]{1,0:T(8,128)(2,1)S(1)} %get-tuple-element.103.refs_0_), channel_id=1, source_target_pairs={{0,8},{8,0},{16,24},{24,16},{1,9},{9,1},{17,25},{25,17},{2,10},{10... | collective-permute-start | bytes 322568 | tf_op jit(solution)/shard_map/ppermute | solution.py:381
  38.2 2.4 %collective-permute-start.13 = (bf16[60,768]{1,0:T(8,128)(2,1)S(1)}, bf16[60,768]{1,0:T(8,128)(2,1)S(1)}, u32[]{:S(2)}, u32[]{:S(2)}) collective-permute-start(bf16[60,768]{1,0:T(8,128)(2,1)S(1)} %get-tuple-element.104.refs_0_), channel_id=1, source_target_pairs={{0,16},{8,24},{16,0},{24,8},{1,17},{9,25},{17,1},{25,9},{2,18},{10... | collective-permute-start | bytes 276488 | tf_op jit(solution)/shard_map/ppermute | solution.py:381
  40.6 0.2 collective-permute-done.14.refs_1_
  40.9 1.3 %collective-permute-start.16 = (bf16[120,896]{1,0:T(8,128)(2,1)S(1)}, bf16[120,896]{1,0:T(8,128)(2,1)S(1)}, u32[]{:S(2)}, u32[]{:S(2)}) collective-permute-start(bf16[120,896]{1,0:T(8,128)(2,1)S(1)} %get-tuple-element.114.refs_0_), channel_id=1, source_target_pairs={{0,16},{8,24},{16,0},{24,8},{1,17},{9,25},{17,1},{25,9},{2,18},{10... | collective-permute-start | bytes 645128 | tf_op jit(solution)/shard_map/ppermute | solution.py:381
  42.3 1.7 %collective-permute-start.17 = (bf16[120,896]{1,0:T(8,128)(2,1)S(1)}, bf16[120,896]{1,0:T(8,128)(2,1)S(1)}, u32[]{:S(2)}, u32[]{:S(2)}) collective-permute-start(bf16[120,896]{1,0:T(8,128)(2,1)S(1)} %get-tuple-element.115.refs_2_), channel_id=1, source_target_pairs={{0,8},{8,0},{16,24},{24,16},{1,9},{9,1},{17,25},{25,17},{2,10},{10... | collective-permute-start | bytes 645128 | tf_op jit(solution)/shard_map/ppermute | solution.py:381
  44.0 0.2 collective-permute-done.13.refs_1_
  44.3 1.9 %collective-permute-start.19 = (bf16[120,896]{1,0:T(8,128)(2,1)S(1)}, bf16[120,896]{1,0:T(8,128)(2,1)S(1)}, u32[]{:S(2)}, u32[]{:S(2)}) collective-permute-start(bf16[120,896]{1,0:T(8,128)(2,1)S(1)} %get-tuple-element.120.refs_0_), channel_id=1, source_target_pairs={{0,16},{8,24},{16,0},{24,8},{1,17},{9,25},{17,1},{25,9},{2,18},{10... | collective-permute-start | bytes 645128 | tf_op jit(solution)/shard_map/ppermute | solution.py:381
  46.2 0.3 collective-permute-start.20
  46.5 0.3 factors_kernel.1
  46.7 2.3 %collective-permute-done.16.refs_1_ = bf16[120,896]{1,0:T(8,128)(2,1)S(1)} collective-permute-done((bf16[120,896]{1,0:T(8,128)(2,1)S(1)}, bf16[120,896]{1,0:T(8,128)(2,1)S(1)}, u32[]{:S(2)}, u32[]{:S(2)}) %collective-permute-start.16) | collective-permute-done | bytes 215072 | tf_op jit(solution)/shard_map/ppermute | solution.py:381
  49.0 0.1 collective-permute-done.17.refs_3_
  49.1 0.1 stack_kernel.2
  49.2 0.1 collective-permute-start.18
  49.3 2.9 %input_grad_kernel.1 = (f32[80,1280]{1,0:T(8,128)S(1)}, f32[8,128]{1,0:T(8,128)S(1)}) custom-call(bf16[240,1792]{1,0:T(8,128)(2,1)S(1)} %get-tuple-element.117.refs_0_.refs_2_, bf16[1280,3456]{1,0:T(8,128)(2,1)S(1)} %get-tuple-element.73.refs_1_.refs_6_, bf16[1280,3456]{1,0:T(8,128)(2,1)S(1)} %get-tuple-element.74.refs_2_.refs_7_, ...), custom_call_target="tpu_custom_call" | custom-call | flops 1 | bytes 1 | tf_op jit(solution)/shard_map/input_grad_kernel/pallas_call | solution.py:62
  52.2 0.1 stack_kernel.3
  52.3 0.6 collective-permute-start.24
  52.8 7.7 %first_grads_kernel.1 = (bf16[1280,3456]{1,0:T(8,128)(2,1)}, bf16[1280,3456]{1,0:T(8,128)(2,1)}, bf16[3456,1280]{1,0:T(8,128)(2,1)}, f32[80,1280]{1,0:T(8,128)S(1)}, f32[8,128]{1,0:T(8,128)S(1)}) custom-call(bf16[1280,160]{1,0:T(8,128)(2,1)S(1)} %get-tuple-element.112.refs_0_, bf16[160,1280]{1,0:T(8,128)(2,1)S(1)} %get-tuple-element.113.refs_1_, ...), custom_call_target="tpu_custom_call" | custom-call | flops 1 | bytes 1 | tf_op jit(solution)/shard_map/first_grads_kernel/pallas_call | solution.py:62
  60.5 0.2 last_kernel.1
  60.7 1.0 %collective-permute-start.21 = (bf16[20,1280]{1,0:T(8,128)(2,1)S(1)}, bf16[20,1280]{1,0:T(8,128)(2,1)S(1)}, u32[]{:S(2)}, u32[]{:S(2)}) collective-permute-start(bf16[20,1280]{1,0:T(8,128)(2,1)S(1)} %get-tuple-element.128), channel_id=1, source_target_pairs={{0,2},{2,0},{4,6},{6,4},{1,3},{3,1},{5,7},{7,5},{8,10},{10,8},{12,... | collective-permute-start | bytes 153608 | tf_op jit(solution)/shard_map/ppermute | solution.py:381
  61.7 1.3 %collective-permute-start.22 = (bf16[20,1280]{1,0:T(8,128)(2,1)S(1)}, bf16[20,1280]{1,0:T(8,128)(2,1)S(1)}, u32[]{:S(2)}, u32[]{:S(2)}) collective-permute-start(bf16[20,1280]{1,0:T(8,128)(2,1)S(1)} %get-tuple-element.129), channel_id=1, source_target_pairs={{0,4},{2,6},{4,0},{6,2},{1,5},{3,7},{5,1},{7,3},{8,12},{10,14},{12... | collective-permute-start | bytes 153608 | tf_op jit(solution)/shard_map/ppermute | solution.py:381
  63.0 2.1 %collective-permute-start.23 = (bf16[20,1280]{1,0:T(8,128)(2,1)S(1)}, bf16[20,1280]{1,0:T(8,128)(2,1)S(1)}, u32[]{:S(2)}, u32[]{:S(2)}) collective-permute-start(bf16[20,1280]{1,0:T(8,128)(2,1)S(1)} %get-tuple-element.130), channel_id=1, source_target_pairs={{0,6},{2,4},{4,2},{6,0},{1,7},{3,5},{5,3},{7,1},{8,14},{10,12},{12... | collective-permute-start | bytes 153608 | tf_op jit(solution)/shard_map/ppermute | solution.py:381
  65.1 5.3 %weight_grad_kernel.1 = (bf16[1280,3456]{1,0:T(8,128)(2,1)}, bf16[1280,3456]{1,0:T(8,128)(2,1)}, bf16[3456,1280]{1,0:T(8,128)(2,1)}, f32[8,128]{1,0:T(8,128)S(1)}) custom-call(bf16[1280,160]{1,0:T(8,128)(2,1)S(1)} %get-tuple-element.112.refs_0_, ...), custom_call_target="tpu_custom_call", output_to_operand_aliasing={{0}: (4, {}), {1}: (5, {}), {2}: (6, {})} | custom-call | flops 1 | bytes 1 | tf_op jit(solution)/shard_map/weight_grad_kernel/pallas_call | solution.py:62
  70.5 0.7 total_kernel.1
  (20 shorter events, 0.2 us)
Async XLA Ops:
  0.6 15.1 %slice-start = ((s8[8847360]{0:T(1024)(128)(4,1)}), s8[4194304]{0:T(1024)(128)(4,1)S(1)}, s32[]{:S(2)}) async-start(s8[8847360]{0:T(1024)(128)(4,1)} %bitcast), calls=%async_computation | async-start | bytes 8388608
  1.7 14.0 %slice-start.1 = ((s8[8847360]{0:T(1024)(128)(4,1)}), s8[4194304]{0:T(1024)(128)(4,1)S(1)}, s32[]{:S(2)}) async-start(s8[8847360]{0:T(1024)(128)(4,1)} %bitcast), calls=%async_computation.1 | async-start | bytes 8388608
  1.7 14.0 %slice-start.2 = ((s8[8847360]{0:T(1024)(128)(4,1)}), s8[458752]{0:T(1024)(128)(4,1)S(1)}, s32[]{:S(2)}) async-start(s8[8847360]{0:T(1024)(128)(4,1)} %bitcast), calls=%async_computation.2 | async-start | bytes 917504
  1.7 12.5 %collective-permute-start = (bf16[40,1280]{1,0:T(8,128)(2,1)S(1)}, bf16[40,1280]{1,0:T(8,128)(2,1)S(1)}, u32[]{:S(2)}, u32[]{:S(2)}) collective-permute-start(bf16[40,1280]{1,0:T(8,128)(2,1)S(1)} %pad_maximum_fusion.refs_0_), channel_id=1, source_target_pairs={{0,2},{2,0},{4,6},{6,4},{1,3},{3,1},{5,7},{7,5},{8,10},{10,8},{12,... | collective-permute-start | bytes 307208 | tf_op jit(solution)/shard_map/ppermute | solution.py:381
  4.8 10.7 %collective-permute-start.1 = (bf16[40,1280]{1,0:T(8,128)(2,1)S(1)}, bf16[40,1280]{1,0:T(8,128)(2,1)S(1)}, u32[]{:S(2)}, u32[]{:S(2)}) collective-permute-start(bf16[40,1280]{1,0:T(8,128)(2,1)S(1)} %pad_maximum_fusion.refs_0_), channel_id=1, source_target_pairs={{0,4},{2,6},{4,0},{6,2},{1,5},{3,7},{5,1},{7,3},{8,12},{10,14},{12... | collective-permute-start | bytes 307208 | tf_op jit(solution)/shard_map/ppermute | solution.py:381
  7.4 8.1 %collective-permute-start.2 = (bf16[40,1280]{1,0:T(8,128)(2,1)S(1)}, bf16[40,1280]{1,0:T(8,128)(2,1)S(1)}, u32[]{:S(2)}, u32[]{:S(2)}) collective-permute-start(bf16[40,1280]{1,0:T(8,128)(2,1)S(1)} %pad_maximum_fusion.refs_0_), channel_id=1, source_target_pairs={{0,6},{2,4},{4,2},{6,0},{1,7},{3,5},{5,3},{7,1},{8,14},{10,12},{12... | collective-permute-start | bytes 307208 | tf_op jit(solution)/shard_map/ppermute | solution.py:381
  17.3 8.8 %collective-permute-start.6 = (bf16[120,896]{1,0:T(8,128)(2,1)S(1)}, bf16[120,896]{1,0:T(8,128)(2,1)S(1)}, u32[]{:S(2)}, u32[]{:S(2)}) collective-permute-start(bf16[120,896]{1,0:T(8,128)(2,1)S(1)} %get-tuple-element.83), channel_id=1, source_target_pairs={{0,8},{8,0},{16,24},{24,16},{1,9},{9,1},{17,25},{25,17},{2,10},{10... | collective-permute-start | bytes 645128 | tf_op jit(solution)/shard_map/ppermute | solution.py:381
  20.3 7.0 %collective-permute-start.5 = (bf16[120,896]{1,0:T(8,128)(2,1)S(1)}, bf16[120,896]{1,0:T(8,128)(2,1)S(1)}, u32[]{:S(2)}, u32[]{:S(2)}) collective-permute-start(bf16[120,896]{1,0:T(8,128)(2,1)S(1)} %get-tuple-element.81), channel_id=1, source_target_pairs={{0,16},{8,24},{16,0},{24,8},{1,17},{9,25},{17,1},{25,9},{2,18},{10... | collective-permute-start | bytes 645128 | tf_op jit(solution)/shard_map/ppermute | solution.py:381
  23.4 6.6 %collective-permute-start.4 = (bf16[120,896]{1,0:T(8,128)(2,1)S(1)}, bf16[120,896]{1,0:T(8,128)(2,1)S(1)}, u32[]{:S(2)}, u32[]{:S(2)}) collective-permute-start(bf16[120,896]{1,0:T(8,128)(2,1)S(1)} %get-tuple-element.79), channel_id=1, source_target_pairs={{0,8},{8,0},{16,24},{24,16},{1,9},{9,1},{17,25},{25,17},{2,10},{10... | collective-permute-start | bytes 645128 | tf_op jit(solution)/shard_map/ppermute | solution.py:381
  25.4 6.0 %collective-permute-start.8 = (bf16[120,768]{1,0:T(8,128)(2,1)S(1)}, bf16[120,768]{1,0:T(8,128)(2,1)S(1)}, u32[]{:S(2)}, u32[]{:S(2)}) collective-permute-start(bf16[120,768]{1,0:T(8,128)(2,1)S(1)} %get-tuple-element.91), channel_id=1, source_target_pairs={{0,16},{8,24},{16,0},{24,8},{1,17},{9,25},{17,1},{25,9},{2,18},{10... | collective-permute-start | bytes 552968 | tf_op jit(solution)/shard_map/ppermute | solution.py:381
  27.4 5.2 %collective-permute-start.11 = (bf16[60,896]{1,0:T(8,128)(2,1)S(1)}, bf16[60,896]{1,0:T(8,128)(2,1)S(1)}, u32[]{:S(2)}, u32[]{:S(2)}) collective-permute-start(bf16[60,896]{1,0:T(8,128)(2,1)S(1)} %get-tuple-element.98), channel_id=1, source_target_pairs={{0,8},{8,0},{16,24},{24,16},{1,9},{9,1},{17,25},{25,17},{2,10},{10... | collective-permute-start | bytes 322568 | tf_op jit(solution)/shard_map/ppermute | solution.py:381
  27.7 7.2 %collective-permute-start.10 = (bf16[60,896]{1,0:T(8,128)(2,1)S(1)}, bf16[60,896]{1,0:T(8,128)(2,1)S(1)}, u32[]{:S(2)}, u32[]{:S(2)}) collective-permute-start(bf16[60,896]{1,0:T(8,128)(2,1)S(1)} %get-tuple-element.96), channel_id=1, source_target_pairs={{0,16},{8,24},{16,0},{24,8},{1,17},{9,25},{17,1},{25,9},{2,18},{10... | collective-permute-start | bytes 322568 | tf_op jit(solution)/shard_map/ppermute | solution.py:381
  30.1 16.4 %collective-permute-start.3 = (bf16[160,1280]{1,0:T(8,128)(2,1)S(1)}, bf16[160,1280]{1,0:T(8,128)(2,1)S(1)}, u32[]{:S(2)}, u32[]{:S(2)}) collective-permute-start(bf16[160,1280]{1,0:T(8,128)(2,1)S(1)} %get-tuple-element.72.refs_0_), channel_id=1, source_target_pairs={{0,1},{1,0},{2,3},{3,2},{4,5},{5,4},{6,7},{7,6},{8,9},{9,8},{10,11... | collective-permute-start | bytes 1228808 | tf_op jit(solution)/shard_map/ppermute | solution.py:381
  30.1 6.1 %collective-permute-start.7 = (bf16[60,896]{1,0:T(8,128)(2,1)S(1)}, bf16[60,896]{1,0:T(8,128)(2,1)S(1)}, u32[]{:S(2)}, u32[]{:S(2)}) collective-permute-start(bf16[60,896]{1,0:T(8,128)(2,1)S(1)} %get-tuple-element.89), channel_id=1, source_target_pairs={{0,16},{8,24},{16,0},{24,8},{1,17},{9,25},{17,1},{25,9},{2,18},{10... | collective-permute-start | bytes 322568 | tf_op jit(solution)/shard_map/ppermute | solution.py:381
  31.5 4.7 %collective-permute-start.9 = (bf16[60,768]{1,0:T(8,128)(2,1)S(1)}, bf16[60,768]{1,0:T(8,128)(2,1)S(1)}, u32[]{:S(2)}, u32[]{:S(2)}) collective-permute-start(bf16[60,768]{1,0:T(8,128)(2,1)S(1)} %get-tuple-element.94), channel_id=1, source_target_pairs={{0,8},{8,0},{16,24},{24,16},{1,9},{9,1},{17,25},{25,17},{2,10},{10... | collective-permute-start | bytes 276488 | tf_op jit(solution)/shard_map/ppermute | solution.py:381
  32.7 7.9 %collective-permute-start.15 = (bf16[60,896]{1,0:T(8,128)(2,1)S(1)}, bf16[60,896]{1,0:T(8,128)(2,1)S(1)}, u32[]{:S(2)}, u32[]{:S(2)}) collective-permute-start(bf16[60,896]{1,0:T(8,128)(2,1)S(1)} %get-tuple-element.106.refs_0_), channel_id=1, source_target_pairs={{0,16},{8,24},{16,0},{24,8},{1,17},{9,25},{17,1},{25,9},{2,18},{10... | collective-permute-start | bytes 322568 | tf_op jit(solution)/shard_map/ppermute | solution.py:381
  35.0 5.9 %collective-permute-start.14 = (bf16[60,896]{1,0:T(8,128)(2,1)S(1)}, bf16[60,896]{1,0:T(8,128)(2,1)S(1)}, u32[]{:S(2)}, u32[]{:S(2)}) collective-permute-start(bf16[60,896]{1,0:T(8,128)(2,1)S(1)} %get-tuple-element.105.refs_0_), channel_id=1, source_target_pairs={{0,8},{8,0},{16,24},{24,16},{1,9},{9,1},{17,25},{25,17},{2,10},{10... | collective-permute-start | bytes 322568 | tf_op jit(solution)/shard_map/ppermute | solution.py:381
  36.3 7.9 %collective-permute-start.12 = (bf16[60,896]{1,0:T(8,128)(2,1)S(1)}, bf16[60,896]{1,0:T(8,128)(2,1)S(1)}, u32[]{:S(2)}, u32[]{:S(2)}) collective-permute-start(bf16[60,896]{1,0:T(8,128)(2,1)S(1)} %get-tuple-element.103.refs_0_), channel_id=1, source_target_pairs={{0,8},{8,0},{16,24},{24,16},{1,9},{9,1},{17,25},{25,17},{2,10},{10... | collective-permute-start | bytes 322568 | tf_op jit(solution)/shard_map/ppermute | solution.py:381
  38.2 6.0 %collective-permute-start.13 = (bf16[60,768]{1,0:T(8,128)(2,1)S(1)}, bf16[60,768]{1,0:T(8,128)(2,1)S(1)}, u32[]{:S(2)}, u32[]{:S(2)}) collective-permute-start(bf16[60,768]{1,0:T(8,128)(2,1)S(1)} %get-tuple-element.104.refs_0_), channel_id=1, source_target_pairs={{0,16},{8,24},{16,0},{24,8},{1,17},{9,25},{17,1},{25,9},{2,18},{10... | collective-permute-start | bytes 276488 | tf_op jit(solution)/shard_map/ppermute | solution.py:381
  40.9 8.1 %collective-permute-start.16 = (bf16[120,896]{1,0:T(8,128)(2,1)S(1)}, bf16[120,896]{1,0:T(8,128)(2,1)S(1)}, u32[]{:S(2)}, u32[]{:S(2)}) collective-permute-start(bf16[120,896]{1,0:T(8,128)(2,1)S(1)} %get-tuple-element.114.refs_0_), channel_id=1, source_target_pairs={{0,16},{8,24},{16,0},{24,8},{1,17},{9,25},{17,1},{25,9},{2,18},{10... | collective-permute-start | bytes 645128 | tf_op jit(solution)/shard_map/ppermute | solution.py:381
  42.3 6.8 %collective-permute-start.17 = (bf16[120,896]{1,0:T(8,128)(2,1)S(1)}, bf16[120,896]{1,0:T(8,128)(2,1)S(1)}, u32[]{:S(2)}, u32[]{:S(2)}) collective-permute-start(bf16[120,896]{1,0:T(8,128)(2,1)S(1)} %get-tuple-element.115.refs_2_), channel_id=1, source_target_pairs={{0,8},{8,0},{16,24},{24,16},{1,9},{9,1},{17,25},{25,17},{2,10},{10... | collective-permute-start | bytes 645128 | tf_op jit(solution)/shard_map/ppermute | solution.py:381
  44.3 7.8 %collective-permute-start.19 = (bf16[120,896]{1,0:T(8,128)(2,1)S(1)}, bf16[120,896]{1,0:T(8,128)(2,1)S(1)}, u32[]{:S(2)}, u32[]{:S(2)}) collective-permute-start(bf16[120,896]{1,0:T(8,128)(2,1)S(1)} %get-tuple-element.120.refs_0_), channel_id=1, source_target_pairs={{0,16},{8,24},{16,0},{24,8},{1,17},{9,25},{17,1},{25,9},{2,18},{10... | collective-permute-start | bytes 645128 | tf_op jit(solution)/shard_map/ppermute | solution.py:381
  46.2 5.9 %collective-permute-start.20 = (bf16[120,768]{1,0:T(8,128)(2,1)S(1)}, bf16[120,768]{1,0:T(8,128)(2,1)S(1)}, u32[]{:S(2)}, u32[]{:S(2)}) collective-permute-start(bf16[120,768]{1,0:T(8,128)(2,1)S(1)} %get-tuple-element.121.refs_2_), channel_id=1, source_target_pairs={{0,8},{8,0},{16,24},{24,16},{1,9},{9,1},{17,25},{25,17},{2,10},{10... | collective-permute-start | bytes 552968 | tf_op jit(solution)/shard_map/ppermute | solution.py:381
  49.2 3.6 %collective-permute-start.18 = (bf16[240,1792]{1,0:T(8,128)(2,1)S(1)}, bf16[240,1792]{1,0:T(8,128)(2,1)S(1)}, u32[]{:S(2)}, u32[]{:S(2)}) collective-permute-start(bf16[240,1792]{1,0:T(8,128)(2,1)S(1)} %get-tuple-element.117.refs_0_.refs_2_), channel_id=1, source_target_pairs={{0,1},{1,0},{2,3},{3,2},{4,5},{5,4},{6,7},{7,6},{8,9},{9,8},{10,11... | collective-permute-start | bytes 2580488 | tf_op jit(solution)/shard_map/ppermute | solution.py:381
  52.3 12.9 %collective-permute-start.24 = (bf16[240,1792]{1,0:T(8,128)(2,1)S(1)}, bf16[240,1792]{1,0:T(8,128)(2,1)S(1)}, u32[]{:S(2)}, u32[]{:S(2)}) collective-permute-start(bf16[240,1792]{1,0:T(8,128)(2,1)S(1)} %get-tuple-element.123.refs_5_.refs_2_), channel_id=1, source_target_pairs={{0,1},{1,0},{2,3},{3,2},{4,5},{5,4},{6,7},{7,6},{8,9},{9,8},{10,11... | collective-permute-start | bytes 2580488 | tf_op jit(solution)/shard_map/ppermute | solution.py:381
  60.7 9.8 %collective-permute-start.21 = (bf16[20,1280]{1,0:T(8,128)(2,1)S(1)}, bf16[20,1280]{1,0:T(8,128)(2,1)S(1)}, u32[]{:S(2)}, u32[]{:S(2)}) collective-permute-start(bf16[20,1280]{1,0:T(8,128)(2,1)S(1)} %get-tuple-element.128), channel_id=1, source_target_pairs={{0,2},{2,0},{4,6},{6,4},{1,3},{3,1},{5,7},{7,5},{8,10},{10,8},{12,... | collective-permute-start | bytes 153608 | tf_op jit(solution)/shard_map/ppermute | solution.py:381
  61.7 8.8 %collective-permute-start.22 = (bf16[20,1280]{1,0:T(8,128)(2,1)S(1)}, bf16[20,1280]{1,0:T(8,128)(2,1)S(1)}, u32[]{:S(2)}, u32[]{:S(2)}) collective-permute-start(bf16[20,1280]{1,0:T(8,128)(2,1)S(1)} %get-tuple-element.129), channel_id=1, source_target_pairs={{0,4},{2,6},{4,0},{6,2},{1,5},{3,7},{5,1},{7,3},{8,12},{10,14},{12... | collective-permute-start | bytes 153608 | tf_op jit(solution)/shard_map/ppermute | solution.py:381
  63.0 7.5 %collective-permute-start.23 = (bf16[20,1280]{1,0:T(8,128)(2,1)S(1)}, bf16[20,1280]{1,0:T(8,128)(2,1)S(1)}, u32[]{:S(2)}, u32[]{:S(2)}) collective-permute-start(bf16[20,1280]{1,0:T(8,128)(2,1)S(1)} %get-tuple-element.130), channel_id=1, source_target_pairs={{0,6},{2,4},{4,2},{6,0},{1,7},{3,5},{5,3},{7,1},{8,14},{10,12},{12... | collective-permute-start | bytes 153608 | tf_op jit(solution)/shard_map/ppermute | solution.py:381

commit v9 on v8

--- a/solution.py
+++ b/solution.py
@@ -269,14 +269,20 @@
             mine, other = self.mine_ref[cut, here], self.other_ref[cut, here]
             self.both[at, :group, here] = jnp.where(first, mine, other)
             self.both[at, group:, here] = jnp.where(first, other, mine)
+        width = self.y_ref.shape[1]
+        blocks = [pl.ds(at, min(TILE, width - at)) for at in range(0, width, TILE)]
         for at, grad in enumerate((self.gate, self.up)):
-            grad[:, here] = jnp.dot(
-                self.xt_ref[...], self.both[at, :, here], preferred_element_type=F32
+            rows = self.both[at, :, here]
+            for block in blocks:
+                grad[block, here] = jnp.dot(
+                    self.xt_ref[block], rows, preferred_element_type=F32
+                ).astype(BF16)
+            self.send(at, grad.at[:, here], self.outs[at].at[:, there])
+        hidden = self.both[2, :, here].T
+        for block in blocks:
+            self.down[here, block] = jnp.dot(
+                hidden, self.y_ref[:, block], preferred_element_type=F32
             ).astype(BF16)
-            self.send(at, grad.at[:, here], self.outs[at].at[:, there])
-        self.down[here, :] = lax.dot_general(
-            self.both[2, :, here], self.y_ref[...], TN, preferred_element_type=F32
-        ).astype(BF16)
         self.send(2, self.down.at[here], self.outs[2].at[there])
 
     def wait(self):

time: 71.3 us -> 71 us (level)
  no operation moved by 1% of the time
where the time goes in v9:
time: 71 us; the launch traced here: 70.9 us
  starting transfers between devices  32.1 us (45%)
  Pallas kernels  30.4 us (43%)
  waiting for transfers between devices  6.44 us (9%)
  other arithmetic  1.03 us (1%)
  between operations  0.88 us (1%)
    ppermute x25, starting transfers between devices, swap(): return lax.ppermute(value, axis, [(at, at ^ step) for at in range(size)])  32.1 us
    pallas_call x26, Pallas kernels, call(): pl.pallas_call(body, in_specs=(in_specs or [IN_VMEM] * count) + [IN_VMEM]...  30.4 us
    ppermute x25, waiting for transfers between devices, swap(): return lax.ppermute(value, axis, [(at, at ^ step) for at in range(size)])  6.44 us
  transfers between devices with their start and end apart: 25, of which 8 were waited for; matrix products, arithmetic and copies ran while one was open for 0% of the time, Pallas kernels for 40%

profile of v9, /device:TPU:0, one launch (start us, length us, event | category | flops | bytes accessed | tf_op | source)
XLA Modules:
  0.0 70.9 jit_solution(16893650393615710591)
XLA Ops:
  0.6 0.0 slice-start
  0.6 1.0 %pad_maximum_fusion.refs_0_ = bf16[40,1280]{1,0:T(8,128)(2,1)S(1)} fusion(bf16[20,1280]{1,0:T(8,128)(2,1)} %param.6, bf16[20,1280]{1,0:T(8,128)(2,1)} %param.5), kind=kLoop, calls=%fused_computation | loop fusion | flops 204800 | bytes 204800 | tf_op jit(solution)/shard_map/concatenate | solution.py:398
  1.7 0.0 slice-start.1
  1.7 0.0 slice-start.2
  1.7 3.1 %collective-permute-start = (bf16[40,1280]{1,0:T(8,128)(2,1)S(1)}, bf16[40,1280]{1,0:T(8,128)(2,1)S(1)}, u32[]{:S(2)}, u32[]{:S(2)}) collective-permute-start(bf16[40,1280]{1,0:T(8,128)(2,1)S(1)} %pad_maximum_fusion.refs_0_), channel_id=1, source_target_pairs={{0,2},{2,0},{4,6},{6,4},{1,3},{3,1},{5,7},{7,5},{8,10},{10,8},{12,... | collective-permute-start | bytes 307208 | tf_op jit(solution)/shard_map/ppermute | solution.py:387
  4.8 2.6 %collective-permute-start.1 = (bf16[40,1280]{1,0:T(8,128)(2,1)S(1)}, bf16[40,1280]{1,0:T(8,128)(2,1)S(1)}, u32[]{:S(2)}, u32[]{:S(2)}) collective-permute-start(bf16[40,1280]{1,0:T(8,128)(2,1)S(1)} %pad_maximum_fusion.refs_0_), channel_id=1, source_target_pairs={{0,4},{2,6},{4,0},{6,2},{1,5},{3,7},{5,1},{7,3},{8,12},{10,14},{12... | collective-permute-start | bytes 307208 | tf_op jit(solution)/shard_map/ppermute | solution.py:387
  7.4 6.8 %load_kernel.1 = (bf16[1280,3456]{1,0:T(8,128)(2,1)S(1)}, bf16[1280,3456]{1,0:T(8,128)(2,1)S(1)}, f32[8,128]{1,0:T(8,128)}) custom-call(bf16[1280,3456]{1,0:T(8,128)(2,1)} %refs_0_.1, bf16[1280,3456]{1,0:T(8,128)(2,1)} %refs_1_.1), custom_call_target="tpu_custom_call" | custom-call | flops 1 | bytes 1 | tf_op jit(solution)/shard_map/load_kernel/pallas_call | solution.py:62
  14.2 0.0 collective-permute-done.refs_1_
  14.2 1.3 %collective-permute-done.1.refs_2_ = bf16[40,1280]{1,0:T(8,128)(2,1)S(1)} collective-permute-done((bf16[40,1280]{1,0:T(8,128)(2,1)S(1)}, bf16[40,1280]{1,0:T(8,128)(2,1)S(1)}, u32[]{:S(2)}, u32[]{:S(2)}) %collective-permute-start.1) | collective-permute-done | bytes 102432 | tf_op jit(solution)/shard_map/ppermute | solution.py:387
  15.5 0.2 order_kernel.1
  15.7 1.5 %forward_kernel.4 = (f32[120,896]{1,0:T(8,128)S(1)}, bf16[120,896]{1,0:T(8,128)(2,1)S(1)}, f32[8,128]{1,0:T(8,128)S(1)}) custom-call(bf16[160,1280]{1,0:T(8,128)(2,1)S(1)} %get-tuple-element.72.refs_0_, bf16[1280,3456]{1,0:T(8,128)(2,1)S(1)} %get-tuple-element.73.refs_1_.refs_6_, bf16[1280,3456]{1,0:T(8,128)(2,1)S(1)} %get-tuple-element.74.refs_2_.refs_7_, ...), custom_call_target="tpu_custom_call" | custom-call | flops 1 | bytes 1 | tf_op jit(solution)/shard_map/forward_kernel/pallas_call | solution.py:62
  17.3 1.6 %collective-permute-start.6 = (bf16[120,896]{1,0:T(8,128)(2,1)S(1)}, bf16[120,896]{1,0:T(8,128)(2,1)S(1)}, u32[]{:S(2)}, u32[]{:S(2)}) collective-permute-start(bf16[120,896]{1,0:T(8,128)(2,1)S(1)} %get-tuple-element.83), channel_id=1, source_target_pairs={{0,8},{8,0},{16,24},{24,16},{1,9},{9,1},{17,25},{25,17},{2,10},{10... | collective-permute-start | bytes 645128 | tf_op jit(solution)/shard_map/ppermute | solution.py:387
  18.8 1.5 %forward_kernel.5 = (f32[120,896]{1,0:T(8,128)S(1)}, bf16[120,896]{1,0:T(8,128)(2,1)S(1)}, f32[8,128]{1,0:T(8,128)S(1)}) custom-call(bf16[160,1280]{1,0:T(8,128)(2,1)S(1)} %get-tuple-element.72.refs_0_, bf16[1280,3456]{1,0:T(8,128)(2,1)S(1)} %get-tuple-element.73.refs_1_.refs_6_, bf16[1280,3456]{1,0:T(8,128)(2,1)S(1)} %get-tuple-element.74.refs_2_.refs_7_, ...), custom_call_target="tpu_custom_call" | custom-call | flops 1 | bytes 1 | tf_op jit(solution)/shard_map/forward_kernel/pallas_call | solution.py:62
  20.3 1.6 %collective-permute-start.5 = (bf16[120,896]{1,0:T(8,128)(2,1)S(1)}, bf16[120,896]{1,0:T(8,128)(2,1)S(1)}, u32[]{:S(2)}, u32[]{:S(2)}) collective-permute-start(bf16[120,896]{1,0:T(8,128)(2,1)S(1)} %get-tuple-element.81), channel_id=1, source_target_pairs={{0,16},{8,24},{16,0},{24,8},{1,17},{9,25},{17,1},{25,9},{2,18},{10... | collective-permute-start | bytes 645128 | tf_op jit(solution)/shard_map/ppermute | solution.py:387
  21.9 1.5 %forward_kernel.6 = (f32[120,896]{1,0:T(8,128)S(1)}, bf16[120,896]{1,0:T(8,128)(2,1)S(1)}, f32[8,128]{1,0:T(8,128)S(1)}) custom-call(bf16[160,1280]{1,0:T(8,128)(2,1)S(1)} %get-tuple-element.72.refs_0_, bf16[1280,3456]{1,0:T(8,128)(2,1)S(1)} %get-tuple-element.73.refs_1_.refs_6_, bf16[1280,3456]{1,0:T(8,128)(2,1)S(1)} %get-tuple-element.74.refs_2_.refs_7_, ...), custom_call_target="tpu_custom_call" | custom-call | flops 1 | bytes 1 | tf_op jit(solution)/shard_map/forward_kernel/pallas_call | solution.py:62
  23.4 0.6 collective-permute-start.4
  24.0 1.4 %forward_kernel.7 = (f32[120,768]{1,0:T(8,128)S(1)}, bf16[120,768]{1,0:T(8,128)(2,1)S(1)}, f32[8,128]{1,0:T(8,128)S(1)}) custom-call(bf16[160,1280]{1,0:T(8,128)(2,1)S(1)} %get-tuple-element.72.refs_0_, bf16[1280,3456]{1,0:T(8,128)(2,1)S(1)} %get-tuple-element.73.refs_1_.refs_6_, bf16[1280,3456]{1,0:T(8,128)(2,1)S(1)} %get-tuple-element.74.refs_2_.refs_7_, ...), custom_call_target="tpu_custom_call" | custom-call | flops 1 | bytes 1 | tf_op jit(solution)/shard_map/forward_kernel/pallas_call | solution.py:62
  25.4 0.6 collective-permute-start.8
  26.0 0.0 collective-permute-done.6.refs_1_
  26.0 0.1 halve_kernel.4
  26.1 1.3 %collective-permute-done.5.refs_1_ = bf16[120,896]{1,0:T(8,128)(2,1)S(1)} collective-permute-done((bf16[120,896]{1,0:T(8,128)(2,1)S(1)}, bf16[120,896]{1,0:T(8,128)(2,1)S(1)}, u32[]{:S(2)}, u32[]{:S(2)}) %collective-permute-start.5) | collective-permute-done | bytes 215072 | tf_op jit(solution)/shard_map/ppermute | solution.py:387
  27.4 0.1 halve_kernel.5
  27.4 0.3 collective-permute-start.11
  27.7 2.3 %collective-permute-start.10 = (bf16[60,896]{1,0:T(8,128)(2,1)S(1)}, bf16[60,896]{1,0:T(8,128)(2,1)S(1)}, u32[]{:S(2)}, u32[]{:S(2)}) collective-permute-start(bf16[60,896]{1,0:T(8,128)(2,1)S(1)} %get-tuple-element.96), channel_id=1, source_target_pairs={{0,16},{8,24},{16,0},{24,8},{1,17},{9,25},{17,1},{25,9},{2,18},{10... | collective-permute-start | bytes 322568 | tf_op jit(solution)/shard_map/ppermute | solution.py:387
  30.1 0.1 halve_kernel.6
  30.1 0.9 %collective-permute-start.7 = (bf16[60,896]{1,0:T(8,128)(2,1)S(1)}, bf16[60,896]{1,0:T(8,128)(2,1)S(1)}, u32[]{:S(2)}, u32[]{:S(2)}) collective-permute-start(bf16[60,896]{1,0:T(8,128)(2,1)S(1)} %get-tuple-element.89), channel_id=1, source_target_pairs={{0,16},{8,24},{16,0},{24,8},{1,17},{9,25},{17,1},{25,9},{2,18},{10... | collective-permute-start | bytes 322568 | tf_op jit(solution)/shard_map/ppermute | solution.py:387
  31.0 0.5 collective-permute-done.8.refs_1_
  31.5 1.2 %collective-permute-start.9 = (bf16[60,768]{1,0:T(8,128)(2,1)S(1)}, bf16[60,768]{1,0:T(8,128)(2,1)S(1)}, u32[]{:S(2)}, u32[]{:S(2)}) collective-permute-start(bf16[60,768]{1,0:T(8,128)(2,1)S(1)} %get-tuple-element.94), channel_id=1, source_target_pairs={{0,8},{8,0},{16,24},{24,16},{1,9},{9,1},{17,25},{25,17},{2,10},{10... | collective-permute-start | bytes 276488 | tf_op jit(solution)/shard_map/ppermute | solution.py:387
  32.7 0.0 collective-permute-done.11.refs_1_
  32.7 0.1 middle_kernel.4
  32.7 2.2 %collective-permute-start.15 = (bf16[60,896]{1,0:T(8,128)(2,1)S(1)}, bf16[60,896]{1,0:T(8,128)(2,1)S(1)}, u32[]{:S(2)}, u32[]{:S(2)}) collective-permute-start(bf16[60,896]{1,0:T(8,128)(2,1)S(1)} %get-tuple-element.106.refs_0_), channel_id=1, source_target_pairs={{0,16},{8,24},{16,0},{24,8},{1,17},{9,25},{17,1},{25,9},{2,18},{10... | collective-permute-start | bytes 322568 | tf_op jit(solution)/shard_map/ppermute | solution.py:387
  34.9 0.1 middle_kernel.5
  35.0 0.7 collective-permute-start.14
  35.7 0.5 collective-permute-done.9.refs_1_
  36.2 0.1 middle_kernel.6
  36.2 0.0 collective-permute-done.7.refs_1_
  36.3 0.1 middle_kernel.7
  36.3 1.9 %collective-permute-start.12 = (bf16[60,896]{1,0:T(8,128)(2,1)S(1)}, bf16[60,896]{1,0:T(8,128)(2,1)S(1)}, u32[]{:S(2)}, u32[]{:S(2)}) collective-permute-start(bf16[60,896]{1,0:T(8,128)(2,1)S(1)} %get-tuple-element.103.refs_0_), channel_id=1, source_target_pairs={{0,8},{8,0},{16,24},{24,16},{1,9},{9,1},{17,25},{25,17},{2,10},{10... | collective-permute-start | bytes 322568 | tf_op jit(solution)/shard_map/ppermute | solution.py:387
  38.2 2.4 %collective-permute-start.13 = (bf16[60,768]{1,0:T(8,128)(2,1)S(1)}, bf16[60,768]{1,0:T(8,128)(2,1)S(1)}, u32[]{:S(2)}, u32[]{:S(2)}) collective-permute-start(bf16[60,768]{1,0:T(8,128)(2,1)S(1)} %get-tuple-element.104.refs_0_), channel_id=1, source_target_pairs={{0,16},{8,24},{16,0},{24,8},{1,17},{9,25},{17,1},{25,9},{2,18},{10... | collective-permute-start | bytes 276488 | tf_op jit(solution)/shard_map/ppermute | solution.py:387
  40.6 0.2 collective-permute-done.14.refs_1_
  40.9 1.3 %collective-permute-start.16 = (bf16[120,896]{1,0:T(8,128)(2,1)S(1)}, bf16[120,896]{1,0:T(8,128)(2,1)S(1)}, u32[]{:S(2)}, u32[]{:S(2)}) collective-permute-start(bf16[120,896]{1,0:T(8,128)(2,1)S(1)} %get-tuple-element.114.refs_0_), channel_id=1, source_target_pairs={{0,16},{8,24},{16,0},{24,8},{1,17},{9,25},{17,1},{25,9},{2,18},{10... | collective-permute-start | bytes 645128 | tf_op jit(solution)/shard_map/ppermute | solution.py:387
  42.3 1.7 %collective-permute-start.17 = (bf16[120,896]{1,0:T(8,128)(2,1)S(1)}, bf16[120,896]{1,0:T(8,128)(2,1)S(1)}, u32[]{:S(2)}, u32[]{:S(2)}) collective-permute-start(bf16[120,896]{1,0:T(8,128)(2,1)S(1)} %get-tuple-element.115.refs_2_), channel_id=1, source_target_pairs={{0,8},{8,0},{16,24},{24,16},{1,9},{9,1},{17,25},{25,17},{2,10},{10... | collective-permute-start | bytes 645128 | tf_op jit(solution)/shard_map/ppermute | solution.py:387
  44.0 0.2 collective-permute-done.13.refs_1_
  44.3 1.9 %collective-permute-start.19 = (bf16[120,896]{1,0:T(8,128)(2,1)S(1)}, bf16[120,896]{1,0:T(8,128)(2,1)S(1)}, u32[]{:S(2)}, u32[]{:S(2)}) collective-permute-start(bf16[120,896]{1,0:T(8,128)(2,1)S(1)} %get-tuple-element.120.refs_0_), channel_id=1, source_target_pairs={{0,16},{8,24},{16,0},{24,8},{1,17},{9,25},{17,1},{25,9},{2,18},{10... | collective-permute-start | bytes 645128 | tf_op jit(solution)/shard_map/ppermute | solution.py:387
  46.2 0.3 collective-permute-start.20
  46.5 0.3 factors_kernel.1
  46.7 2.3 %collective-permute-done.16.refs_1_ = bf16[120,896]{1,0:T(8,128)(2,1)S(1)} collective-permute-done((bf16[120,896]{1,0:T(8,128)(2,1)S(1)}, bf16[120,896]{1,0:T(8,128)(2,1)S(1)}, u32[]{:S(2)}, u32[]{:S(2)}) %collective-permute-start.16) | collective-permute-done | bytes 215072 | tf_op jit(solution)/shard_map/ppermute | solution.py:387
  49.0 0.1 collective-permute-done.17.refs_3_
  49.1 0.1 stack_kernel.2
  49.2 0.1 collective-permute-start.18
  49.3 2.9 %input_grad_kernel.1 = (f32[80,1280]{1,0:T(8,128)S(1)}, f32[8,128]{1,0:T(8,128)S(1)}) custom-call(bf16[240,1792]{1,0:T(8,128)(2,1)S(1)} %get-tuple-element.117.refs_0_.refs_2_, bf16[1280,3456]{1,0:T(8,128)(2,1)S(1)} %get-tuple-element.73.refs_1_.refs_6_, bf16[1280,3456]{1,0:T(8,128)(2,1)S(1)} %get-tuple-element.74.refs_2_.refs_7_, ...), custom_call_target="tpu_custom_call" | custom-call | flops 1 | bytes 1 | tf_op jit(solution)/shard_map/input_grad_kernel/pallas_call | solution.py:62
  52.1 0.0 collective-permute-done.20.refs_3_
  52.2 0.0 collective-permute-done.19.refs_1_
  52.2 0.1 stack_kernel.3
  52.3 0.6 collective-permute-start.24
  52.8 0.0 collective-permute-done.18.refs_3_
  52.8 7.6 %first_grads_kernel.1 = (bf16[1280,3456]{1,0:T(8,128)(2,1)}, bf16[1280,3456]{1,0:T(8,128)(2,1)}, bf16[3456,1280]{1,0:T(8,128)(2,1)}, f32[80,1280]{1,0:T(8,128)S(1)}, f32[8,128]{1,0:T(8,128)S(1)}) custom-call(bf16[1280,160]{1,0:T(8,128)(2,1)S(1)} %get-tuple-element.112.refs_0_, bf16[160,1280]{1,0:T(8,128)(2,1)S(1)} %get-tuple-element.113.refs_1_, ...), custom_call_target="tpu_custom_call" | custom-call | flops 1 | bytes 1 | tf_op jit(solution)/shard_map/first_grads_kernel/pallas_call | solution.py:62
  60.4 0.2 last_kernel.1
  60.6 1.0 %collective-permute-start.21 = (bf16[20,1280]{1,0:T(8,128)(2,1)S(1)}, bf16[20,1280]{1,0:T(8,128)(2,1)S(1)}, u32[]{:S(2)}, u32[]{:S(2)}) collective-permute-start(bf16[20,1280]{1,0:T(8,128)(2,1)S(1)} %get-tuple-element.128), channel_id=1, source_target_pairs={{0,2},{2,0},{4,6},{6,4},{1,3},{3,1},{5,7},{7,5},{8,10},{10,8},{12,... | collective-permute-start | bytes 153608 | tf_op jit(solution)/shard_map/ppermute | solution.py:387
  61.6 1.3 %collective-permute-start.22 = (bf16[20,1280]{1,0:T(8,128)(2,1)S(1)}, bf16[20,1280]{1,0:T(8,128)(2,1)S(1)}, u32[]{:S(2)}, u32[]{:S(2)}) collective-permute-start(bf16[20,1280]{1,0:T(8,128)(2,1)S(1)} %get-tuple-element.129), channel_id=1, source_target_pairs={{0,4},{2,6},{4,0},{6,2},{1,5},{3,7},{5,1},{7,3},{8,12},{10,14},{12... | collective-permute-start | bytes 153608 | tf_op jit(solution)/shard_map/ppermute | solution.py:387
  62.9 2.1 %collective-permute-start.23 = (bf16[20,1280]{1,0:T(8,128)(2,1)S(1)}, bf16[20,1280]{1,0:T(8,128)(2,1)S(1)}, u32[]{:S(2)}, u32[]{:S(2)}) collective-permute-start(bf16[20,1280]{1,0:T(8,128)(2,1)S(1)} %get-tuple-element.130), channel_id=1, source_target_pairs={{0,6},{2,4},{4,2},{6,0},{1,7},{3,5},{5,3},{7,1},{8,14},{10,12},{12... | collective-permute-start | bytes 153608 | tf_op jit(solution)/shard_map/ppermute | solution.py:387
  65.0 0.0 collective-permute-done.24.refs_3_
  65.0 5.1 %weight_grad_kernel.1 = (bf16[1280,3456]{1,0:T(8,128)(2,1)}, bf16[1280,3456]{1,0:T(8,128)(2,1)}, bf16[3456,1280]{1,0:T(8,128)(2,1)}, f32[8,128]{1,0:T(8,128)S(1)}) custom-call(bf16[1280,160]{1,0:T(8,128)(2,1)S(1)} %get-tuple-element.112.refs_0_, ...), custom_call_target="tpu_custom_call", output_to_operand_aliasing={{0}: (4, {}), {1}: (5, {}), {2}: (6, {})} | custom-call | flops 1 | bytes 1 | tf_op jit(solution)/shard_map/weight_grad_kernel/pallas_call | solution.py:62
  70.2 0.7 total_kernel.1
  (20 shorter events, 0.2 us)
Async XLA Ops:
  0.6 15.1 %slice-start = ((s8[8847360]{0:T(1024)(128)(4,1)}), s8[4194304]{0:T(1024)(128)(4,1)S(1)}, s32[]{:S(2)}) async-start(s8[8847360]{0:T(1024)(128)(4,1)} %bitcast), calls=%async_computation | async-start | bytes 8388608
  1.7 14.0 %slice-start.1 = ((s8[8847360]{0:T(1024)(128)(4,1)}), s8[4194304]{0:T(1024)(128)(4,1)S(1)}, s32[]{:S(2)}) async-start(s8[8847360]{0:T(1024)(128)(4,1)} %bitcast), calls=%async_computation.1 | async-start | bytes 8388608
  1.7 14.0 %slice-start.2 = ((s8[8847360]{0:T(1024)(128)(4,1)}), s8[458752]{0:T(1024)(128)(4,1)S(1)}, s32[]{:S(2)}) async-start(s8[8847360]{0:T(1024)(128)(4,1)} %bitcast), calls=%async_computation.2 | async-start | bytes 917504
  1.7 12.5 %collective-permute-start = (bf16[40,1280]{1,0:T(8,128)(2,1)S(1)}, bf16[40,1280]{1,0:T(8,128)(2,1)S(1)}, u32[]{:S(2)}, u32[]{:S(2)}) collective-permute-start(bf16[40,1280]{1,0:T(8,128)(2,1)S(1)} %pad_maximum_fusion.refs_0_), channel_id=1, source_target_pairs={{0,2},{2,0},{4,6},{6,4},{1,3},{3,1},{5,7},{7,5},{8,10},{10,8},{12,... | collective-permute-start | bytes 307208 | tf_op jit(solution)/shard_map/ppermute | solution.py:387
  4.8 10.7 %collective-permute-start.1 = (bf16[40,1280]{1,0:T(8,128)(2,1)S(1)}, bf16[40,1280]{1,0:T(8,128)(2,1)S(1)}, u32[]{:S(2)}, u32[]{:S(2)}) collective-permute-start(bf16[40,1280]{1,0:T(8,128)(2,1)S(1)} %pad_maximum_fusion.refs_0_), channel_id=1, source_target_pairs={{0,4},{2,6},{4,0},{6,2},{1,5},{3,7},{5,1},{7,3},{8,12},{10,14},{12... | collective-permute-start | bytes 307208 | tf_op jit(solution)/shard_map/ppermute | solution.py:387
  7.4 8.1 %collective-permute-start.2 = (bf16[40,1280]{1,0:T(8,128)(2,1)S(1)}, bf16[40,1280]{1,0:T(8,128)(2,1)S(1)}, u32[]{:S(2)}, u32[]{:S(2)}) collective-permute-start(bf16[40,1280]{1,0:T(8,128)(2,1)S(1)} %pad_maximum_fusion.refs_0_), channel_id=1, source_target_pairs={{0,6},{2,4},{4,2},{6,0},{1,7},{3,5},{5,3},{7,1},{8,14},{10,12},{12... | collective-permute-start | bytes 307208 | tf_op jit(solution)/shard_map/ppermute | solution.py:387
  17.3 8.8 %collective-permute-start.6 = (bf16[120,896]{1,0:T(8,128)(2,1)S(1)}, bf16[120,896]{1,0:T(8,128)(2,1)S(1)}, u32[]{:S(2)}, u32[]{:S(2)}) collective-permute-start(bf16[120,896]{1,0:T(8,128)(2,1)S(1)} %get-tuple-element.83), channel_id=1, source_target_pairs={{0,8},{8,0},{16,24},{24,16},{1,9},{9,1},{17,25},{25,17},{2,10},{10... | collective-permute-start | bytes 645128 | tf_op jit(solution)/shard_map/ppermute | solution.py:387
  20.3 7.0 %collective-permute-start.5 = (bf16[120,896]{1,0:T(8,128)(2,1)S(1)}, bf16[120,896]{1,0:T(8,128)(2,1)S(1)}, u32[]{:S(2)}, u32[]{:S(2)}) collective-permute-start(bf16[120,896]{1,0:T(8,128)(2,1)S(1)} %get-tuple-element.81), channel_id=1, source_target_pairs={{0,16},{8,24},{16,0},{24,8},{1,17},{9,25},{17,1},{25,9},{2,18},{10... | collective-permute-start | bytes 645128 | tf_op jit(solution)/shard_map/ppermute | solution.py:387
  23.4 6.6 %collective-permute-start.4 = (bf16[120,896]{1,0:T(8,128)(2,1)S(1)}, bf16[120,896]{1,0:T(8,128)(2,1)S(1)}, u32[]{:S(2)}, u32[]{:S(2)}) collective-permute-start(bf16[120,896]{1,0:T(8,128)(2,1)S(1)} %get-tuple-element.79), channel_id=1, source_target_pairs={{0,8},{8,0},{16,24},{24,16},{1,9},{9,1},{17,25},{25,17},{2,10},{10... | collective-permute-start | bytes 645128 | tf_op jit(solution)/shard_map/ppermute | solution.py:387
  25.4 6.0 %collective-permute-start.8 = (bf16[120,768]{1,0:T(8,128)(2,1)S(1)}, bf16[120,768]{1,0:T(8,128)(2,1)S(1)}, u32[]{:S(2)}, u32[]{:S(2)}) collective-permute-start(bf16[120,768]{1,0:T(8,128)(2,1)S(1)} %get-tuple-element.91), channel_id=1, source_target_pairs={{0,16},{8,24},{16,0},{24,8},{1,17},{9,25},{17,1},{25,9},{2,18},{10... | collective-permute-start | bytes 552968 | tf_op jit(solution)/shard_map/ppermute | solution.py:387
  27.4 5.2 %collective-permute-start.11 = (bf16[60,896]{1,0:T(8,128)(2,1)S(1)}, bf16[60,896]{1,0:T(8,128)(2,1)S(1)}, u32[]{:S(2)}, u32[]{:S(2)}) collective-permute-start(bf16[60,896]{1,0:T(8,128)(2,1)S(1)} %get-tuple-element.98), channel_id=1, source_target_pairs={{0,8},{8,0},{16,24},{24,16},{1,9},{9,1},{17,25},{25,17},{2,10},{10... | collective-permute-start | bytes 322568 | tf_op jit(solution)/shard_map/ppermute | solution.py:387
  27.7 7.2 %collective-permute-start.10 = (bf16[60,896]{1,0:T(8,128)(2,1)S(1)}, bf16[60,896]{1,0:T(8,128)(2,1)S(1)}, u32[]{:S(2)}, u32[]{:S(2)}) collective-permute-start(bf16[60,896]{1,0:T(8,128)(2,1)S(1)} %get-tuple-element.96), channel_id=1, source_target_pairs={{0,16},{8,24},{16,0},{24,8},{1,17},{9,25},{17,1},{25,9},{2,18},{10... | collective-permute-start | bytes 322568 | tf_op jit(solution)/shard_map/ppermute | solution.py:387
  30.1 16.4 %collective-permute-start.3 = (bf16[160,1280]{1,0:T(8,128)(2,1)S(1)}, bf16[160,1280]{1,0:T(8,128)(2,1)S(1)}, u32[]{:S(2)}, u32[]{:S(2)}) collective-permute-start(bf16[160,1280]{1,0:T(8,128)(2,1)S(1)} %get-tuple-element.72.refs_0_), channel_id=1, source_target_pairs={{0,1},{1,0},{2,3},{3,2},{4,5},{5,4},{6,7},{7,6},{8,9},{9,8},{10,11... | collective-permute-start | bytes 1228808 | tf_op jit(solution)/shard_map/ppermute | solution.py:387
  30.1 6.1 %collective-permute-start.7 = (bf16[60,896]{1,0:T(8,128)(2,1)S(1)}, bf16[60,896]{1,0:T(8,128)(2,1)S(1)}, u32[]{:S(2)}, u32[]{:S(2)}) collective-permute-start(bf16[60,896]{1,0:T(8,128)(2,1)S(1)} %get-tuple-element.89), channel_id=1, source_target_pairs={{0,16},{8,24},{16,0},{24,8},{1,17},{9,25},{17,1},{25,9},{2,18},{10... | collective-permute-start | bytes 322568 | tf_op jit(solution)/shard_map/ppermute | solution.py:387
  31.5 4.7 %collective-permute-start.9 = (bf16[60,768]{1,0:T(8,128)(2,1)S(1)}, bf16[60,768]{1,0:T(8,128)(2,1)S(1)}, u32[]{:S(2)}, u32[]{:S(2)}) collective-permute-start(bf16[60,768]{1,0:T(8,128)(2,1)S(1)} %get-tuple-element.94), channel_id=1, source_target_pairs={{0,8},{8,0},{16,24},{24,16},{1,9},{9,1},{17,25},{25,17},{2,10},{10... | collective-permute-start | bytes 276488 | tf_op jit(solution)/shard_map/ppermute | solution.py:387
  32.7 7.9 %collective-permute-start.15 = (bf16[60,896]{1,0:T(8,128)(2,1)S(1)}, bf16[60,896]{1,0:T(8,128)(2,1)S(1)}, u32[]{:S(2)}, u32[]{:S(2)}) collective-permute-start(bf16[60,896]{1,0:T(8,128)(2,1)S(1)} %get-tuple-element.106.refs_0_), channel_id=1, source_target_pairs={{0,16},{8,24},{16,0},{24,8},{1,17},{9,25},{17,1},{25,9},{2,18},{10... | collective-permute-start | bytes 322568 | tf_op jit(solution)/shard_map/ppermute | solution.py:387
  35.0 5.9 %collective-permute-start.14 = (bf16[60,896]{1,0:T(8,128)(2,1)S(1)}, bf16[60,896]{1,0:T(8,128)(2,1)S(1)}, u32[]{:S(2)}, u32[]{:S(2)}) collective-permute-start(bf16[60,896]{1,0:T(8,128)(2,1)S(1)} %get-tuple-element.105.refs_0_), channel_id=1, source_target_pairs={{0,8},{8,0},{16,24},{24,16},{1,9},{9,1},{17,25},{25,17},{2,10},{10... | collective-permute-start | bytes 322568 | tf_op jit(solution)/shard_map/ppermute | solution.py:387
  36.3 7.9 %collective-permute-start.12 = (bf16[60,896]{1,0:T(8,128)(2,1)S(1)}, bf16[60,896]{1,0:T(8,128)(2,1)S(1)}, u32[]{:S(2)}, u32[]{:S(2)}) collective-permute-start(bf16[60,896]{1,0:T(8,128)(2,1)S(1)} %get-tuple-element.103.refs_0_), channel_id=1, source_target_pairs={{0,8},{8,0},{16,24},{24,16},{1,9},{9,1},{17,25},{25,17},{2,10},{10... | collective-permute-start | bytes 322568 | tf_op jit(solution)/shard_map/ppermute | solution.py:387
  38.2 6.0 %collective-permute-start.13 = (bf16[60,768]{1,0:T(8,128)(2,1)S(1)}, bf16[60,768]{1,0:T(8,128)(2,1)S(1)}, u32[]{:S(2)}, u32[]{:S(2)}) collective-permute-start(bf16[60,768]{1,0:T(8,128)(2,1)S(1)} %get-tuple-element.104.refs_0_), channel_id=1, source_target_pairs={{0,16},{8,24},{16,0},{24,8},{1,17},{9,25},{17,1},{25,9},{2,18},{10... | collective-permute-start | bytes 276488 | tf_op jit(solution)/shard_map/ppermute | solution.py:387
  40.9 8.1 %collective-permute-start.16 = (bf16[120,896]{1,0:T(8,128)(2,1)S(1)}, bf16[120,896]{1,0:T(8,128)(2,1)S(1)}, u32[]{:S(2)}, u32[]{:S(2)}) collective-permute-start(bf16[120,896]{1,0:T(8,128)(2,1)S(1)} %get-tuple-element.114.refs_0_), channel_id=1, source_target_pairs={{0,16},{8,24},{16,0},{24,8},{1,17},{9,25},{17,1},{25,9},{2,18},{10... | collective-permute-start | bytes 645128 | tf_op jit(solution)/shard_map/ppermute | solution.py:387
  42.3 6.8 %collective-permute-start.17 = (bf16[120,896]{1,0:T(8,128)(2,1)S(1)}, bf16[120,896]{1,0:T(8,128)(2,1)S(1)}, u32[]{:S(2)}, u32[]{:S(2)}) collective-permute-start(bf16[120,896]{1,0:T(8,128)(2,1)S(1)} %get-tuple-element.115.refs_2_), channel_id=1, source_target_pairs={{0,8},{8,0},{16,24},{24,16},{1,9},{9,1},{17,25},{25,17},{2,10},{10... | collective-permute-start | bytes 645128 | tf_op jit(solution)/shard_map/ppermute | solution.py:387
  44.3 7.8 %collective-permute-start.19 = (bf16[120,896]{1,0:T(8,128)(2,1)S(1)}, bf16[120,896]{1,0:T(8,128)(2,1)S(1)}, u32[]{:S(2)}, u32[]{:S(2)}) collective-permute-start(bf16[120,896]{1,0:T(8,128)(2,1)S(1)} %get-tuple-element.120.refs_0_), channel_id=1, source_target_pairs={{0,16},{8,24},{16,0},{24,8},{1,17},{9,25},{17,1},{25,9},{2,18},{10... | collective-permute-start | bytes 645128 | tf_op jit(solution)/shard_map/ppermute | solution.py:387
  46.2 5.9 %collective-permute-start.20 = (bf16[120,768]{1,0:T(8,128)(2,1)S(1)}, bf16[120,768]{1,0:T(8,128)(2,1)S(1)}, u32[]{:S(2)}, u32[]{:S(2)}) collective-permute-start(bf16[120,768]{1,0:T(8,128)(2,1)S(1)} %get-tuple-element.121.refs_2_), channel_id=1, source_target_pairs={{0,8},{8,0},{16,24},{24,16},{1,9},{9,1},{17,25},{25,17},{2,10},{10... | collective-permute-start | bytes 552968 | tf_op jit(solution)/shard_map/ppermute | solution.py:387
  49.2 3.6 %collective-permute-start.18 = (bf16[240,1792]{1,0:T(8,128)(2,1)S(1)}, bf16[240,1792]{1,0:T(8,128)(2,1)S(1)}, u32[]{:S(2)}, u32[]{:S(2)}) collective-permute-start(bf16[240,1792]{1,0:T(8,128)(2,1)S(1)} %get-tuple-element.117.refs_0_.refs_2_), channel_id=1, source_target_pairs={{0,1},{1,0},{2,3},{3,2},{4,5},{5,4},{6,7},{7,6},{8,9},{9,8},{10,11... | collective-permute-start | bytes 2580488 | tf_op jit(solution)/shard_map/ppermute | solution.py:387
  52.3 12.8 %collective-permute-start.24 = (bf16[240,1792]{1,0:T(8,128)(2,1)S(1)}, bf16[240,1792]{1,0:T(8,128)(2,1)S(1)}, u32[]{:S(2)}, u32[]{:S(2)}) collective-permute-start(bf16[240,1792]{1,0:T(8,128)(2,1)S(1)} %get-tuple-element.123.refs_5_.refs_2_), channel_id=1, source_target_pairs={{0,1},{1,0},{2,3},{3,2},{4,5},{5,4},{6,7},{7,6},{8,9},{9,8},{10,11... | collective-permute-start | bytes 2580488 | tf_op jit(solution)/shard_map/ppermute | solution.py:387
  60.6 9.6 %collective-permute-start.21 = (bf16[20,1280]{1,0:T(8,128)(2,1)S(1)}, bf16[20,1280]{1,0:T(8,128)(2,1)S(1)}, u32[]{:S(2)}, u32[]{:S(2)}) collective-permute-start(bf16[20,1280]{1,0:T(8,128)(2,1)S(1)} %get-tuple-element.128), channel_id=1, source_target_pairs={{0,2},{2,0},{4,6},{6,4},{1,3},{3,1},{5,7},{7,5},{8,10},{10,8},{12,... | collective-permute-start | bytes 153608 | tf_op jit(solution)/shard_map/ppermute | solution.py:387
  61.6 8.6 %collective-permute-start.22 = (bf16[20,1280]{1,0:T(8,128)(2,1)S(1)}, bf16[20,1280]{1,0:T(8,128)(2,1)S(1)}, u32[]{:S(2)}, u32[]{:S(2)}) collective-permute-start(bf16[20,1280]{1,0:T(8,128)(2,1)S(1)} %get-tuple-element.129), channel_id=1, source_target_pairs={{0,4},{2,6},{4,0},{6,2},{1,5},{3,7},{5,1},{7,3},{8,12},{10,14},{12... | collective-permute-start | bytes 153608 | tf_op jit(solution)/shard_map/ppermute | solution.py:387
  62.9 7.3 %collective-permute-start.23 = (bf16[20,1280]{1,0:T(8,128)(2,1)S(1)}, bf16[20,1280]{1,0:T(8,128)(2,1)S(1)}, u32[]{:S(2)}, u32[]{:S(2)}) collective-permute-start(bf16[20,1280]{1,0:T(8,128)(2,1)S(1)} %get-tuple-element.130), channel_id=1, source_target_pairs={{0,6},{2,4},{4,2},{6,0},{1,7},{3,5},{5,3},{7,1},{8,14},{10,12},{12... | collective-permute-start | bytes 153608 | tf_op jit(solution)/shard_map/ppermute | solution.py:387

commit v10 on v9

--- a/solution.py
+++ b/solution.py
@@ -194,12 +194,11 @@
         cuts = [slots[slot][k * rows : (k + 1) * rows] for k in range(3) for slot in range(4)]
         out_ref[:, begin : begin + columns] = joined(*cuts).astype(BF16)
         begin += columns
-    if begin < out_ref.shape[1]:
-        out_ref[:, begin:] = jnp.zeros((out_ref.shape[0], out_ref.shape[1] - begin), BF16)
-
-
-def stack(line, axes, blocks, columns):
+
+
+def stack(line, axes, blocks):
     rows = 2 * blocks[0][0].shape[0]
+    columns = sum(mine.shape[1] for mine, _ in blocks)
     return line.call(
         functools.partial(stack_kernel, axes),
         [block for pair in blocks for block in pair],
@@ -207,27 +206,24 @@
     )[0]
 
 
-def input_grad_kernel(begin, mine_ref, gate_ref, up_ref, grad_ref):
-    grad_ref[...] = input_grad_part(begin, mine_ref, gate_ref, up_ref, 0, grad_ref.shape[1])
-
-
-def input_grad_part(begin, mine_ref, gate_ref, up_ref, start, size):
-    group = mine_ref.shape[0] // 3
-    columns = min(mine_ref.shape[1], gate_ref.shape[1] - begin)
-    here, there, used = pl.ds(start, size), pl.ds(begin, columns), pl.ds(0, columns)
-    return lax.dot_general(
-        mine_ref[:group, used], gate_ref[here, there], NT, preferred_element_type=F32
+def input_grad_kernel(begin, stack_ref, gate_ref, up_ref, *refs):
+    there = pl.ds(begin, stack_ref.shape[1])
+    group = stack_ref.shape[0] // 3
+    grad = lax.dot_general(
+        stack_ref[:group], gate_ref[:, there], NT, preferred_element_type=F32
     ) + lax.dot_general(
-        mine_ref[group : 2 * group, used], up_ref[here, there], NT, preferred_element_type=F32
-    )
-
-
-def input_grad(line, begin, mine, gate, up):
+        stack_ref[group : 2 * group], up_ref[:, there], NT, preferred_element_type=F32
+    )
+    refs[-1][...] = grad + refs[0][...] if len(refs) > 1 else grad
+
+
+def input_grad(line, begin, stacked, gate_weight, up_weight, start):
+    shape = (stacked.shape[0] // 3, gate_weight.shape[0])
     return line.call(
         functools.partial(input_grad_kernel, begin),
-        (mine, gate, up),
-        [shaped(mine.shape[0] // 3, gate.shape[0], F32)],
-    )[0]
+        (stacked, gate_weight, up_weight, *start),
+        [shaped(*shape, F32)],
+    )
 
 
 def factors_kernel(mine_ref, other_ref, xt_ref, y_all_ref):
@@ -290,23 +286,6 @@
             copy.wait()
 
 
-def first_grads_kernel(begins, *refs):
-    xt_ref, y_ref, mine_ref, other_ref, start_ref, last_ref, gate_ref, up_ref, *refs = refs
-    *outs, grad_ref = refs[:4]
-    writer = Writer(begins[0], xt_ref, y_ref, mine_ref, other_ref, outs, refs[4:])
-    width = grad_ref.shape[1]
-    pieces = [(at, min(TILE, width - at)) for at in range(0, width, TILE)]
-    for step in range(max(len(pieces), len(writer.tiles))):
-        if step < len(writer.tiles):
-            writer.tile(*writer.tiles[step])
-        if step < len(pieces):
-            here = pl.ds(*pieces[step])
-            grad_ref[:, here] = start_ref[:, here] + input_grad_part(
-                begins[1], last_ref, gate_ref, up_ref, *pieces[step]
-            )
-    writer.wait()
-
-
 def grad_shapes(width, hidden_width):
     return [(width, hidden_width), (width, hidden_width), (hidden_width, width)]
 
@@ -319,57 +298,47 @@
     ]
 
 
-def first_grads(line, begins, xt, y, mine, other, start, last, gate_weight, up_weight):
-    width, hidden_width = gate_weight.shape
-    shapes = [shaped(*shape) for shape in grad_shapes(width, hidden_width)]
-    return line.call(
-        functools.partial(first_grads_kernel, begins),
-        (xt, y, mine, other, start, last, gate_weight, up_weight),
-        shapes + [shaped(*start.shape, F32)],
-        out_specs=[IN_HBM] * 3 + [IN_VMEM],
-        scratch=writer_scratch(width, y.shape[0], mine.shape[1]),
-        limit=24,
-    )
-
-
-def weight_grad_kernel(begin, xt_ref, y_ref, mine_ref, other_ref, *refs):
-    writer = Writer(begin, xt_ref, y_ref, mine_ref, other_ref, refs[3:6], refs[6:])
+def weight_grad_kernel(begin, held, xt_ref, y_ref, mine_ref, other_ref, _, *refs):
+    outs, scratch = refs[held : held + 3], refs[held + 3 :]
+    writer = Writer(begin, xt_ref, y_ref, mine_ref, other_ref, outs, scratch)
     for tile in writer.tiles:
         writer.tile(*tile)
     writer.wait()
 
 
-def weight_grad(line, begin, xt, y, mine, other, grads):
+def weight_grad(line, begin, hidden_width, xt, y, mine, other, grads, after):
+    shapes = grad_shapes(xt.shape[0], hidden_width)
     return line.call(
-        functools.partial(weight_grad_kernel, begin),
-        (xt, y, mine, other, *grads),
-        [shaped(*grad.shape) for grad in grads],
-        in_specs=[IN_VMEM] * 4 + [IN_HBM] * 3,
+        functools.partial(weight_grad_kernel, begin, len(grads)),
+        (xt, y, mine, other, after, *grads),
+        [shaped(*shape) for shape in shapes],
+        in_specs=[IN_VMEM] * 5 + [IN_HBM] * len(grads),
         out_specs=[IN_HBM] * 3,
         scratch=writer_scratch(xt.shape[0], y.shape[0], mine.shape[1]),
-        aliases={4 + at: at for at in range(3)},
+        aliases={5 + at: at for at in range(len(grads))},
         limit=24,
     )
 
 
-def last_kernel(grad_ref, *out_refs):
+def last_kernel(grad_ref, keep_ref, send_ref):
     grad = grad_ref[...]
-    rows = out_refs[0].shape[0]
-    cuts = [grad[slot * rows : (slot + 1) * rows] for slot in range(len(out_refs))]
+    rows = keep_ref.shape[0] // 2
+    cuts = [grad[slot * rows : (slot + 1) * rows] for slot in range(4)]
     wa = lax.axis_index("wa")
-    for step, out_ref in enumerate(out_refs):
+    pieces = []
+    for step in range(4):
         at = wa ^ step
         piece = cuts[0]
         for slot in range(1, len(cuts)):
             piece = jnp.where(at == slot, cuts[slot], piece)
-        out_ref[...] = piece.astype(out_ref.dtype)
-
-
-def last_pieces(line, parts, grad):
-    shape = (grad.shape[0] // parts, grad.shape[1])
-    return line.call(
-        last_kernel, (grad,), [shaped(*shape, F32)] + [shaped(*shape)] * (parts - 1)
-    )
+        pieces.append(piece)
+    keep_ref[...] = joined(*pieces[:2])
+    send_ref[...] = joined(*pieces[2:]).astype(BF16)
+
+
+def last_pieces(line, grad):
+    shape = (grad.shape[0] // 2, grad.shape[1])
+    return line.call(last_kernel, (grad,), [shaped(*shape, F32), shaped(*shape)])
 
 
 def total_kernel(own_ref, *refs):
@@ -419,21 +388,21 @@
         got[at] = swap(kept[at], "wa", n_wa, far)
 
     xt, y_all = factors(line, xy, xy_other)
-    mine, other = [], []
-    widths = [sum(c for _, c in chunks[at : at + 2]) for at in range(0, CHUNKS, 2)]
-    widest = max(widths)
-    begins = [chunks[at][0] for at in range(0, CHUNKS, 2)]
+    mine, other, grad = [], [], ()
     for at in range(0, CHUNKS, 2):
         pair = slice(at, at + 2)
-        mine.append(stack(line, axes[pair], list(zip(kept, got))[pair], widest))
+        mine.append(stack(line, axes[pair], list(zip(kept, got))[pair]))
         other.append(swap(mine[-1], "row", n_row, 1))
-        if at == 0:
-            grad = input_grad(line, begins[0], mine[0], gate, up)
-    *grads, grad = first_grads(line, begins, xt, y_all, mine[0], other[0], grad, mine[1], gate, up)
-    own, *sends = last_pieces(line, n_ha, grad)
-    received = [swap(sent, "ha", n_ha, k + 1) for k, sent in enumerate(sends)]
-    grads = weight_grad(line, begins[1], xt, y_all, mine[1], other[1], grads)
-    return (total(line, own, received), *grads)
+        grad = input_grad(line, chunks[at][0], mine[-1], gate, up, grad)
+    keep, send = last_pieces(line, grad[0])
+    received = swap(send, "ha", n_ha, 2)
+    grads = weight_grad(line, 0, hidden_width, xt, y_all, mine[0], other[0], (), other[1])
+    keep, send = halve(line, keep, received)
+    received = swap(send, "ha", n_ha, 1)
+    grads = weight_grad(
+        line, mine[0].shape[1], hidden_width, xt, y_all, mine[1], other[1], grads, other[0]
+    )
+    return (total(line, keep, [received]), *grads)
 
 
 def plain_body(tokens, cotangent, gate_weight, up_weight, down_weight):

time: 71 us -> 69.7 us (0.982)
  starting transfers between devices: 32.1 us -> 29.6 us
    ppermute x25 -> x24, starting transfers between devices: 32.1 us -> 29.6 us  [swap(): return lax.ppermute(value, axis, [(at, at ^ step) for at in range(size)])]
    ppermute x25 -> x24, waiting for transfers between devices: 6.44 us -> 7.02 us  [swap(): return lax.ppermute(value, axis, [(at, at ^ step) for at in range(size)])]
    pallas_call x26 -> x28, Pallas kernels: 30.4 us -> 31 us  [call(): pl.pallas_call(body, in_specs=(in_specs or [IN_VMEM] * count) + [IN_VMEM]...]
  transfers between devices with their start and end apart: 25 -> 24, of which waited for: 8 -> 9; matrix products, arithmetic and copies ran while one was open for 0% -> 0% of each run, Pallas kernels for 40% -> 41%
where the time goes in v10:
time: 69.7 us; the launch traced here: 69.6 us
  Pallas kernels  31 us (44%)
  starting transfers between devices  29.6 us (42%)
  waiting for transfers between devices  7.02 us (10%)
  other arithmetic  1.03 us (1%)
  between operations  0.89 us (1%)
    pallas_call x28, Pallas kernels, call(): pl.pallas_call(body, in_specs=(in_specs or [IN_VMEM] * count) + [IN_VMEM]...  31 us
    ppermute x24, starting transfers between devices, swap(): return lax.ppermute(value, axis, [(at, at ^ step) for at in range(size)])  29.6 us
    ppermute x24, waiting for transfers between devices, swap(): return lax.ppermute(value, axis, [(at, at ^ step) for at in range(size)])  7.02 us
  transfers between devices with their start and end apart: 24, of which 9 were waited for; matrix products, arithmetic and copies ran while one was open for 0% of the time, Pallas kernels for 41%

profile of v10, /device:TPU:0, one launch (start us, length us, event | category | flops | bytes accessed | tf_op | source)
XLA Modules:
  0.0 69.6 jit_solution(4105895854829471081)
XLA Ops:
  0.6 0.0 slice-start
  0.6 1.0 %pad_maximum_fusion.refs_0_ = bf16[40,1280]{1,0:T(8,128)(2,1)S(1)} fusion(bf16[20,1280]{1,0:T(8,128)(2,1)} %param.6, bf16[20,1280]{1,0:T(8,128)(2,1)} %param.5), kind=kLoop, calls=%fused_computation | loop fusion | flops 204800 | bytes 204800 | tf_op jit(solution)/shard_map/concatenate | solution.py:367
  1.7 0.0 slice-start.1
  1.7 0.0 slice-start.2
  1.7 3.1 %collective-permute-start = (bf16[40,1280]{1,0:T(8,128)(2,1)S(1)}, bf16[40,1280]{1,0:T(8,128)(2,1)S(1)}, u32[]{:S(2)}, u32[]{:S(2)}) collective-permute-start(bf16[40,1280]{1,0:T(8,128)(2,1)S(1)} %pad_maximum_fusion.refs_0_), channel_id=1, source_target_pairs={{0,2},{2,0},{4,6},{6,4},{1,3},{3,1},{5,7},{7,5},{8,10},{10,8},{12,... | collective-permute-start | bytes 307208 | tf_op jit(solution)/shard_map/ppermute | solution.py:356
  4.8 2.6 %collective-permute-start.1 = (bf16[40,1280]{1,0:T(8,128)(2,1)S(1)}, bf16[40,1280]{1,0:T(8,128)(2,1)S(1)}, u32[]{:S(2)}, u32[]{:S(2)}) collective-permute-start(bf16[40,1280]{1,0:T(8,128)(2,1)S(1)} %pad_maximum_fusion.refs_0_), channel_id=1, source_target_pairs={{0,4},{2,6},{4,0},{6,2},{1,5},{3,7},{5,1},{7,3},{8,12},{10,14},{12... | collective-permute-start | bytes 307208 | tf_op jit(solution)/shard_map/ppermute | solution.py:356
  7.4 6.8 %load_kernel.1 = (bf16[1280,3456]{1,0:T(8,128)(2,1)S(1)}, bf16[1280,3456]{1,0:T(8,128)(2,1)S(1)}, f32[8,128]{1,0:T(8,128)}) custom-call(bf16[1280,3456]{1,0:T(8,128)(2,1)} %refs_0_.1, bf16[1280,3456]{1,0:T(8,128)(2,1)} %refs_1_.1), custom_call_target="tpu_custom_call" | custom-call | flops 1 | bytes 1 | tf_op jit(solution)/shard_map/load_kernel/pallas_call | solution.py:62
  14.2 1.3 %collective-permute-done.1.refs_2_ = bf16[40,1280]{1,0:T(8,128)(2,1)S(1)} collective-permute-done((bf16[40,1280]{1,0:T(8,128)(2,1)S(1)}, bf16[40,1280]{1,0:T(8,128)(2,1)S(1)}, u32[]{:S(2)}, u32[]{:S(2)}) %collective-permute-start.1) | collective-permute-done | bytes 102432 | tf_op jit(solution)/shard_map/ppermute | solution.py:356
  15.5 0.2 order_kernel.1
  15.7 1.5 %forward_kernel.4 = (f32[120,896]{1,0:T(8,128)S(1)}, bf16[120,896]{1,0:T(8,128)(2,1)S(1)}, f32[8,128]{1,0:T(8,128)S(1)}) custom-call(bf16[160,1280]{1,0:T(8,128)(2,1)S(1)} %get-tuple-element.74.refs_0_, bf16[1280,3456]{1,0:T(8,128)(2,1)S(1)} %get-tuple-element.75.refs_1_, bf16[1280,3456]{1,0:T(8,128)(2,1)S(1)} %get-tuple-element.76.refs_2_, ...), custom_call_target="tpu_custom_call" | custom-call | flops 1 | bytes 1 | tf_op jit(solution)/shard_map/forward_kernel/pallas_call | solution.py:62
  17.3 1.6 %collective-permute-start.5 = (bf16[120,896]{1,0:T(8,128)(2,1)S(1)}, bf16[120,896]{1,0:T(8,128)(2,1)S(1)}, u32[]{:S(2)}, u32[]{:S(2)}) collective-permute-start(bf16[120,896]{1,0:T(8,128)(2,1)S(1)} %get-tuple-element.85), channel_id=1, source_target_pairs={{0,8},{8,0},{16,24},{24,16},{1,9},{9,1},{17,25},{25,17},{2,10},{10... | collective-permute-start | bytes 645128 | tf_op jit(solution)/shard_map/ppermute | solution.py:356
  18.8 1.5 %forward_kernel.5 = (f32[120,896]{1,0:T(8,128)S(1)}, bf16[120,896]{1,0:T(8,128)(2,1)S(1)}, f32[8,128]{1,0:T(8,128)S(1)}) custom-call(bf16[160,1280]{1,0:T(8,128)(2,1)S(1)} %get-tuple-element.74.refs_0_, bf16[1280,3456]{1,0:T(8,128)(2,1)S(1)} %get-tuple-element.75.refs_1_, bf16[1280,3456]{1,0:T(8,128)(2,1)S(1)} %get-tuple-element.76.refs_2_, ...), custom_call_target="tpu_custom_call" | custom-call | flops 1 | bytes 1 | tf_op jit(solution)/shard_map/forward_kernel/pallas_call | solution.py:62
  20.3 1.6 %collective-permute-start.4 = (bf16[120,896]{1,0:T(8,128)(2,1)S(1)}, bf16[120,896]{1,0:T(8,128)(2,1)S(1)}, u32[]{:S(2)}, u32[]{:S(2)}) collective-permute-start(bf16[120,896]{1,0:T(8,128)(2,1)S(1)} %get-tuple-element.83), channel_id=1, source_target_pairs={{0,16},{8,24},{16,0},{24,8},{1,17},{9,25},{17,1},{25,9},{2,18},{10... | collective-permute-start | bytes 645128 | tf_op jit(solution)/shard_map/ppermute | solution.py:356
  21.9 1.5 %forward_kernel.6 = (f32[120,896]{1,0:T(8,128)S(1)}, bf16[120,896]{1,0:T(8,128)(2,1)S(1)}, f32[8,128]{1,0:T(8,128)S(1)}) custom-call(bf16[160,1280]{1,0:T(8,128)(2,1)S(1)} %get-tuple-element.74.refs_0_, bf16[1280,3456]{1,0:T(8,128)(2,1)S(1)} %get-tuple-element.75.refs_1_, bf16[1280,3456]{1,0:T(8,128)(2,1)S(1)} %get-tuple-element.76.refs_2_, ...), custom_call_target="tpu_custom_call" | custom-call | flops 1 | bytes 1 | tf_op jit(solution)/shard_map/forward_kernel/pallas_call | solution.py:62
  23.4 0.6 collective-permute-start.3
  24.0 1.4 %forward_kernel.7 = (f32[120,768]{1,0:T(8,128)S(1)}, bf16[120,768]{1,0:T(8,128)(2,1)S(1)}, f32[8,128]{1,0:T(8,128)S(1)}) custom-call(bf16[160,1280]{1,0:T(8,128)(2,1)S(1)} %get-tuple-element.74.refs_0_, bf16[1280,3456]{1,0:T(8,128)(2,1)S(1)} %get-tuple-element.75.refs_1_, bf16[1280,3456]{1,0:T(8,128)(2,1)S(1)} %get-tuple-element.76.refs_2_, ...), custom_call_target="tpu_custom_call" | custom-call | flops 1 | bytes 1 | tf_op jit(solution)/shard_map/forward_kernel/pallas_call | solution.py:62
  25.4 0.6 collective-permute-start.7
  26.0 0.1 halve_kernel.5
  26.1 1.3 %collective-permute-done.4.refs_1_ = bf16[120,896]{1,0:T(8,128)(2,1)S(1)} collective-permute-done((bf16[120,896]{1,0:T(8,128)(2,1)S(1)}, bf16[120,896]{1,0:T(8,128)(2,1)S(1)}, u32[]{:S(2)}, u32[]{:S(2)}) %collective-permute-start.4) | collective-permute-done | bytes 215072 | tf_op jit(solution)/shard_map/ppermute | solution.py:356
  27.3 0.1 halve_kernel.6
  27.4 0.3 collective-permute-start.10
  27.7 2.3 %collective-permute-start.9 = (bf16[60,896]{1,0:T(8,128)(2,1)S(1)}, bf16[60,896]{1,0:T(8,128)(2,1)S(1)}, u32[]{:S(2)}, u32[]{:S(2)}) collective-permute-start(bf16[60,896]{1,0:T(8,128)(2,1)S(1)} %get-tuple-element.98), channel_id=1, source_target_pairs={{0,16},{8,24},{16,0},{24,8},{1,17},{9,25},{17,1},{25,9},{2,18},{10... | collective-permute-start | bytes 322568 | tf_op jit(solution)/shard_map/ppermute | solution.py:356
  30.0 0.0 collective-permute-start.19
  30.0 0.0 collective-permute-done.3.refs_1_
  30.0 0.1 halve_kernel.7
  30.1 0.9 %collective-permute-start.6 = (bf16[60,896]{1,0:T(8,128)(2,1)S(1)}, bf16[60,896]{1,0:T(8,128)(2,1)S(1)}, u32[]{:S(2)}, u32[]{:S(2)}) collective-permute-start(bf16[60,896]{1,0:T(8,128)(2,1)S(1)} %get-tuple-element.91), channel_id=1, source_target_pairs={{0,16},{8,24},{16,0},{24,8},{1,17},{9,25},{17,1},{25,9},{2,18},{10... | collective-permute-start | bytes 322568 | tf_op jit(solution)/shard_map/ppermute | solution.py:356
  31.0 0.5 collective-permute-done.7.refs_1_
  31.4 0.1 halve_kernel.8
  31.5 1.2 %collective-permute-start.8 = (bf16[60,768]{1,0:T(8,128)(2,1)S(1)}, bf16[60,768]{1,0:T(8,128)(2,1)S(1)}, u32[]{:S(2)}, u32[]{:S(2)}) collective-permute-start(bf16[60,768]{1,0:T(8,128)(2,1)S(1)} %get-tuple-element.96), channel_id=1, source_target_pairs={{0,8},{8,0},{16,24},{24,16},{1,9},{9,1},{17,25},{25,17},{2,10},{10... | collective-permute-start | bytes 276488 | tf_op jit(solution)/shard_map/ppermute | solution.py:356
  32.7 0.0 collective-permute-done.10.refs_1_
  32.7 0.1 middle_kernel.4
  32.7 2.1 %collective-permute-start.14 = (bf16[60,896]{1,0:T(8,128)(2,1)S(1)}, bf16[60,896]{1,0:T(8,128)(2,1)S(1)}, u32[]{:S(2)}, u32[]{:S(2)}) collective-permute-start(bf16[60,896]{1,0:T(8,128)(2,1)S(1)} %get-tuple-element.108.refs_0_), channel_id=1, source_target_pairs={{0,16},{8,24},{16,0},{24,8},{1,17},{9,25},{17,1},{25,9},{2,18},{10... | collective-permute-start | bytes 322568 | tf_op jit(solution)/shard_map/ppermute | solution.py:356
  34.9 0.0 collective-permute-done.9.refs_1_
  34.9 0.1 middle_kernel.5
  35.0 0.7 collective-permute-start.13
  35.7 0.5 collective-permute-done.8.refs_1_
  36.2 0.1 middle_kernel.6
  36.2 0.0 collective-permute-done.6.refs_1_
  36.3 0.1 middle_kernel.7
  36.3 1.9 %collective-permute-start.11 = (bf16[60,896]{1,0:T(8,128)(2,1)S(1)}, bf16[60,896]{1,0:T(8,128)(2,1)S(1)}, u32[]{:S(2)}, u32[]{:S(2)}) collective-permute-start(bf16[60,896]{1,0:T(8,128)(2,1)S(1)} %get-tuple-element.105.refs_0_), channel_id=1, source_target_pairs={{0,8},{8,0},{16,24},{24,16},{1,9},{9,1},{17,25},{25,17},{2,10},{10... | collective-permute-start | bytes 322568 | tf_op jit(solution)/shard_map/ppermute | solution.py:356
  38.2 2.4 %collective-permute-start.12 = (bf16[60,768]{1,0:T(8,128)(2,1)S(1)}, bf16[60,768]{1,0:T(8,128)(2,1)S(1)}, u32[]{:S(2)}, u32[]{:S(2)}) collective-permute-start(bf16[60,768]{1,0:T(8,128)(2,1)S(1)} %get-tuple-element.106.refs_0_), channel_id=1, source_target_pairs={{0,16},{8,24},{16,0},{24,8},{1,17},{9,25},{17,1},{25,9},{2,18},{10... | collective-permute-start | bytes 276488 | tf_op jit(solution)/shard_map/ppermute | solution.py:356
  40.6 0.2 collective-permute-done.13.refs_1_
  40.9 1.4 %collective-permute-start.17 = (bf16[120,896]{1,0:T(8,128)(2,1)S(1)}, bf16[120,896]{1,0:T(8,128)(2,1)S(1)}, u32[]{:S(2)}, u32[]{:S(2)}) collective-permute-start(bf16[120,896]{1,0:T(8,128)(2,1)S(1)} %get-tuple-element.115.refs_0_), channel_id=1, source_target_pairs={{0,16},{8,24},{16,0},{24,8},{1,17},{9,25},{17,1},{25,9},{2,18},{10... | collective-permute-start | bytes 645128 | tf_op jit(solution)/shard_map/ppermute | solution.py:356
  42.3 1.7 %collective-permute-start.18 = (bf16[120,896]{1,0:T(8,128)(2,1)S(1)}, bf16[120,896]{1,0:T(8,128)(2,1)S(1)}, u32[]{:S(2)}, u32[]{:S(2)}) collective-permute-start(bf16[120,896]{1,0:T(8,128)(2,1)S(1)} %get-tuple-element.116.refs_2_), channel_id=1, source_target_pairs={{0,8},{8,0},{16,24},{24,16},{1,9},{9,1},{17,25},{25,17},{2,10},{10... | collective-permute-start | bytes 645128 | tf_op jit(solution)/shard_map/ppermute | solution.py:356
  44.0 0.2 collective-permute-done.12.refs_1_
  44.3 0.0 collective-permute-done.11.refs_1_
  44.3 1.9 %collective-permute-start.15 = (bf16[120,896]{1,0:T(8,128)(2,1)S(1)}, bf16[120,896]{1,0:T(8,128)(2,1)S(1)}, u32[]{:S(2)}, u32[]{:S(2)}) collective-permute-start(bf16[120,896]{1,0:T(8,128)(2,1)S(1)} %get-tuple-element.113.refs_0_), channel_id=1, source_target_pairs={{0,16},{8,24},{16,0},{24,8},{1,17},{9,25},{17,1},{25,9},{2,18},{10... | collective-permute-start | bytes 645128 | tf_op jit(solution)/shard_map/ppermute | solution.py:356
  46.2 0.2 collective-permute-start.16
  46.5 0.3 factors_kernel.1
  46.7 2.3 %collective-permute-done.17.refs_1_ = bf16[120,896]{1,0:T(8,128)(2,1)S(1)} collective-permute-done((bf16[120,896]{1,0:T(8,128)(2,1)S(1)}, bf16[120,896]{1,0:T(8,128)(2,1)S(1)}, u32[]{:S(2)}, u32[]{:S(2)}) %collective-permute-start.17) | collective-permute-done | bytes 215072 | tf_op jit(solution)/shard_map/ppermute | solution.py:356
  49.0 0.1 collective-permute-done.18.refs_3_
  49.1 0.1 stack_kernel.2
  49.2 0.1 collective-permute-start.21
  49.3 2.9 %input_grad_kernel.2 = (f32[80,1280]{1,0:T(8,128)S(1)}, f32[8,128]{1,0:T(8,128)S(1)}) custom-call(bf16[240,1792]{1,0:T(8,128)(2,1)S(1)} %get-tuple-element.119.refs_0_.refs_2_, bf16[1280,3456]{1,0:T(8,128)(2,1)S(1)} %get-tuple-element.75.refs_1_, bf16[1280,3456]{1,0:T(8,128)(2,1)S(1)} %get-tuple-element.76.refs_2_, f32[8,128]{1,0:T(8,128)S(1)} %get-tuple-element.120.refs_3_), custom_call_target="tpu_custom_call" | custom-call | flops 1 | bytes 1 | tf_op jit(solution)/shard_map/input_grad_kernel/pallas_call | solution.py:62
  52.2 0.1 stack_kernel.3
  52.3 0.6 collective-permute-start.22
  52.8 2.7 %input_grad_kernel.3 = (f32[80,1280]{1,0:T(8,128)S(1)}, f32[8,128]{1,0:T(8,128)S(1)}) custom-call(bf16[240,1664]{1,0:T(8,128)(2,1)S(1)} %get-tuple-element.122.refs_0_.refs_2_, bf16[1280,3456]{1,0:T(8,128)(2,1)S(1)} %get-tuple-element.75.refs_1_, bf16[1280,3456]{1,0:T(8,128)(2,1)S(1)} %get-tuple-element.76.refs_2_, ...), custom_call_target="tpu_custom_call" | custom-call | flops 1 | bytes 1 | tf_op jit(solution)/shard_map/input_grad_kernel/pallas_call | solution.py:62
  55.5 0.1 last_kernel.1
  55.7 1.9 %collective-permute-start.20 = (bf16[40,1280]{1,0:T(8,128)(2,1)S(1)}, bf16[40,1280]{1,0:T(8,128)(2,1)S(1)}, u32[]{:S(2)}, u32[]{:S(2)}) collective-permute-start(bf16[40,1280]{1,0:T(8,128)(2,1)S(1)} %get-tuple-element.128), channel_id=1, source_target_pairs={{0,4},{2,6},{4,0},{6,2},{1,5},{3,7},{5,1},{7,3},{8,12},{10,14},{12... | collective-permute-start | bytes 307208 | tf_op jit(solution)/shard_map/ppermute | solution.py:356
  57.6 5.4 %weight_grad_kernel.2 = (bf16[1280,3456]{1,0:T(8,128)(2,1)}, bf16[1280,3456]{1,0:T(8,128)(2,1)}, bf16[3456,1280]{1,0:T(8,128)(2,1)}, f32[8,128]{1,0:T(8,128)S(1)}) custom-call(bf16[1280,160]{1,0:T(8,128)(2,1)S(1)} %get-tuple-element.129.refs_0_, bf16[160,1280]{1,0:T(8,128)(2,1)S(1)} %get-tuple-element.130.refs_1_, ...), custom_call_target="tpu_custom_call" | custom-call | flops 1 | bytes 1 | tf_op jit(solution)/shard_map/weight_grad_kernel/pallas_call | solution.py:62
  63.1 0.6 collective-permute-done.20.refs_1_
  63.7 0.1 collective-permute-start.23
  63.7 5.2 %weight_grad_kernel.3 = (bf16[1280,3456]{1,0:T(8,128)(2,1)}, bf16[1280,3456]{1,0:T(8,128)(2,1)}, bf16[3456,1280]{1,0:T(8,128)(2,1)}, f32[8,128]{1,0:T(8,128)S(1)}) custom-call(bf16[1280,160]{1,0:T(8,128)(2,1)S(1)} %get-tuple-element.129.refs_0_, ...), custom_call_target="tpu_custom_call", output_to_operand_aliasing={{0}: (5, {}), {1}: (6, {}), {2}: (7, {})} | custom-call | flops 1 | bytes 1 | tf_op jit(solution)/shard_map/weight_grad_kernel/pallas_call | solution.py:62
  68.9 0.6 total_kernel.1
  (20 shorter events, 0.2 us)
Async XLA Ops:
  0.6 15.1 %slice-start = ((s8[8847360]{0:T(1024)(128)(4,1)}), s8[4194304]{0:T(1024)(128)(4,1)S(1)}, s32[]{:S(2)}) async-start(s8[8847360]{0:T(1024)(128)(4,1)} %bitcast), calls=%async_computation | async-start | bytes 8388608
  1.7 14.0 %slice-start.1 = ((s8[8847360]{0:T(1024)(128)(4,1)}), s8[4194304]{0:T(1024)(128)(4,1)S(1)}, s32[]{:S(2)}) async-start(s8[8847360]{0:T(1024)(128)(4,1)} %bitcast), calls=%async_computation.1 | async-start | bytes 8388608
  1.7 14.0 %slice-start.2 = ((s8[8847360]{0:T(1024)(128)(4,1)}), s8[458752]{0:T(1024)(128)(4,1)S(1)}, s32[]{:S(2)}) async-start(s8[8847360]{0:T(1024)(128)(4,1)} %bitcast), calls=%async_computation.2 | async-start | bytes 917504
  1.7 12.5 %collective-permute-start = (bf16[40,1280]{1,0:T(8,128)(2,1)S(1)}, bf16[40,1280]{1,0:T(8,128)(2,1)S(1)}, u32[]{:S(2)}, u32[]{:S(2)}) collective-permute-start(bf16[40,1280]{1,0:T(8,128)(2,1)S(1)} %pad_maximum_fusion.refs_0_), channel_id=1, source_target_pairs={{0,2},{2,0},{4,6},{6,4},{1,3},{3,1},{5,7},{7,5},{8,10},{10,8},{12,... | collective-permute-start | bytes 307208 | tf_op jit(solution)/shard_map/ppermute | solution.py:356
  4.8 10.7 %collective-permute-start.1 = (bf16[40,1280]{1,0:T(8,128)(2,1)S(1)}, bf16[40,1280]{1,0:T(8,128)(2,1)S(1)}, u32[]{:S(2)}, u32[]{:S(2)}) collective-permute-start(bf16[40,1280]{1,0:T(8,128)(2,1)S(1)} %pad_maximum_fusion.refs_0_), channel_id=1, source_target_pairs={{0,4},{2,6},{4,0},{6,2},{1,5},{3,7},{5,1},{7,3},{8,12},{10,14},{12... | collective-permute-start | bytes 307208 | tf_op jit(solution)/shard_map/ppermute | solution.py:356
  7.4 8.1 %collective-permute-start.2 = (bf16[40,1280]{1,0:T(8,128)(2,1)S(1)}, bf16[40,1280]{1,0:T(8,128)(2,1)S(1)}, u32[]{:S(2)}, u32[]{:S(2)}) collective-permute-start(bf16[40,1280]{1,0:T(8,128)(2,1)S(1)} %pad_maximum_fusion.refs_0_), channel_id=1, source_target_pairs={{0,6},{2,4},{4,2},{6,0},{1,7},{3,5},{5,3},{7,1},{8,14},{10,12},{12... | collective-permute-start | bytes 307208 | tf_op jit(solution)/shard_map/ppermute | solution.py:356
  17.3 8.8 %collective-permute-start.5 = (bf16[120,896]{1,0:T(8,128)(2,1)S(1)}, bf16[120,896]{1,0:T(8,128)(2,1)S(1)}, u32[]{:S(2)}, u32[]{:S(2)}) collective-permute-start(bf16[120,896]{1,0:T(8,128)(2,1)S(1)} %get-tuple-element.85), channel_id=1, source_target_pairs={{0,8},{8,0},{16,24},{24,16},{1,9},{9,1},{17,25},{25,17},{2,10},{10... | collective-permute-start | bytes 645128 | tf_op jit(solution)/shard_map/ppermute | solution.py:356
  20.3 7.0 %collective-permute-start.4 = (bf16[120,896]{1,0:T(8,128)(2,1)S(1)}, bf16[120,896]{1,0:T(8,128)(2,1)S(1)}, u32[]{:S(2)}, u32[]{:S(2)}) collective-permute-start(bf16[120,896]{1,0:T(8,128)(2,1)S(1)} %get-tuple-element.83), channel_id=1, source_target_pairs={{0,16},{8,24},{16,0},{24,8},{1,17},{9,25},{17,1},{25,9},{2,18},{10... | collective-permute-start | bytes 645128 | tf_op jit(solution)/shard_map/ppermute | solution.py:356
  23.4 6.6 %collective-permute-start.3 = (bf16[120,896]{1,0:T(8,128)(2,1)S(1)}, bf16[120,896]{1,0:T(8,128)(2,1)S(1)}, u32[]{:S(2)}, u32[]{:S(2)}) collective-permute-start(bf16[120,896]{1,0:T(8,128)(2,1)S(1)} %get-tuple-element.81), channel_id=1, source_target_pairs={{0,8},{8,0},{16,24},{24,16},{1,9},{9,1},{17,25},{25,17},{2,10},{10... | collective-permute-start | bytes 645128 | tf_op jit(solution)/shard_map/ppermute | solution.py:356
  25.4 6.0 %collective-permute-start.7 = (bf16[120,768]{1,0:T(8,128)(2,1)S(1)}, bf16[120,768]{1,0:T(8,128)(2,1)S(1)}, u32[]{:S(2)}, u32[]{:S(2)}) collective-permute-start(bf16[120,768]{1,0:T(8,128)(2,1)S(1)} %get-tuple-element.93), channel_id=1, source_target_pairs={{0,16},{8,24},{16,0},{24,8},{1,17},{9,25},{17,1},{25,9},{2,18},{10... | collective-permute-start | bytes 552968 | tf_op jit(solution)/shard_map/ppermute | solution.py:356
  27.4 5.3 %collective-permute-start.10 = (bf16[60,896]{1,0:T(8,128)(2,1)S(1)}, bf16[60,896]{1,0:T(8,128)(2,1)S(1)}, u32[]{:S(2)}, u32[]{:S(2)}) collective-permute-start(bf16[60,896]{1,0:T(8,128)(2,1)S(1)} %get-tuple-element.100), channel_id=1, source_target_pairs={{0,8},{8,0},{16,24},{24,16},{1,9},{9,1},{17,25},{25,17},{2,10},{10... | collective-permute-start | bytes 322568 | tf_op jit(solution)/shard_map/ppermute | solution.py:356
  27.7 7.2 %collective-permute-start.9 = (bf16[60,896]{1,0:T(8,128)(2,1)S(1)}, bf16[60,896]{1,0:T(8,128)(2,1)S(1)}, u32[]{:S(2)}, u32[]{:S(2)}) collective-permute-start(bf16[60,896]{1,0:T(8,128)(2,1)S(1)} %get-tuple-element.98), channel_id=1, source_target_pairs={{0,16},{8,24},{16,0},{24,8},{1,17},{9,25},{17,1},{25,9},{2,18},{10... | collective-permute-start | bytes 322568 | tf_op jit(solution)/shard_map/ppermute | solution.py:356
  30.0 16.4 %collective-permute-start.19 = (bf16[160,1280]{1,0:T(8,128)(2,1)S(1)}, bf16[160,1280]{1,0:T(8,128)(2,1)S(1)}, u32[]{:S(2)}, u32[]{:S(2)}) collective-permute-start(bf16[160,1280]{1,0:T(8,128)(2,1)S(1)} %get-tuple-element.74.refs_0_), channel_id=1, source_target_pairs={{0,1},{1,0},{2,3},{3,2},{4,5},{5,4},{6,7},{7,6},{8,9},{9,8},{10,11... | collective-permute-start | bytes 1228808 | tf_op jit(solution)/shard_map/ppermute | solution.py:356
  30.1 6.1 %collective-permute-start.6 = (bf16[60,896]{1,0:T(8,128)(2,1)S(1)}, bf16[60,896]{1,0:T(8,128)(2,1)S(1)}, u32[]{:S(2)}, u32[]{:S(2)}) collective-permute-start(bf16[60,896]{1,0:T(8,128)(2,1)S(1)} %get-tuple-element.91), channel_id=1, source_target_pairs={{0,16},{8,24},{16,0},{24,8},{1,17},{9,25},{17,1},{25,9},{2,18},{10... | collective-permute-start | bytes 322568 | tf_op jit(solution)/shard_map/ppermute | solution.py:356
  31.5 4.7 %collective-permute-start.8 = (bf16[60,768]{1,0:T(8,128)(2,1)S(1)}, bf16[60,768]{1,0:T(8,128)(2,1)S(1)}, u32[]{:S(2)}, u32[]{:S(2)}) collective-permute-start(bf16[60,768]{1,0:T(8,128)(2,1)S(1)} %get-tuple-element.96), channel_id=1, source_target_pairs={{0,8},{8,0},{16,24},{24,16},{1,9},{9,1},{17,25},{25,17},{2,10},{10... | collective-permute-start | bytes 276488 | tf_op jit(solution)/shard_map/ppermute | solution.py:356
  32.7 7.8 %collective-permute-start.14 = (bf16[60,896]{1,0:T(8,128)(2,1)S(1)}, bf16[60,896]{1,0:T(8,128)(2,1)S(1)}, u32[]{:S(2)}, u32[]{:S(2)}) collective-permute-start(bf16[60,896]{1,0:T(8,128)(2,1)S(1)} %get-tuple-element.108.refs_0_), channel_id=1, source_target_pairs={{0,16},{8,24},{16,0},{24,8},{1,17},{9,25},{17,1},{25,9},{2,18},{10... | collective-permute-start | bytes 322568 | tf_op jit(solution)/shard_map/ppermute | solution.py:356
  35.0 5.9 %collective-permute-start.13 = (bf16[60,896]{1,0:T(8,128)(2,1)S(1)}, bf16[60,896]{1,0:T(8,128)(2,1)S(1)}, u32[]{:S(2)}, u32[]{:S(2)}) collective-permute-start(bf16[60,896]{1,0:T(8,128)(2,1)S(1)} %get-tuple-element.107.refs_0_), channel_id=1, source_target_pairs={{0,8},{8,0},{16,24},{24,16},{1,9},{9,1},{17,25},{25,17},{2,10},{10... | collective-permute-start | bytes 322568 | tf_op jit(solution)/shard_map/ppermute | solution.py:356
  36.3 7.9 %collective-permute-start.11 = (bf16[60,896]{1,0:T(8,128)(2,1)S(1)}, bf16[60,896]{1,0:T(8,128)(2,1)S(1)}, u32[]{:S(2)}, u32[]{:S(2)}) collective-permute-start(bf16[60,896]{1,0:T(8,128)(2,1)S(1)} %get-tuple-element.105.refs_0_), channel_id=1, source_target_pairs={{0,8},{8,0},{16,24},{24,16},{1,9},{9,1},{17,25},{25,17},{2,10},{10... | collective-permute-start | bytes 322568 | tf_op jit(solution)/shard_map/ppermute | solution.py:356
  38.2 6.0 %collective-permute-start.12 = (bf16[60,768]{1,0:T(8,128)(2,1)S(1)}, bf16[60,768]{1,0:T(8,128)(2,1)S(1)}, u32[]{:S(2)}, u32[]{:S(2)}) collective-permute-start(bf16[60,768]{1,0:T(8,128)(2,1)S(1)} %get-tuple-element.106.refs_0_), channel_id=1, source_target_pairs={{0,16},{8,24},{16,0},{24,8},{1,17},{9,25},{17,1},{25,9},{2,18},{10... | collective-permute-start | bytes 276488 | tf_op jit(solution)/shard_map/ppermute | solution.py:356
  40.9 8.1 %collective-permute-start.17 = (bf16[120,896]{1,0:T(8,128)(2,1)S(1)}, bf16[120,896]{1,0:T(8,128)(2,1)S(1)}, u32[]{:S(2)}, u32[]{:S(2)}) collective-permute-start(bf16[120,896]{1,0:T(8,128)(2,1)S(1)} %get-tuple-element.115.refs_0_), channel_id=1, source_target_pairs={{0,16},{8,24},{16,0},{24,8},{1,17},{9,25},{17,1},{25,9},{2,18},{10... | collective-permute-start | bytes 645128 | tf_op jit(solution)/shard_map/ppermute | solution.py:356
  42.3 6.8 %collective-permute-start.18 = (bf16[120,896]{1,0:T(8,128)(2,1)S(1)}, bf16[120,896]{1,0:T(8,128)(2,1)S(1)}, u32[]{:S(2)}, u32[]{:S(2)}) collective-permute-start(bf16[120,896]{1,0:T(8,128)(2,1)S(1)} %get-tuple-element.116.refs_2_), channel_id=1, source_target_pairs={{0,8},{8,0},{16,24},{24,16},{1,9},{9,1},{17,25},{25,17},{2,10},{10... | collective-permute-start | bytes 645128 | tf_op jit(solution)/shard_map/ppermute | solution.py:356
  44.3 7.8 %collective-permute-start.15 = (bf16[120,896]{1,0:T(8,128)(2,1)S(1)}, bf16[120,896]{1,0:T(8,128)(2,1)S(1)}, u32[]{:S(2)}, u32[]{:S(2)}) collective-permute-start(bf16[120,896]{1,0:T(8,128)(2,1)S(1)} %get-tuple-element.113.refs_0_), channel_id=1, source_target_pairs={{0,16},{8,24},{16,0},{24,8},{1,17},{9,25},{17,1},{25,9},{2,18},{10... | collective-permute-start | bytes 645128 | tf_op jit(solution)/shard_map/ppermute | solution.py:356
  46.2 5.9 %collective-permute-start.16 = (bf16[120,768]{1,0:T(8,128)(2,1)S(1)}, bf16[120,768]{1,0:T(8,128)(2,1)S(1)}, u32[]{:S(2)}, u32[]{:S(2)}) collective-permute-start(bf16[120,768]{1,0:T(8,128)(2,1)S(1)} %get-tuple-element.114.refs_2_), channel_id=1, source_target_pairs={{0,8},{8,0},{16,24},{24,16},{1,9},{9,1},{17,25},{25,17},{2,10},{10... | collective-permute-start | bytes 552968 | tf_op jit(solution)/shard_map/ppermute | solution.py:356
  49.2 8.4 %collective-permute-start.21 = (bf16[240,1792]{1,0:T(8,128)(2,1)S(1)}, bf16[240,1792]{1,0:T(8,128)(2,1)S(1)}, u32[]{:S(2)}, u32[]{:S(2)}) collective-permute-start(bf16[240,1792]{1,0:T(8,128)(2,1)S(1)} %get-tuple-element.119.refs_0_.refs_2_), channel_id=1, source_target_pairs={{0,1},{1,0},{2,3},{3,2},{4,5},{5,4},{6,7},{7,6},{8,9},{9,8},{10,11... | collective-permute-start | bytes 2580488 | tf_op jit(solution)/shard_map/ppermute | solution.py:356
  52.3 5.3 %collective-permute-start.22 = (bf16[240,1664]{1,0:T(8,128)(2,1)S(1)}, bf16[240,1664]{1,0:T(8,128)(2,1)S(1)}, u32[]{:S(2)}, u32[]{:S(2)}) collective-permute-start(bf16[240,1664]{1,0:T(8,128)(2,1)S(1)} %get-tuple-element.122.refs_0_.refs_2_), channel_id=1, source_target_pairs={{0,1},{1,0},{2,3},{3,2},{4,5},{5,4},{6,7},{7,6},{8,9},{9,8},{10,11... | collective-permute-start | bytes 2396168 | tf_op jit(solution)/shard_map/ppermute | solution.py:356
  55.7 8.0 %collective-permute-start.20 = (bf16[40,1280]{1,0:T(8,128)(2,1)S(1)}, bf16[40,1280]{1,0:T(8,128)(2,1)S(1)}, u32[]{:S(2)}, u32[]{:S(2)}) collective-permute-start(bf16[40,1280]{1,0:T(8,128)(2,1)S(1)} %get-tuple-element.128), channel_id=1, source_target_pairs={{0,4},{2,6},{4,0},{6,2},{1,5},{3,7},{5,1},{7,3},{8,12},{10,14},{12... | collective-permute-start | bytes 307208 | tf_op jit(solution)/shard_map/ppermute | solution.py:356
  63.7 5.2 %collective-permute-start.23 = (bf16[20,1280]{1,0:T(8,128)(2,1)S(1)}, bf16[20,1280]{1,0:T(8,128)(2,1)S(1)}, u32[]{:S(2)}, u32[]{:S(2)}) collective-permute-start(bf16[20,1280]{1,0:T(8,128)(2,1)S(1)} %get-tuple-element.134), channel_id=1, source_target_pairs={{0,2},{2,0},{4,6},{6,4},{1,3},{3,1},{5,7},{7,5},{8,10},{10,8},{12,... | collective-permute-start | bytes 153608 | tf_op jit(solution)/shard_map/ppermute | solution.py:356

commit v11 on v7

--- a/solution.py
+++ b/solution.py
@@ -182,45 +182,47 @@
     return line.call(join_kernel, (first, second), [shaped(rows, first.shape[1])])[0]
 
 
-def stack_kernel(axes, *refs):
-    out_ref = refs[-1]
+def stack_kernel(axes, ahead, *refs):
+    *refs, out_ref = refs
     begin = 0
-    for at, (near, far) in enumerate(axes):
-        mine, other = refs[2 * at][...].astype(F32), refs[2 * at + 1][...].astype(F32)
-        columns = mine.shape[1]
-        half, rows = mine.shape[0] // 2, mine.shape[0] // 6
-        slots = {0: mine[:half], near: mine[half:]}
-        slots |= {far: other[:half], near ^ far: other[half:]}
-        cuts = [slots[slot][k * rows : (k + 1) * rows] for k in range(3) for slot in range(4)]
-        out_ref[:, begin : begin + columns] = joined(*cuts).astype(BF16)
-        begin += columns
-
-
-def stack(line, axes, blocks):
-    rows = 2 * blocks[0][0].shape[0]
-    columns = sum(mine.shape[1] for mine, _ in blocks)
-    return line.call(
-        functools.partial(stack_kernel, axes),
-        [block for pair in blocks for block in pair],
+    for ref in refs[2:]:
+        out_ref[:, begin : begin + ref.shape[1]] = ref[...]
+        begin += ref.shape[1]
+    near, far = axes
+    mine, other = refs[0][...].astype(F32), refs[1][...].astype(F32)
+    half, rows = mine.shape[0] // 2, mine.shape[0] // 6
+    slots = {0: mine[:half], near: mine[half:]}
+    slots |= {far: other[:half], near ^ far: other[half:]}
+    cuts = [slots[slot][k * rows : (k + 1) * rows] for k in range(3) for slot in range(4)]
+    out_ref[:, begin:] = joined(*cuts).astype(BF16)
+
+
+def stack(line, axes, mine, other, ahead):
+    rows = 2 * mine.shape[0]
+    columns = mine.shape[1] + sum(block.shape[1] for block in ahead)
+    return line.call(
+        functools.partial(stack_kernel, axes, len(ahead)),
+        (mine, other, *ahead),
         [shaped(rows, columns)],
     )[0]
 
 
-def input_grad_kernel(begin, stack_ref, gate_ref, up_ref, *refs):
-    there = pl.ds(begin, stack_ref.shape[1])
+def input_grad_kernel(begin, columns, stack_ref, gate_ref, up_ref, *refs):
+    there = pl.ds(begin, columns)
+    here = pl.ds(stack_ref.shape[1] - columns, columns)
     group = stack_ref.shape[0] // 3
     grad = lax.dot_general(
-        stack_ref[:group], gate_ref[:, there], NT, preferred_element_type=F32
+        stack_ref[:group, here], gate_ref[:, there], NT, preferred_element_type=F32
     ) + lax.dot_general(
-        stack_ref[group : 2 * group], up_ref[:, there], NT, preferred_element_type=F32
+        stack_ref[group : 2 * group, here], up_ref[:, there], NT, preferred_element_type=F32
     )
     refs[-1][...] = grad + refs[0][...] if len(refs) > 1 else grad
 
 
-def input_grad(line, begin, stacked, gate_weight, up_weight, start):
+def input_grad(line, begin, columns, stacked, gate_weight, up_weight, start):
     shape = (stacked.shape[0] // 3, gate_weight.shape[0])
     return line.call(
-        functools.partial(input_grad_kernel, begin),
+        functools.partial(input_grad_kernel, begin, columns),
         (stacked, gate_weight, up_weight, *start),
         [shaped(*shape, F32)],
     )
@@ -253,6 +255,8 @@
         copies.append(pltpu.make_async_copy(source, target, sems.at[at, len(copies) // 3]))
         copies[-1].start()
 
+    width = y_ref.shape[1]
+    blocks = [pl.ds(at, min(TILE, width - at)) for at in range(0, width, TILE)]
     begin = 0
     for mine_ref, other_ref in zip(mine_refs, other_refs):
         columns = mine_ref.shape[1]
@@ -264,17 +268,18 @@
                 mine, other = mine_ref[cut, source], other_ref[cut, source]
                 both[at, :group, here] = jnp.where(first, mine, other)
                 both[at, group:, here] = jnp.where(first, other, mine)
-            gate[:, here] = jnp.dot(
-                xt_ref[...], both[0, :, here], preferred_element_type=F32
-            ).astype(BF16)
-            send(0, gate.at[:, here], outs[0].at[:, here])
-            up[:, here] = jnp.dot(
-                xt_ref[...], both[1, :, here], preferred_element_type=F32
-            ).astype(BF16)
-            send(1, up.at[:, here], outs[1].at[:, here])
-            down[here, :] = lax.dot_general(
-                both[2, :, here], y_ref[...], TN, preferred_element_type=F32
-            ).astype(BF16)
+            for at, grad in enumerate((gate, up)):
+                rows = both[at, :, here]
+                for block in blocks:
+                    grad[block, here] = jnp.dot(
+                        xt_ref[block], rows, preferred_element_type=F32
+                    ).astype(BF16)
+                send(at, grad.at[:, here], outs[at].at[:, here])
+            hidden = both[2, :, here].T
+            for block in blocks:
+                down[here, block] = jnp.dot(
+                    hidden, y_ref[:, block], preferred_element_type=F32
+                ).astype(BF16)
             send(2, down.at[here], outs[2].at[here])
         begin += columns
     for copy in copies:
@@ -367,12 +372,16 @@
         got[at] = swap(kept[at], "wa", n_wa, far)
 
     xt, y_all = factors(line, xy, xy_other)
-    mine, other, grad = [], [], ()
-    for at in range(0, CHUNKS, 2):
-        pair = slice(at, at + 2)
-        mine.append(stack(line, axes[pair], list(zip(kept, got))[pair]))
-        other.append(swap(mine[-1], "row", n_row, 1))
-        grad = input_grad(line, chunks[at][0], mine[-1], gate, up, grad)
+    mine, other, ahead, grad = [], [], [], ()
+    for at, (begin, columns) in enumerate(chunks):
+        stacked = stack(line, axes[at], kept[at], got[at], ahead)
+        if at in [1, 3]:
+            mine.append(stacked)
+            other.append(swap(stacked, "row", n_row, 1))
+            ahead = []
+        else:
+            ahead = [stacked]
+        grad = input_grad(line, begin, columns, stacked, gate, up, grad)
     own, *sends = last_pieces(line, n_ha, grad[0])
     received = [swap(sent, "ha", n_ha, k + 1) for k, sent in enumerate(sends)]
     grads = weight_grad(line, xt, y_all, mine, other)

time: 69.9 us -> 70.1 us (level)
    pallas_call x26 -> x30, Pallas kernels: 30 us -> 30.3 us  [call(): pl.pallas_call(body, in_specs=(in_specs or [IN_VMEM] * count) + [IN_VMEM]...]
  transfers between devices with their start and end apart: 25 -> 25, of which waited for: 9 -> 8; matrix products, arithmetic and copies ran while one was open for 0% -> 0% of each run, Pallas kernels for 40% -> 40%
where the time goes in v11:
time: 70.1 us; the launch traced here: 70 us
  Pallas kernels  30.3 us (43%)
  starting transfers between devices  29.7 us (42%)
  waiting for transfers between devices  7.99 us (11%)
  other arithmetic  1.03 us (1%)
  between operations  0.92 us (1%)
    pallas_call x30, Pallas kernels, call(): pl.pallas_call(body, in_specs=(in_specs or [IN_VMEM] * count) + [IN_VMEM]...  30.3 us
    ppermute x25, starting transfers between devices, swap(): return lax.ppermute(value, axis, [(at, at ^ step) for at in range(size)])  29.7 us
    ppermute x25, waiting for transfers between devices, swap(): return lax.ppermute(value, axis, [(at, at ^ step) for at in range(size)])  7.99 us
  transfers between devices with their start and end apart: 25, of which 8 were waited for; matrix products, arithmetic and copies ran while one was open for 0% of the time, Pallas kernels for 40%

profile of v11, /device:TPU:0, one launch (start us, length us, event | category | flops | bytes accessed | tf_op | source)
XLA Modules:
  0.0 70.0 jit_solution(17139817660900152555)
XLA Ops:
  0.6 0.0 slice-start
  0.6 1.0 %pad_maximum_fusion.refs_0_ = bf16[40,1280]{1,0:T(8,128)(2,1)S(1)} fusion(bf16[20,1280]{1,0:T(8,128)(2,1)} %param.6, bf16[20,1280]{1,0:T(8,128)(2,1)} %param.5), kind=kLoop, calls=%fused_computation | loop fusion | flops 204800 | bytes 204800 | tf_op jit(solution)/shard_map/concatenate | solution.py:351
  1.7 0.0 slice-start.1
  1.7 5.1 %collective-permute-start.2 = (bf16[40,1280]{1,0:T(8,128)(2,1)S(1)}, bf16[40,1280]{1,0:T(8,128)(2,1)S(1)}, u32[]{:S(2)}, u32[]{:S(2)}) collective-permute-start(bf16[40,1280]{1,0:T(8,128)(2,1)S(1)} %pad_maximum_fusion.refs_0_), channel_id=1, source_target_pairs={{0,6},{2,4},{4,2},{6,0},{1,7},{3,5},{5,3},{7,1},{8,14},{10,12},{12... | collective-permute-start | bytes 307208 | tf_op jit(solution)/shard_map/ppermute | solution.py:340
  6.8 0.6 collective-permute-start
  7.5 6.8 %load_kernel.1 = (bf16[1280,3456]{1,0:T(8,128)(2,1)S(1)}, bf16[1280,3456]{1,0:T(8,128)(2,1)S(1)}, f32[8,128]{1,0:T(8,128)}) custom-call(bf16[1280,3456]{1,0:T(8,128)(2,1)} %refs_0_.1, bf16[1280,3456]{1,0:T(8,128)(2,1)} %refs_1_.1), custom_call_target="tpu_custom_call" | custom-call | flops 1 | bytes 1 | tf_op jit(solution)/shard_map/load_kernel/pallas_call | solution.py:62
  14.3 1.2 %collective-permute-done.1.refs_2_ = bf16[40,1280]{1,0:T(8,128)(2,1)S(1)} collective-permute-done((bf16[40,1280]{1,0:T(8,128)(2,1)S(1)}, bf16[40,1280]{1,0:T(8,128)(2,1)S(1)}, u32[]{:S(2)}, u32[]{:S(2)}) %collective-permute-start.1) | collective-permute-done | bytes 102432 | tf_op jit(solution)/shard_map/ppermute | solution.py:340
  15.4 0.2 order_kernel.1
  15.7 1.5 %forward_kernel.4 = (f32[120,896]{1,0:T(8,128)S(1)}, bf16[120,896]{1,0:T(8,128)(2,1)S(1)}, f32[8,128]{1,0:T(8,128)S(1)}) custom-call(bf16[160,1280]{1,0:T(8,128)(2,1)S(1)} %get-tuple-element.77.refs_0_, bf16[1280,3456]{1,0:T(8,128)(2,1)S(1)} %get-tuple-element.78.refs_1_, bf16[1280,3456]{1,0:T(8,128)(2,1)S(1)} %get-tuple-element.79.refs_2_, ...), custom_call_target="tpu_custom_call" | custom-call | flops 1 | bytes 1 | tf_op jit(solution)/shard_map/forward_kernel/pallas_call | solution.py:62
  17.2 1.6 %collective-permute-start.6 = (bf16[120,896]{1,0:T(8,128)(2,1)S(1)}, bf16[120,896]{1,0:T(8,128)(2,1)S(1)}, u32[]{:S(2)}, u32[]{:S(2)}) collective-permute-start(bf16[120,896]{1,0:T(8,128)(2,1)S(1)} %get-tuple-element.91), channel_id=1, source_target_pairs={{0,8},{8,0},{16,24},{24,16},{1,9},{9,1},{17,25},{25,17},{2,10},{10... | collective-permute-start | bytes 645128 | tf_op jit(solution)/shard_map/ppermute | solution.py:340
  18.7 1.5 %forward_kernel.5 = (f32[120,896]{1,0:T(8,128)S(1)}, bf16[120,896]{1,0:T(8,128)(2,1)S(1)}, f32[8,128]{1,0:T(8,128)S(1)}) custom-call(bf16[160,1280]{1,0:T(8,128)(2,1)S(1)} %get-tuple-element.77.refs_0_, bf16[1280,3456]{1,0:T(8,128)(2,1)S(1)} %get-tuple-element.78.refs_1_, bf16[1280,3456]{1,0:T(8,128)(2,1)S(1)} %get-tuple-element.79.refs_2_, ...), custom_call_target="tpu_custom_call" | custom-call | flops 1 | bytes 1 | tf_op jit(solution)/shard_map/forward_kernel/pallas_call | solution.py:62
  20.2 1.6 %collective-permute-start.5 = (bf16[120,896]{1,0:T(8,128)(2,1)S(1)}, bf16[120,896]{1,0:T(8,128)(2,1)S(1)}, u32[]{:S(2)}, u32[]{:S(2)}) collective-permute-start(bf16[120,896]{1,0:T(8,128)(2,1)S(1)} %get-tuple-element.89), channel_id=1, source_target_pairs={{0,16},{8,24},{16,0},{24,8},{1,17},{9,25},{17,1},{25,9},{2,18},{10... | collective-permute-start | bytes 645128 | tf_op jit(solution)/shard_map/ppermute | solution.py:340
  21.8 1.5 %forward_kernel.6 = (f32[120,896]{1,0:T(8,128)S(1)}, bf16[120,896]{1,0:T(8,128)(2,1)S(1)}, f32[8,128]{1,0:T(8,128)S(1)}) custom-call(bf16[160,1280]{1,0:T(8,128)(2,1)S(1)} %get-tuple-element.77.refs_0_, bf16[1280,3456]{1,0:T(8,128)(2,1)S(1)} %get-tuple-element.78.refs_1_, bf16[1280,3456]{1,0:T(8,128)(2,1)S(1)} %get-tuple-element.79.refs_2_, ...), custom_call_target="tpu_custom_call" | custom-call | flops 1 | bytes 1 | tf_op jit(solution)/shard_map/forward_kernel/pallas_call | solution.py:62
  23.3 0.6 collective-permute-start.4
  23.9 1.4 %forward_kernel.7 = (f32[120,768]{1,0:T(8,128)S(1)}, bf16[120,768]{1,0:T(8,128)(2,1)S(1)}, f32[8,128]{1,0:T(8,128)S(1)}) custom-call(bf16[160,1280]{1,0:T(8,128)(2,1)S(1)} %get-tuple-element.77.refs_0_, bf16[1280,3456]{1,0:T(8,128)(2,1)S(1)} %get-tuple-element.78.refs_1_, bf16[1280,3456]{1,0:T(8,128)(2,1)S(1)} %get-tuple-element.79.refs_2_, ...), custom_call_target="tpu_custom_call" | custom-call | flops 1 | bytes 1 | tf_op jit(solution)/shard_map/forward_kernel/pallas_call | solution.py:62
  25.3 0.6 collective-permute-start.3
  25.9 0.1 halve_kernel.4
  26.0 0.4 collective-permute-done.5.refs_1_
  26.4 0.1 halve_kernel.5
  26.5 1.2 %collective-permute-start.9 = (bf16[60,896]{1,0:T(8,128)(2,1)S(1)}, bf16[60,896]{1,0:T(8,128)(2,1)S(1)}, u32[]{:S(2)}, u32[]{:S(2)}) collective-permute-start(bf16[60,896]{1,0:T(8,128)(2,1)S(1)} %get-tuple-element.101), channel_id=1, source_target_pairs={{0,8},{8,0},{16,24},{24,16},{1,9},{9,1},{17,25},{25,17},{2,10},{10... | collective-permute-start | bytes 322568 | tf_op jit(solution)/shard_map/ppermute | solution.py:340
  27.6 1.5 %collective-permute-start.8 = (bf16[60,896]{1,0:T(8,128)(2,1)S(1)}, bf16[60,896]{1,0:T(8,128)(2,1)S(1)}, u32[]{:S(2)}, u32[]{:S(2)}) collective-permute-start(bf16[60,896]{1,0:T(8,128)(2,1)S(1)} %get-tuple-element.99), channel_id=1, source_target_pairs={{0,16},{8,24},{16,0},{24,8},{1,17},{9,25},{17,1},{25,9},{2,18},{10... | collective-permute-start | bytes 322568 | tf_op jit(solution)/shard_map/ppermute | solution.py:340
  29.1 0.0 collective-permute-start.19
  29.1 1.4 %collective-permute-done.4.refs_1_ = bf16[120,896]{1,0:T(8,128)(2,1)S(1)} collective-permute-done((bf16[120,896]{1,0:T(8,128)(2,1)S(1)}, bf16[120,896]{1,0:T(8,128)(2,1)S(1)}, u32[]{:S(2)}, u32[]{:S(2)}) %collective-permute-start.4) | collective-permute-done | bytes 215072 | tf_op jit(solution)/shard_map/ppermute | solution.py:340
  30.5 0.1 halve_kernel.6
  30.6 0.6 collective-permute-start.13
  31.1 0.4 collective-permute-done.3.refs_1_
  31.6 0.1 halve_kernel.7
  31.6 1.5 %collective-permute-start.7 = (bf16[60,768]{1,0:T(8,128)(2,1)S(1)}, bf16[60,768]{1,0:T(8,128)(2,1)S(1)}, u32[]{:S(2)}, u32[]{:S(2)}) collective-permute-start(bf16[60,768]{1,0:T(8,128)(2,1)S(1)} %get-tuple-element.97), channel_id=1, source_target_pairs={{0,8},{8,0},{16,24},{24,16},{1,9},{9,1},{17,25},{25,17},{2,10},{10... | collective-permute-start | bytes 276488 | tf_op jit(solution)/shard_map/ppermute | solution.py:340
  33.1 0.0 collective-permute-done.9.refs_1_
  33.1 0.1 middle_kernel.4
  33.2 0.8 %collective-permute-start.12 = (bf16[60,896]{1,0:T(8,128)(2,1)S(1)}, bf16[60,896]{1,0:T(8,128)(2,1)S(1)}, u32[]{:S(2)}, u32[]{:S(2)}) collective-permute-start(bf16[60,896]{1,0:T(8,128)(2,1)S(1)} %get-tuple-element.107.refs_0_), channel_id=1, source_target_pairs={{0,16},{8,24},{16,0},{24,8},{1,17},{9,25},{17,1},{25,9},{2,18},{10... | collective-permute-start | bytes 322568 | tf_op jit(solution)/shard_map/ppermute | solution.py:340
  33.9 0.1 middle_kernel.5
  34.0 1.6 %collective-permute-start.11 = (bf16[60,896]{1,0:T(8,128)(2,1)S(1)}, bf16[60,896]{1,0:T(8,128)(2,1)S(1)}, u32[]{:S(2)}, u32[]{:S(2)}) collective-permute-start(bf16[60,896]{1,0:T(8,128)(2,1)S(1)} %get-tuple-element.106.refs_0_), channel_id=1, source_target_pairs={{0,8},{8,0},{16,24},{24,16},{1,9},{9,1},{17,25},{25,17},{2,10},{10... | collective-permute-start | bytes 322568 | tf_op jit(solution)/shard_map/ppermute | solution.py:340
  35.6 1.1 %collective-permute-done.7.refs_1_ = bf16[60,768]{1,0:T(8,128)(2,1)S(1)} collective-permute-done((bf16[60,768]{1,0:T(8,128)(2,1)S(1)}, bf16[60,768]{1,0:T(8,128)(2,1)S(1)}, u32[]{:S(2)}, u32[]{:S(2)}) %collective-permute-start.7) | collective-permute-done | bytes 92192 | tf_op jit(solution)/shard_map/ppermute | solution.py:340
  36.8 0.1 middle_kernel.6
  36.8 0.0 collective-permute-done.13.refs_1_
  36.8 0.1 middle_kernel.7
  36.9 1.8 %collective-permute-start.15 = (bf16[60,896]{1,0:T(8,128)(2,1)S(1)}, bf16[60,896]{1,0:T(8,128)(2,1)S(1)}, u32[]{:S(2)}, u32[]{:S(2)}) collective-permute-start(bf16[60,896]{1,0:T(8,128)(2,1)S(1)} %get-tuple-element.115.refs_0_), channel_id=1, source_target_pairs={{0,8},{8,0},{16,24},{24,16},{1,9},{9,1},{17,25},{25,17},{2,10},{10... | collective-permute-start | bytes 322568 | tf_op jit(solution)/shard_map/ppermute | solution.py:340
  38.7 0.9 %collective-permute-start.10 = (bf16[60,768]{1,0:T(8,128)(2,1)S(1)}, bf16[60,768]{1,0:T(8,128)(2,1)S(1)}, u32[]{:S(2)}, u32[]{:S(2)}) collective-permute-start(bf16[60,768]{1,0:T(8,128)(2,1)S(1)} %get-tuple-element.105.refs_0_), channel_id=1, source_target_pairs={{0,16},{8,24},{16,0},{24,8},{1,17},{9,25},{17,1},{25,9},{2,18},{10... | collective-permute-start | bytes 276488 | tf_op jit(solution)/shard_map/ppermute | solution.py:340
  39.6 0.0 collective-permute-done.12.refs_1_
  39.7 0.3 collective-permute-done.11.refs_1_
  40.0 1.0 %collective-permute-start.18 = (bf16[120,896]{1,0:T(8,128)(2,1)S(1)}, bf16[120,896]{1,0:T(8,128)(2,1)S(1)}, u32[]{:S(2)}, u32[]{:S(2)}) collective-permute-start(bf16[120,896]{1,0:T(8,128)(2,1)S(1)} %get-tuple-element.119.refs_0_), channel_id=1, source_target_pairs={{0,16},{8,24},{16,0},{24,8},{1,17},{9,25},{17,1},{25,9},{2,18},{10... | collective-permute-start | bytes 645128 | tf_op jit(solution)/shard_map/ppermute | solution.py:340
  41.0 1.7 %collective-permute-start.17 = (bf16[120,896]{1,0:T(8,128)(2,1)S(1)}, bf16[120,896]{1,0:T(8,128)(2,1)S(1)}, u32[]{:S(2)}, u32[]{:S(2)}) collective-permute-start(bf16[120,896]{1,0:T(8,128)(2,1)S(1)} %get-tuple-element.118.refs_0_), channel_id=1, source_target_pairs={{0,8},{8,0},{16,24},{24,16},{1,9},{9,1},{17,25},{25,17},{2,10},{10... | collective-permute-start | bytes 645128 | tf_op jit(solution)/shard_map/ppermute | solution.py:340
  42.7 1.7 %collective-permute-done.10.refs_1_ = bf16[60,768]{1,0:T(8,128)(2,1)S(1)} collective-permute-done((bf16[60,768]{1,0:T(8,128)(2,1)S(1)}, bf16[60,768]{1,0:T(8,128)(2,1)S(1)}, u32[]{:S(2)}, u32[]{:S(2)}) %collective-permute-start.10) | collective-permute-done | bytes 92192 | tf_op jit(solution)/shard_map/ppermute | solution.py:340
  44.5 1.0 %collective-permute-start.16 = (bf16[120,896]{1,0:T(8,128)(2,1)S(1)}, bf16[120,896]{1,0:T(8,128)(2,1)S(1)}, u32[]{:S(2)}, u32[]{:S(2)}) collective-permute-start(bf16[120,896]{1,0:T(8,128)(2,1)S(1)} %get-tuple-element.117.refs_0_), channel_id=1, source_target_pairs={{0,16},{8,24},{16,0},{24,8},{1,17},{9,25},{17,1},{25,9},{2,18},{10... | collective-permute-start | bytes 645128 | tf_op jit(solution)/shard_map/ppermute | solution.py:340
  45.5 1.1 %collective-permute-start.14 = (bf16[120,768]{1,0:T(8,128)(2,1)S(1)}, bf16[120,768]{1,0:T(8,128)(2,1)S(1)}, u32[]{:S(2)}, u32[]{:S(2)}) collective-permute-start(bf16[120,768]{1,0:T(8,128)(2,1)S(1)} %get-tuple-element.114.refs_0_), channel_id=1, source_target_pairs={{0,8},{8,0},{16,24},{24,16},{1,9},{9,1},{17,25},{25,17},{2,10},{10... | collective-permute-start | bytes 552968 | tf_op jit(solution)/shard_map/ppermute | solution.py:340
  46.6 0.3 factors_kernel.1
  46.9 1.4 %collective-permute-done.18.refs_1_ = bf16[120,896]{1,0:T(8,128)(2,1)S(1)} collective-permute-done((bf16[120,896]{1,0:T(8,128)(2,1)S(1)}, bf16[120,896]{1,0:T(8,128)(2,1)S(1)}, u32[]{:S(2)}, u32[]{:S(2)}) %collective-permute-start.18) | collective-permute-done | bytes 215072 | tf_op jit(solution)/shard_map/ppermute | solution.py:340
  48.3 0.1 stack_kernel.4
  48.4 1.5 %input_grad_kernel.4 = (f32[80,1280]{1,0:T(8,128)S(1)}, f32[8,128]{1,0:T(8,128)S(1)}) custom-call(bf16[240,896]{1,0:T(8,128)(2,1)S(1)} %get-tuple-element.122.refs_0_.refs_2_, bf16[1280,3456]{1,0:T(8,128)(2,1)S(1)} %get-tuple-element.78.refs_1_, bf16[1280,3456]{1,0:T(8,128)(2,1)S(1)} %get-tuple-element.79.refs_2_, f32[8,128]{1,0:T(8,128)S(1)} %get-tuple-element.123.refs_3_), custom_call_target="tpu_custom_call" | custom-call | flops 1 | bytes 1 | tf_op jit(solution)/shard_map/input_grad_kernel/pallas_call | solution.py:62
  49.9 0.1 stack_kernel.5
  50.0 0.1 collective-permute-start.23
  50.1 1.5 %input_grad_kernel.5 = (f32[80,1280]{1,0:T(8,128)S(1)}, f32[8,128]{1,0:T(8,128)S(1)}) custom-call(bf16[240,1792]{1,0:T(8,128)(2,1)S(1)} %get-tuple-element.125.refs_0_.refs_2_, bf16[1280,3456]{1,0:T(8,128)(2,1)S(1)} %get-tuple-element.78.refs_1_, bf16[1280,3456]{1,0:T(8,128)(2,1)S(1)} %get-tuple-element.79.refs_2_, ...), custom_call_target="tpu_custom_call" | custom-call | flops 1 | bytes 1 | tf_op jit(solution)/shard_map/input_grad_kernel/pallas_call | solution.py:62
  51.6 0.1 stack_kernel.6
  51.7 1.5 %input_grad_kernel.6 = (f32[80,1280]{1,0:T(8,128)S(1)}, f32[8,128]{1,0:T(8,128)S(1)}) custom-call(bf16[240,896]{1,0:T(8,128)(2,1)S(1)} %get-tuple-element.129.refs_0_.refs_2_, bf16[1280,3456]{1,0:T(8,128)(2,1)S(1)} %get-tuple-element.78.refs_1_, bf16[1280,3456]{1,0:T(8,128)(2,1)S(1)} %get-tuple-element.79.refs_2_, ...), custom_call_target="tpu_custom_call" | custom-call | flops 1 | bytes 1 | tf_op jit(solution)/shard_map/input_grad_kernel/pallas_call | solution.py:62
  53.2 0.1 stack_kernel.7
  53.3 0.6 collective-permute-start.24
  53.9 1.3 %input_grad_kernel.7 = (f32[80,1280]{1,0:T(8,128)S(1)}, f32[8,128]{1,0:T(8,128)S(1)}) custom-call(bf16[240,1664]{1,0:T(8,128)(2,1)S(1)} %get-tuple-element.133.refs_0_.refs_3_, bf16[1280,3456]{1,0:T(8,128)(2,1)S(1)} %get-tuple-element.78.refs_1_, bf16[1280,3456]{1,0:T(8,128)(2,1)S(1)} %get-tuple-element.79.refs_2_, ...), custom_call_target="tpu_custom_call" | custom-call | flops 1 | bytes 1 | tf_op jit(solution)/shard_map/input_grad_kernel/pallas_call | solution.py:62
  55.2 0.2 last_kernel.1
  55.3 0.4 collective-permute-start.20
  55.7 2.6 %collective-permute-start.21 = (bf16[20,1280]{1,0:T(8,128)(2,1)S(1)}, bf16[20,1280]{1,0:T(8,128)(2,1)S(1)}, u32[]{:S(2)}, u32[]{:S(2)}) collective-permute-start(bf16[20,1280]{1,0:T(8,128)(2,1)S(1)} %get-tuple-element.140), channel_id=1, source_target_pairs={{0,4},{2,6},{4,0},{6,2},{1,5},{3,7},{5,1},{7,3},{8,12},{10,14},{12... | collective-permute-start | bytes 153608 | tf_op jit(solution)/shard_map/ppermute | solution.py:340
  58.4 1.4 %collective-permute-start.22 = (bf16[20,1280]{1,0:T(8,128)(2,1)S(1)}, bf16[20,1280]{1,0:T(8,128)(2,1)S(1)}, u32[]{:S(2)}, u32[]{:S(2)}) collective-permute-start(bf16[20,1280]{1,0:T(8,128)(2,1)S(1)} %get-tuple-element.141), channel_id=1, source_target_pairs={{0,6},{2,4},{4,2},{6,0},{1,7},{3,5},{5,3},{7,1},{8,14},{10,12},{12... | collective-permute-start | bytes 153608 | tf_op jit(solution)/shard_map/ppermute | solution.py:340
  59.8 9.5 %weight_grad_kernel.1 = (bf16[1280,3456]{1,0:T(8,128)(2,1)}, bf16[1280,3456]{1,0:T(8,128)(2,1)}, bf16[3456,1280]{1,0:T(8,128)(2,1)}, f32[8,128]{1,0:T(8,128)S(1)}) custom-call(bf16[1280,160]{1,0:T(8,128)(2,1)S(1)} %get-tuple-element.142.refs_0_, bf16[160,1280]{1,0:T(8,128)(2,1)S(1)} %get-tuple-element.143.refs_1_, ...), custom_call_target="tpu_custom_call" | custom-call | flops 1 | bytes 1 | tf_op jit(solution)/shard_map/weight_grad_kernel/pallas_call | solution.py:62
  69.3 0.7 total_kernel.1
  (24 shorter events, 0.2 us)
Async XLA Ops:
  0.6 15.0 %slice-start = ((s8[8847360]{0:T(1024)(128)(4,1)}), s8[4194304]{0:T(1024)(128)(4,1)S(1)}, s32[]{:S(2)}) async-start(s8[8847360]{0:T(1024)(128)(4,1)} %bitcast), calls=%async_computation | async-start | bytes 8388608
  1.7 14.0 %slice-start.1 = ((s8[8847360]{0:T(1024)(128)(4,1)}), s8[4194304]{0:T(1024)(128)(4,1)S(1)}, s32[]{:S(2)}) async-start(s8[8847360]{0:T(1024)(128)(4,1)} %bitcast), calls=%async_computation.1 | async-start | bytes 8388608
  1.7 14.0 %slice-start.2 = ((s8[8847360]{0:T(1024)(128)(4,1)}), s8[458752]{0:T(1024)(128)(4,1)S(1)}, s32[]{:S(2)}) async-start(s8[8847360]{0:T(1024)(128)(4,1)} %bitcast), calls=%async_computation.2 | async-start | bytes 917504
  1.7 12.5 %collective-permute-start.2 = (bf16[40,1280]{1,0:T(8,128)(2,1)S(1)}, bf16[40,1280]{1,0:T(8,128)(2,1)S(1)}, u32[]{:S(2)}, u32[]{:S(2)}) collective-permute-start(bf16[40,1280]{1,0:T(8,128)(2,1)S(1)} %pad_maximum_fusion.refs_0_), channel_id=1, source_target_pairs={{0,6},{2,4},{4,2},{6,0},{1,7},{3,5},{5,3},{7,1},{8,14},{10,12},{12... | collective-permute-start | bytes 307208 | tf_op jit(solution)/shard_map/ppermute | solution.py:340
  6.8 8.6 %collective-permute-start.1 = (bf16[40,1280]{1,0:T(8,128)(2,1)S(1)}, bf16[40,1280]{1,0:T(8,128)(2,1)S(1)}, u32[]{:S(2)}, u32[]{:S(2)}) collective-permute-start(bf16[40,1280]{1,0:T(8,128)(2,1)S(1)} %pad_maximum_fusion.refs_0_), channel_id=1, source_target_pairs={{0,4},{2,6},{4,0},{6,2},{1,5},{3,7},{5,1},{7,3},{8,12},{10,14},{12... | collective-permute-start | bytes 307208 | tf_op jit(solution)/shard_map/ppermute | solution.py:340
  6.8 8.6 %collective-permute-start = (bf16[40,1280]{1,0:T(8,128)(2,1)S(1)}, bf16[40,1280]{1,0:T(8,128)(2,1)S(1)}, u32[]{:S(2)}, u32[]{:S(2)}) collective-permute-start(bf16[40,1280]{1,0:T(8,128)(2,1)S(1)} %pad_maximum_fusion.refs_0_), channel_id=1, source_target_pairs={{0,2},{2,0},{4,6},{6,4},{1,3},{3,1},{5,7},{7,5},{8,10},{10,8},{12,... | collective-permute-start | bytes 307208 | tf_op jit(solution)/shard_map/ppermute | solution.py:340
  17.2 8.8 %collective-permute-start.6 = (bf16[120,896]{1,0:T(8,128)(2,1)S(1)}, bf16[120,896]{1,0:T(8,128)(2,1)S(1)}, u32[]{:S(2)}, u32[]{:S(2)}) collective-permute-start(bf16[120,896]{1,0:T(8,128)(2,1)S(1)} %get-tuple-element.91), channel_id=1, source_target_pairs={{0,8},{8,0},{16,24},{24,16},{1,9},{9,1},{17,25},{25,17},{2,10},{10... | collective-permute-start | bytes 645128 | tf_op jit(solution)/shard_map/ppermute | solution.py:340
  20.2 6.2 %collective-permute-start.5 = (bf16[120,896]{1,0:T(8,128)(2,1)S(1)}, bf16[120,896]{1,0:T(8,128)(2,1)S(1)}, u32[]{:S(2)}, u32[]{:S(2)}) collective-permute-start(bf16[120,896]{1,0:T(8,128)(2,1)S(1)} %get-tuple-element.89), channel_id=1, source_target_pairs={{0,16},{8,24},{16,0},{24,8},{1,17},{9,25},{17,1},{25,9},{2,18},{10... | collective-permute-start | bytes 645128 | tf_op jit(solution)/shard_map/ppermute | solution.py:340
  23.3 7.2 %collective-permute-start.4 = (bf16[120,896]{1,0:T(8,128)(2,1)S(1)}, bf16[120,896]{1,0:T(8,128)(2,1)S(1)}, u32[]{:S(2)}, u32[]{:S(2)}) collective-permute-start(bf16[120,896]{1,0:T(8,128)(2,1)S(1)} %get-tuple-element.87), channel_id=1, source_target_pairs={{0,8},{8,0},{16,24},{24,16},{1,9},{9,1},{17,25},{25,17},{2,10},{10... | collective-permute-start | bytes 645128 | tf_op jit(solution)/shard_map/ppermute | solution.py:340
  25.3 6.2 %collective-permute-start.3 = (bf16[120,768]{1,0:T(8,128)(2,1)S(1)}, bf16[120,768]{1,0:T(8,128)(2,1)S(1)}, u32[]{:S(2)}, u32[]{:S(2)}) collective-permute-start(bf16[120,768]{1,0:T(8,128)(2,1)S(1)} %get-tuple-element.85), channel_id=1, source_target_pairs={{0,16},{8,24},{16,0},{24,8},{1,17},{9,25},{17,1},{25,9},{2,18},{10... | collective-permute-start | bytes 552968 | tf_op jit(solution)/shard_map/ppermute | solution.py:340
  26.5 6.6 %collective-permute-start.9 = (bf16[60,896]{1,0:T(8,128)(2,1)S(1)}, bf16[60,896]{1,0:T(8,128)(2,1)S(1)}, u32[]{:S(2)}, u32[]{:S(2)}) collective-permute-start(bf16[60,896]{1,0:T(8,128)(2,1)S(1)} %get-tuple-element.101), channel_id=1, source_target_pairs={{0,8},{8,0},{16,24},{24,16},{1,9},{9,1},{17,25},{25,17},{2,10},{10... | collective-permute-start | bytes 322568 | tf_op jit(solution)/shard_map/ppermute | solution.py:340
  27.6 6.3 %collective-permute-start.8 = (bf16[60,896]{1,0:T(8,128)(2,1)S(1)}, bf16[60,896]{1,0:T(8,128)(2,1)S(1)}, u32[]{:S(2)}, u32[]{:S(2)}) collective-permute-start(bf16[60,896]{1,0:T(8,128)(2,1)S(1)} %get-tuple-element.99), channel_id=1, source_target_pairs={{0,16},{8,24},{16,0},{24,8},{1,17},{9,25},{17,1},{25,9},{2,18},{10... | collective-permute-start | bytes 322568 | tf_op jit(solution)/shard_map/ppermute | solution.py:340
  29.1 17.5 %collective-permute-start.19 = (bf16[160,1280]{1,0:T(8,128)(2,1)S(1)}, bf16[160,1280]{1,0:T(8,128)(2,1)S(1)}, u32[]{:S(2)}, u32[]{:S(2)}) collective-permute-start(bf16[160,1280]{1,0:T(8,128)(2,1)S(1)} %get-tuple-element.77.refs_0_), channel_id=1, source_target_pairs={{0,1},{1,0},{2,3},{3,2},{4,5},{5,4},{6,7},{7,6},{8,9},{9,8},{10,11... | collective-permute-start | bytes 1228808 | tf_op jit(solution)/shard_map/ppermute | solution.py:340
  30.6 6.3 %collective-permute-start.13 = (bf16[60,896]{1,0:T(8,128)(2,1)S(1)}, bf16[60,896]{1,0:T(8,128)(2,1)S(1)}, u32[]{:S(2)}, u32[]{:S(2)}) collective-permute-start(bf16[60,896]{1,0:T(8,128)(2,1)S(1)} %get-tuple-element.109), channel_id=1, source_target_pairs={{0,16},{8,24},{16,0},{24,8},{1,17},{9,25},{17,1},{25,9},{2,18},{10... | collective-permute-start | bytes 322568 | tf_op jit(solution)/shard_map/ppermute | solution.py:340
  31.6 5.1 %collective-permute-start.7 = (bf16[60,768]{1,0:T(8,128)(2,1)S(1)}, bf16[60,768]{1,0:T(8,128)(2,1)S(1)}, u32[]{:S(2)}, u32[]{:S(2)}) collective-permute-start(bf16[60,768]{1,0:T(8,128)(2,1)S(1)} %get-tuple-element.97), channel_id=1, source_target_pairs={{0,8},{8,0},{16,24},{24,16},{1,9},{9,1},{17,25},{25,17},{2,10},{10... | collective-permute-start | bytes 276488 | tf_op jit(solution)/shard_map/ppermute | solution.py:340
  33.2 6.5 %collective-permute-start.12 = (bf16[60,896]{1,0:T(8,128)(2,1)S(1)}, bf16[60,896]{1,0:T(8,128)(2,1)S(1)}, u32[]{:S(2)}, u32[]{:S(2)}) collective-permute-start(bf16[60,896]{1,0:T(8,128)(2,1)S(1)} %get-tuple-element.107.refs_0_), channel_id=1, source_target_pairs={{0,16},{8,24},{16,0},{24,8},{1,17},{9,25},{17,1},{25,9},{2,18},{10... | collective-permute-start | bytes 322568 | tf_op jit(solution)/shard_map/ppermute | solution.py:340
  34.0 6.0 %collective-permute-start.11 = (bf16[60,896]{1,0:T(8,128)(2,1)S(1)}, bf16[60,896]{1,0:T(8,128)(2,1)S(1)}, u32[]{:S(2)}, u32[]{:S(2)}) collective-permute-start(bf16[60,896]{1,0:T(8,128)(2,1)S(1)} %get-tuple-element.106.refs_0_), channel_id=1, source_target_pairs={{0,8},{8,0},{16,24},{24,16},{1,9},{9,1},{17,25},{25,17},{2,10},{10... | collective-permute-start | bytes 322568 | tf_op jit(solution)/shard_map/ppermute | solution.py:340
  36.9 7.5 %collective-permute-start.15 = (bf16[60,896]{1,0:T(8,128)(2,1)S(1)}, bf16[60,896]{1,0:T(8,128)(2,1)S(1)}, u32[]{:S(2)}, u32[]{:S(2)}) collective-permute-start(bf16[60,896]{1,0:T(8,128)(2,1)S(1)} %get-tuple-element.115.refs_0_), channel_id=1, source_target_pairs={{0,8},{8,0},{16,24},{24,16},{1,9},{9,1},{17,25},{25,17},{2,10},{10... | collective-permute-start | bytes 322568 | tf_op jit(solution)/shard_map/ppermute | solution.py:340
  38.7 5.7 %collective-permute-start.10 = (bf16[60,768]{1,0:T(8,128)(2,1)S(1)}, bf16[60,768]{1,0:T(8,128)(2,1)S(1)}, u32[]{:S(2)}, u32[]{:S(2)}) collective-permute-start(bf16[60,768]{1,0:T(8,128)(2,1)S(1)} %get-tuple-element.105.refs_0_), channel_id=1, source_target_pairs={{0,16},{8,24},{16,0},{24,8},{1,17},{9,25},{17,1},{25,9},{2,18},{10... | collective-permute-start | bytes 276488 | tf_op jit(solution)/shard_map/ppermute | solution.py:340
  40.0 8.3 %collective-permute-start.18 = (bf16[120,896]{1,0:T(8,128)(2,1)S(1)}, bf16[120,896]{1,0:T(8,128)(2,1)S(1)}, u32[]{:S(2)}, u32[]{:S(2)}) collective-permute-start(bf16[120,896]{1,0:T(8,128)(2,1)S(1)} %get-tuple-element.119.refs_0_), channel_id=1, source_target_pairs={{0,16},{8,24},{16,0},{24,8},{1,17},{9,25},{17,1},{25,9},{2,18},{10... | collective-permute-start | bytes 645128 | tf_op jit(solution)/shard_map/ppermute | solution.py:340
  41.0 8.8 %collective-permute-start.17 = (bf16[120,896]{1,0:T(8,128)(2,1)S(1)}, bf16[120,896]{1,0:T(8,128)(2,1)S(1)}, u32[]{:S(2)}, u32[]{:S(2)}) collective-permute-start(bf16[120,896]{1,0:T(8,128)(2,1)S(1)} %get-tuple-element.118.refs_0_), channel_id=1, source_target_pairs={{0,8},{8,0},{16,24},{24,16},{1,9},{9,1},{17,25},{25,17},{2,10},{10... | collective-permute-start | bytes 645128 | tf_op jit(solution)/shard_map/ppermute | solution.py:340
  44.5 7.1 %collective-permute-start.16 = (bf16[120,896]{1,0:T(8,128)(2,1)S(1)}, bf16[120,896]{1,0:T(8,128)(2,1)S(1)}, u32[]{:S(2)}, u32[]{:S(2)}) collective-permute-start(bf16[120,896]{1,0:T(8,128)(2,1)S(1)} %get-tuple-element.117.refs_0_), channel_id=1, source_target_pairs={{0,16},{8,24},{16,0},{24,8},{1,17},{9,25},{17,1},{25,9},{2,18},{10... | collective-permute-start | bytes 645128 | tf_op jit(solution)/shard_map/ppermute | solution.py:340
  45.5 7.7 %collective-permute-start.14 = (bf16[120,768]{1,0:T(8,128)(2,1)S(1)}, bf16[120,768]{1,0:T(8,128)(2,1)S(1)}, u32[]{:S(2)}, u32[]{:S(2)}) collective-permute-start(bf16[120,768]{1,0:T(8,128)(2,1)S(1)} %get-tuple-element.114.refs_0_), channel_id=1, source_target_pairs={{0,8},{8,0},{16,24},{24,16},{1,9},{9,1},{17,25},{25,17},{2,10},{10... | collective-permute-start | bytes 552968 | tf_op jit(solution)/shard_map/ppermute | solution.py:340
  50.0 9.8 %collective-permute-start.23 = (bf16[240,1792]{1,0:T(8,128)(2,1)S(1)}, bf16[240,1792]{1,0:T(8,128)(2,1)S(1)}, u32[]{:S(2)}, u32[]{:S(2)}) collective-permute-start(bf16[240,1792]{1,0:T(8,128)(2,1)S(1)} %get-tuple-element.125.refs_0_.refs_2_), channel_id=1, source_target_pairs={{0,1},{1,0},{2,3},{3,2},{4,5},{5,4},{6,7},{7,6},{8,9},{9,8},{10,11... | collective-permute-start | bytes 2580488 | tf_op jit(solution)/shard_map/ppermute | solution.py:340
  53.3 6.5 %collective-permute-start.24 = (bf16[240,1664]{1,0:T(8,128)(2,1)S(1)}, bf16[240,1664]{1,0:T(8,128)(2,1)S(1)}, u32[]{:S(2)}, u32[]{:S(2)}) collective-permute-start(bf16[240,1664]{1,0:T(8,128)(2,1)S(1)} %get-tuple-element.133.refs_0_.refs_3_), channel_id=1, source_target_pairs={{0,1},{1,0},{2,3},{3,2},{4,5},{5,4},{6,7},{7,6},{8,9},{9,8},{10,11... | collective-permute-start | bytes 2396168 | tf_op jit(solution)/shard_map/ppermute | solution.py:340
  55.3 13.9 %collective-permute-start.20 = (bf16[20,1280]{1,0:T(8,128)(2,1)S(1)}, bf16[20,1280]{1,0:T(8,128)(2,1)S(1)}, u32[]{:S(2)}, u32[]{:S(2)}) collective-permute-start(bf16[20,1280]{1,0:T(8,128)(2,1)S(1)} %get-tuple-element.139), channel_id=1, source_target_pairs={{0,2},{2,0},{4,6},{6,4},{1,3},{3,1},{5,7},{7,5},{8,10},{10,8},{12,... | collective-permute-start | bytes 153608 | tf_op jit(solution)/shard_map/ppermute | solution.py:340
  55.7 13.5 %collective-permute-start.21 = (bf16[20,1280]{1,0:T(8,128)(2,1)S(1)}, bf16[20,1280]{1,0:T(8,128)(2,1)S(1)}, u32[]{:S(2)}, u32[]{:S(2)}) collective-permute-start(bf16[20,1280]{1,0:T(8,128)(2,1)S(1)} %get-tuple-element.140), channel_id=1, source_target_pairs={{0,4},{2,6},{4,0},{6,2},{1,5},{3,7},{5,1},{7,3},{8,12},{10,14},{12... | collective-permute-start | bytes 153608 | tf_op jit(solution)/shard_map/ppermute | solution.py:340
  58.4 10.9 %collective-permute-start.22 = (bf16[20,1280]{1,0:T(8,128)(2,1)S(1)}, bf16[20,1280]{1,0:T(8,128)(2,1)S(1)}, u32[]{:S(2)}, u32[]{:S(2)}) collective-permute-start(bf16[20,1280]{1,0:T(8,128)(2,1)S(1)} %get-tuple-element.141), channel_id=1, source_target_pairs={{0,6},{2,4},{4,2},{6,0},{1,7},{3,5},{5,3},{7,1},{8,14},{10,12},{12... | collective-permute-start | bytes 153608 | tf_op jit(solution)/shard_map/ppermute | solution.py:340

commit v12 on v10

--- a/solution.py
+++ b/solution.py
@@ -102,14 +102,18 @@
     )
 
 
+def turned(value, row):
+    return (1 - row) * value + row * (((value & 1) << 1) | (value >> 1))
+
+
 def order_kernel(*refs):
     *piece_refs, out_ref = refs
     pieces = [ref[...].astype(F32) for ref in piece_refs]
     rows = pieces[0].shape[0] // 2
-    wa = lax.axis_index("wa")
+    wa, row = lax.axis_index("wa"), lax.axis_index("row")
     slots = []
     for slot in range(len(pieces)):
-        at = wa ^ slot
+        at = wa ^ turned(slot, row)
         piece = pieces[0]
         for other in range(1, len(pieces)):
             piece = jnp.where(at == other, pieces[other], piece)
@@ -324,10 +328,10 @@
     grad = grad_ref[...]
     rows = keep_ref.shape[0] // 2
     cuts = [grad[slot * rows : (slot + 1) * rows] for slot in range(4)]
-    wa = lax.axis_index("wa")
+    wa, row = lax.axis_index("wa"), lax.axis_index("row")
     pieces = []
     for step in range(4):
-        at = wa ^ step
+        at = turned(wa ^ step, row)
         piece = cuts[0]
         for slot in range(1, len(cuts)):
             piece = jnp.where(at == slot, cuts[slot], piece)
@@ -354,6 +358,15 @@
 
 def swap(value, axis, size, step):
     return lax.ppermute(value, axis, [(at, at ^ step) for at in range(size)])
+
+
+def exchange(value, n_wa, n_row, step):
+    pairs = [
+        (at * n_row + row, (at ^ turned(step, row)) * n_row + row)
+        for at in range(n_wa)
+        for row in range(n_row)
+    ]
+    return lax.ppermute(value, ("wa", "row"), pairs)
 
 
 def fast_body(n_wa, n_ha, n_row, tokens, cotangent, gate_weight, up_weight, down_weight):
@@ -374,18 +387,18 @@
     for at, ((begin, columns), axis) in enumerate(zip(chunks, axes)):
         keep, send = forward(line, begin, columns, axis, xy, gate, up, down_weight)
         kept.append(keep)
-        got.append(swap(send, "wa", n_wa, axis[0]))
+        got.append(exchange(send, n_wa, n_row, axis[0]))
     for at, (_, far) in enumerate(axes):
         kept[at], send = halve(line, kept[at], got[at])
-        got[at] = swap(send, "wa", n_wa, far)
+        got[at] = exchange(send, n_wa, n_row, far)
     order = [1, 0, 3, 2]
     for at in order:
         kept[at] = middle(line, kept[at], got[at])
-        got[at] = swap(kept[at], "wa", n_wa, axes[at][0])
+        got[at] = exchange(kept[at], n_wa, n_row, axes[at][0])
     for at in [1, 0, 3, 2]:
         far = axes[at][1]
         kept[at] = join(line, kept[at], got[at])
-        got[at] = swap(kept[at], "wa", n_wa, far)
+        got[at] = exchange(kept[at], n_wa, n_row, far)
 
     xt, y_all = factors(line, xy, xy_other)
     mine, other, grad = [], [], ()

time: 69.7 us -> 70.6 us (1.013)
  waiting for transfers between devices: 7.02 us -> 11.8 us
  starting transfers between devices: 29.6 us -> 25.7 us
    ppermute x24 -> x8, starting transfers between devices: 29.6 us -> 9.8 us  [swap(): return lax.ppermute(value, axis, [(at, at ^ step) for at in range(size)])]
    ppermute x0 -> x16, starting transfers between devices: none -> 15.9 us  [exchange(): return lax.ppermute(value, ('wa', 'row'), pairs)]
    ppermute x0 -> x16, waiting for transfers between devices: none -> 10.4 us  [exchange(): return lax.ppermute(value, ('wa', 'row'), pairs)]
    ppermute x24 -> x8, waiting for transfers between devices: 7.02 us -> 1.36 us  [swap(): return lax.ppermute(value, axis, [(at, at ^ step) for at in range(size)])]
where the time goes in v12:
time: 70.6 us; the launch traced here: 70.4 us
  Pallas kernels  31 us (44%)
  starting transfers between devices  25.7 us (36%)
  waiting for transfers between devices  11.8 us (17%)
  other arithmetic  1.03 us (1%)
  between operations  0.89 us (1%)
    pallas_call x28, Pallas kernels, call(): pl.pallas_call(body, in_specs=(in_specs or [IN_VMEM] * count) + [IN_VMEM]...  31 us
    ppermute x16, starting transfers between devices, exchange(): return lax.ppermute(value, ('wa', 'row'), pairs)  15.9 us
    ppermute x16, waiting for transfers between devices, exchange(): return lax.ppermute(value, ('wa', 'row'), pairs)  10.4 us
    ppermute x8, starting transfers between devices, swap(): return lax.ppermute(value, axis, [(at, at ^ step) for at in range(size)])  9.8 us
  transfers between devices with their start and end apart: 24, of which 9 were waited for; matrix products, arithmetic and copies ran while one was open for 0% of the time, Pallas kernels for 41%

profile of v12, /device:TPU:0, one launch (start us, length us, event | category | flops | bytes accessed | tf_op | source)
XLA Modules:
  0.0 70.4 jit_solution(12071378725231081773)
XLA Ops:
  0.6 0.0 slice-start
  0.6 1.0 %pad_maximum_fusion.refs_0_ = bf16[40,1280]{1,0:T(8,128)(2,1)S(1)} fusion(bf16[20,1280]{1,0:T(8,128)(2,1)} %param.6, bf16[20,1280]{1,0:T(8,128)(2,1)} %param.5), kind=kLoop, calls=%fused_computation | loop fusion | flops 204800 | bytes 204800 | tf_op jit(solution)/shard_map/concatenate | solution.py:380
  1.7 0.0 slice-start.1
  1.7 0.0 slice-start.2
  1.7 3.1 %collective-permute-start = (bf16[40,1280]{1,0:T(8,128)(2,1)S(1)}, bf16[40,1280]{1,0:T(8,128)(2,1)S(1)}, u32[]{:S(2)}, u32[]{:S(2)}) collective-permute-start(bf16[40,1280]{1,0:T(8,128)(2,1)S(1)} %pad_maximum_fusion.refs_0_), channel_id=1, source_target_pairs={{0,2},{2,0},{4,6},{6,4},{1,3},{3,1},{5,7},{7,5},{8,10},{10,8},{12,... | collective-permute-start | bytes 307208 | tf_op jit(solution)/shard_map/ppermute | solution.py:360
  4.8 2.6 %collective-permute-start.1 = (bf16[40,1280]{1,0:T(8,128)(2,1)S(1)}, bf16[40,1280]{1,0:T(8,128)(2,1)S(1)}, u32[]{:S(2)}, u32[]{:S(2)}) collective-permute-start(bf16[40,1280]{1,0:T(8,128)(2,1)S(1)} %pad_maximum_fusion.refs_0_), channel_id=1, source_target_pairs={{0,4},{2,6},{4,0},{6,2},{1,5},{3,7},{5,1},{7,3},{8,12},{10,14},{12... | collective-permute-start | bytes 307208 | tf_op jit(solution)/shard_map/ppermute | solution.py:360
  7.4 0.0 collective-permute-start.2
  7.4 6.8 %load_kernel.1 = (bf16[1280,3456]{1,0:T(8,128)(2,1)S(1)}, bf16[1280,3456]{1,0:T(8,128)(2,1)S(1)}, f32[8,128]{1,0:T(8,128)}) custom-call(bf16[1280,3456]{1,0:T(8,128)(2,1)} %refs_0_.1, bf16[1280,3456]{1,0:T(8,128)(2,1)} %refs_1_.1), custom_call_target="tpu_custom_call" | custom-call | flops 1 | bytes 1 | tf_op jit(solution)/shard_map/load_kernel/pallas_call | solution.py:62
  14.2 1.3 %collective-permute-done.1.refs_2_ = bf16[40,1280]{1,0:T(8,128)(2,1)S(1)} collective-permute-done((bf16[40,1280]{1,0:T(8,128)(2,1)S(1)}, bf16[40,1280]{1,0:T(8,128)(2,1)S(1)}, u32[]{:S(2)}, u32[]{:S(2)}) %collective-permute-start.1) | collective-permute-done | bytes 102432 | tf_op jit(solution)/shard_map/ppermute | solution.py:360
  15.5 0.2 order_kernel.1
  15.7 1.5 %forward_kernel.4 = (f32[120,896]{1,0:T(8,128)S(1)}, bf16[120,896]{1,0:T(8,128)(2,1)S(1)}, f32[8,128]{1,0:T(8,128)S(1)}) custom-call(bf16[160,1280]{1,0:T(8,128)(2,1)S(1)} %get-tuple-element.74.refs_0_, bf16[1280,3456]{1,0:T(8,128)(2,1)S(1)} %get-tuple-element.75.refs_1_, bf16[1280,3456]{1,0:T(8,128)(2,1)S(1)} %get-tuple-element.76.refs_2_, ...), custom_call_target="tpu_custom_call" | custom-call | flops 1 | bytes 1 | tf_op jit(solution)/shard_map/forward_kernel/pallas_call | solution.py:62
  17.3 1.6 %collective-permute-start.5 = (bf16[120,896]{1,0:T(8,128)(2,1)S(1)}, bf16[120,896]{1,0:T(8,128)(2,1)S(1)}, u32[]{:S(2)}, u32[]{:S(2)}) collective-permute-start(bf16[120,896]{1,0:T(8,128)(2,1)S(1)} %get-tuple-element.85), channel_id=1, source_target_pairs={{0,8},{1,17},{8,0},{9,25},{16,24},{17,1},{24,16},{25,9},{2,10},{3,... | collective-permute-start | bytes 645128 | tf_op jit(solution)/shard_map/ppermute | solution.py:369
  18.8 1.5 %forward_kernel.5 = (f32[120,896]{1,0:T(8,128)S(1)}, bf16[120,896]{1,0:T(8,128)(2,1)S(1)}, f32[8,128]{1,0:T(8,128)S(1)}) custom-call(bf16[160,1280]{1,0:T(8,128)(2,1)S(1)} %get-tuple-element.74.refs_0_, bf16[1280,3456]{1,0:T(8,128)(2,1)S(1)} %get-tuple-element.75.refs_1_, bf16[1280,3456]{1,0:T(8,128)(2,1)S(1)} %get-tuple-element.76.refs_2_, ...), custom_call_target="tpu_custom_call" | custom-call | flops 1 | bytes 1 | tf_op jit(solution)/shard_map/forward_kernel/pallas_call | solution.py:62
  20.3 1.6 %collective-permute-start.4 = (bf16[120,896]{1,0:T(8,128)(2,1)S(1)}, bf16[120,896]{1,0:T(8,128)(2,1)S(1)}, u32[]{:S(2)}, u32[]{:S(2)}) collective-permute-start(bf16[120,896]{1,0:T(8,128)(2,1)S(1)} %get-tuple-element.83), channel_id=1, source_target_pairs={{0,16},{1,9},{8,24},{9,1},{16,0},{17,25},{24,8},{25,17},{2,18},{3,... | collective-permute-start | bytes 645128 | tf_op jit(solution)/shard_map/ppermute | solution.py:369
  21.9 1.5 %forward_kernel.6 = (f32[120,896]{1,0:T(8,128)S(1)}, bf16[120,896]{1,0:T(8,128)(2,1)S(1)}, f32[8,128]{1,0:T(8,128)S(1)}) custom-call(bf16[160,1280]{1,0:T(8,128)(2,1)S(1)} %get-tuple-element.74.refs_0_, bf16[1280,3456]{1,0:T(8,128)(2,1)S(1)} %get-tuple-element.75.refs_1_, bf16[1280,3456]{1,0:T(8,128)(2,1)S(1)} %get-tuple-element.76.refs_2_, ...), custom_call_target="tpu_custom_call" | custom-call | flops 1 | bytes 1 | tf_op jit(solution)/shard_map/forward_kernel/pallas_call | solution.py:62
  23.4 0.6 collective-permute-start.3
  24.0 1.4 %forward_kernel.7 = (f32[120,768]{1,0:T(8,128)S(1)}, bf16[120,768]{1,0:T(8,128)(2,1)S(1)}, f32[8,128]{1,0:T(8,128)S(1)}) custom-call(bf16[160,1280]{1,0:T(8,128)(2,1)S(1)} %get-tuple-element.74.refs_0_, bf16[1280,3456]{1,0:T(8,128)(2,1)S(1)} %get-tuple-element.75.refs_1_, bf16[1280,3456]{1,0:T(8,128)(2,1)S(1)} %get-tuple-element.76.refs_2_, ...), custom_call_target="tpu_custom_call" | custom-call | flops 1 | bytes 1 | tf_op jit(solution)/shard_map/forward_kernel/pallas_call | solution.py:62
  25.4 0.6 collective-permute-start.7
  26.0 0.1 halve_kernel.5
  26.1 2.1 %collective-permute-done.4.refs_1_ = bf16[120,896]{1,0:T(8,128)(2,1)S(1)} collective-permute-done((bf16[120,896]{1,0:T(8,128)(2,1)S(1)}, bf16[120,896]{1,0:T(8,128)(2,1)S(1)}, u32[]{:S(2)}, u32[]{:S(2)}) %collective-permute-start.4) | collective-permute-done | bytes 215072 | tf_op jit(solution)/shard_map/ppermute | solution.py:369
  28.2 0.1 halve_kernel.6
  28.2 0.5 collective-permute-start.10
  28.7 0.5 collective-permute-start.9
  29.2 0.0 collective-permute-start.19
  29.2 1.5 %collective-permute-done.3.refs_1_ = bf16[120,896]{1,0:T(8,128)(2,1)S(1)} collective-permute-done((bf16[120,896]{1,0:T(8,128)(2,1)S(1)}, bf16[120,896]{1,0:T(8,128)(2,1)S(1)}, u32[]{:S(2)}, u32[]{:S(2)}) %collective-permute-start.3) | collective-permute-done | bytes 215072 | tf_op jit(solution)/shard_map/ppermute | solution.py:369
  30.8 0.1 halve_kernel.7
  30.9 1.4 %collective-permute-start.6 = (bf16[60,896]{1,0:T(8,128)(2,1)S(1)}, bf16[60,896]{1,0:T(8,128)(2,1)S(1)}, u32[]{:S(2)}, u32[]{:S(2)}) collective-permute-start(bf16[60,896]{1,0:T(8,128)(2,1)S(1)} %get-tuple-element.91), channel_id=1, source_target_pairs={{0,16},{1,9},{8,24},{9,1},{16,0},{17,25},{24,8},{25,17},{2,18},{3,... | collective-permute-start | bytes 322568 | tf_op jit(solution)/shard_map/ppermute | solution.py:369
  32.3 0.1 halve_kernel.8
  32.4 0.4 collective-permute-start.8
  32.7 0.9 %collective-permute-done.10.refs_1_ = bf16[60,896]{1,0:T(8,128)(2,1)S(1)} collective-permute-done((bf16[60,896]{1,0:T(8,128)(2,1)S(1)}, bf16[60,896]{1,0:T(8,128)(2,1)S(1)}, u32[]{:S(2)}, u32[]{:S(2)}) %collective-permute-start.10) | collective-permute-done | bytes 107552 | tf_op jit(solution)/shard_map/ppermute | solution.py:369
  33.7 0.1 middle_kernel.4
  33.7 1.0 %collective-permute-start.14 = (bf16[60,896]{1,0:T(8,128)(2,1)S(1)}, bf16[60,896]{1,0:T(8,128)(2,1)S(1)}, u32[]{:S(2)}, u32[]{:S(2)}) collective-permute-start(bf16[60,896]{1,0:T(8,128)(2,1)S(1)} %get-tuple-element.108.refs_0_), channel_id=1, source_target_pairs={{0,16},{1,9},{8,24},{9,1},{16,0},{17,25},{24,8},{25,17},{2,18},{3,... | collective-permute-start | bytes 322568 | tf_op jit(solution)/shard_map/ppermute | solution.py:369
  34.7 0.1 middle_kernel.5
  34.8 1.2 %collective-permute-start.13 = (bf16[60,896]{1,0:T(8,128)(2,1)S(1)}, bf16[60,896]{1,0:T(8,128)(2,1)S(1)}, u32[]{:S(2)}, u32[]{:S(2)}) collective-permute-start(bf16[60,896]{1,0:T(8,128)(2,1)S(1)} %get-tuple-element.107.refs_0_), channel_id=1, source_target_pairs={{0,8},{1,17},{8,0},{9,25},{16,24},{17,1},{24,16},{25,9},{2,10},{3,... | collective-permute-start | bytes 322568 | tf_op jit(solution)/shard_map/ppermute | solution.py:369
  36.0 1.6 %collective-permute-done.8.refs_1_ = bf16[60,768]{1,0:T(8,128)(2,1)S(1)} collective-permute-done((bf16[60,768]{1,0:T(8,128)(2,1)S(1)}, bf16[60,768]{1,0:T(8,128)(2,1)S(1)}, u32[]{:S(2)}, u32[]{:S(2)}) %collective-permute-start.8) | collective-permute-done | bytes 92192 | tf_op jit(solution)/shard_map/ppermute | solution.py:369
  37.6 0.1 middle_kernel.6
  37.7 0.0 collective-permute-done.6.refs_1_
  37.7 0.1 middle_kernel.7
  37.7 0.5 collective-permute-start.11
  38.2 1.1 %collective-permute-start.12 = (bf16[60,768]{1,0:T(8,128)(2,1)S(1)}, bf16[60,768]{1,0:T(8,128)(2,1)S(1)}, u32[]{:S(2)}, u32[]{:S(2)}) collective-permute-start(bf16[60,768]{1,0:T(8,128)(2,1)S(1)} %get-tuple-element.106.refs_0_), channel_id=1, source_target_pairs={{0,16},{1,9},{8,24},{9,1},{16,0},{17,25},{24,8},{25,17},{2,18},{3,... | collective-permute-start | bytes 276488 | tf_op jit(solution)/shard_map/ppermute | solution.py:369
  39.4 0.2 collective-permute-done.13.refs_1_
  39.7 1.3 %collective-permute-start.17 = (bf16[120,896]{1,0:T(8,128)(2,1)S(1)}, bf16[120,896]{1,0:T(8,128)(2,1)S(1)}, u32[]{:S(2)}, u32[]{:S(2)}) collective-permute-start(bf16[120,896]{1,0:T(8,128)(2,1)S(1)} %get-tuple-element.115.refs_0_), channel_id=1, source_target_pairs={{0,16},{1,9},{8,24},{9,1},{16,0},{17,25},{24,8},{25,17},{2,18},{3,... | collective-permute-start | bytes 645128 | tf_op jit(solution)/shard_map/ppermute | solution.py:369
  41.0 1.3 %collective-permute-start.18 = (bf16[120,896]{1,0:T(8,128)(2,1)S(1)}, bf16[120,896]{1,0:T(8,128)(2,1)S(1)}, u32[]{:S(2)}, u32[]{:S(2)}) collective-permute-start(bf16[120,896]{1,0:T(8,128)(2,1)S(1)} %get-tuple-element.116.refs_2_), channel_id=1, source_target_pairs={{0,8},{1,17},{8,0},{9,25},{16,24},{17,1},{24,16},{25,9},{2,10},{3,... | collective-permute-start | bytes 645128 | tf_op jit(solution)/shard_map/ppermute | solution.py:369
  42.3 1.6 %collective-permute-done.12.refs_1_ = bf16[60,768]{1,0:T(8,128)(2,1)S(1)} collective-permute-done((bf16[60,768]{1,0:T(8,128)(2,1)S(1)}, bf16[60,768]{1,0:T(8,128)(2,1)S(1)}, u32[]{:S(2)}, u32[]{:S(2)}) %collective-permute-start.12) | collective-permute-done | bytes 92192 | tf_op jit(solution)/shard_map/ppermute | solution.py:369
  44.0 0.0 collective-permute-done.11.refs_1_
  44.0 1.1 %collective-permute-start.15 = (bf16[120,896]{1,0:T(8,128)(2,1)S(1)}, bf16[120,896]{1,0:T(8,128)(2,1)S(1)}, u32[]{:S(2)}, u32[]{:S(2)}) collective-permute-start(bf16[120,896]{1,0:T(8,128)(2,1)S(1)} %get-tuple-element.113.refs_0_), channel_id=1, source_target_pairs={{0,16},{1,9},{8,24},{9,1},{16,0},{17,25},{24,8},{25,17},{2,18},{3,... | collective-permute-start | bytes 645128 | tf_op jit(solution)/shard_map/ppermute | solution.py:369
  45.1 1.2 %collective-permute-start.16 = (bf16[120,768]{1,0:T(8,128)(2,1)S(1)}, bf16[120,768]{1,0:T(8,128)(2,1)S(1)}, u32[]{:S(2)}, u32[]{:S(2)}) collective-permute-start(bf16[120,768]{1,0:T(8,128)(2,1)S(1)} %get-tuple-element.114.refs_2_), channel_id=1, source_target_pairs={{0,8},{1,17},{8,0},{9,25},{16,24},{17,1},{24,16},{25,9},{2,10},{3,... | collective-permute-start | bytes 552968 | tf_op jit(solution)/shard_map/ppermute | solution.py:369
  46.4 0.0 collective-permute-done.19.refs_1_
  46.4 0.3 factors_kernel.1
  46.7 1.9 %collective-permute-done.17.refs_1_ = bf16[120,896]{1,0:T(8,128)(2,1)S(1)} collective-permute-done((bf16[120,896]{1,0:T(8,128)(2,1)S(1)}, bf16[120,896]{1,0:T(8,128)(2,1)S(1)}, u32[]{:S(2)}, u32[]{:S(2)}) %collective-permute-start.17) | collective-permute-done | bytes 215072 | tf_op jit(solution)/shard_map/ppermute | solution.py:369
  48.5 0.5 collective-permute-done.18.refs_3_
  49.0 0.1 stack_kernel.2
  49.2 0.1 collective-permute-start.21
  49.2 2.9 %input_grad_kernel.2 = (f32[80,1280]{1,0:T(8,128)S(1)}, f32[8,128]{1,0:T(8,128)S(1)}) custom-call(bf16[240,1792]{1,0:T(8,128)(2,1)S(1)} %get-tuple-element.119.refs_0_.refs_2_, bf16[1280,3456]{1,0:T(8,128)(2,1)S(1)} %get-tuple-element.75.refs_1_, bf16[1280,3456]{1,0:T(8,128)(2,1)S(1)} %get-tuple-element.76.refs_2_, f32[8,128]{1,0:T(8,128)S(1)} %get-tuple-element.120.refs_3_), custom_call_target="tpu_custom_call" | custom-call | flops 1 | bytes 1 | tf_op jit(solution)/shard_map/input_grad_kernel/pallas_call | solution.py:62
  52.1 0.1 stack_kernel.3
  52.2 0.6 collective-permute-start.22
  52.8 2.7 %input_grad_kernel.3 = (f32[80,1280]{1,0:T(8,128)S(1)}, f32[8,128]{1,0:T(8,128)S(1)}) custom-call(bf16[240,1664]{1,0:T(8,128)(2,1)S(1)} %get-tuple-element.122.refs_0_.refs_2_, bf16[1280,3456]{1,0:T(8,128)(2,1)S(1)} %get-tuple-element.75.refs_1_, bf16[1280,3456]{1,0:T(8,128)(2,1)S(1)} %get-tuple-element.76.refs_2_, ...), custom_call_target="tpu_custom_call" | custom-call | flops 1 | bytes 1 | tf_op jit(solution)/shard_map/input_grad_kernel/pallas_call | solution.py:62
  55.5 0.1 last_kernel.1
  55.6 2.9 %collective-permute-start.20 = (bf16[40,1280]{1,0:T(8,128)(2,1)S(1)}, bf16[40,1280]{1,0:T(8,128)(2,1)S(1)}, u32[]{:S(2)}, u32[]{:S(2)}) collective-permute-start(bf16[40,1280]{1,0:T(8,128)(2,1)S(1)} %get-tuple-element.128), channel_id=1, source_target_pairs={{0,4},{2,6},{4,0},{6,2},{1,5},{3,7},{5,1},{7,3},{8,12},{10,14},{12... | collective-permute-start | bytes 307208 | tf_op jit(solution)/shard_map/ppermute | solution.py:360
  58.5 5.4 %weight_grad_kernel.2 = (bf16[1280,3456]{1,0:T(8,128)(2,1)}, bf16[1280,3456]{1,0:T(8,128)(2,1)}, bf16[3456,1280]{1,0:T(8,128)(2,1)}, f32[8,128]{1,0:T(8,128)S(1)}) custom-call(bf16[1280,160]{1,0:T(8,128)(2,1)S(1)} %get-tuple-element.129.refs_0_, bf16[160,1280]{1,0:T(8,128)(2,1)S(1)} %get-tuple-element.130.refs_1_, ...), custom_call_target="tpu_custom_call" | custom-call | flops 1 | bytes 1 | tf_op jit(solution)/shard_map/weight_grad_kernel/pallas_call | solution.py:62
  63.9 0.0 collective-permute-done.20.refs_1_
  64.0 0.6 collective-permute-start.23
  64.6 5.2 %weight_grad_kernel.3 = (bf16[1280,3456]{1,0:T(8,128)(2,1)}, bf16[1280,3456]{1,0:T(8,128)(2,1)}, bf16[3456,1280]{1,0:T(8,128)(2,1)}, f32[8,128]{1,0:T(8,128)S(1)}) custom-call(bf16[1280,160]{1,0:T(8,128)(2,1)S(1)} %get-tuple-element.129.refs_0_, ...), custom_call_target="tpu_custom_call", output_to_operand_aliasing={{0}: (5, {}), {1}: (6, {}), {2}: (7, {})} | custom-call | flops 1 | bytes 1 | tf_op jit(solution)/shard_map/weight_grad_kernel/pallas_call | solution.py:62
  69.8 0.6 total_kernel.1
  (20 shorter events, 0.2 us)
Async XLA Ops:
  0.6 15.1 %slice-start = ((s8[8847360]{0:T(1024)(128)(4,1)}), s8[4194304]{0:T(1024)(128)(4,1)S(1)}, s32[]{:S(2)}) async-start(s8[8847360]{0:T(1024)(128)(4,1)} %bitcast), calls=%async_computation | async-start | bytes 8388608
  1.7 14.0 %slice-start.1 = ((s8[8847360]{0:T(1024)(128)(4,1)}), s8[4194304]{0:T(1024)(128)(4,1)S(1)}, s32[]{:S(2)}) async-start(s8[8847360]{0:T(1024)(128)(4,1)} %bitcast), calls=%async_computation.1 | async-start | bytes 8388608
  1.7 14.0 %slice-start.2 = ((s8[8847360]{0:T(1024)(128)(4,1)}), s8[458752]{0:T(1024)(128)(4,1)S(1)}, s32[]{:S(2)}) async-start(s8[8847360]{0:T(1024)(128)(4,1)} %bitcast), calls=%async_computation.2 | async-start | bytes 917504
  1.7 12.5 %collective-permute-start = (bf16[40,1280]{1,0:T(8,128)(2,1)S(1)}, bf16[40,1280]{1,0:T(8,128)(2,1)S(1)}, u32[]{:S(2)}, u32[]{:S(2)}) collective-permute-start(bf16[40,1280]{1,0:T(8,128)(2,1)S(1)} %pad_maximum_fusion.refs_0_), channel_id=1, source_target_pairs={{0,2},{2,0},{4,6},{6,4},{1,3},{3,1},{5,7},{7,5},{8,10},{10,8},{12,... | collective-permute-start | bytes 307208 | tf_op jit(solution)/shard_map/ppermute | solution.py:360
  4.8 10.7 %collective-permute-start.1 = (bf16[40,1280]{1,0:T(8,128)(2,1)S(1)}, bf16[40,1280]{1,0:T(8,128)(2,1)S(1)}, u32[]{:S(2)}, u32[]{:S(2)}) collective-permute-start(bf16[40,1280]{1,0:T(8,128)(2,1)S(1)} %pad_maximum_fusion.refs_0_), channel_id=1, source_target_pairs={{0,4},{2,6},{4,0},{6,2},{1,5},{3,7},{5,1},{7,3},{8,12},{10,14},{12... | collective-permute-start | bytes 307208 | tf_op jit(solution)/shard_map/ppermute | solution.py:360
  7.4 8.1 %collective-permute-start.2 = (bf16[40,1280]{1,0:T(8,128)(2,1)S(1)}, bf16[40,1280]{1,0:T(8,128)(2,1)S(1)}, u32[]{:S(2)}, u32[]{:S(2)}) collective-permute-start(bf16[40,1280]{1,0:T(8,128)(2,1)S(1)} %pad_maximum_fusion.refs_0_), channel_id=1, source_target_pairs={{0,6},{2,4},{4,2},{6,0},{1,7},{3,5},{5,3},{7,1},{8,14},{10,12},{12... | collective-permute-start | bytes 307208 | tf_op jit(solution)/shard_map/ppermute | solution.py:360
  17.3 8.8 %collective-permute-start.5 = (bf16[120,896]{1,0:T(8,128)(2,1)S(1)}, bf16[120,896]{1,0:T(8,128)(2,1)S(1)}, u32[]{:S(2)}, u32[]{:S(2)}) collective-permute-start(bf16[120,896]{1,0:T(8,128)(2,1)S(1)} %get-tuple-element.85), channel_id=1, source_target_pairs={{0,8},{1,17},{8,0},{9,25},{16,24},{17,1},{24,16},{25,9},{2,10},{3,... | collective-permute-start | bytes 645128 | tf_op jit(solution)/shard_map/ppermute | solution.py:369
  20.3 7.8 %collective-permute-start.4 = (bf16[120,896]{1,0:T(8,128)(2,1)S(1)}, bf16[120,896]{1,0:T(8,128)(2,1)S(1)}, u32[]{:S(2)}, u32[]{:S(2)}) collective-permute-start(bf16[120,896]{1,0:T(8,128)(2,1)S(1)} %get-tuple-element.83), channel_id=1, source_target_pairs={{0,16},{1,9},{8,24},{9,1},{16,0},{17,25},{24,8},{25,17},{2,18},{3,... | collective-permute-start | bytes 645128 | tf_op jit(solution)/shard_map/ppermute | solution.py:369
  23.4 7.3 %collective-permute-start.3 = (bf16[120,896]{1,0:T(8,128)(2,1)S(1)}, bf16[120,896]{1,0:T(8,128)(2,1)S(1)}, u32[]{:S(2)}, u32[]{:S(2)}) collective-permute-start(bf16[120,896]{1,0:T(8,128)(2,1)S(1)} %get-tuple-element.81), channel_id=1, source_target_pairs={{0,8},{1,17},{8,0},{9,25},{16,24},{17,1},{24,16},{25,9},{2,10},{3,... | collective-permute-start | bytes 645128 | tf_op jit(solution)/shard_map/ppermute | solution.py:369
  25.4 6.9 %collective-permute-start.7 = (bf16[120,768]{1,0:T(8,128)(2,1)S(1)}, bf16[120,768]{1,0:T(8,128)(2,1)S(1)}, u32[]{:S(2)}, u32[]{:S(2)}) collective-permute-start(bf16[120,768]{1,0:T(8,128)(2,1)S(1)} %get-tuple-element.93), channel_id=1, source_target_pairs={{0,16},{1,9},{8,24},{9,1},{16,0},{17,25},{24,8},{25,17},{2,18},{3,... | collective-permute-start | bytes 552968 | tf_op jit(solution)/shard_map/ppermute | solution.py:369
  28.2 5.4 %collective-permute-start.10 = (bf16[60,896]{1,0:T(8,128)(2,1)S(1)}, bf16[60,896]{1,0:T(8,128)(2,1)S(1)}, u32[]{:S(2)}, u32[]{:S(2)}) collective-permute-start(bf16[60,896]{1,0:T(8,128)(2,1)S(1)} %get-tuple-element.100), channel_id=1, source_target_pairs={{0,8},{1,17},{8,0},{9,25},{16,24},{17,1},{24,16},{25,9},{2,10},{3,... | collective-permute-start | bytes 322568 | tf_op jit(solution)/shard_map/ppermute | solution.py:369
  28.7 6.0 %collective-permute-start.9 = (bf16[60,896]{1,0:T(8,128)(2,1)S(1)}, bf16[60,896]{1,0:T(8,128)(2,1)S(1)}, u32[]{:S(2)}, u32[]{:S(2)}) collective-permute-start(bf16[60,896]{1,0:T(8,128)(2,1)S(1)} %get-tuple-element.98), channel_id=1, source_target_pairs={{0,16},{1,9},{8,24},{9,1},{16,0},{17,25},{24,8},{25,17},{2,18},{3,... | collective-permute-start | bytes 322568 | tf_op jit(solution)/shard_map/ppermute | solution.py:369
  29.2 17.2 %collective-permute-start.19 = (bf16[160,1280]{1,0:T(8,128)(2,1)S(1)}, bf16[160,1280]{1,0:T(8,128)(2,1)S(1)}, u32[]{:S(2)}, u32[]{:S(2)}) collective-permute-start(bf16[160,1280]{1,0:T(8,128)(2,1)S(1)} %get-tuple-element.74.refs_0_), channel_id=1, source_target_pairs={{0,1},{1,0},{2,3},{3,2},{4,5},{5,4},{6,7},{7,6},{8,9},{9,8},{10,11... | collective-permute-start | bytes 1228808 | tf_op jit(solution)/shard_map/ppermute | solution.py:360
  30.9 6.8 %collective-permute-start.6 = (bf16[60,896]{1,0:T(8,128)(2,1)S(1)}, bf16[60,896]{1,0:T(8,128)(2,1)S(1)}, u32[]{:S(2)}, u32[]{:S(2)}) collective-permute-start(bf16[60,896]{1,0:T(8,128)(2,1)S(1)} %get-tuple-element.91), channel_id=1, source_target_pairs={{0,16},{1,9},{8,24},{9,1},{16,0},{17,25},{24,8},{25,17},{2,18},{3,... | collective-permute-start | bytes 322568 | tf_op jit(solution)/shard_map/ppermute | solution.py:369
  32.4 5.2 %collective-permute-start.8 = (bf16[60,768]{1,0:T(8,128)(2,1)S(1)}, bf16[60,768]{1,0:T(8,128)(2,1)S(1)}, u32[]{:S(2)}, u32[]{:S(2)}) collective-permute-start(bf16[60,768]{1,0:T(8,128)(2,1)S(1)} %get-tuple-element.96), channel_id=1, source_target_pairs={{0,8},{1,17},{8,0},{9,25},{16,24},{17,1},{24,16},{25,9},{2,10},{3,... | collective-permute-start | bytes 276488 | tf_op jit(solution)/shard_map/ppermute | solution.py:369
  33.7 5.7 %collective-permute-start.14 = (bf16[60,896]{1,0:T(8,128)(2,1)S(1)}, bf16[60,896]{1,0:T(8,128)(2,1)S(1)}, u32[]{:S(2)}, u32[]{:S(2)}) collective-permute-start(bf16[60,896]{1,0:T(8,128)(2,1)S(1)} %get-tuple-element.108.refs_0_), channel_id=1, source_target_pairs={{0,16},{1,9},{8,24},{9,1},{16,0},{17,25},{24,8},{25,17},{2,18},{3,... | collective-permute-start | bytes 322568 | tf_op jit(solution)/shard_map/ppermute | solution.py:369
  34.8 4.9 %collective-permute-start.13 = (bf16[60,896]{1,0:T(8,128)(2,1)S(1)}, bf16[60,896]{1,0:T(8,128)(2,1)S(1)}, u32[]{:S(2)}, u32[]{:S(2)}) collective-permute-start(bf16[60,896]{1,0:T(8,128)(2,1)S(1)} %get-tuple-element.107.refs_0_), channel_id=1, source_target_pairs={{0,8},{1,17},{8,0},{9,25},{16,24},{17,1},{24,16},{25,9},{2,10},{3,... | collective-permute-start | bytes 322568 | tf_op jit(solution)/shard_map/ppermute | solution.py:369
  37.7 6.2 %collective-permute-start.11 = (bf16[60,896]{1,0:T(8,128)(2,1)S(1)}, bf16[60,896]{1,0:T(8,128)(2,1)S(1)}, u32[]{:S(2)}, u32[]{:S(2)}) collective-permute-start(bf16[60,896]{1,0:T(8,128)(2,1)S(1)} %get-tuple-element.105.refs_0_), channel_id=1, source_target_pairs={{0,8},{1,17},{8,0},{9,25},{16,24},{17,1},{24,16},{25,9},{2,10},{3,... | collective-permute-start | bytes 322568 | tf_op jit(solution)/shard_map/ppermute | solution.py:369
  38.2 5.7 %collective-permute-start.12 = (bf16[60,768]{1,0:T(8,128)(2,1)S(1)}, bf16[60,768]{1,0:T(8,128)(2,1)S(1)}, u32[]{:S(2)}, u32[]{:S(2)}) collective-permute-start(bf16[60,768]{1,0:T(8,128)(2,1)S(1)} %get-tuple-element.106.refs_0_), channel_id=1, source_target_pairs={{0,16},{1,9},{8,24},{9,1},{16,0},{17,25},{24,8},{25,17},{2,18},{3,... | collective-permute-start | bytes 276488 | tf_op jit(solution)/shard_map/ppermute | solution.py:369
  39.7 8.8 %collective-permute-start.17 = (bf16[120,896]{1,0:T(8,128)(2,1)S(1)}, bf16[120,896]{1,0:T(8,128)(2,1)S(1)}, u32[]{:S(2)}, u32[]{:S(2)}) collective-permute-start(bf16[120,896]{1,0:T(8,128)(2,1)S(1)} %get-tuple-element.115.refs_0_), channel_id=1, source_target_pairs={{0,16},{1,9},{8,24},{9,1},{16,0},{17,25},{24,8},{25,17},{2,18},{3,... | collective-permute-start | bytes 645128 | tf_op jit(solution)/shard_map/ppermute | solution.py:369
  41.0 8.0 %collective-permute-start.18 = (bf16[120,896]{1,0:T(8,128)(2,1)S(1)}, bf16[120,896]{1,0:T(8,128)(2,1)S(1)}, u32[]{:S(2)}, u32[]{:S(2)}) collective-permute-start(bf16[120,896]{1,0:T(8,128)(2,1)S(1)} %get-tuple-element.116.refs_2_), channel_id=1, source_target_pairs={{0,8},{1,17},{8,0},{9,25},{16,24},{17,1},{24,16},{25,9},{2,10},{3,... | collective-permute-start | bytes 645128 | tf_op jit(solution)/shard_map/ppermute | solution.py:369
  44.0 8.1 %collective-permute-start.15 = (bf16[120,896]{1,0:T(8,128)(2,1)S(1)}, bf16[120,896]{1,0:T(8,128)(2,1)S(1)}, u32[]{:S(2)}, u32[]{:S(2)}) collective-permute-start(bf16[120,896]{1,0:T(8,128)(2,1)S(1)} %get-tuple-element.113.refs_0_), channel_id=1, source_target_pairs={{0,16},{1,9},{8,24},{9,1},{16,0},{17,25},{24,8},{25,17},{2,18},{3,... | collective-permute-start | bytes 645128 | tf_op jit(solution)/shard_map/ppermute | solution.py:369
  45.1 7.0 %collective-permute-start.16 = (bf16[120,768]{1,0:T(8,128)(2,1)S(1)}, bf16[120,768]{1,0:T(8,128)(2,1)S(1)}, u32[]{:S(2)}, u32[]{:S(2)}) collective-permute-start(bf16[120,768]{1,0:T(8,128)(2,1)S(1)} %get-tuple-element.114.refs_2_), channel_id=1, source_target_pairs={{0,8},{1,17},{8,0},{9,25},{16,24},{17,1},{24,16},{25,9},{2,10},{3,... | collective-permute-start | bytes 552968 | tf_op jit(solution)/shard_map/ppermute | solution.py:369
  49.2 9.3 %collective-permute-start.21 = (bf16[240,1792]{1,0:T(8,128)(2,1)S(1)}, bf16[240,1792]{1,0:T(8,128)(2,1)S(1)}, u32[]{:S(2)}, u32[]{:S(2)}) collective-permute-start(bf16[240,1792]{1,0:T(8,128)(2,1)S(1)} %get-tuple-element.119.refs_0_.refs_2_), channel_id=1, source_target_pairs={{0,1},{1,0},{2,3},{3,2},{4,5},{5,4},{6,7},{7,6},{8,9},{9,8},{10,11... | collective-permute-start | bytes 2580488 | tf_op jit(solution)/shard_map/ppermute | solution.py:360
  52.2 6.3 %collective-permute-start.22 = (bf16[240,1664]{1,0:T(8,128)(2,1)S(1)}, bf16[240,1664]{1,0:T(8,128)(2,1)S(1)}, u32[]{:S(2)}, u32[]{:S(2)}) collective-permute-start(bf16[240,1664]{1,0:T(8,128)(2,1)S(1)} %get-tuple-element.122.refs_0_.refs_2_), channel_id=1, source_target_pairs={{0,1},{1,0},{2,3},{3,2},{4,5},{5,4},{6,7},{7,6},{8,9},{9,8},{10,11... | collective-permute-start | bytes 2396168 | tf_op jit(solution)/shard_map/ppermute | solution.py:360
  55.6 8.3 %collective-permute-start.20 = (bf16[40,1280]{1,0:T(8,128)(2,1)S(1)}, bf16[40,1280]{1,0:T(8,128)(2,1)S(1)}, u32[]{:S(2)}, u32[]{:S(2)}) collective-permute-start(bf16[40,1280]{1,0:T(8,128)(2,1)S(1)} %get-tuple-element.128), channel_id=1, source_target_pairs={{0,4},{2,6},{4,0},{6,2},{1,5},{3,7},{5,1},{7,3},{8,12},{10,14},{12... | collective-permute-start | bytes 307208 | tf_op jit(solution)/shard_map/ppermute | solution.py:360
  64.0 5.8 %collective-permute-start.23 = (bf16[20,1280]{1,0:T(8,128)(2,1)S(1)}, bf16[20,1280]{1,0:T(8,128)(2,1)S(1)}, u32[]{:S(2)}, u32[]{:S(2)}) collective-permute-start(bf16[20,1280]{1,0:T(8,128)(2,1)S(1)} %get-tuple-element.134), channel_id=1, source_target_pairs={{0,2},{2,0},{4,6},{6,4},{1,3},{3,1},{5,7},{7,5},{8,10},{10,8},{12,... | collective-permute-start | bytes 153608 | tf_op jit(solution)/shard_map/ppermute | solution.py:360

commit v13 on v10

--- a/solution.py
+++ b/solution.py
@@ -387,7 +387,6 @@
         kept[at] = join(line, kept[at], got[at])
         got[at] = swap(kept[at], "wa", n_wa, far)
 
-    xt, y_all = factors(line, xy, xy_other)
     mine, other, grad = [], [], ()
     for at in range(0, CHUNKS, 2):
         pair = slice(at, at + 2)
@@ -396,6 +395,7 @@
         grad = input_grad(line, chunks[at][0], mine[-1], gate, up, grad)
     keep, send = last_pieces(line, grad[0])
     received = swap(send, "ha", n_ha, 2)
+    xt, y_all = factors(line, xy, xy_other)
     grads = weight_grad(line, 0, hidden_width, xt, y_all, mine[0], other[0], (), other[1])
     keep, send = halve(line, keep, received)
     received = swap(send, "ha", n_ha, 1)

time: 69.7 us -> 70.6 us (1.013)
  waiting for transfers between devices: 7.02 us -> 9.64 us
  starting transfers between devices: 29.6 us -> 27.9 us
    ppermute x24, waiting for transfers between devices: 7.02 us -> 9.64 us  [swap(): return lax.ppermute(value, axis, [(at, at ^ step) for at in range(size)])]
    ppermute x24, starting transfers between devices: 29.6 us -> 27.9 us  [swap(): return lax.ppermute(value, axis, [(at, at ^ step) for at in range(size)])]
where the time goes in v13:
time: 70.6 us; the launch traced here: 70.5 us
  Pallas kernels  31 us (44%)
  starting transfers between devices  27.9 us (40%)
  waiting for transfers between devices  9.64 us (14%)
  other arithmetic  1.03 us (1%)
  between operations  0.88 us (1%)
    pallas_call x28, Pallas kernels, call(): pl.pallas_call(body, in_specs=(in_specs or [IN_VMEM] * count) + [IN_VMEM]...  31 us
    ppermute x24, starting transfers between devices, swap(): return lax.ppermute(value, axis, [(at, at ^ step) for at in range(size)])  27.9 us
    ppermute x24, waiting for transfers between devices, swap(): return lax.ppermute(value, axis, [(at, at ^ step) for at in range(size)])  9.64 us
  transfers between devices with their start and end apart: 24, of which 9 were waited for; matrix products, arithmetic and copies ran while one was open for 0% of the time, Pallas kernels for 41%

profile of v13, /device:TPU:0, one launch (start us, length us, event | category | flops | bytes accessed | tf_op | source)
XLA Modules:
  0.0 70.5 jit_solution(3066819381124582271)
XLA Ops:
  0.6 0.0 slice-start
  0.6 1.0 %pad_maximum_fusion.refs_0_ = bf16[40,1280]{1,0:T(8,128)(2,1)S(1)} fusion(bf16[20,1280]{1,0:T(8,128)(2,1)} %param.6, bf16[20,1280]{1,0:T(8,128)(2,1)} %param.5), kind=kLoop, calls=%fused_computation | loop fusion | flops 204800 | bytes 204800 | tf_op jit(solution)/shard_map/concatenate | solution.py:367
  1.7 0.0 slice-start.1
  1.7 3.1 %collective-permute-start = (bf16[40,1280]{1,0:T(8,128)(2,1)S(1)}, bf16[40,1280]{1,0:T(8,128)(2,1)S(1)}, u32[]{:S(2)}, u32[]{:S(2)}) collective-permute-start(bf16[40,1280]{1,0:T(8,128)(2,1)S(1)} %pad_maximum_fusion.refs_0_), channel_id=1, source_target_pairs={{0,2},{2,0},{4,6},{6,4},{1,3},{3,1},{5,7},{7,5},{8,10},{10,8},{12,... | collective-permute-start | bytes 307208 | tf_op jit(solution)/shard_map/ppermute | solution.py:356
  4.8 2.6 %collective-permute-start.1 = (bf16[40,1280]{1,0:T(8,128)(2,1)S(1)}, bf16[40,1280]{1,0:T(8,128)(2,1)S(1)}, u32[]{:S(2)}, u32[]{:S(2)}) collective-permute-start(bf16[40,1280]{1,0:T(8,128)(2,1)S(1)} %pad_maximum_fusion.refs_0_), channel_id=1, source_target_pairs={{0,4},{2,6},{4,0},{6,2},{1,5},{3,7},{5,1},{7,3},{8,12},{10,14},{12... | collective-permute-start | bytes 307208 | tf_op jit(solution)/shard_map/ppermute | solution.py:356
  7.4 0.0 collective-permute-start.2
  7.4 6.8 %load_kernel.1 = (bf16[1280,3456]{1,0:T(8,128)(2,1)S(1)}, bf16[1280,3456]{1,0:T(8,128)(2,1)S(1)}, f32[8,128]{1,0:T(8,128)}) custom-call(bf16[1280,3456]{1,0:T(8,128)(2,1)} %refs_0_.1, bf16[1280,3456]{1,0:T(8,128)(2,1)} %refs_1_.1), custom_call_target="tpu_custom_call" | custom-call | flops 1 | bytes 1 | tf_op jit(solution)/shard_map/load_kernel/pallas_call | solution.py:62
  14.2 1.3 %collective-permute-done.1.refs_2_ = bf16[40,1280]{1,0:T(8,128)(2,1)S(1)} collective-permute-done((bf16[40,1280]{1,0:T(8,128)(2,1)S(1)}, bf16[40,1280]{1,0:T(8,128)(2,1)S(1)}, u32[]{:S(2)}, u32[]{:S(2)}) %collective-permute-start.1) | collective-permute-done | bytes 102432 | tf_op jit(solution)/shard_map/ppermute | solution.py:356
  15.5 0.0 collective-permute-done.2.refs_3_
  15.5 0.2 order_kernel.1
  15.7 1.5 %forward_kernel.4 = (f32[120,896]{1,0:T(8,128)S(1)}, bf16[120,896]{1,0:T(8,128)(2,1)S(1)}, f32[8,128]{1,0:T(8,128)S(1)}) custom-call(bf16[160,1280]{1,0:T(8,128)(2,1)S(1)} %get-tuple-element.74.refs_0_, bf16[1280,3456]{1,0:T(8,128)(2,1)S(1)} %get-tuple-element.75.refs_1_, bf16[1280,3456]{1,0:T(8,128)(2,1)S(1)} %get-tuple-element.76.refs_2_, ...), custom_call_target="tpu_custom_call" | custom-call | flops 1 | bytes 1 | tf_op jit(solution)/shard_map/forward_kernel/pallas_call | solution.py:62
  17.3 1.6 %collective-permute-start.5 = (bf16[120,896]{1,0:T(8,128)(2,1)S(1)}, bf16[120,896]{1,0:T(8,128)(2,1)S(1)}, u32[]{:S(2)}, u32[]{:S(2)}) collective-permute-start(bf16[120,896]{1,0:T(8,128)(2,1)S(1)} %get-tuple-element.85), channel_id=1, source_target_pairs={{0,8},{8,0},{16,24},{24,16},{1,9},{9,1},{17,25},{25,17},{2,10},{10... | collective-permute-start | bytes 645128 | tf_op jit(solution)/shard_map/ppermute | solution.py:356
  18.8 1.5 %forward_kernel.5 = (f32[120,896]{1,0:T(8,128)S(1)}, bf16[120,896]{1,0:T(8,128)(2,1)S(1)}, f32[8,128]{1,0:T(8,128)S(1)}) custom-call(bf16[160,1280]{1,0:T(8,128)(2,1)S(1)} %get-tuple-element.74.refs_0_, bf16[1280,3456]{1,0:T(8,128)(2,1)S(1)} %get-tuple-element.75.refs_1_, bf16[1280,3456]{1,0:T(8,128)(2,1)S(1)} %get-tuple-element.76.refs_2_, ...), custom_call_target="tpu_custom_call" | custom-call | flops 1 | bytes 1 | tf_op jit(solution)/shard_map/forward_kernel/pallas_call | solution.py:62
  20.3 1.6 %collective-permute-start.4 = (bf16[120,896]{1,0:T(8,128)(2,1)S(1)}, bf16[120,896]{1,0:T(8,128)(2,1)S(1)}, u32[]{:S(2)}, u32[]{:S(2)}) collective-permute-start(bf16[120,896]{1,0:T(8,128)(2,1)S(1)} %get-tuple-element.83), channel_id=1, source_target_pairs={{0,16},{8,24},{16,0},{24,8},{1,17},{9,25},{17,1},{25,9},{2,18},{10... | collective-permute-start | bytes 645128 | tf_op jit(solution)/shard_map/ppermute | solution.py:356
  21.9 1.5 %forward_kernel.6 = (f32[120,896]{1,0:T(8,128)S(1)}, bf16[120,896]{1,0:T(8,128)(2,1)S(1)}, f32[8,128]{1,0:T(8,128)S(1)}) custom-call(bf16[160,1280]{1,0:T(8,128)(2,1)S(1)} %get-tuple-element.74.refs_0_, bf16[1280,3456]{1,0:T(8,128)(2,1)S(1)} %get-tuple-element.75.refs_1_, bf16[1280,3456]{1,0:T(8,128)(2,1)S(1)} %get-tuple-element.76.refs_2_, ...), custom_call_target="tpu_custom_call" | custom-call | flops 1 | bytes 1 | tf_op jit(solution)/shard_map/forward_kernel/pallas_call | solution.py:62
  23.4 0.6 collective-permute-start.3
  24.0 1.4 %forward_kernel.7 = (f32[120,768]{1,0:T(8,128)S(1)}, bf16[120,768]{1,0:T(8,128)(2,1)S(1)}, f32[8,128]{1,0:T(8,128)S(1)}) custom-call(bf16[160,1280]{1,0:T(8,128)(2,1)S(1)} %get-tuple-element.74.refs_0_, bf16[1280,3456]{1,0:T(8,128)(2,1)S(1)} %get-tuple-element.75.refs_1_, bf16[1280,3456]{1,0:T(8,128)(2,1)S(1)} %get-tuple-element.76.refs_2_, ...), custom_call_target="tpu_custom_call" | custom-call | flops 1 | bytes 1 | tf_op jit(solution)/shard_map/forward_kernel/pallas_call | solution.py:62
  25.4 0.6 collective-permute-start.7
  26.0 0.1 halve_kernel.5
  26.1 1.3 %collective-permute-done.4.refs_1_ = bf16[120,896]{1,0:T(8,128)(2,1)S(1)} collective-permute-done((bf16[120,896]{1,0:T(8,128)(2,1)S(1)}, bf16[120,896]{1,0:T(8,128)(2,1)S(1)}, u32[]{:S(2)}, u32[]{:S(2)}) %collective-permute-start.4) | collective-permute-done | bytes 215072 | tf_op jit(solution)/shard_map/ppermute | solution.py:356
  27.4 0.1 halve_kernel.6
  27.5 0.3 collective-permute-start.10
  27.7 2.4 %collective-permute-start.9 = (bf16[60,896]{1,0:T(8,128)(2,1)S(1)}, bf16[60,896]{1,0:T(8,128)(2,1)S(1)}, u32[]{:S(2)}, u32[]{:S(2)}) collective-permute-start(bf16[60,896]{1,0:T(8,128)(2,1)S(1)} %get-tuple-element.98), channel_id=1, source_target_pairs={{0,16},{8,24},{16,0},{24,8},{1,17},{9,25},{17,1},{25,9},{2,18},{10... | collective-permute-start | bytes 322568 | tf_op jit(solution)/shard_map/ppermute | solution.py:356
  30.1 0.0 collective-permute-done.3.refs_1_
  30.1 0.1 halve_kernel.7
  30.2 0.9 %collective-permute-start.6 = (bf16[60,896]{1,0:T(8,128)(2,1)S(1)}, bf16[60,896]{1,0:T(8,128)(2,1)S(1)}, u32[]{:S(2)}, u32[]{:S(2)}) collective-permute-start(bf16[60,896]{1,0:T(8,128)(2,1)S(1)} %get-tuple-element.91), channel_id=1, source_target_pairs={{0,16},{8,24},{16,0},{24,8},{1,17},{9,25},{17,1},{25,9},{2,18},{10... | collective-permute-start | bytes 322568 | tf_op jit(solution)/shard_map/ppermute | solution.py:356
  31.0 2.0 %collective-permute-done.7.refs_1_ = bf16[120,768]{1,0:T(8,128)(2,1)S(1)} collective-permute-done((bf16[120,768]{1,0:T(8,128)(2,1)S(1)}, bf16[120,768]{1,0:T(8,128)(2,1)S(1)}, u32[]{:S(2)}, u32[]{:S(2)}) %collective-permute-start.7) | collective-permute-done | bytes 184352 | tf_op jit(solution)/shard_map/ppermute | solution.py:356
  33.1 0.1 halve_kernel.8
  33.1 0.4 collective-permute-start.8
  33.5 0.0 collective-permute-done.10.refs_1_
  33.5 0.1 middle_kernel.4
  33.6 1.6 %collective-permute-start.14 = (bf16[60,896]{1,0:T(8,128)(2,1)S(1)}, bf16[60,896]{1,0:T(8,128)(2,1)S(1)}, u32[]{:S(2)}, u32[]{:S(2)}) collective-permute-start(bf16[60,896]{1,0:T(8,128)(2,1)S(1)} %get-tuple-element.108.refs_0_), channel_id=1, source_target_pairs={{0,16},{8,24},{16,0},{24,8},{1,17},{9,25},{17,1},{25,9},{2,18},{10... | collective-permute-start | bytes 322568 | tf_op jit(solution)/shard_map/ppermute | solution.py:356
  35.3 0.0 collective-permute-done.9.refs_1_
  35.3 0.1 middle_kernel.5
  35.3 0.9 %collective-permute-start.13 = (bf16[60,896]{1,0:T(8,128)(2,1)S(1)}, bf16[60,896]{1,0:T(8,128)(2,1)S(1)}, u32[]{:S(2)}, u32[]{:S(2)}) collective-permute-start(bf16[60,896]{1,0:T(8,128)(2,1)S(1)} %get-tuple-element.107.refs_0_), channel_id=1, source_target_pairs={{0,8},{8,0},{16,24},{24,16},{1,9},{9,1},{17,25},{25,17},{2,10},{10... | collective-permute-start | bytes 322568 | tf_op jit(solution)/shard_map/ppermute | solution.py:356
  36.3 2.1 %collective-permute-done.8.refs_1_ = bf16[60,768]{1,0:T(8,128)(2,1)S(1)} collective-permute-done((bf16[60,768]{1,0:T(8,128)(2,1)S(1)}, bf16[60,768]{1,0:T(8,128)(2,1)S(1)}, u32[]{:S(2)}, u32[]{:S(2)}) %collective-permute-start.8) | collective-permute-done | bytes 92192 | tf_op jit(solution)/shard_map/ppermute | solution.py:356
  38.4 0.1 middle_kernel.6
  38.5 0.0 collective-permute-done.6.refs_1_
  38.5 0.1 middle_kernel.7
  38.6 0.4 collective-permute-start.11
  38.9 1.4 %collective-permute-start.12 = (bf16[60,768]{1,0:T(8,128)(2,1)S(1)}, bf16[60,768]{1,0:T(8,128)(2,1)S(1)}, u32[]{:S(2)}, u32[]{:S(2)}) collective-permute-start(bf16[60,768]{1,0:T(8,128)(2,1)S(1)} %get-tuple-element.106.refs_0_), channel_id=1, source_target_pairs={{0,16},{8,24},{16,0},{24,8},{1,17},{9,25},{17,1},{25,9},{2,18},{10... | collective-permute-start | bytes 276488 | tf_op jit(solution)/shard_map/ppermute | solution.py:356
  40.4 0.5 collective-permute-done.13.refs_1_
  40.8 1.7 %collective-permute-start.17 = (bf16[120,896]{1,0:T(8,128)(2,1)S(1)}, bf16[120,896]{1,0:T(8,128)(2,1)S(1)}, u32[]{:S(2)}, u32[]{:S(2)}) collective-permute-start(bf16[120,896]{1,0:T(8,128)(2,1)S(1)} %get-tuple-element.115.refs_0_), channel_id=1, source_target_pairs={{0,16},{8,24},{16,0},{24,8},{1,17},{9,25},{17,1},{25,9},{2,18},{10... | collective-permute-start | bytes 645128 | tf_op jit(solution)/shard_map/ppermute | solution.py:356
  42.5 1.1 %collective-permute-start.18 = (bf16[120,896]{1,0:T(8,128)(2,1)S(1)}, bf16[120,896]{1,0:T(8,128)(2,1)S(1)}, u32[]{:S(2)}, u32[]{:S(2)}) collective-permute-start(bf16[120,896]{1,0:T(8,128)(2,1)S(1)} %get-tuple-element.116.refs_2_), channel_id=1, source_target_pairs={{0,8},{8,0},{16,24},{24,16},{1,9},{9,1},{17,25},{25,17},{2,10},{10... | collective-permute-start | bytes 645128 | tf_op jit(solution)/shard_map/ppermute | solution.py:356
  43.7 0.7 collective-permute-done.12.refs_1_
  44.4 0.4 collective-permute-done.11.refs_1_
  44.8 1.3 %collective-permute-start.15 = (bf16[120,896]{1,0:T(8,128)(2,1)S(1)}, bf16[120,896]{1,0:T(8,128)(2,1)S(1)}, u32[]{:S(2)}, u32[]{:S(2)}) collective-permute-start(bf16[120,896]{1,0:T(8,128)(2,1)S(1)} %get-tuple-element.113.refs_0_), channel_id=1, source_target_pairs={{0,16},{8,24},{16,0},{24,8},{1,17},{9,25},{17,1},{25,9},{2,18},{10... | collective-permute-start | bytes 645128 | tf_op jit(solution)/shard_map/ppermute | solution.py:356
  46.0 1.2 %collective-permute-start.16 = (bf16[120,768]{1,0:T(8,128)(2,1)S(1)}, bf16[120,768]{1,0:T(8,128)(2,1)S(1)}, u32[]{:S(2)}, u32[]{:S(2)}) collective-permute-start(bf16[120,768]{1,0:T(8,128)(2,1)S(1)} %get-tuple-element.114.refs_2_), channel_id=1, source_target_pairs={{0,8},{8,0},{16,24},{24,16},{1,9},{9,1},{17,25},{25,17},{2,10},{10... | collective-permute-start | bytes 552968 | tf_op jit(solution)/shard_map/ppermute | solution.py:356
  47.3 1.1 %collective-permute-done.18.refs_3_ = bf16[120,896]{1,0:T(8,128)(2,1)S(1)} collective-permute-done((bf16[120,896]{1,0:T(8,128)(2,1)S(1)}, bf16[120,896]{1,0:T(8,128)(2,1)S(1)}, u32[]{:S(2)}, u32[]{:S(2)}) %collective-permute-start.18) | collective-permute-done | bytes 215072 | tf_op jit(solution)/shard_map/ppermute | solution.py:356
  48.4 0.1 stack_kernel.2
  48.5 0.1 collective-permute-start.21
  48.6 2.9 %input_grad_kernel.2 = (f32[80,1280]{1,0:T(8,128)S(1)}, f32[8,128]{1,0:T(8,128)S(1)}) custom-call(bf16[240,1792]{1,0:T(8,128)(2,1)S(1)} %get-tuple-element.118.refs_0_.refs_2_, bf16[1280,3456]{1,0:T(8,128)(2,1)S(1)} %get-tuple-element.75.refs_1_, bf16[1280,3456]{1,0:T(8,128)(2,1)S(1)} %get-tuple-element.76.refs_2_, f32[8,128]{1,0:T(8,128)S(1)} %get-tuple-element.119.refs_3_), custom_call_target="tpu_custom_call" | custom-call | flops 1 | bytes 1 | tf_op jit(solution)/shard_map/input_grad_kernel/pallas_call | solution.py:62
  51.5 0.1 collective-permute-done.16.refs_3_
  51.6 0.1 stack_kernel.3
  51.7 0.5 collective-permute-start.22
  52.2 0.1 collective-permute-start.20
  52.3 2.7 %input_grad_kernel.3 = (f32[80,1280]{1,0:T(8,128)S(1)}, f32[8,128]{1,0:T(8,128)S(1)}) custom-call(bf16[240,1664]{1,0:T(8,128)(2,1)S(1)} %get-tuple-element.121.refs_0_.refs_2_, bf16[1280,3456]{1,0:T(8,128)(2,1)S(1)} %get-tuple-element.75.refs_1_, bf16[1280,3456]{1,0:T(8,128)(2,1)S(1)} %get-tuple-element.76.refs_2_, ...), custom_call_target="tpu_custom_call" | custom-call | flops 1 | bytes 1 | tf_op jit(solution)/shard_map/input_grad_kernel/pallas_call | solution.py:62
  55.0 0.1 last_kernel.1
  55.1 3.1 %collective-permute-start.19 = (bf16[40,1280]{1,0:T(8,128)(2,1)S(1)}, bf16[40,1280]{1,0:T(8,128)(2,1)S(1)}, u32[]{:S(2)}, u32[]{:S(2)}) collective-permute-start(bf16[40,1280]{1,0:T(8,128)(2,1)S(1)} %get-tuple-element.127), channel_id=1, source_target_pairs={{0,4},{2,6},{4,0},{6,2},{1,5},{3,7},{5,1},{7,3},{8,12},{10,14},{12... | collective-permute-start | bytes 307208 | tf_op jit(solution)/shard_map/ppermute | solution.py:356
  58.3 0.3 factors_kernel.1
  58.5 5.4 %weight_grad_kernel.2 = (bf16[1280,3456]{1,0:T(8,128)(2,1)}, bf16[1280,3456]{1,0:T(8,128)(2,1)}, bf16[3456,1280]{1,0:T(8,128)(2,1)}, f32[8,128]{1,0:T(8,128)S(1)}) custom-call(bf16[1280,160]{1,0:T(8,128)(2,1)S(1)} %get-tuple-element.129.refs_0_, bf16[160,1280]{1,0:T(8,128)(2,1)S(1)} %get-tuple-element.130.refs_1_, ...), custom_call_target="tpu_custom_call" | custom-call | flops 1 | bytes 1 | tf_op jit(solution)/shard_map/weight_grad_kernel/pallas_call | solution.py:62
  64.0 0.7 collective-permute-start.23
  64.7 5.1 %weight_grad_kernel.3 = (bf16[1280,3456]{1,0:T(8,128)(2,1)}, bf16[1280,3456]{1,0:T(8,128)(2,1)}, bf16[3456,1280]{1,0:T(8,128)(2,1)}, f32[8,128]{1,0:T(8,128)S(1)}) custom-call(bf16[1280,160]{1,0:T(8,128)(2,1)S(1)} %get-tuple-element.129.refs_0_, ...), custom_call_target="tpu_custom_call", output_to_operand_aliasing={{0}: (5, {}), {1}: (6, {}), {2}: (7, {})} | custom-call | flops 1 | bytes 1 | tf_op jit(solution)/shard_map/weight_grad_kernel/pallas_call | solution.py:62
  69.8 0.6 total_kernel.1
  (20 shorter events, 0.2 us)
Async XLA Ops:
  0.6 15.1 %slice-start = ((s8[8847360]{0:T(1024)(128)(4,1)}), s8[4194304]{0:T(1024)(128)(4,1)S(1)}, s32[]{:S(2)}) async-start(s8[8847360]{0:T(1024)(128)(4,1)} %bitcast), calls=%async_computation | async-start | bytes 8388608
  1.7 14.0 %slice-start.1 = ((s8[8847360]{0:T(1024)(128)(4,1)}), s8[4194304]{0:T(1024)(128)(4,1)S(1)}, s32[]{:S(2)}) async-start(s8[8847360]{0:T(1024)(128)(4,1)} %bitcast), calls=%async_computation.1 | async-start | bytes 8388608
  1.7 14.0 %slice-start.2 = ((s8[8847360]{0:T(1024)(128)(4,1)}), s8[458752]{0:T(1024)(128)(4,1)S(1)}, s32[]{:S(2)}) async-start(s8[8847360]{0:T(1024)(128)(4,1)} %bitcast), calls=%async_computation.2 | async-start | bytes 917504
  1.7 12.5 %collective-permute-start = (bf16[40,1280]{1,0:T(8,128)(2,1)S(1)}, bf16[40,1280]{1,0:T(8,128)(2,1)S(1)}, u32[]{:S(2)}, u32[]{:S(2)}) collective-permute-start(bf16[40,1280]{1,0:T(8,128)(2,1)S(1)} %pad_maximum_fusion.refs_0_), channel_id=1, source_target_pairs={{0,2},{2,0},{4,6},{6,4},{1,3},{3,1},{5,7},{7,5},{8,10},{10,8},{12,... | collective-permute-start | bytes 307208 | tf_op jit(solution)/shard_map/ppermute | solution.py:356
  4.8 10.7 %collective-permute-start.1 = (bf16[40,1280]{1,0:T(8,128)(2,1)S(1)}, bf16[40,1280]{1,0:T(8,128)(2,1)S(1)}, u32[]{:S(2)}, u32[]{:S(2)}) collective-permute-start(bf16[40,1280]{1,0:T(8,128)(2,1)S(1)} %pad_maximum_fusion.refs_0_), channel_id=1, source_target_pairs={{0,4},{2,6},{4,0},{6,2},{1,5},{3,7},{5,1},{7,3},{8,12},{10,14},{12... | collective-permute-start | bytes 307208 | tf_op jit(solution)/shard_map/ppermute | solution.py:356
  7.4 8.1 %collective-permute-start.2 = (bf16[40,1280]{1,0:T(8,128)(2,1)S(1)}, bf16[40,1280]{1,0:T(8,128)(2,1)S(1)}, u32[]{:S(2)}, u32[]{:S(2)}) collective-permute-start(bf16[40,1280]{1,0:T(8,128)(2,1)S(1)} %pad_maximum_fusion.refs_0_), channel_id=1, source_target_pairs={{0,6},{2,4},{4,2},{6,0},{1,7},{3,5},{5,3},{7,1},{8,14},{10,12},{12... | collective-permute-start | bytes 307208 | tf_op jit(solution)/shard_map/ppermute | solution.py:356
  17.3 8.7 %collective-permute-start.5 = (bf16[120,896]{1,0:T(8,128)(2,1)S(1)}, bf16[120,896]{1,0:T(8,128)(2,1)S(1)}, u32[]{:S(2)}, u32[]{:S(2)}) collective-permute-start(bf16[120,896]{1,0:T(8,128)(2,1)S(1)} %get-tuple-element.85), channel_id=1, source_target_pairs={{0,8},{8,0},{16,24},{24,16},{1,9},{9,1},{17,25},{25,17},{2,10},{10... | collective-permute-start | bytes 645128 | tf_op jit(solution)/shard_map/ppermute | solution.py:356
  20.3 7.0 %collective-permute-start.4 = (bf16[120,896]{1,0:T(8,128)(2,1)S(1)}, bf16[120,896]{1,0:T(8,128)(2,1)S(1)}, u32[]{:S(2)}, u32[]{:S(2)}) collective-permute-start(bf16[120,896]{1,0:T(8,128)(2,1)S(1)} %get-tuple-element.83), channel_id=1, source_target_pairs={{0,16},{8,24},{16,0},{24,8},{1,17},{9,25},{17,1},{25,9},{2,18},{10... | collective-permute-start | bytes 645128 | tf_op jit(solution)/shard_map/ppermute | solution.py:356
  23.4 6.6 %collective-permute-start.3 = (bf16[120,896]{1,0:T(8,128)(2,1)S(1)}, bf16[120,896]{1,0:T(8,128)(2,1)S(1)}, u32[]{:S(2)}, u32[]{:S(2)}) collective-permute-start(bf16[120,896]{1,0:T(8,128)(2,1)S(1)} %get-tuple-element.81), channel_id=1, source_target_pairs={{0,8},{8,0},{16,24},{24,16},{1,9},{9,1},{17,25},{25,17},{2,10},{10... | collective-permute-start | bytes 645128 | tf_op jit(solution)/shard_map/ppermute | solution.py:356
  25.4 7.6 %collective-permute-start.7 = (bf16[120,768]{1,0:T(8,128)(2,1)S(1)}, bf16[120,768]{1,0:T(8,128)(2,1)S(1)}, u32[]{:S(2)}, u32[]{:S(2)}) collective-permute-start(bf16[120,768]{1,0:T(8,128)(2,1)S(1)} %get-tuple-element.93), channel_id=1, source_target_pairs={{0,16},{8,24},{16,0},{24,8},{1,17},{9,25},{17,1},{25,9},{2,18},{10... | collective-permute-start | bytes 552968 | tf_op jit(solution)/shard_map/ppermute | solution.py:356
  27.5 6.1 %collective-permute-start.10 = (bf16[60,896]{1,0:T(8,128)(2,1)S(1)}, bf16[60,896]{1,0:T(8,128)(2,1)S(1)}, u32[]{:S(2)}, u32[]{:S(2)}) collective-permute-start(bf16[60,896]{1,0:T(8,128)(2,1)S(1)} %get-tuple-element.100), channel_id=1, source_target_pairs={{0,8},{8,0},{16,24},{24,16},{1,9},{9,1},{17,25},{25,17},{2,10},{10... | collective-permute-start | bytes 322568 | tf_op jit(solution)/shard_map/ppermute | solution.py:356
  27.7 7.5 %collective-permute-start.9 = (bf16[60,896]{1,0:T(8,128)(2,1)S(1)}, bf16[60,896]{1,0:T(8,128)(2,1)S(1)}, u32[]{:S(2)}, u32[]{:S(2)}) collective-permute-start(bf16[60,896]{1,0:T(8,128)(2,1)S(1)} %get-tuple-element.98), channel_id=1, source_target_pairs={{0,16},{8,24},{16,0},{24,8},{1,17},{9,25},{17,1},{25,9},{2,18},{10... | collective-permute-start | bytes 322568 | tf_op jit(solution)/shard_map/ppermute | solution.py:356
  30.2 8.3 %collective-permute-start.6 = (bf16[60,896]{1,0:T(8,128)(2,1)S(1)}, bf16[60,896]{1,0:T(8,128)(2,1)S(1)}, u32[]{:S(2)}, u32[]{:S(2)}) collective-permute-start(bf16[60,896]{1,0:T(8,128)(2,1)S(1)} %get-tuple-element.91), channel_id=1, source_target_pairs={{0,16},{8,24},{16,0},{24,8},{1,17},{9,25},{17,1},{25,9},{2,18},{10... | collective-permute-start | bytes 322568 | tf_op jit(solution)/shard_map/ppermute | solution.py:356
  33.1 5.3 %collective-permute-start.8 = (bf16[60,768]{1,0:T(8,128)(2,1)S(1)}, bf16[60,768]{1,0:T(8,128)(2,1)S(1)}, u32[]{:S(2)}, u32[]{:S(2)}) collective-permute-start(bf16[60,768]{1,0:T(8,128)(2,1)S(1)} %get-tuple-element.96), channel_id=1, source_target_pairs={{0,8},{8,0},{16,24},{24,16},{1,9},{9,1},{17,25},{25,17},{2,10},{10... | collective-permute-start | bytes 276488 | tf_op jit(solution)/shard_map/ppermute | solution.py:356
  33.6 6.7 %collective-permute-start.14 = (bf16[60,896]{1,0:T(8,128)(2,1)S(1)}, bf16[60,896]{1,0:T(8,128)(2,1)S(1)}, u32[]{:S(2)}, u32[]{:S(2)}) collective-permute-start(bf16[60,896]{1,0:T(8,128)(2,1)S(1)} %get-tuple-element.108.refs_0_), channel_id=1, source_target_pairs={{0,16},{8,24},{16,0},{24,8},{1,17},{9,25},{17,1},{25,9},{2,18},{10... | collective-permute-start | bytes 322568 | tf_op jit(solution)/shard_map/ppermute | solution.py:356
  35.3 5.5 %collective-permute-start.13 = (bf16[60,896]{1,0:T(8,128)(2,1)S(1)}, bf16[60,896]{1,0:T(8,128)(2,1)S(1)}, u32[]{:S(2)}, u32[]{:S(2)}) collective-permute-start(bf16[60,896]{1,0:T(8,128)(2,1)S(1)} %get-tuple-element.107.refs_0_), channel_id=1, source_target_pairs={{0,8},{8,0},{16,24},{24,16},{1,9},{9,1},{17,25},{25,17},{2,10},{10... | collective-permute-start | bytes 322568 | tf_op jit(solution)/shard_map/ppermute | solution.py:356
  38.6 6.2 %collective-permute-start.11 = (bf16[60,896]{1,0:T(8,128)(2,1)S(1)}, bf16[60,896]{1,0:T(8,128)(2,1)S(1)}, u32[]{:S(2)}, u32[]{:S(2)}) collective-permute-start(bf16[60,896]{1,0:T(8,128)(2,1)S(1)} %get-tuple-element.105.refs_0_), channel_id=1, source_target_pairs={{0,8},{8,0},{16,24},{24,16},{1,9},{9,1},{17,25},{25,17},{2,10},{10... | collective-permute-start | bytes 322568 | tf_op jit(solution)/shard_map/ppermute | solution.py:356
  38.9 5.4 %collective-permute-start.12 = (bf16[60,768]{1,0:T(8,128)(2,1)S(1)}, bf16[60,768]{1,0:T(8,128)(2,1)S(1)}, u32[]{:S(2)}, u32[]{:S(2)}) collective-permute-start(bf16[60,768]{1,0:T(8,128)(2,1)S(1)} %get-tuple-element.106.refs_0_), channel_id=1, source_target_pairs={{0,16},{8,24},{16,0},{24,8},{1,17},{9,25},{17,1},{25,9},{2,18},{10... | collective-permute-start | bytes 276488 | tf_op jit(solution)/shard_map/ppermute | solution.py:356
  40.8 6.4 %collective-permute-start.17 = (bf16[120,896]{1,0:T(8,128)(2,1)S(1)}, bf16[120,896]{1,0:T(8,128)(2,1)S(1)}, u32[]{:S(2)}, u32[]{:S(2)}) collective-permute-start(bf16[120,896]{1,0:T(8,128)(2,1)S(1)} %get-tuple-element.115.refs_0_), channel_id=1, source_target_pairs={{0,16},{8,24},{16,0},{24,8},{1,17},{9,25},{17,1},{25,9},{2,18},{10... | collective-permute-start | bytes 645128 | tf_op jit(solution)/shard_map/ppermute | solution.py:356
  42.5 5.9 %collective-permute-start.18 = (bf16[120,896]{1,0:T(8,128)(2,1)S(1)}, bf16[120,896]{1,0:T(8,128)(2,1)S(1)}, u32[]{:S(2)}, u32[]{:S(2)}) collective-permute-start(bf16[120,896]{1,0:T(8,128)(2,1)S(1)} %get-tuple-element.116.refs_2_), channel_id=1, source_target_pairs={{0,8},{8,0},{16,24},{24,16},{1,9},{9,1},{17,25},{25,17},{2,10},{10... | collective-permute-start | bytes 645128 | tf_op jit(solution)/shard_map/ppermute | solution.py:356
  44.8 6.8 %collective-permute-start.15 = (bf16[120,896]{1,0:T(8,128)(2,1)S(1)}, bf16[120,896]{1,0:T(8,128)(2,1)S(1)}, u32[]{:S(2)}, u32[]{:S(2)}) collective-permute-start(bf16[120,896]{1,0:T(8,128)(2,1)S(1)} %get-tuple-element.113.refs_0_), channel_id=1, source_target_pairs={{0,16},{8,24},{16,0},{24,8},{1,17},{9,25},{17,1},{25,9},{2,18},{10... | collective-permute-start | bytes 645128 | tf_op jit(solution)/shard_map/ppermute | solution.py:356
  46.0 5.5 %collective-permute-start.16 = (bf16[120,768]{1,0:T(8,128)(2,1)S(1)}, bf16[120,768]{1,0:T(8,128)(2,1)S(1)}, u32[]{:S(2)}, u32[]{:S(2)}) collective-permute-start(bf16[120,768]{1,0:T(8,128)(2,1)S(1)} %get-tuple-element.114.refs_2_), channel_id=1, source_target_pairs={{0,8},{8,0},{16,24},{24,16},{1,9},{9,1},{17,25},{25,17},{2,10},{10... | collective-permute-start | bytes 552968 | tf_op jit(solution)/shard_map/ppermute | solution.py:356
  48.5 10.0 %collective-permute-start.21 = (bf16[240,1792]{1,0:T(8,128)(2,1)S(1)}, bf16[240,1792]{1,0:T(8,128)(2,1)S(1)}, u32[]{:S(2)}, u32[]{:S(2)}) collective-permute-start(bf16[240,1792]{1,0:T(8,128)(2,1)S(1)} %get-tuple-element.118.refs_0_.refs_2_), channel_id=1, source_target_pairs={{0,1},{1,0},{2,3},{3,2},{4,5},{5,4},{6,7},{7,6},{8,9},{9,8},{10,11... | collective-permute-start | bytes 2580488 | tf_op jit(solution)/shard_map/ppermute | solution.py:356
  51.7 6.8 %collective-permute-start.22 = (bf16[240,1664]{1,0:T(8,128)(2,1)S(1)}, bf16[240,1664]{1,0:T(8,128)(2,1)S(1)}, u32[]{:S(2)}, u32[]{:S(2)}) collective-permute-start(bf16[240,1664]{1,0:T(8,128)(2,1)S(1)} %get-tuple-element.121.refs_0_.refs_2_), channel_id=1, source_target_pairs={{0,1},{1,0},{2,3},{3,2},{4,5},{5,4},{6,7},{7,6},{8,9},{9,8},{10,11... | collective-permute-start | bytes 2396168 | tf_op jit(solution)/shard_map/ppermute | solution.py:356
  52.2 6.1 %collective-permute-start.20 = (bf16[160,1280]{1,0:T(8,128)(2,1)S(1)}, bf16[160,1280]{1,0:T(8,128)(2,1)S(1)}, u32[]{:S(2)}, u32[]{:S(2)}) collective-permute-start(bf16[160,1280]{1,0:T(8,128)(2,1)S(1)} %get-tuple-element.74.refs_0_), channel_id=1, source_target_pairs={{0,1},{1,0},{2,3},{3,2},{4,5},{5,4},{6,7},{7,6},{8,9},{9,8},{10,11... | collective-permute-start | bytes 1228808 | tf_op jit(solution)/shard_map/ppermute | solution.py:356
  55.1 8.9 %collective-permute-start.19 = (bf16[40,1280]{1,0:T(8,128)(2,1)S(1)}, bf16[40,1280]{1,0:T(8,128)(2,1)S(1)}, u32[]{:S(2)}, u32[]{:S(2)}) collective-permute-start(bf16[40,1280]{1,0:T(8,128)(2,1)S(1)} %get-tuple-element.127), channel_id=1, source_target_pairs={{0,4},{2,6},{4,0},{6,2},{1,5},{3,7},{5,1},{7,3},{8,12},{10,14},{12... | collective-permute-start | bytes 307208 | tf_op jit(solution)/shard_map/ppermute | solution.py:356
  64.0 5.8 %collective-permute-start.23 = (bf16[20,1280]{1,0:T(8,128)(2,1)S(1)}, bf16[20,1280]{1,0:T(8,128)(2,1)S(1)}, u32[]{:S(2)}, u32[]{:S(2)}) collective-permute-start(bf16[20,1280]{1,0:T(8,128)(2,1)S(1)} %get-tuple-element.134), channel_id=1, source_target_pairs={{0,2},{2,0},{4,6},{6,4},{1,3},{3,1},{5,7},{7,5},{8,10},{10,8},{12,... | collective-permute-start | bytes 153608 | tf_op jit(solution)/shard_map/ppermute | solution.py:356
